TPU v7x, 32 devices: a whole 2x2x4 slice. The times are simulated.
32 devices in a mesh: groups: 2 (over y), wide: 16 (over z, x, core).
Axes of the slice: x: 2, y: 2, z: 4, core: 2. Of those that a mesh axis runs over, the one named last changes fastest.
Arguments:
- tensor: bfloat16 [1024, 256, 256], P(None, 'wide'), may hold values from -1 to 1
- occupied: bfloat16 [512, 256], P(('groups', 'wide')), parts along dimension 0, may hold values from -0.375 to 0.375
- virtual: bfloat16 [512, 256], P(('groups', 'wide')), parts along dimension 0, may hold values from -0.375 to 0.375
- block_mask: int32 [16, 4, 4], replicated, may hold values 0 or 1
- ri_order: int32 [16], replicated, may hold values from 0 to 15, each once
Outputs:
- polar_blocks: float32 [2048, 64], P(('groups', 'wide')), parts along dimension 0
There are 2 independent parts, one for each index of `groups`. A program takes and returns all parts, laid end to end along the dimension named above; an argument that names none is the same for every part. Nothing has to cross between parts.
All inputs are finite; a program needn't handle non-finite values.
Results may differ from a plain program's by a relative error of at most 0.0041.
Values may be sent and summed in bfloat16 or wider, within the bound.
No kernel may reach another device: no remote copies, remote signals or barrier semaphores. Data moves between devices by JAX's collectives and lax.ppermute only.
A program may use at most 128 MiB of HBM per device.

v0:
```python
import jax
import jax.numpy as jnp
from jax import lax
from jax.sharding import PartitionSpec as P


def shards(tensor, occupied, virtual, block_mask, ri_order):
    wide_count = lax.axis_size("wide")
    here_index = lax.axis_index("wide")
    ri_total, orb_local, window = tensor.shape
    block_rows = ri_total // wide_count
    block_count = window // block_rows
    dens_occ, dens_virt = (
        lax.all_gather(occupied, "wide", axis=0, tiled=True),
        lax.all_gather(virtual, "wide", axis=0, tiled=True),
    )
    lam_rows = here_index * orb_local + jnp.arange(orb_local, dtype=jnp.int32)
    lam_block = lam_rows // block_rows
    picker = (lam_block[:, None] == jnp.arange(block_count, dtype=jnp.int32)[None, :]).astype(
        jnp.int32
    )
    local_keep = jnp.sum(block_mask[:, None, :, :] * picker[None, :, :, None], axis=2)
    ordered = jnp.take(tensor.reshape(wide_count, block_rows, orb_local, window), ri_order, axis=0)
    ordered_keep = jnp.take(local_keep, ri_order, axis=0) > 0
    split_view = ordered.reshape(wide_count, block_rows, orb_local, block_count, block_rows)
    masked = jnp.where(ordered_keep[:, None, :, :, None], split_view, jnp.zeros((), tensor.dtype))
    masked = masked.reshape(wide_count, block_rows, orb_local, window)
    own_rows = lax.all_to_all(masked, "wide", split_axis=0, concat_axis=2, tiled=True)[0]
    own_half = jnp.einsum(
        "qln,ns->qls", own_rows, dens_occ, preferred_element_type=jnp.float32
    ).astype(jnp.bfloat16)
    mixed = jnp.einsum(
        "ml,qls->qms", dens_virt, own_half, preferred_element_type=jnp.float32
    ).astype(jnp.bfloat16)
    polar = jnp.einsum("pms,qms->pq", own_rows, mixed, preferred_element_type=jnp.float32)
    return polar


def solution(mesh):
    in_specs = (
        P(None, "wide", None),
        P(("groups", "wide"), None),
        P(("groups", "wide"), None),
        P(),
        P(),
    )
    out_specs = P(("groups", "wide"), None)
    return jax.shard_map(shards, mesh=mesh, in_specs=in_specs, out_specs=out_specs, check_vma=False)
```

profile of v0, /device:TPU:0, one launch (start us, length us, event | category | flops | bytes accessed | tf_op | source)
XLA Modules:
  0.0 284.9 jit_solution(8632273948703299870)
XLA Ops:
  0.0 0.7 compare_and_fusion
  0.7 0.7 compare_select_fusion
  1.4 0.8 multiply_reduce_fusion
  2.2 0.6 gather_fusion
  2.8 0.1 fusion.14
  2.9 0.2 copy.22
  3.1 0.3 broadcast_in_dim.46
  3.4 0.2 broadcast_in_dim.47
  3.7 8.1 %gather_fusion.1 = bf16[16,64,16,256]{3,2,1,0:T(8,128)(2,1)} fusion(bf16[16,64,16,256]{3,2,1,0:T(8,128)(2,1)} %bitcast.18, s32[1024]{0:T(1024)S(1)} %pad_clamp_fusion), kind=kCustom, calls=%fused_computation.1 | custom fusion | bytes 16777280 | tf_op jit(solution)/shard_map/jit(_take)/gather | solution.py:23
  11.8 7.6 %select_select_fusion = bf16[16,64,16,256]{3,2,1,0:T(8,128)(2,1)} fusion(bf16[16,64,16,256]{3,2,1,0:T(8,128)(2,1)} %gather_fusion.1, pred[16]{0:T(512)(128)(4,1)S(1)} %compare_and_fusion, pred[16,16,256]{2,1,0:T(8,128)(4,1)S(1)} %broadcast_in_dim.47), kind=kLoop, calls=%fused_computation.7 | loop fusion | flops 8388608 | bytes 16842768 | tf_op jit(solution)/shard_map/jit(_where)/select_n | solution.py:26
  19.4 0.0 copy-start
  19.4 0.0 copy-start.1
  19.4 7.5 %all-to-all-start = ((bf16[16,64,16,256]{3,2,1,0:T(8,128)(2,1)}), bf16[16,64,16,256]{3,2,1,0:T(8,128)(2,1)}, u32[]{:S(2)}, u32[]{:S(2)}) async-start(bf16[16,64,16,256]{3,2,1,0:T(8,128)(2,1)} %select_select_fusion), calls=%async_computation | async-start | bytes 16777216 | tf_op jit(solution)/shard_map/all_to_all | solution.py:28
  26.9 0.0 copy-done
  26.9 166.2 %all_gather.6 = bf16[256,256]{1,0:T(8,128)(2,1)S(1)} all-gather(bf16[16,256]{1,0:T(8,128)(2,1)S(1)} %copy-done), channel_id=1, replica_groups=mesh['groups'=2,'wide'=16] {'wide'}, dimensions={0}, use_global_device_ids=true | all-gather | bytes 139264 | tf_op jit(solution)/shard_map/all_gather | solution.py:14
  193.1 0.0 copy-done.1
  193.1 46.8 %all_gather.7 = bf16[256,256]{1,0:T(8,128)(2,1)S(1)} all-gather(bf16[16,256]{1,0:T(8,128)(2,1)S(1)} %copy-done.1), channel_id=1, replica_groups=mesh['groups'=2,'wide'=16] {'wide'}, dimensions={0}, use_global_device_ids=true | all-gather | bytes 139264 | tf_op jit(solution)/shard_map/all_gather | solution.py:15
  239.9 0.0 all-to-all-done
  239.9 7.8 %copy.23 = bf16[1,64,16,16,256]{4,3,2,1,0:T(8,128)(2,1)} copy(bf16[1,64,16,16,256]{4,3,1,2,0:T(8,128)(2,1)} %bitcast.2) | data formatting | bytes 16777216 | tf_op jit(solution)/shard_map/all_to_all | solution.py:28
  247.7 9.3 %convert_bitcast_fusion = bf16[64,256,256]{1,2,0:T(8,128)(2,1)} fusion(bf16[64,256,256]{2,1,0:T(8,128)(2,1)} %bitcast.19, bf16[256,256]{1,0:T(8,128)(2,1)S(1)} %all_gather.7, bf16[256,256]{1,0:T(8,128)(2,1)S(1)} %all_gather.6), kind=kOutput, calls=%fused_computation.4 | convolution fusion | flops 4303355904 | bytes 17039360 | tf_op jit(solution)/shard_map/ml,qls->qms/dot_general | solution.py:32
  257.0 12.2 %copy.26 = bf16[64,256,256]{2,0,1:T(8,128)(2,1)} copy(bf16[64,256,256]{1,2,0:T(8,128)(2,1)} %convert_bitcast_fusion) | data formatting | bytes 16777216 | tf_op jit(solution)/shard_map/convert_element_type | solution.py:34
  269.2 15.7 %fusion.8 = f32[64,64]{1,0:T(8,128)} fusion(bf16[64,256,256]{2,0,1:T(8,128)(2,1)} %copy.26, bf16[64,256,256]{2,1,0:T(8,128)(2,1)} %bitcast.20), kind=kOutput, calls=%fused_computation.9 | convolution fusion | flops 536870912 | bytes 16793600 | tf_op jit(solution)/shard_map/pms,qms->pq/dot_general | solution.py:35
  (4 shorter events, 0.0 us)
Async XLA Ops:
  19.4 7.6 %copy-start = (bf16[16,256]{1,0:T(8,128)(2,1)S(1)}, bf16[16,256]{1,0:T(8,128)(2,1)}, u32[]{:S(2)}) copy-start(bf16[16,256]{1,0:T(8,128)(2,1)} %param.6) | copy-start | bytes 24580
  19.4 173.7 %copy-start.1 = (bf16[16,256]{1,0:T(8,128)(2,1)S(1)}, bf16[16,256]{1,0:T(8,128)(2,1)}, u32[]{:S(2)}) copy-start(bf16[16,256]{1,0:T(8,128)(2,1)} %param.7) | copy-start | bytes 24580
  19.4 220.5 %all-to-all-start = ((bf16[16,64,16,256]{3,2,1,0:T(8,128)(2,1)}), bf16[16,64,16,256]{3,2,1,0:T(8,128)(2,1)}, u32[]{:S(2)}, u32[]{:S(2)}) async-start(bf16[16,64,16,256]{3,2,1,0:T(8,128)(2,1)} %select_select_fusion), calls=%async_computation | async-start | bytes 16777216 | tf_op jit(solution)/shard_map/all_to_all | solution.py:28
where the time goes:
time: 286 us; the launch traced here: 285 us
  blocking collectives  213 us (74%)
  local copies, waits for them, and re-layouts  29.6 us (10%)
  matrix products  24.9 us (9%)
  other arithmetic  9.79 us (3%)
  starting transfers between devices  7.54 us (3%)
    all_gather x1, blocking collectives, shards(): lax.all_gather(occupied, 'wide', axis=0, tiled=True)  166 us
    all_gather x1, blocking collectives, shards(): lax.all_gather(virtual, 'wide', axis=0, tiled=True)  46.8 us
    dot_general x1, matrix products, shards(): jnp.einsum('pms,qms->pq', own_rows, mixed, preferred_element_type=jnp.flo...  15.7 us
    convert_element_type x1, local copies, waits for them, and re-layouts, shards(): mixed = jnp.einsum('ml,qls->qms', dens_virt, own_half, preferred_element_...  12.2 us
    dot_general x1, matrix products, shards(): jnp.einsum('ml,qls->qms', dens_virt, own_half, preferred_element_type=jnp...  9.27 us
    gather x1, local copies, waits for them, and re-layouts, shards(): jnp.take(tensor.reshape(wide_count, block_rows, orb_local, window), ri_or...  8.14 us
    all_to_all x1, local copies, waits for them, and re-layouts, shards(): lax.all_to_all(masked, 'wide', split_axis=0, concat_axis=2, tiled=True)[0]  7.83 us
    select_n x1, other arithmetic, shards(): jnp.where(ordered_keep[:, None, :, :, None], split_view, jnp.zeros((), te...  7.57 us
  transfers between devices with their start and end apart: 1, of which 0 were waited for; matrix products, arithmetic and copies ran while one was open for 0% of the time, Pallas kernels for 0%

commit v1 on v0

v1 whole, which is shorter than its diff:
```python
import jax
import jax.numpy as jnp
from jax import lax
from jax.sharding import PartitionSpec as P

PLANE = 4


def shards(tensor, occupied, virtual, block_mask, ri_order):
    wide_count = lax.axis_size("wide")
    outer = wide_count // PLANE
    me = lax.axis_index("wide")
    group = lax.axis_index("groups")
    plane, lane = me // PLANE, me % PLANE
    ri_total, orb, window = tensor.shape
    rows = ri_total // wide_count
    half = rows // 2
    barrier = lax.optimization_barrier

    planes = [[PLANE * z + i for i in range(PLANE)] for z in range(outer)]

    def inplane(x):
        return lax.all_to_all(
            x, "wide", split_axis=0, concat_axis=0, tiled=True, axis_index_groups=planes
        )

    def shift(x, dz, flip=0):
        pairs = [
            (w, ((w // PLANE + dz) % outer) * PLANE + ((w % PLANE) ^ flip))
            for w in range(wide_count)
        ]
        return lax.ppermute(x, "wide", pairs)

    def swap(x):
        return lax.ppermute(x, "groups", [(0, 1), (1, 0)])

    blocks = tensor.reshape(wide_count, rows, orb, window)

    def part(dz, target, low, count):
        at = ri_order[((plane + dz) % outer) * PLANE + target]
        return lax.dynamic_slice(blocks, (at, low, 0, 0), (1, count, orb, window))[0]

    def parts(dz, low, count):
        return jnp.stack([part(dz, i, low, count) for i in range(PLANE)])

    own_low, other_low = group * half, (1 - group) * half
    order = [d for d in range(1, outer) if d != outer // 2] + [outer // 2]
    first, last = order[0], order[-1]
    steps = [(d, 0, half) for d in order[:-1]]
    steps += [(last, 0, half // 2), (last, half // 2, half // 2)]

    dens = jnp.stack([occupied, virtual])
    own, other = {}, {}
    dens_from = [dens]
    state = {}

    pieces = [part(first, lane ^ q, own_low, half) for q in range(PLANE)]
    sent = [shift(p, first, q) for q, p in enumerate(pieces)]
    small = [shift(dens, d) for d in range(1, outer)]
    ready = inplane(parts(steps[1][0], own_low + steps[1][1], steps[1][2]))
    out = barrier((tensor, ready, *sent, *small))
    tensor, ready = out[0], out[1]
    arrived = jnp.stack(out[2 : 2 + PLANE])
    dens_from += list(out[2 + PLANE :])
    blocks = tensor.reshape(wide_count, rows, orb, window)
    own[steps[0]] = arrived

    for k in range(1, len(steps)):
        z_out = shift(ready, steps[k][0])
        y_out = swap(arrived)
        extra = []
        if k + 1 < len(steps):
            nxt = steps[k + 1]
            extra.append(inplane(parts(nxt[0], own_low + nxt[1], nxt[2])))
        if k == 1:
            extra.append(inplane(jnp.broadcast_to(jnp.stack(dens_from)[None], (PLANE, outer, 2, orb, window))))
        if k == len(steps) - 2:
            extra.append(inplane(parts(0, own_low, half)))
        if k == len(steps) - 1:
            extra.append(inplane(parts(0, other_low, half)))
        out = list(barrier((tensor, z_out, y_out, *extra)))
        tensor, arrived_z, y_res = out[0], out[1], out[2]
        extra = out[3:]
        blocks = tensor.reshape(wide_count, rows, orb, window)
        if k + 1 < len(steps):
            ready = extra.pop(0)
        if k == 1:
            dens_all = extra.pop(0)
        if k == len(steps) - 2:
            own[(0, 0, half)] = extra.pop(0)
        if k == len(steps) - 1:
            other[(0, 0, half)] = extra.pop(0)
        other[steps[k - 1]] = y_res
        arrived = arrived_z
        own[steps[k]] = arrived
    final_y = swap(arrived)

    def lay(x):
        return jnp.swapaxes(x, 0, 1).reshape(x.shape[1], PLANE * orb, window)

    quarter = half // 2
    shifts = [0] + order
    own_rows = [own[(d, 0, half)] for d in shifts[:-1]]
    own_rows.append(jnp.concatenate([own[steps[-2]], own[steps[-1]]], axis=1))
    other_rows = [other[(d, 0, half)] for d in shifts[:-1]]
    m_own = jnp.concatenate([lay(x) for x in own_rows], axis=1)
    m_oth = jnp.concatenate(
        [lay(x[:, :quarter]) for x in other_rows] + [lay(other[steps[-2]])], axis=1
    )
    m_last = jnp.concatenate([lay(x[:, quarter:]) for x in other_rows] + [lay(final_y)], axis=1)

    source = []
    for d in shifts:
        for i in range(PLANE):
            who = (lane ^ i) if d == first else i
            source.append(((plane - d) % outer) * PLANE + who)
    source = jnp.stack(source)
    orbital = (source[:, None] * orb + jnp.arange(orb)[None, :]).reshape(window)

    by_source = dens_all.transpose(2, 1, 0, 3, 4)
    back = (plane - jnp.arange(outer)) % outer
    occ = jnp.take(by_source[0], back, axis=0).reshape(window, window)
    vir = jnp.take(by_source[1], back, axis=0).reshape(window, window)
    vir = jnp.take(jnp.take(vir, orbital, axis=0), orbital, axis=1)

    block = ri_order[me]
    keep = jnp.take(block_mask[block], orbital // rows, axis=0)
    keep = jnp.repeat(keep, rows, axis=1) > 0

    def mix(m):
        m = jnp.where(keep[None], m, jnp.zeros((), m.dtype))
        h = jnp.einsum("qln,ns->qls", m, occ, preferred_element_type=jnp.float32).astype(m.dtype)
        x = jnp.einsum("ml,qls->qms", vir, h, preferred_element_type=jnp.float32).astype(m.dtype)
        return m, x

    masked, mixed = zip(mix(m_own), mix(m_oth), mix(m_last))
    masked, mixed = jnp.concatenate(masked), jnp.concatenate(mixed)
    polar = jnp.einsum("pms,qms->pq", masked, mixed, preferred_element_type=jnp.float32)
    turned = jnp.roll(polar, (half, half), (0, 1))
    return jnp.where(group == 0, polar, turned)


def solution(mesh):
    in_specs = (
        P(None, "wide", None),
        P(("groups", "wide"), None),
        P(("groups", "wide"), None),
        P(),
        P(),
    )
    out_specs = P(("groups", "wide"), None)
    return jax.shard_map(shards, mesh=mesh, in_specs=in_specs, out_specs=out_specs, check_vma=False)
```

time: 286 us -> 243 us (0.85)
  blocking collectives: 213 us -> 0 us
  waiting for transfers between devices: 0.01 us -> 76.9 us
  starting transfers between devices: 7.54 us -> 40.3 us
  between operations: 0.06 us -> 32.8 us
  other arithmetic: 9.79 us -> 26.1 us
  local copies, waits for them, and re-layouts: 29.6 us -> 38.7 us
    all_gather x2 -> x0, blocking collectives: 213 us -> none  [the longest x1 166 us: shards(): lax.all_gather(occupied, 'wide', axis=0, tiled=True)]
    ppermute x0 -> x14, waiting for transfers between devices: none -> 67.1 us  [the longest x10 67.1 us: shift(): return lax.ppermute(x, 'wide', pairs)]
    ppermute x0 -> x14, starting transfers between devices: none -> 17.1 us  [the longest x10 14.3 us: shift(): return lax.ppermute(x, 'wide', pairs)]
    all_to_all x1 -> x6, starting transfers between devices: 7.54 us -> 23.1 us  [inplane(): lax.all_to_all(x, 'wide', split_axis=0, concat_axis=0, tiled=True, axis_i...]
    concatenate x0 -> x1, local copies, waits for them, and re-layouts: none -> 12.3 us  [shards(): masked, mixed = (jnp.concatenate(masked), jnp.concatenate(mixed))]
    convert_element_type x1 -> x0, local copies, waits for them, and re-layouts: 12.2 us -> none  [shards(): mixed = jnp.einsum('ml,qls->qms', dens_virt, own_half, preferred_element_...]
    all_to_all x1 -> x6, waiting for transfers between devices: 0.01 us -> 9.78 us  [inplane(): lax.all_to_all(x, 'wide', split_axis=0, concat_axis=0, tiled=True, axis_i...]
    dynamic_slice x0 -> x11, local copies, waits for them, and re-layouts: none -> 9.57 us  [the longest x9 7.36 us: part(): lax.dynamic_slice(blocks, (at, low, 0, 0), (1, count, orb, window))[0]]
  transfers between devices with their start and end apart: 1 -> 20, of which waited for: 0 -> 6; matrix products, arithmetic and copies ran while one was open for 0% -> 15% of each run, Pallas kernels for 0% -> 0%
where the time goes in v1:
time: 243 us; the launch traced here: 241 us
  waiting for transfers between devices  76.9 us (32%)
  starting transfers between devices  40.3 us (17%)
  local copies, waits for them, and re-layouts  38.7 us (16%)
  between operations  32.8 us (13%)
  matrix products  26.3 us (11%)
  other arithmetic  26.1 us (11%)
    ppermute x10, waiting for transfers between devices, shift(): return lax.ppermute(x, 'wide', pairs)  67.1 us
    all_to_all x6, starting transfers between devices, inplane(): lax.all_to_all(x, 'wide', split_axis=0, concat_axis=0, tiled=True, axis_i...  23.1 us
    dot_general x3, matrix products, mix(): jnp.einsum('ml,qls->qms', vir, h, preferred_element_type=jnp.float32)  19.8 us
    ppermute x10, starting transfers between devices, shift(): return lax.ppermute(x, 'wide', pairs)  14.3 us
    concatenate x1, local copies, waits for them, and re-layouts, shards(): masked, mixed = (jnp.concatenate(masked), jnp.concatenate(mixed))  12.3 us
    all_to_all x6, waiting for transfers between devices, inplane(): lax.all_to_all(x, 'wide', split_axis=0, concat_axis=0, tiled=True, axis_i...  9.78 us
    select_n x2, other arithmetic, mix(): m = jnp.where(keep[None], m, jnp.zeros((), m.dtype))  8.09 us
    dynamic_slice x9, local copies, waits for them, and re-layouts, part(): lax.dynamic_slice(blocks, (at, low, 0, 0), (1, count, orb, window))[0]  7.36 us
  transfers between devices with their start and end apart: 20, of which 6 were waited for; matrix products, arithmetic and copies ran while one was open for 15% of the time, Pallas kernels for 0%

profile of v1, /device:TPU:0, one launch (start us, length us, event | category | flops | bytes accessed | tf_op | source)
XLA Modules:
  0.0 241.1 jit_solution(17764444624207975799)
XLA Ops:
  0.0 2.0 fusion.57
  16.7 1.7 constant_dynamic-slice_fusion.16
  18.8 1.2 pad_maximum_fusion.1
  20.0 4.2 %all-to-all-start = ((bf16[4,32,16,256]{3,1,2,0:T(8,128)(2,1)}), bf16[4,32,16,256]{3,1,2,0:T(8,128)(2,1)S(1)}, u32[]{:S(2)}, u32[]{:S(2)}) async-start(bf16[4,32,16,256]{3,1,2,0:T(8,128)(2,1)} %pad_maximum_fusion.1), calls=%async_computation | async-start | bytes 2097152 | tf_op jit(solution)/shard_map/all_to_all | solution.py:23
  24.3 3.8 %collective-permute-start.2 = (bf16[32,16,256]{2,0,1:T(8,128)(2,1)S(1)}, bf16[32,16,256]{2,0,1:T(8,128)(2,1)S(1)}, u32[]{:S(2)}, u32[]{:S(2)}) collective-permute-start(bf16[32,16,256]{2,0,1:T(8,128)(2,1)S(1)} %bitcast.143), channel_id=1, source_target_pairs={{0,6},{1,7},{2,4},{3,5},{4,10},{5,11},{6,8},{7,9},{8,14},{9,15},{1... | collective-permute-start | bytes 786440 | tf_op jit(solution)/shard_map/ppermute | solution.py:32
  28.2 1.1 collective-permute-start.1
  29.3 1.6 collective-permute-start
  31.7 3.2 %collective-permute-start.6 = (bf16[2,16,256]{2,1,0:T(8,128)(2,1)S(1)}, bf16[2,16,256]{2,1,0:T(8,128)(2,1)S(1)}, u32[]{:S(2)}, u32[]{:S(2)}) collective-permute-start(bf16[2,16,256]{2,1,0:T(8,128)(2,1)S(1)} %get-tuple-element.87), channel_id=1, source_target_pairs={{0,12},{1,13},{2,14},{3,15},{4,0},{5,1},{6,2},{7,3},{8,4},{9,5},{1... | collective-permute-start | bytes 49160 | tf_op jit(solution)/shard_map/ppermute | solution.py:32
  35.0 18.2 %collective-permute-done.6 = bf16[2,16,256]{2,1,0:T(8,128)(2,1)S(1)} collective-permute-done((bf16[2,16,256]{2,1,0:T(8,128)(2,1)S(1)}, bf16[2,16,256]{2,1,0:T(8,128)(2,1)S(1)}, u32[]{:S(2)}, u32[]{:S(2)}) %collective-permute-start.6) | collective-permute-done | bytes 16416 | tf_op jit(solution)/shard_map/ppermute | solution.py:32
  53.7 4.2 %collective-permute-done.5 = bf16[2,16,256]{2,1,0:T(8,128)(2,1)S(1)} collective-permute-done((bf16[2,16,256]{2,1,0:T(8,128)(2,1)S(1)}, bf16[2,16,256]{2,1,0:T(8,128)(2,1)S(1)}, u32[]{:S(2)}, u32[]{:S(2)}) %collective-permute-start.5) | collective-permute-done | bytes 16416 | tf_op jit(solution)/shard_map/ppermute | solution.py:32
  67.3 1.2 pad_maximum_fusion.2
  68.5 2.3 collective-permute-start.8
  70.8 3.4 %collective-permute-start.7 = (bf16[4,32,16,256]{3,1,2,0:T(8,128)(2,1)S(1)}, bf16[4,32,16,256]{3,1,2,0:T(8,128)(2,1)}, u32[]{:S(2)}, u32[]{:S(2)}) collective-permute-start(bf16[4,32,16,256]{3,1,2,0:T(8,128)(2,1)S(1)} %all-to-all-done), channel_id=1, source_target_pairs={{0,12},{1,13},{2,14},{3,15},{4,0},{5,1},{6,2},{7,3},{8,4},{9,5},{1... | collective-permute-start | bytes 3145736 | tf_op jit(solution)/shard_map/ppermute | solution.py:32
  74.2 0.8 pad_maximum_fusion.8
  75.8 3.4 %all-to-all-start.2 = ((bf16[4,4,2,16,256]{4,3,2,1,0:T(8,128)(2,1)}), bf16[4,4,2,16,256]{4,3,2,1,0:T(8,128)(2,1)S(1)}, u32[]{:S(2)}, u32[]{:S(2)}) async-start(bf16[4,4,2,16,256]{4,3,2,1,0:T(8,128)(2,1)} %broadcast_in_dim.83), calls=%async_computation.2 | async-start | bytes 524288 | tf_op jit(solution)/shard_map/all_to_all | solution.py:23
  79.2 1.1 constant_dynamic-slice_fusion.15
  80.5 0.9 pad_maximum_fusion.6
  81.4 3.8 %all-to-all-done.2 = bf16[4,4,2,16,256]{4,3,2,1,0:T(8,128)(2,1)S(1)} async-done(((bf16[4,4,2,16,256]{4,3,2,1,0:T(8,128)(2,1)}), bf16[4,4,2,16,256]{4,3,2,1,0:T(8,128)(2,1)S(1)}, u32[]{:S(2)}, u32[]{:S(2)}) %all-to-all-start.2) | async-done | bytes 262176 | tf_op jit(solution)/shard_map/all_to_all | solution.py:23
  85.2 4.2 %all-to-all-start.1 = ((bf16[4,16,16,256]{3,1,2,0:T(8,128)(2,1)}), bf16[4,16,16,256]{3,1,2,0:T(8,128)(2,1)}, u32[]{:S(2)}, u32[]{:S(2)}) async-start(bf16[4,16,16,256]{3,1,2,0:T(8,128)(2,1)} %pad_maximum_fusion.6), calls=%async_computation.1 | async-start | bytes 1048576 | tf_op jit(solution)/shard_map/all_to_all | solution.py:23
  96.7 1.3 gather_fusion
  98.0 1.0 copy.59
  101.5 1.5 constant_dynamic-slice_fusion.11
  103.2 0.9 pad_maximum_fusion.7
  104.1 4.1 %all-to-all-start.3 = ((bf16[4,16,16,256]{3,1,2,0:T(8,128)(2,1)}), bf16[4,16,16,256]{3,1,2,0:T(8,128)(2,1)}, u32[]{:S(2)}, u32[]{:S(2)}) async-start(bf16[4,16,16,256]{3,1,2,0:T(8,128)(2,1)} %pad_maximum_fusion.7), calls=%async_computation.3 | async-start | bytes 1048576 | tf_op jit(solution)/shard_map/all_to_all | solution.py:23
  108.4 1.3 constant_dynamic-slice_fusion.7
  110.1 1.1 pad_maximum_fusion.3
  111.2 6.0 %all-to-all-done.3 = bf16[4,16,16,256]{3,1,2,0:T(8,128)(2,1)} async-done(((bf16[4,16,16,256]{3,1,2,0:T(8,128)(2,1)}), bf16[4,16,16,256]{3,1,2,0:T(8,128)(2,1)}, u32[]{:S(2)}, u32[]{:S(2)}) %all-to-all-start.3) | async-done | bytes 524320 | tf_op jit(solution)/shard_map/all_to_all | solution.py:23
  117.2 3.5 %all-to-all-start.4 = ((bf16[4,32,16,256]{3,1,2,0:T(8,128)(2,1)}), bf16[4,32,16,256]{3,1,2,0:T(8,128)(2,1)S(1)}, u32[]{:S(2)}, u32[]{:S(2)}) async-start(bf16[4,32,16,256]{3,1,2,0:T(8,128)(2,1)} %pad_maximum_fusion.3), calls=%async_computation.4 | async-start | bytes 2097152 | tf_op jit(solution)/shard_map/all_to_all | solution.py:23
  122.8 23.5 %collective-permute-done.9 = bf16[4,16,16,256]{3,1,2,0:T(8,128)(2,1)S(1)} collective-permute-done((bf16[4,16,16,256]{3,1,2,0:T(8,128)(2,1)}, bf16[4,16,16,256]{3,1,2,0:T(8,128)(2,1)S(1)}, u32[]{:S(2)}, u32[]{:S(2)}) %collective-permute-start.9) | collective-permute-done | bytes 524320 | tf_op jit(solution)/shard_map/ppermute | solution.py:32
  146.3 1.5 constant_dynamic-slice_fusion.3
  148.1 1.1 pad_maximum_fusion.4
  149.2 3.7 %all-to-all-start.5 = ((bf16[4,32,16,256]{3,1,2,0:T(8,128)(2,1)}), bf16[4,32,16,256]{3,1,2,0:T(8,128)(2,1)S(1)}, u32[]{:S(2)}, u32[]{:S(2)}) async-start(bf16[4,32,16,256]{3,1,2,0:T(8,128)(2,1)} %pad_maximum_fusion.4), calls=%async_computation.5 | async-start | bytes 2097152 | tf_op jit(solution)/shard_map/all_to_all | solution.py:23
  153.7 1.1 gather_fusion.1
  155.0 1.8 gather_fusion.2
  156.9 2.3 fusion.54
  159.2 2.3 fusion.55
  161.4 21.2 %collective-permute-done.11 = bf16[4,16,16,256]{3,1,2,0:T(8,128)(2,1)S(1)} collective-permute-done((bf16[4,16,16,256]{3,1,2,0:T(8,128)(2,1)}, bf16[4,16,16,256]{3,1,2,0:T(8,128)(2,1)S(1)}, u32[]{:S(2)}, u32[]{:S(2)}) %collective-permute-start.11) | collective-permute-done | bytes 524320 | tf_op jit(solution)/shard_map/ppermute | solution.py:32
  182.6 0.8 copy-done.13
  183.4 1.3 pad_maximum_fusion.5
  185.1 1.1 fusion.53
  186.2 4.5 %maximum_select_fusion = bf16[32,256,256]{2,0,1:T(8,128)(2,1)} fusion(bf16[32,64,256]{2,0,1:T(8,128)(2,1)S(1)} %bitcast.130, bf16[32,64,256]{2,0,1:T(8,128)(2,1)} %bitcast.57, bf16[32,64,256]{2,0,1:T(8,128)(2,1)S(1)} %bitcast.128, bf16[32,64,256]{2,0,1:T(8,128)(2,1)S(1)} %bitcast.129, pred[256,256]{1,0:T(8,128)(4,1)S(1)} %copy-done.11), kind=kLoop, calls=%fused_computation.12 | loop fusion | flops 8388608 | bytes 8454144 | tf_op jit(solution)/shard_map/jit(_where)/select_n | solution.py:131
  190.7 10.9 %convert_bitcast_fusion = bf16[32,256,256]{1,2,0:T(8,128)(2,1)} fusion(bf16[256,256,1]{1,0,2:T(8,128)(2,1)S(1)} %bitcast.152, bf16[32,256,256]{2,0,1:T(8,128)(2,1)} %maximum_select_fusion, bf16[256,256]{1,0:T(8,128)(2,1)} %gather_fusion.2, pred[256]{0:T(512)(128)(4,1)S(1)} %get-tuple-element.88), kind=kOutput, calls=%fused_computation.15 | convolution fusion | flops 2151743488 | bytes 8651008 | tf_op jit(solution)/shard_map/ml,qls->qms/dot_general | solution.py:133
  201.6 3.6 %maximum_select_fusion.1 = (bf16[16,256,256]{2,0,1:T(8,128)(2,1)}, bf16[16,256,256]{2,0,1:T(8,128)(2,1)}) fusion(bf16[16,64,256]{2,0,1:T(8,128)(2,1)} %bitcast.68, bf16[16,64,256]{2,0,1:T(8,128)(2,1)S(1)} %bitcast.138, bf16[16,64,256]{2,0,1:T(8,128)(2,1)S(1)} %bitcast.136, bf16[16,64,256]{2,0,1:T(8,128)(2,1)S(1)} %bitcast.140, ...), kind=kLoop, calls=%fused_computation.18 | loop fusion | flops 8388608 | bytes 8454144 | tf_op jit(solution)/shard_map/jit(_where)/select_n | solution.py:131
  205.3 5.3 %convert_bitcast_fusion.2 = bf16[16,256,256]{1,2,0:T(8,128)(2,1)} fusion(bf16[256,256,1]{1,0,2:T(8,128)(2,1)S(1)} %bitcast.153, bf16[16,256,256]{2,0,1:T(8,128)(2,1)} %get-tuple-element.82, bf16[256,256]{1,0:T(8,128)(2,1)S(1)} %copy-done.17, pred[256]{0:T(512)(128)(4,1)S(1)} %get-tuple-element.88), kind=kOutput, calls=%fused_computation.27 | convolution fusion | flops 1075904512 | bytes 4456704 | tf_op jit(solution)/shard_map/ml,qls->qms/dot_general | solution.py:133
  210.6 3.6 %convert_bitcast_fusion.1 = bf16[16,256,256]{1,2,0:T(8,128)(2,1)} fusion(bf16[256,256,1]{1,0,2:T(8,128)(2,1)S(1)} %bitcast.154, bf16[16,256,256]{2,0,1:T(8,128)(2,1)S(1)} %copy-done.9, bf16[256,256]{1,0:T(8,128)(2,1)S(1)} %copy-done.17, pred[256]{0:T(512)(128)(4,1)S(1)} %get-tuple-element.88), kind=kOutput, calls=%fused_computation.24 | convolution fusion | flops 1075904512 | bytes 4456704 | tf_op jit(solution)/shard_map/ml,qls->qms/dot_general | solution.py:133
  214.2 7.2 %pad_maximum_fusion = bf16[64,256,256]{1,2,0:T(8,128)(2,1)} fusion(bf16[16,256,256]{1,2,0:T(8,128)(2,1)} %convert_bitcast_fusion.1, bf16[16,256,256]{1,2,0:T(8,128)(2,1)} %convert_bitcast_fusion.2, bf16[32,256,256]{1,2,0:T(8,128)(2,1)} %convert_bitcast_fusion), kind=kLoop, calls=%fused_computation.11 | loop fusion | flops 8388608 | bytes 16777216 | tf_op jit(solution)/shard_map/concatenate | solution.py:137
  221.4 12.3 %copy.93 = bf16[64,256,256]{2,0,1:T(8,128)(2,1)} copy(bf16[64,256,256]{1,2,0:T(8,128)(2,1)} %pad_maximum_fusion) | data formatting | bytes 16777216 | tf_op jit(solution)/shard_map/concatenate | solution.py:137
  233.7 6.5 %fusion.42 = f32[64,64]{1,0:T(8,128)S(1)} fusion(bf16[64,256,256]{2,0,1:T(8,128)(2,1)} %copy.93, bf16[16,256,256]{2,0,1:T(8,128)(2,1)} %get-tuple-element.83, bf16[16,256,256]{2,0,1:T(8,128)(2,1)S(1)} %copy-done.8, bf16[32,256,256]{2,0,1:T(8,128)(2,1)} %maximum_select_fusion), kind=kOutput, calls=%fused_computation.30 | convolution fusion | flops 562036736 | bytes 16793600 | tf_op jit(solution)/shard_map/pms,qms->pq/dot_general | solution.py:138
  (118 shorter events, 9.7 us)
Async XLA Ops:
  0.0 96.4 %copy-start = (s32[16,4,4]{0,2,1:T(4,128)S(1)}, s32[16,4,4]{0,2,1:T(4,128)}, u32[]{:S(2)}) copy-start(s32[16,4,4]{0,2,1:T(4,128)} %param.10) | copy-start | bytes 3076
  18.4 12.7 %copy-start.21 = (bf16[16,256]{1,0:T(8,128)(2,1)S(1)}, bf16[16,256]{1,0:T(8,128)(2,1)}, u32[]{:S(2)}) copy-start(bf16[16,256]{1,0:T(8,128)(2,1)} %param.9) | copy-start | bytes 24580
  18.4 12.7 %copy-start.22 = (bf16[16,256]{1,0:T(8,128)(2,1)S(1)}, bf16[16,256]{1,0:T(8,128)(2,1)}, u32[]{:S(2)}) copy-start(bf16[16,256]{1,0:T(8,128)(2,1)} %param.8) | copy-start | bytes 24580
  20.0 46.6 %all-to-all-start = ((bf16[4,32,16,256]{3,1,2,0:T(8,128)(2,1)}), bf16[4,32,16,256]{3,1,2,0:T(8,128)(2,1)S(1)}, u32[]{:S(2)}, u32[]{:S(2)}) async-start(bf16[4,32,16,256]{3,1,2,0:T(8,128)(2,1)} %pad_maximum_fusion.1), calls=%async_computation | async-start | bytes 2097152 | tf_op jit(solution)/shard_map/all_to_all | solution.py:23
  24.3 42.3 %collective-permute-start.2 = (bf16[32,16,256]{2,0,1:T(8,128)(2,1)S(1)}, bf16[32,16,256]{2,0,1:T(8,128)(2,1)S(1)}, u32[]{:S(2)}, u32[]{:S(2)}) collective-permute-start(bf16[32,16,256]{2,0,1:T(8,128)(2,1)S(1)} %bitcast.143), channel_id=1, source_target_pairs={{0,6},{1,7},{2,4},{3,5},{4,10},{5,11},{6,8},{7,9},{8,14},{9,15},{1... | collective-permute-start | bytes 786440 | tf_op jit(solution)/shard_map/ppermute | solution.py:32
  28.2 38.4 %collective-permute-start.1 = (bf16[32,16,256]{2,0,1:T(8,128)(2,1)S(1)}, bf16[32,16,256]{2,0,1:T(8,128)(2,1)S(1)}, u32[]{:S(2)}, u32[]{:S(2)}) collective-permute-start(bf16[32,16,256]{2,0,1:T(8,128)(2,1)S(1)} %bitcast.144), channel_id=1, source_target_pairs={{0,5},{1,4},{2,7},{3,6},{4,9},{5,8},{6,11},{7,10},{8,13},{9,12},{1... | collective-permute-start | bytes 786440 | tf_op jit(solution)/shard_map/ppermute | solution.py:32
  29.3 37.2 %collective-permute-start = (bf16[32,16,256]{2,0,1:T(8,128)(2,1)S(1)}, bf16[32,16,256]{2,0,1:T(8,128)(2,1)S(1)}, u32[]{:S(2)}, u32[]{:S(2)}) collective-permute-start(bf16[32,16,256]{2,0,1:T(8,128)(2,1)S(1)} %bitcast.145), channel_id=1, source_target_pairs={{0,4},{1,5},{2,6},{3,7},{4,8},{5,9},{6,10},{7,11},{8,12},{9,13},{1... | collective-permute-start | bytes 786440 | tf_op jit(solution)/shard_map/ppermute | solution.py:32
  31.0 35.5 %collective-permute-start.3 = (bf16[32,16,256]{2,0,1:T(8,128)(2,1)S(1)}, bf16[32,16,256]{2,0,1:T(8,128)(2,1)S(1)}, u32[]{:S(2)}, u32[]{:S(2)}) collective-permute-start(bf16[32,16,256]{2,0,1:T(8,128)(2,1)S(1)} %bitcast.146), channel_id=1, source_target_pairs={{0,7},{1,6},{2,5},{3,4},{4,11},{5,10},{6,9},{7,8},{8,15},{9,14},{1... | collective-permute-start | bytes 786440 | tf_op jit(solution)/shard_map/ppermute | solution.py:32
  31.7 21.4 %collective-permute-start.6 = (bf16[2,16,256]{2,1,0:T(8,128)(2,1)S(1)}, bf16[2,16,256]{2,1,0:T(8,128)(2,1)S(1)}, u32[]{:S(2)}, u32[]{:S(2)}) collective-permute-start(bf16[2,16,256]{2,1,0:T(8,128)(2,1)S(1)} %get-tuple-element.87), channel_id=1, source_target_pairs={{0,12},{1,13},{2,14},{3,15},{4,0},{5,1},{6,2},{7,3},{8,4},{9,5},{1... | collective-permute-start | bytes 49160 | tf_op jit(solution)/shard_map/ppermute | solution.py:32
  53.2 13.4 %copy-start.18 = (bf16[2,16,256]{2,1,0:T(8,128)(2,1)}, bf16[2,16,256]{2,1,0:T(8,128)(2,1)S(1)}, u32[]{:S(2)}) copy-start(bf16[2,16,256]{2,1,0:T(8,128)(2,1)S(1)} %collective-permute-done.6) | copy-start | bytes 49156
  53.2 4.8 %collective-permute-start.5 = (bf16[2,16,256]{2,1,0:T(8,128)(2,1)S(1)}, bf16[2,16,256]{2,1,0:T(8,128)(2,1)S(1)}, u32[]{:S(2)}, u32[]{:S(2)}) collective-permute-start(bf16[2,16,256]{2,1,0:T(8,128)(2,1)S(1)} %get-tuple-element.87), channel_id=1, source_target_pairs={{0,8},{1,9},{2,10},{3,11},{4,12},{5,13},{6,14},{7,15},{8,0},{9,1},... | collective-permute-start | bytes 49160 | tf_op jit(solution)/shard_map/ppermute | solution.py:32
  57.9 8.7 %copy-start.19 = (bf16[2,16,256]{2,1,0:T(8,128)(2,1)}, bf16[2,16,256]{2,1,0:T(8,128)(2,1)S(1)}, u32[]{:S(2)}) copy-start(bf16[2,16,256]{2,1,0:T(8,128)(2,1)S(1)} %collective-permute-done.5) | copy-start | bytes 49156
  57.9 8.6 %collective-permute-start.4 = (bf16[2,16,256]{2,1,0:T(8,128)(2,1)S(1)}, bf16[2,16,256]{2,1,0:T(8,128)(2,1)S(1)}, u32[]{:S(2)}, u32[]{:S(2)}) collective-permute-start(bf16[2,16,256]{2,1,0:T(8,128)(2,1)S(1)} %get-tuple-element.87), channel_id=1, source_target_pairs={{0,4},{1,5},{2,6},{3,7},{4,8},{5,9},{6,10},{7,11},{8,12},{9,13},{1... | collective-permute-start | bytes 49160 | tf_op jit(solution)/shard_map/ppermute | solution.py:32
  66.5 0.6 copy-start.20
  66.5 0.7 copy-start.14
  66.6 0.8 copy-start.15
  68.5 33.0 %collective-permute-start.8 = (bf16[4,32,16,256]{3,1,2,0:T(8,128)(2,1)S(1)}, bf16[4,32,16,256]{3,1,2,0:T(8,128)(2,1)S(1)}, u32[]{:S(2)}, u32[]{:S(2)}) collective-permute-start(bf16[4,32,16,256]{3,1,2,0:T(8,128)(2,1)S(1)} %pad_maximum_fusion.2), channel_id=1, source_target_pairs={{0,16},{16,0},{1,17},{17,1},{2,18},{18,2},{3,19},{19,3},{4,20},{20... | collective-permute-start | bytes 3145736 | tf_op jit(solution)/shard_map/ppermute | solution.py:35
  70.8 30.7 %collective-permute-start.7 = (bf16[4,32,16,256]{3,1,2,0:T(8,128)(2,1)S(1)}, bf16[4,32,16,256]{3,1,2,0:T(8,128)(2,1)}, u32[]{:S(2)}, u32[]{:S(2)}) collective-permute-start(bf16[4,32,16,256]{3,1,2,0:T(8,128)(2,1)S(1)} %all-to-all-done), channel_id=1, source_target_pairs={{0,12},{1,13},{2,14},{3,15},{4,0},{5,1},{6,2},{7,3},{8,4},{9,5},{1... | collective-permute-start | bytes 3145736 | tf_op jit(solution)/shard_map/ppermute | solution.py:32
  75.8 9.4 %all-to-all-start.2 = ((bf16[4,4,2,16,256]{4,3,2,1,0:T(8,128)(2,1)}), bf16[4,4,2,16,256]{4,3,2,1,0:T(8,128)(2,1)S(1)}, u32[]{:S(2)}, u32[]{:S(2)}) async-start(bf16[4,4,2,16,256]{4,3,2,1,0:T(8,128)(2,1)} %broadcast_in_dim.83), calls=%async_computation.2 | async-start | bytes 524288 | tf_op jit(solution)/shard_map/all_to_all | solution.py:23
  85.2 16.3 %all-to-all-start.1 = ((bf16[4,16,16,256]{3,1,2,0:T(8,128)(2,1)}), bf16[4,16,16,256]{3,1,2,0:T(8,128)(2,1)}, u32[]{:S(2)}, u32[]{:S(2)}) async-start(bf16[4,16,16,256]{3,1,2,0:T(8,128)(2,1)} %pad_maximum_fusion.6), calls=%async_computation.1 | async-start | bytes 1048576 | tf_op jit(solution)/shard_map/all_to_all | solution.py:23
  101.5 8.5 %copy-start.10 = (bf16[4,32,16,256]{3,1,2,0:T(8,128)(2,1)}, bf16[4,32,16,256]{3,1,2,0:T(8,128)(2,1)S(1)}, u32[]{:S(2)}) copy-start(bf16[4,32,16,256]{3,1,2,0:T(8,128)(2,1)S(1)} %collective-permute-done.8) | copy-start | bytes 3145732
  104.1 13.1 %all-to-all-start.3 = ((bf16[4,16,16,256]{3,1,2,0:T(8,128)(2,1)}), bf16[4,16,16,256]{3,1,2,0:T(8,128)(2,1)}, u32[]{:S(2)}, u32[]{:S(2)}) async-start(bf16[4,16,16,256]{3,1,2,0:T(8,128)(2,1)} %pad_maximum_fusion.7), calls=%async_computation.3 | async-start | bytes 1048576 | tf_op jit(solution)/shard_map/all_to_all | solution.py:23
  108.3 38.0 %collective-permute-start.10 = (bf16[4,32,16,256]{3,1,2,0:T(8,128)(2,1)}, bf16[4,32,16,256]{3,1,2,0:T(8,128)(2,1)}, u32[]{:S(2)}, u32[]{:S(2)}) collective-permute-start(bf16[4,32,16,256]{3,1,2,0:T(8,128)(2,1)} %collective-permute-done.7), channel_id=1, source_target_pairs={{0,16},{16,0},{1,17},{17,1},{2,18},{18,2},{3,19},{19,3},{4,20},{20... | collective-permute-start | bytes 3145736 | tf_op jit(solution)/shard_map/ppermute | solution.py:35
  117.2 29.1 %all-to-all-start.4 = ((bf16[4,32,16,256]{3,1,2,0:T(8,128)(2,1)}), bf16[4,32,16,256]{3,1,2,0:T(8,128)(2,1)S(1)}, u32[]{:S(2)}, u32[]{:S(2)}) async-start(bf16[4,32,16,256]{3,1,2,0:T(8,128)(2,1)} %pad_maximum_fusion.3), calls=%async_computation.4 | async-start | bytes 2097152 | tf_op jit(solution)/shard_map/all_to_all | solution.py:23
  121.5 24.7 %collective-permute-start.9 = (bf16[4,16,16,256]{3,1,2,0:T(8,128)(2,1)}, bf16[4,16,16,256]{3,1,2,0:T(8,128)(2,1)S(1)}, u32[]{:S(2)}, u32[]{:S(2)}) collective-permute-start(bf16[4,16,16,256]{3,1,2,0:T(8,128)(2,1)} %all-to-all-done.1), channel_id=1, source_target_pairs={{0,8},{1,9},{2,10},{3,11},{4,12},{5,13},{6,14},{7,15},{8,0},{9,1},... | collective-permute-start | bytes 1572872 | tf_op jit(solution)/shard_map/ppermute | solution.py:32
  146.3 2.9 %copy-start.12 = (bf16[4,16,16,256]{3,1,2,0:T(8,128)(2,1)}, bf16[4,16,16,256]{3,1,2,0:T(8,128)(2,1)S(1)}, u32[]{:S(2)}) copy-start(bf16[4,16,16,256]{3,1,2,0:T(8,128)(2,1)S(1)} %collective-permute-done.9) | copy-start | bytes 1572868
  149.2 34.2 %all-to-all-start.5 = ((bf16[4,32,16,256]{3,1,2,0:T(8,128)(2,1)}), bf16[4,32,16,256]{3,1,2,0:T(8,128)(2,1)S(1)}, u32[]{:S(2)}, u32[]{:S(2)}) async-start(bf16[4,32,16,256]{3,1,2,0:T(8,128)(2,1)} %pad_maximum_fusion.4), calls=%async_computation.5 | async-start | bytes 2097152 | tf_op jit(solution)/shard_map/all_to_all | solution.py:23
  156.8 29.4 %copy-start.11 = (pred[256,256]{1,0:T(8,128)(4,1)S(1)}, pred[256,256]{1,0:T(8,128)(4,1)}, u32[]{:S(2)}) copy-start(pred[256,256]{1,0:T(8,128)(4,1)} %copy.60) | copy-start | bytes 196612
  156.8 25.8 %collective-permute-start.11 = (bf16[4,16,16,256]{3,1,2,0:T(8,128)(2,1)}, bf16[4,16,16,256]{3,1,2,0:T(8,128)(2,1)S(1)}, u32[]{:S(2)}, u32[]{:S(2)}) collective-permute-start(bf16[4,16,16,256]{3,1,2,0:T(8,128)(2,1)} %all-to-all-done.3), channel_id=1, source_target_pairs={{0,8},{1,9},{2,10},{3,11},{4,12},{5,13},{6,14},{7,15},{8,0},{9,1},... | collective-permute-start | bytes 1572872 | tf_op jit(solution)/shard_map/ppermute | solution.py:32
  156.8 26.6 %collective-permute-start.12 = (bf16[4,16,16,256]{3,1,2,0:T(8,128)(2,1)}, bf16[4,16,16,256]{3,1,2,0:T(8,128)(2,1)}, u32[]{:S(2)}, u32[]{:S(2)}) collective-permute-start(bf16[4,16,16,256]{3,1,2,0:T(8,128)(2,1)} %copy-done.12), channel_id=1, source_target_pairs={{0,16},{16,0},{1,17},{17,1},{2,18},{18,2},{3,19},{19,3},{4,20},{20... | collective-permute-start | bytes 1572872 | tf_op jit(solution)/shard_map/ppermute | solution.py:35
  182.6 0.8 copy-start.13
  184.8 16.8 %collective-permute-start.13 = (bf16[4,16,16,256]{3,1,2,0:T(8,128)(2,1)}, bf16[4,16,16,256]{3,1,2,0:T(8,128)(2,1)}, u32[]{:S(2)}, u32[]{:S(2)}) collective-permute-start(bf16[4,16,16,256]{3,1,2,0:T(8,128)(2,1)} %copy-done.13), channel_id=1, source_target_pairs={{0,16},{16,0},{1,17},{17,1},{2,18},{18,2},{3,19},{19,3},{4,20},{20... | collective-permute-start | bytes 1572872 | tf_op jit(solution)/shard_map/ppermute | solution.py:35
  186.2 4.5 %copy-start.16 = (bf16[4,4,16,256]{3,2,1,0:T(8,128)(2,1)S(1)}, bf16[4,4,16,256]{3,2,1,0:T(8,128)(2,1)}, u32[]{:S(2)}) copy-start(bf16[4,4,16,256]{3,2,1,0:T(8,128)(2,1)} %get-tuple-element.93) | copy-start | bytes 393220
  190.7 10.9 %copy-start.2 = (bf16[4,16,16,256]{3,1,2,0:T(8,128)(2,1)S(1)}, bf16[4,16,16,256]{3,1,2,0:T(8,128)(2,1)}, u32[]{:S(2)}) copy-start(bf16[4,16,16,256]{3,1,2,0:T(8,128)(2,1)} %get-tuple-element.76) | copy-start | bytes 1572868
  190.7 10.9 %copy-start.3 = (bf16[4,16,16,256]{3,1,2,0:T(8,128)(2,1)S(1)}, bf16[4,16,16,256]{3,1,2,0:T(8,128)(2,1)}, u32[]{:S(2)}) copy-start(bf16[4,16,16,256]{3,1,2,0:T(8,128)(2,1)} %get-tuple-element.77) | copy-start | bytes 1572868
  190.7 10.9 %copy-start.4 = (bf16[4,16,16,256]{3,1,2,0:T(8,128)(2,1)S(1)}, bf16[4,16,16,256]{3,1,2,0:T(8,128)(2,1)}, u32[]{:S(2)}) copy-start(bf16[4,16,16,256]{3,1,2,0:T(8,128)(2,1)} %get-tuple-element.78) | copy-start | bytes 1572868
  190.7 10.9 %copy-start.5 = (bf16[4,16,16,256]{3,1,2,0:T(8,128)(2,1)S(1)}, bf16[4,16,16,256]{3,1,2,0:T(8,128)(2,1)}, u32[]{:S(2)}) copy-start(bf16[4,16,16,256]{3,1,2,0:T(8,128)(2,1)} %get-tuple-element.79) | copy-start | bytes 1572868
  190.7 10.9 %copy-start.6 = (bf16[4,16,16,256]{3,1,2,0:T(8,128)(2,1)S(1)}, bf16[4,16,16,256]{3,1,2,0:T(8,128)(2,1)}, u32[]{:S(2)}) copy-start(bf16[4,16,16,256]{3,1,2,0:T(8,128)(2,1)} %get-tuple-element.74) | copy-start | bytes 1572868
  190.7 10.9 %copy-start.7 = (bf16[4,16,16,256]{3,1,2,0:T(8,128)(2,1)S(1)}, bf16[4,16,16,256]{3,1,2,0:T(8,128)(2,1)}, u32[]{:S(2)}) copy-start(bf16[4,16,16,256]{3,1,2,0:T(8,128)(2,1)} %get-tuple-element.75) | copy-start | bytes 1572868
  201.6 3.6 %copy-start.17 = (bf16[256,256]{1,0:T(8,128)(2,1)S(1)}, bf16[256,256]{1,0:T(8,128)(2,1)}, u32[]{:S(2)}) copy-start(bf16[256,256]{1,0:T(8,128)(2,1)} %gather_fusion.2) | copy-start | bytes 393220
  205.3 5.3 %copy-start.9 = (bf16[16,256,256]{2,0,1:T(8,128)(2,1)S(1)}, bf16[16,256,256]{2,0,1:T(8,128)(2,1)}, u32[]{:S(2)}) copy-start(bf16[16,256,256]{2,0,1:T(8,128)(2,1)} %get-tuple-element.83) | copy-start | bytes 6291460
  221.4 12.3 %copy-start.8 = (bf16[16,256,256]{2,0,1:T(8,128)(2,1)S(1)}, bf16[16,256,256]{2,0,1:T(8,128)(2,1)}, u32[]{:S(2)}) copy-start(bf16[16,256,256]{2,0,1:T(8,128)(2,1)} %get-tuple-element.82) | copy-start | bytes 6291460
  233.7 7.3 %copy-start.1 = (s32[16,4,4]{0,2,1:T(4,128)S(1)}, s32[16,4,4]{0,2,1:T(4,128)}, u32[]{:S(2)}) copy-start(s32[16,4,4]{0,2,1:T(4,128)} %param.10) | copy-start | bytes 3076

commit v2 on v0

v2 whole, which is shorter than its diff:
```python
import functools

import jax
import jax.numpy as jnp
from jax import lax
from jax.experimental import pallas as pl
from jax.experimental.pallas import tpu as pltpu
from jax.sharding import PartitionSpec as P

PLANE = 4
ROWS = 16
VMEM = pl.BlockSpec(memory_space=pltpu.VMEM)
SMEM = pl.BlockSpec(memory_space=pltpu.SMEM)
HBM = pl.BlockSpec(memory_space=pl.ANY)
DOT = functools.partial(jnp.dot, preferred_element_type=jnp.float32)


def gather_kernel(plan, outer, half, count, order_ref, blocks_ref, *rest):
    outs, sems = rest[:count], rest[count]
    me = lax.axis_index("wide")
    group = lax.axis_index("groups")
    plane, lane = me // PLANE, me % PLANE
    copies = []
    for n, (out, place, dz, target, flip, start, rows, own) in enumerate(plan):
        who = (lane ^ target) if flip else target
        block = order_ref[lax.rem(plane + dz, outer) * PLANE + who]
        low = (group if own else 1 - group) * half + start
        to = outs[out] if place is None else outs[out].at[place[0], pl.ds(place[1], rows)]
        copies.append(
            pltpu.make_async_copy(blocks_ref.at[block, pl.ds(low, rows)], to, sems.at[n])
        )
    for copy in copies:
        copy.start()
    for copy in copies:
        copy.wait()


def gather(plan, shapes, outer, half, ri_order, blocks):
    size = sum(s.size for s in shapes) * 4
    return pl.pallas_call(
        functools.partial(gather_kernel, plan, outer, half, len(shapes)),
        out_shape=shapes,
        in_specs=[SMEM, HBM],
        out_specs=[HBM] * len(shapes),
        scratch_shapes=[pltpu.SemaphoreType.DMA((len(plan),))],
        cost_estimate=pl.CostEstimate(flops=0, bytes_accessed=size, transcendentals=0),
    )(ri_order, blocks)


def load(pieces, held, sems, base=0):
    groups = {}
    n = base
    for ref, lead, low, rows, to, at in pieces:
        src = ref if lead is None else ref.at[lead]
        height = src.shape[1]
        for r in range(0, rows, ROWS):
            copy = pltpu.make_async_copy(
                src.at[pl.ds(low + r, ROWS)],
                held.at[pl.ds(to + r, ROWS), pl.ds(at, height)],
                sems.at[n],
            )
            groups.setdefault((to + r) // ROWS, []).append(copy)
            n += 1
    for g in sorted(groups):
        for copy in groups[g]:
            copy.start()
    return groups


def half_step(held, first, occ, vir, keep, mask_t, mix_t, to):
    window = occ.shape[0]
    m = held[first : first + ROWS] * keep[None]
    mask_t[:, to : to + ROWS, :] = jnp.swapaxes(m, 0, 1)
    h = DOT(m.reshape(ROWS * window, window), occ).astype(jnp.bfloat16)
    mixed = [
        DOT(vir, h[p * window : (p + 1) * window]).astype(jnp.bfloat16)[None] for p in range(ROWS)
    ]
    mix_t[:, to : to + ROWS, :] = jnp.swapaxes(jnp.concatenate(mixed), 0, 1)


def front_kernel(places, shifts, outer, orb, count, order_ref, mask_ref, dens_ref, *rest):
    refs = rest[:count]
    mask_t, mix_t, occ_ref, vir_ref, keep_ref, held, sems = rest[count:]
    pieces = [(refs[p[0]],) + p[1:] for p in places]
    groups = load(pieces, held, sems)
    me = lax.axis_index("wide")
    plane, lane = me // PLANE, me % PLANE
    window = occ_ref.shape[0]
    nblk = mask_ref.shape[2]
    block_rows = window // nblk

    def assembled(shape, dim):
        at = lax.broadcasted_iota(jnp.int32, shape, dim)
        place = at // (PLANE * orb)
        device = (at // orb) % PLANE
        source = jnp.zeros(shape, jnp.int32)
        for n, dz in enumerate(shifts):
            who = (device ^ lane) if n == 1 else device
            from_plane = lax.rem(plane + (outer - dz), outer)
            source = jnp.where(place == n, from_plane * PLANE + who, source)
        return source * orb + at % orb

    arrived = lax.broadcasted_iota(jnp.int32, (window, 2 * window), 1)
    kind = (arrived // orb) % 2
    dz = (arrived // (2 * orb)) % outer
    device = arrived // (2 * orb * outer)
    source = lax.rem(plane - dz + outer, outer) * PLANE + device
    orbital = source * orb + arrived % orb
    rows = lax.broadcasted_iota(jnp.int32, (window, 2 * window), 0)
    pick = jnp.where((rows == orbital) & (kind == 0), 1.0, 0.0).astype(jnp.bfloat16)
    dens = dens_ref[...]
    occ = DOT(pick, dens).astype(jnp.bfloat16)
    pick = (assembled((window, 2 * window), 0) == orbital) & (kind == 1)
    pick = jnp.where(pick, 1.0, 0.0).astype(jnp.bfloat16)
    vir = DOT(pick, dens).astype(jnp.bfloat16)
    rows = lax.broadcasted_iota(jnp.int32, (window, window), 0)
    pick = jnp.where(rows == assembled((window, window), 1), 1.0, 0.0).astype(jnp.bfloat16)
    vir = DOT(vir, pick).astype(jnp.bfloat16)
    block = order_ref[me]
    lam = assembled((window, window), 0) // block_rows
    sig = lax.broadcasted_iota(jnp.int32, (window, window), 1) // block_rows
    keep = jnp.zeros((window, window), jnp.int32)
    for a in range(nblk):
        for b in range(nblk):
            keep = jnp.where((lam == a) & (sig == b), mask_ref[block, a, b], keep)
    keep = jnp.where(keep > 0, 1.0, 0.0).astype(jnp.bfloat16)
    occ_ref[...] = occ
    vir_ref[...] = vir
    keep_ref[...] = keep
    for g in sorted(groups):
        for copy in groups[g]:
            copy.wait()
        half_step(held, g * ROWS, occ, vir, keep, mask_t, mix_t, g * ROWS)


def back_kernel(places, count, occ_ref, vir_ref, keep_ref, front_mask, front_mix, *rest):
    refs = rest[:count]
    out_ref, mask_t, mix_t, held, sems = rest[count:]
    done = front_mask.shape[1]
    pieces = [(refs[p[0]],) + p[1:] for p in places]
    groups = load(pieces, held, sems, 2)
    first = pltpu.make_async_copy(front_mask, mask_t.at[:, pl.ds(0, done)], sems.at[0])
    second = pltpu.make_async_copy(front_mix, mix_t.at[:, pl.ds(0, done)], sems.at[1])
    first.start()
    second.start()
    occ, vir, keep = occ_ref[...], vir_ref[...], keep_ref[...]
    for g in sorted(groups):
        for copy in groups[g]:
            copy.wait()
        half_step(held, g * ROWS, occ, vir, keep, mask_t, mix_t, done + g * ROWS)
    first.wait()
    second.wait()
    window, rows = mask_t.shape[0], mask_t.shape[1]
    deep = 16

    def body(step, total):
        for k in range(deep):
            m = step * deep + k
            total += lax.dot_general(
                mask_t[m], mix_t[m], (((1,), (1,)), ((), ())), preferred_element_type=jnp.float32
            )
        return total

    total = lax.fori_loop(0, window // deep, body, jnp.zeros((rows, rows), jnp.float32))
    half = rows // 2
    turned = jnp.concatenate([total[half:], total[:half]], axis=0)
    turned = jnp.concatenate([turned[:, half:], turned[:, :half]], axis=1)
    out_ref[...] = jnp.where(lax.axis_index("groups") == 0, total, turned)


def shards(tensor, occupied, virtual, block_mask, ri_order):
    wide_count = lax.axis_size("wide")
    outer = wide_count // PLANE
    ri_total, orb, window = tensor.shape
    rows = ri_total // wide_count
    half = rows // 2
    quarter = half // 2
    kind = tensor.dtype
    barrier = lax.optimization_barrier
    planes = [[PLANE * z + i for i in range(PLANE)] for z in range(outer)]

    def inplane(x):
        return lax.all_to_all(
            x, "wide", split_axis=0, concat_axis=0, tiled=True, axis_index_groups=planes
        )

    def shift(x, dz, flip=0):
        pairs = [
            (w, ((w // PLANE + dz) % outer) * PLANE + ((w % PLANE) ^ flip))
            for w in range(wide_count)
        ]
        return lax.ppermute(x, "wide", pairs)

    def swap(x):
        return lax.ppermute(x, "groups", [(0, 1), (1, 0)])

    order = [d for d in range(1, outer) if d != outer // 2] + [outer // 2]
    first, last = order[0], order[-1]
    shape = lambda *s: jax.ShapeDtypeStruct(s + (orb, window), kind)
    blocks = tensor.reshape(wide_count, rows, orb, window)

    plan = [(q, None, first, q, True, 0, half, True) for q in range(PLANE)]
    pieces = gather(plan, [shape(half)] * PLANE, outer, half, ri_order, blocks)
    held_back, *pieces = barrier((blocks, *pieces))
    plan, shapes = [], []
    for d in order[1:]:
        plan += [(len(shapes), (i, 0), d, i, False, 0, half, True) for i in range(PLANE)]
        shapes.append(shape(PLANE, half))
    for own in (True, False):
        low = 0 if own else half
        plan += [(len(shapes), (i, low), 0, i, False, 0, half, own) for i in range(PLANE)]
    shapes.append(shape(PLANE, rows))
    *to_send, to_near = gather(plan, shapes, outer, half, ri_order, held_back)

    base = jnp.stack([occupied, virtual])
    dens, small = [base], list(range(1, outer))
    per_phase = -(-len(small) // (outer - 2))
    own_in, swapped = [], []
    for k in range(outer):
        if k == 0:
            moved = [shift(p, first, q) for q, p in enumerate(pieces)]
        elif k <= outer - 3:
            moved = [shift(ready, order[k])]
        else:
            moved = [shift(ready[k - outer + 2], last)]
        turn = [swap(own_in[-1])] if k else []
        tiny, near_by = [], []
        if 1 <= k <= outer - 2:
            tiny = [shift(base, d) for d in small[:per_phase]]
            small = small[per_phase:]
        if k <= outer - 3:
            near_by = [inplane(to_send[k])]
        elif k == outer - 2:
            near = inplane(to_near)
        else:
            spread = jnp.broadcast_to(jnp.stack(dens)[None], (PLANE, outer, 2, orb, window))
            near_by = [inplane(spread), near]
        moved, turn, tiny, near_by, to_send, to_near, base = barrier(
            (moved, turn, tiny, near_by, to_send, to_near, base)
        )
        own_in.append(moved[0] if k else jnp.stack(moved))
        swapped += turn
        dens += tiny
        if k <= outer - 3:
            ready = near_by[0]
            if k == outer - 3:
                ready = [ready[:, :quarter], ready[:, quarter:]]
    dens_all, near = near_by
    swapped.append(swap(own_in[-1]))

    front, back = [], []
    for i in range(PLANE):
        for n in range(outer):
            at = (n * PLANE + i) * orb
            if n == 0:
                front += [(near, i, 0, half + quarter, 0, at)]
                back += [(near, i, half + quarter, quarter, 0, at)]
            elif n < outer - 1:
                front += [(own_in[n - 1], i, 0, half, 0, at)]
                front += [(swapped[n - 1], i, 0, quarter, half, at)]
                back += [(swapped[n - 1], i, quarter, quarter, 0, at)]
            else:
                front += [(own_in[-2], i, 0, quarter, 0, at)]
                front += [(own_in[-1], i, 0, quarter, quarter, at)]
                front += [(swapped[-2], i, 0, quarter, half, at)]
                back += [(swapped[-1], i, 0, quarter, 0, at)]

    def places(listed):
        if orb % ROWS == 0:
            arrays = []
            for p in listed:
                if not any(p[0] is a for a in arrays):
                    arrays.append(p[0])
            number = lambda x: [x is a for a in arrays].index(True)
            return [(number(p[0]),) + p[1:] for p in listed], arrays
        size = max(p[4] + p[3] for p in listed)
        whole = []
        for r in range(0, size, ROWS):
            row = sorted((p for p in listed if p[4] <= r < p[4] + p[3]), key=lambda p: p[5])
            cut = [lax.slice_in_dim(p[0][p[1]], p[2] + r - p[4], p[2] + r - p[4] + ROWS) for p in row]
            whole.append(jnp.concatenate(cut, axis=1))
        return [(0, None, 0, size, 0, 0)], [jnp.concatenate(whole)]

    def copies(table):
        return sum(p[3] // ROWS for p in table)

    params = pltpu.CompilerParams(vmem_limit_bytes=48 * 2**20)
    table, arrays = places(front)
    done = half + quarter
    mat = jax.ShapeDtypeStruct((window, window), kind)
    tall = jax.ShapeDtypeStruct((window, done, window), kind)
    front_mask, front_mix, occ, vir, keep = pl.pallas_call(
        functools.partial(front_kernel, table, [0] + order, outer, orb, len(arrays)),
        out_shape=[tall, tall, mat, mat, mat],
        in_specs=[SMEM, SMEM, VMEM] + [HBM] * len(arrays),
        out_specs=[VMEM] * 5,
        scratch_shapes=[
            pltpu.VMEM((done, window, window), kind),
            pltpu.SemaphoreType.DMA((copies(table),)),
        ],
        compiler_params=params,
        cost_estimate=pl.CostEstimate(
            flops=4 * done * window**3, bytes_accessed=6 * done * window**2, transcendentals=0
        ),
    )(ri_order, block_mask, dens_all.reshape(2 * window, window), *arrays)
    table, arrays = places(back)
    return pl.pallas_call(
        functools.partial(back_kernel, table, len(arrays)),
        out_shape=jax.ShapeDtypeStruct((rows, rows), jnp.float32),
        in_specs=[VMEM] * 3 + [HBM] * (2 + len(arrays)),
        out_specs=VMEM,
        scratch_shapes=[
            pltpu.VMEM((window, rows, window), kind),
            pltpu.VMEM((window, rows, window), kind),
            pltpu.VMEM((quarter, window, window), kind),
            pltpu.SemaphoreType.DMA((2 + copies(table),)),
        ],
        compiler_params=params,
        cost_estimate=pl.CostEstimate(
            flops=4 * quarter * window**3, bytes_accessed=4 * rows * window**2, transcendentals=0
        ),
    )(occ, vir, keep, front_mask, front_mix, *arrays)


def solution(mesh):
    in_specs = (
        P(None, "wide", None),
        P(("groups", "wide"), None),
        P(("groups", "wide"), None),
        P(),
        P(),
    )
    out_specs = P(("groups", "wide"), None)
    return jax.shard_map(shards, mesh=mesh, in_specs=in_specs, out_specs=out_specs, check_vma=False)
```

time: 286 us -> 327 us (1.14)
  blocking collectives: 213 us -> 8.42 us
  Pallas kernels: 0 us -> 186 us
  waiting for transfers between devices: 0.01 us -> 88.3 us
  matrix products: 24.9 us -> 0 us
  starting transfers between devices: 7.54 us -> 30.5 us
  local copies, waits for them, and re-layouts: 29.6 us -> 12.8 us
  other arithmetic: 9.79 us -> 0.15 us
    all_gather x2 -> x0, blocking collectives: 213 us -> none  [the longest x1 166 us: shards(): lax.all_gather(occupied, 'wide', axis=0, tiled=True)]
    pallas_call x0 -> x4, Pallas kernels: none -> 186 us  [the longest x2 163 us: gather(): pl.pallas_call(functools.partial(gather_kernel, plan, outer, half, len(sh...]
    ppermute x0 -> x14, waiting for transfers between devices: none -> 88.3 us  [the longest x10 88.3 us: shift(): return lax.ppermute(x, 'wide', pairs)]
    dot_general x2 -> x0, matrix products: 24.9 us -> none  [the longest x1 15.7 us: shards(): jnp.einsum('pms,qms->pq', own_rows, mixed, preferred_element_type=jnp.flo...]
    ppermute x0 -> x14, starting transfers between devices: none -> 18.4 us  [the longest x10 13.5 us: shift(): return lax.ppermute(x, 'wide', pairs)]
    convert_element_type x1 -> x0, local copies, waits for them, and re-layouts: 12.2 us -> none  [shards(): mixed = jnp.einsum('ml,qls->qms', dens_virt, own_half, preferred_element_...]
    unnamed x4 -> x43, local copies, waits for them, and re-layouts: 0.01 us -> 10.7 us
    gather x2 -> x0, local copies, waits for them, and re-layouts: 8.73 us -> none  [the longest x1 8.14 us: shards(): jnp.take(tensor.reshape(wide_count, block_rows, orb_local, window), ri_or...]
  transfers between devices with their start and end apart: 1 -> 17, of which waited for: 0 -> 8; matrix products, arithmetic and copies ran while one was open for 0% -> 1% of each run, Pallas kernels for 0% -> 4%
where the time goes in v2:
time: 327 us; the launch traced here: 326 us
  Pallas kernels  186 us (57%)
  waiting for transfers between devices  88.3 us (27%)
  starting transfers between devices  30.5 us (9%)
  local copies, waits for them, and re-layouts  12.8 us (4%)
  blocking collectives  8.42 us (3%)
    pallas_call x2, Pallas kernels, gather(): pl.pallas_call(functools.partial(gather_kernel, plan, outer, half, len(sh...  163 us
    ppermute x10, waiting for transfers between devices, shift(): return lax.ppermute(x, 'wide', pairs)  88.3 us
    ppermute x10, starting transfers between devices, shift(): return lax.ppermute(x, 'wide', pairs)  13.5 us
    pallas_call x1, Pallas kernels, shards(): pl.pallas_call(functools.partial(front_kernel, table, [0] + order, outer,...  12.6 us
    all_to_all x3, starting transfers between devices, inplane(): lax.all_to_all(x, 'wide', split_axis=0, concat_axis=0, tiled=True, axis_i...  12.1 us
    unnamed x43, local copies, waits for them, and re-layouts  10.7 us
    pallas_call x1, Pallas kernels, shards(): pl.pallas_call(functools.partial(back_kernel, table, len(arrays)), out_sh...  10.5 us
    all_to_all x1, blocking collectives, inplane(): lax.all_to_all(x, 'wide', split_axis=0, concat_axis=0, tiled=True, axis_i...  8.42 us
  transfers between devices with their start and end apart: 17, of which 8 were waited for; matrix products, arithmetic and copies ran while one was open for 1% of the time, Pallas kernels for 4%

profile of v2, /device:TPU:0, one launch (start us, length us, event | category | flops | bytes accessed | tf_op | source)
XLA Modules:
  0.0 326.2 jit_solution(3716511660433543838)
XLA Ops:
  0.0 33.6 %shard_map.55 = (bf16[32,16,256]{2,1,0:T(8,128)(2,1)}, bf16[32,16,256]{2,1,0:T(8,128)(2,1)}, bf16[32,16,256]{2,1,0:T(8,128)(2,1)}, bf16[32,16,256]{2,1,0:T(8,128)(2,1)}) custom-call(s32[16]{0:T(128)} %order_ref.5, bf16[16,64,16,256]{3,2,1,0:T(8,128)(2,1)} %bitcast.14), custom_call_target="tpu_custom_call" | custom-call | bytes 2097152 | tf_op jit(solution)/shard_map/pallas_call | solution.py:40
  33.6 0.0 copy-start.15
  33.6 0.0 copy-start.16
  33.7 129.1 %shard_map.56 = (bf16[4,32,16,256]{3,2,1,0:T(8,128)(2,1)}, bf16[4,32,16,256]{3,2,1,0:T(8,128)(2,1)}, bf16[4,64,16,256]{3,2,1,0:T(8,128)(2,1)}) custom-call(s32[16]{0:T(128)} %order_ref.5, bf16[16,64,16,256]{3,2,1,0:T(8,128)(2,1)} %bitcast.15), custom_call_target="tpu_custom_call" | custom-call | bytes 8388608 | tf_op jit(solution)/shard_map/pallas_call | solution.py:40
  162.8 4.2 %all-to-all-start = ((bf16[4,32,16,256]{3,2,1,0:T(8,128)(2,1)}), bf16[4,32,16,256]{3,2,1,0:T(8,128)(2,1)S(1)}, u32[]{:S(2)}, u32[]{:S(2)}) async-start(bf16[4,32,16,256]{3,2,1,0:T(8,128)(2,1)} %get-tuple-element.53), calls=%async_computation | async-start | bytes 2097152 | tf_op jit(solution)/shard_map/all_to_all | solution.py:183
  167.0 2.4 collective-permute-start
  169.4 1.3 collective-permute-start.1
  170.8 2.7 collective-permute-start.2
  173.5 0.3 collective-permute-start.3
  173.8 4.8 %collective-permute-done = bf16[32,16,256]{2,1,0:T(8,128)(2,1)S(1)} collective-permute-done((bf16[32,16,256]{2,1,0:T(8,128)(2,1)S(1)}, bf16[32,16,256]{2,1,0:T(8,128)(2,1)S(1)}, u32[]{:S(2)}, u32[]{:S(2)}) %collective-permute-start) | collective-permute-done | bytes 262176 | tf_op jit(solution)/shard_map/ppermute | solution.py:192
  178.6 5.1 %collective-permute-done.1 = bf16[32,16,256]{2,1,0:T(8,128)(2,1)S(1)} collective-permute-done((bf16[32,16,256]{2,1,0:T(8,128)(2,1)S(1)}, bf16[32,16,256]{2,1,0:T(8,128)(2,1)S(1)}, u32[]{:S(2)}, u32[]{:S(2)}) %collective-permute-start.1) | collective-permute-done | bytes 262176 | tf_op jit(solution)/shard_map/ppermute | solution.py:192
  183.7 7.5 %collective-permute-done.2 = bf16[32,16,256]{2,1,0:T(8,128)(2,1)S(1)} collective-permute-done((bf16[32,16,256]{2,1,0:T(8,128)(2,1)S(1)}, bf16[32,16,256]{2,1,0:T(8,128)(2,1)S(1)}, u32[]{:S(2)}, u32[]{:S(2)}) %collective-permute-start.2) | collective-permute-done | bytes 262176 | tf_op jit(solution)/shard_map/ppermute | solution.py:192
  191.2 4.7 %collective-permute-done.3 = bf16[32,16,256]{2,1,0:T(8,128)(2,1)S(1)} collective-permute-done((bf16[32,16,256]{2,1,0:T(8,128)(2,1)S(1)}, bf16[32,16,256]{2,1,0:T(8,128)(2,1)S(1)}, u32[]{:S(2)}, u32[]{:S(2)}) %collective-permute-start.3) | collective-permute-done | bytes 262176 | tf_op jit(solution)/shard_map/ppermute | solution.py:192
  195.9 1.0 copy-done.13
  196.8 0.1 pad_maximum_fusion.rest_1_
  197.0 1.3 collective-permute-start.5
  198.3 1.7 collective-permute-start.4
  200.0 4.3 %all-to-all-start.1 = ((bf16[4,32,16,256]{3,2,1,0:T(8,128)(2,1)}), bf16[4,32,16,256]{3,2,1,0:T(8,128)(2,1)}, u32[]{:S(2)}, u32[]{:S(2)}) async-start(bf16[4,32,16,256]{3,2,1,0:T(8,128)(2,1)} %get-tuple-element.62), calls=%async_computation.1 | async-start | bytes 2097152 | tf_op jit(solution)/shard_map/all_to_all | solution.py:183
  204.3 0.4 collective-permute-start.6
  204.7 0.7 collective-permute-start.7
  205.3 19.2 %collective-permute-done.6 = bf16[2,16,256]{2,1,0:T(8,128)(2,1)S(1)} collective-permute-done((bf16[2,16,256]{2,1,0:T(8,128)(2,1)S(1)}, bf16[2,16,256]{2,1,0:T(8,128)(2,1)S(1)}, u32[]{:S(2)}, u32[]{:S(2)}) %collective-permute-start.6) | collective-permute-done | bytes 16416 | tf_op jit(solution)/shard_map/ppermute | solution.py:192
  224.6 0.0 collective-permute-done.4.rest_3_
  224.6 0.6 collective-permute-start.10
  225.2 2.1 fusion.1
  227.3 2.7 collective-permute-start.9
  229.9 1.3 collective-permute-start.11
  231.2 10.1 %collective-permute-done.11 = bf16[2,16,256]{2,1,0:T(8,128)(2,1)S(1)} collective-permute-done((bf16[2,16,256]{2,1,0:T(8,128)(2,1)S(1)}, bf16[2,16,256]{2,1,0:T(8,128)(2,1)S(1)}, u32[]{:S(2)}, u32[]{:S(2)}) %collective-permute-start.11) | collective-permute-done | bytes 16416 | tf_op jit(solution)/shard_map/ppermute | solution.py:192
  241.4 11.8 %collective-permute-done.9.rest_5_ = bf16[4,16,16,256]{3,2,1,0:T(8,128)(2,1)S(1)} collective-permute-done((bf16[4,16,16,256]{3,2,1,0:T(8,128)(2,1)S(1)}, bf16[4,16,16,256]{3,2,1,0:T(8,128)(2,1)S(1)}, u32[]{:S(2)}, u32[]{:S(2)}) %collective-permute-start.9) | collective-permute-done | bytes 524320 | tf_op jit(solution)/shard_map/ppermute | solution.py:192
  253.1 0.8 copy-done.7
  253.9 8.4 %all_to_all.20 = bf16[4,4,2,16,256]{4,3,2,1,0:T(8,128)(2,1)S(1)} all-to-all(bf16[4,4,2,16,256]{4,3,2,1,0:T(8,128)(2,1)S(1)} %broadcast_in_dim.2), channel_id=1, replica_groups={{0,1,2,3},{4,5,6,7},{8,9,10,11},{12,13,14,15},{16,17,18,19},{20,21,22,2..., dimensions={0} | all-to-all | bytes 524288 | tf_op jit(solution)/shard_map/all_to_all | solution.py:183
  262.4 3.6 %all-to-all-start.3 = ((bf16[4,64,16,256]{3,2,1,0:T(8,128)(2,1)}), bf16[4,64,16,256]{3,2,1,0:T(8,128)(2,1)S(1)}, u32[]{:S(2)}, u32[]{:S(2)}) async-start(bf16[4,64,16,256]{3,2,1,0:T(8,128)(2,1)} %get-tuple-element.67), calls=%async_computation.3 | async-start | bytes 4194304 | tf_op jit(solution)/shard_map/all_to_all | solution.py:183
  266.0 0.1 collective-permute-start.8
  266.1 1.5 collective-permute-start.12
  267.6 25.1 %collective-permute-done.8.rest_6_ = bf16[4,16,16,256]{3,2,1,0:T(8,128)(2,1)S(1)} collective-permute-done((bf16[4,16,16,256]{3,2,1,0:T(8,128)(2,1)}, bf16[4,16,16,256]{3,2,1,0:T(8,128)(2,1)S(1)}, u32[]{:S(2)}, u32[]{:S(2)}) %collective-permute-start.8) | collective-permute-done | bytes 524320 | tf_op jit(solution)/shard_map/ppermute | solution.py:192
  292.7 0.8 copy-done.9
  293.5 0.0 collective-permute-done.12.rest_7_
  293.5 0.8 copy-done.11
  294.3 0.0 all-to-all-done.3.rest_0_
  294.3 1.4 collective-permute-start.13
  295.8 0.1 copy.6.mask_ref
  295.9 1.2 copy-done.3
  297.1 1.2 copy-done.6
  298.3 1.0 copy-done.8
  299.4 1.0 copy-done.10
  300.4 1.0 copy-done.12
  301.5 12.6 %shard_map.57 = (bf16[256,48,256]{2,1,0:T(8,128)(2,1)}, bf16[256,48,256]{2,1,0:T(8,128)(2,1)}, bf16[256,256]{1,0:T(8,128)(2,1)S(1)}, bf16[256,256]{1,0:T(8,128)(2,1)S(1)}, bf16[256,256]{1,0:T(8,128)(2,1)S(1)}) custom-call(s32[16]{0:T(128)S(1)} %copy-done.4, s32[16,4,4]{2,1,0:T(4,128)S(1)} %copy.6.mask_ref, bf16[512,256]{1,0:T(8,128)(2,1)S(1)} %bitcast.13, ...), custom_call_target="tpu_custom_call" | custom-call | flops 3221225472 | bytes 18874368 | tf_op jit(solution)/shard_map/pallas_call | solution.py:292
  314.1 1.6 copy-done.1
  315.7 10.5 %shard_map.58 = f32[64,64]{1,0:T(8,128)} custom-call(bf16[256,256]{1,0:T(8,128)(2,1)S(1)} %get-tuple-element.78.occ_ref, bf16[256,256]{1,0:T(8,128)(2,1)S(1)} %get-tuple-element.79.vir_ref, bf16[256,256]{1,0:T(8,128)(2,1)S(1)} %get-tuple-element.80.keep_ref, bf16[256,48,256]{2,1,0:T(8,128)(2,1)} %get-tuple-element.81.front_mask, ...), custom_call_target="tpu_custom_call" | custom-call | flops 1073741824 | bytes 16777216 | tf_op jit(solution)/shard_map/pallas_call | solution.py:307
  (39 shorter events, 0.1 us)
Async XLA Ops:
  33.6 133.4 %copy-start.20 = (bf16[32,16,256]{2,1,0:T(8,128)(2,1)S(1)}, bf16[32,16,256]{2,1,0:T(8,128)(2,1)}, u32[]{:S(2)}) copy-start(bf16[32,16,256]{2,1,0:T(8,128)(2,1)} %get-tuple-element.48) | copy-start | bytes 786436
  33.6 135.8 %copy-start.19 = (bf16[32,16,256]{2,1,0:T(8,128)(2,1)S(1)}, bf16[32,16,256]{2,1,0:T(8,128)(2,1)}, u32[]{:S(2)}) copy-start(bf16[32,16,256]{2,1,0:T(8,128)(2,1)} %get-tuple-element.49) | copy-start | bytes 786436
  33.6 137.2 %copy-start.18 = (bf16[32,16,256]{2,1,0:T(8,128)(2,1)S(1)}, bf16[32,16,256]{2,1,0:T(8,128)(2,1)}, u32[]{:S(2)}) copy-start(bf16[32,16,256]{2,1,0:T(8,128)(2,1)} %get-tuple-element.50) | copy-start | bytes 786436
  33.6 139.8 %copy-start.17 = (bf16[32,16,256]{2,1,0:T(8,128)(2,1)S(1)}, bf16[32,16,256]{2,1,0:T(8,128)(2,1)}, u32[]{:S(2)}) copy-start(bf16[32,16,256]{2,1,0:T(8,128)(2,1)} %get-tuple-element.51) | copy-start | bytes 786436
  33.6 140.1 %copy-start.15 = (bf16[16,256]{1,0:T(8,128)(2,1)S(1)}, bf16[16,256]{1,0:T(8,128)(2,1)}, u32[]{:S(2)}) copy-start(bf16[16,256]{1,0:T(8,128)(2,1)} %param.7) | copy-start | bytes 24580
  33.6 140.1 %copy-start.16 = (bf16[16,256]{1,0:T(8,128)(2,1)S(1)}, bf16[16,256]{1,0:T(8,128)(2,1)}, u32[]{:S(2)}) copy-start(bf16[16,256]{1,0:T(8,128)(2,1)} %param.6) | copy-start | bytes 24580
  162.8 33.1 %all-to-all-start = ((bf16[4,32,16,256]{3,2,1,0:T(8,128)(2,1)}), bf16[4,32,16,256]{3,2,1,0:T(8,128)(2,1)S(1)}, u32[]{:S(2)}, u32[]{:S(2)}) async-start(bf16[4,32,16,256]{3,2,1,0:T(8,128)(2,1)} %get-tuple-element.53), calls=%async_computation | async-start | bytes 2097152 | tf_op jit(solution)/shard_map/all_to_all | solution.py:183
  167.0 128.8 %copy-start.14 = (s32[16,4,4]{0,2,1:T(4,128)S(1)}, s32[16,4,4]{0,2,1:T(4,128)}, u32[]{:S(2)}) copy-start(s32[16,4,4]{0,2,1:T(4,128)} %param.8) | copy-start | bytes 3076
  167.0 128.9 %copy-start.4 = (s32[16]{0:T(128)S(1)}, s32[16]{0:T(128)}, u32[]{:S(2)}) copy-start(s32[16]{0:T(128)} %order_ref.5) | copy-start | bytes 196
  167.0 11.6 %collective-permute-start = (bf16[32,16,256]{2,1,0:T(8,128)(2,1)S(1)}, bf16[32,16,256]{2,1,0:T(8,128)(2,1)S(1)}, u32[]{:S(2)}, u32[]{:S(2)}) collective-permute-start(bf16[32,16,256]{2,1,0:T(8,128)(2,1)S(1)} %copy-done.20), channel_id=1, source_target_pairs={{0,4},{1,5},{2,6},{3,7},{4,8},{5,9},{6,10},{7,11},{8,12},{9,13},{1... | collective-permute-start | bytes 786440 | tf_op jit(solution)/shard_map/ppermute | solution.py:192
  169.4 14.3 %collective-permute-start.1 = (bf16[32,16,256]{2,1,0:T(8,128)(2,1)S(1)}, bf16[32,16,256]{2,1,0:T(8,128)(2,1)S(1)}, u32[]{:S(2)}, u32[]{:S(2)}) collective-permute-start(bf16[32,16,256]{2,1,0:T(8,128)(2,1)S(1)} %copy-done.19), channel_id=1, source_target_pairs={{0,5},{1,4},{2,7},{3,6},{4,9},{5,8},{6,11},{7,10},{8,13},{9,12},{1... | collective-permute-start | bytes 786440 | tf_op jit(solution)/shard_map/ppermute | solution.py:192
  170.8 20.4 %collective-permute-start.2 = (bf16[32,16,256]{2,1,0:T(8,128)(2,1)S(1)}, bf16[32,16,256]{2,1,0:T(8,128)(2,1)S(1)}, u32[]{:S(2)}, u32[]{:S(2)}) collective-permute-start(bf16[32,16,256]{2,1,0:T(8,128)(2,1)S(1)} %copy-done.18), channel_id=1, source_target_pairs={{0,6},{1,7},{2,4},{3,5},{4,10},{5,11},{6,8},{7,9},{8,14},{9,15},{1... | collective-permute-start | bytes 786440 | tf_op jit(solution)/shard_map/ppermute | solution.py:192
  173.5 22.4 %collective-permute-start.3 = (bf16[32,16,256]{2,1,0:T(8,128)(2,1)S(1)}, bf16[32,16,256]{2,1,0:T(8,128)(2,1)S(1)}, u32[]{:S(2)}, u32[]{:S(2)}) collective-permute-start(bf16[32,16,256]{2,1,0:T(8,128)(2,1)S(1)} %copy-done.17), channel_id=1, source_target_pairs={{0,7},{1,6},{2,5},{3,4},{4,11},{5,10},{6,9},{7,8},{8,15},{9,14},{1... | collective-permute-start | bytes 786440 | tf_op jit(solution)/shard_map/ppermute | solution.py:192
  195.9 1.0 copy-start.13
  197.0 65.4 %copy-start.2 = (bf16[4,32,16,256]{3,2,1,0:T(8,128)(2,1)}, bf16[4,32,16,256]{3,2,1,0:T(8,128)(2,1)S(1)}, u32[]{:S(2)}) copy-start(bf16[4,32,16,256]{3,2,1,0:T(8,128)(2,1)S(1)} %pad_maximum_fusion.rest_1_) | copy-start | bytes 3145732
  197.0 27.6 %collective-permute-start.5 = (bf16[4,32,16,256]{3,2,1,0:T(8,128)(2,1)S(1)}, bf16[4,32,16,256]{3,2,1,0:T(8,128)(2,1)S(1)}, u32[]{:S(2)}, u32[]{:S(2)}) collective-permute-start(bf16[4,32,16,256]{3,2,1,0:T(8,128)(2,1)S(1)} %pad_maximum_fusion.rest_1_), channel_id=1, source_target_pairs={{0,16},{16,0},{1,17},{17,1},{2,18},{18,2},{3,19},{19,3},{4,20},{20... | collective-permute-start | bytes 3145736 | tf_op jit(solution)/shard_map/ppermute | solution.py:195
  198.3 26.3 %collective-permute-start.4 = (bf16[4,32,16,256]{3,2,1,0:T(8,128)(2,1)}, bf16[4,32,16,256]{3,2,1,0:T(8,128)(2,1)S(1)}, u32[]{:S(2)}, u32[]{:S(2)}) collective-permute-start(bf16[4,32,16,256]{3,2,1,0:T(8,128)(2,1)} %copy-done.13), channel_id=1, source_target_pairs={{0,12},{1,13},{2,14},{3,15},{4,0},{5,1},{6,2},{7,3},{8,4},{9,5},{1... | collective-permute-start | bytes 3145736 | tf_op jit(solution)/shard_map/ppermute | solution.py:192
  200.0 24.6 %all-to-all-start.1 = ((bf16[4,32,16,256]{3,2,1,0:T(8,128)(2,1)}), bf16[4,32,16,256]{3,2,1,0:T(8,128)(2,1)}, u32[]{:S(2)}, u32[]{:S(2)}) async-start(bf16[4,32,16,256]{3,2,1,0:T(8,128)(2,1)} %get-tuple-element.62), calls=%async_computation.1 | async-start | bytes 2097152 | tf_op jit(solution)/shard_map/all_to_all | solution.py:183
  204.3 20.3 %collective-permute-start.6 = (bf16[2,16,256]{2,1,0:T(8,128)(2,1)S(1)}, bf16[2,16,256]{2,1,0:T(8,128)(2,1)S(1)}, u32[]{:S(2)}, u32[]{:S(2)}) collective-permute-start(bf16[2,16,256]{2,1,0:T(8,128)(2,1)S(1)} %get-tuple-element.66), channel_id=1, source_target_pairs={{0,4},{1,5},{2,6},{3,7},{4,8},{5,9},{6,10},{7,11},{8,12},{9,13},{1... | collective-permute-start | bytes 49160 | tf_op jit(solution)/shard_map/ppermute | solution.py:192
  204.7 19.9 %collective-permute-start.7 = (bf16[2,16,256]{2,1,0:T(8,128)(2,1)S(1)}, bf16[2,16,256]{2,1,0:T(8,128)(2,1)S(1)}, u32[]{:S(2)}, u32[]{:S(2)}) collective-permute-start(bf16[2,16,256]{2,1,0:T(8,128)(2,1)S(1)} %get-tuple-element.66), channel_id=1, source_target_pairs={{0,8},{1,9},{2,10},{3,11},{4,12},{5,13},{6,14},{7,15},{8,0},{9,1},... | collective-permute-start | bytes 49160 | tf_op jit(solution)/shard_map/ppermute | solution.py:192
  224.6 37.8 %copy-start.5 = (bf16[4,32,16,256]{3,2,1,0:T(8,128)(2,1)}, bf16[4,32,16,256]{3,2,1,0:T(8,128)(2,1)S(1)}, u32[]{:S(2)}) copy-start(bf16[4,32,16,256]{3,2,1,0:T(8,128)(2,1)S(1)} %collective-permute-done.4.rest_3_) | copy-start | bytes 3145732
  224.6 28.5 %collective-permute-start.10 = (bf16[4,32,16,256]{3,2,1,0:T(8,128)(2,1)S(1)}, bf16[4,32,16,256]{3,2,1,0:T(8,128)(2,1)}, u32[]{:S(2)}, u32[]{:S(2)}) collective-permute-start(bf16[4,32,16,256]{3,2,1,0:T(8,128)(2,1)S(1)} %collective-permute-done.4.rest_3_), channel_id=1, source_target_pairs={{0,16},{16,0},{1,17},{17,1},{2,18},{18,2},{3,19},{19,3},{4,20},{20... | collective-permute-start | bytes 3145736 | tf_op jit(solution)/shard_map/ppermute | solution.py:195
  227.3 25.8 %collective-permute-start.9 = (bf16[4,16,16,256]{3,2,1,0:T(8,128)(2,1)S(1)}, bf16[4,16,16,256]{3,2,1,0:T(8,128)(2,1)S(1)}, u32[]{:S(2)}, u32[]{:S(2)}) collective-permute-start(bf16[4,16,16,256]{3,2,1,0:T(8,128)(2,1)S(1)} %get-tuple-element.83), channel_id=1, source_target_pairs={{0,8},{1,9},{2,10},{3,11},{4,12},{5,13},{6,14},{7,15},{8,0},{9,1},... | collective-permute-start | bytes 1572872 | tf_op jit(solution)/shard_map/ppermute | solution.py:192
  229.9 11.4 %collective-permute-start.11 = (bf16[2,16,256]{2,1,0:T(8,128)(2,1)S(1)}, bf16[2,16,256]{2,1,0:T(8,128)(2,1)S(1)}, u32[]{:S(2)}, u32[]{:S(2)}) collective-permute-start(bf16[2,16,256]{2,1,0:T(8,128)(2,1)S(1)} %get-tuple-element.66), channel_id=1, source_target_pairs={{0,12},{1,13},{2,14},{3,15},{4,0},{5,1},{6,2},{7,3},{8,4},{9,5},{1... | collective-permute-start | bytes 49160 | tf_op jit(solution)/shard_map/ppermute | solution.py:192
  253.1 0.8 copy-start.7
  262.4 31.9 %all-to-all-start.3 = ((bf16[4,64,16,256]{3,2,1,0:T(8,128)(2,1)}), bf16[4,64,16,256]{3,2,1,0:T(8,128)(2,1)S(1)}, u32[]{:S(2)}, u32[]{:S(2)}) async-start(bf16[4,64,16,256]{3,2,1,0:T(8,128)(2,1)} %get-tuple-element.67), calls=%async_computation.3 | async-start | bytes 4194304 | tf_op jit(solution)/shard_map/all_to_all | solution.py:183
  266.0 26.7 %collective-permute-start.8 = (bf16[4,16,16,256]{3,2,1,0:T(8,128)(2,1)}, bf16[4,16,16,256]{3,2,1,0:T(8,128)(2,1)S(1)}, u32[]{:S(2)}, u32[]{:S(2)}) collective-permute-start(bf16[4,16,16,256]{3,2,1,0:T(8,128)(2,1)} %get-tuple-element.84), channel_id=1, source_target_pairs={{0,8},{1,9},{2,10},{3,11},{4,12},{5,13},{6,14},{7,15},{8,0},{9,1},... | collective-permute-start | bytes 1572872 | tf_op jit(solution)/shard_map/ppermute | solution.py:192
  266.1 27.4 %collective-permute-start.12 = (bf16[4,16,16,256]{3,2,1,0:T(8,128)(2,1)}, bf16[4,16,16,256]{3,2,1,0:T(8,128)(2,1)S(1)}, u32[]{:S(2)}, u32[]{:S(2)}) collective-permute-start(bf16[4,16,16,256]{3,2,1,0:T(8,128)(2,1)} %copy-done.7), channel_id=1, source_target_pairs={{0,16},{16,0},{1,17},{17,1},{2,18},{18,2},{3,19},{19,3},{4,20},{20... | collective-permute-start | bytes 1572872 | tf_op jit(solution)/shard_map/ppermute | solution.py:195
  292.7 0.8 copy-start.9
  293.5 0.8 copy-start.11
  294.3 1.6 copy-start
  294.3 19.8 %collective-permute-start.13 = (bf16[4,16,16,256]{3,2,1,0:T(8,128)(2,1)}, bf16[4,16,16,256]{3,2,1,0:T(8,128)(2,1)}, u32[]{:S(2)}, u32[]{:S(2)}) collective-permute-start(bf16[4,16,16,256]{3,2,1,0:T(8,128)(2,1)} %copy-done.9), channel_id=1, source_target_pairs={{0,16},{16,0},{1,17},{17,1},{2,18},{18,2},{3,19},{19,3},{4,20},{20... | collective-permute-start | bytes 1572872 | tf_op jit(solution)/shard_map/ppermute | solution.py:195
  295.9 1.2 copy-start.3
  297.1 1.2 copy-start.6
  298.3 1.0 copy-start.8
  299.4 1.0 copy-start.10
  300.4 1.0 copy-start.12
  314.1 1.6 copy-start.1

commit v3 on v2

--- a/solution.py
+++ b/solution.py
@@ -41,7 +41,8 @@
         functools.partial(gather_kernel, plan, outer, half, len(shapes)),
         out_shape=shapes,
         in_specs=[SMEM, HBM],
-        out_specs=[HBM] * len(shapes),
+        out_specs=[VMEM] * len(shapes),
+        compiler_params=pltpu.CompilerParams(vmem_limit_bytes=24 * 2**20),
         scratch_shapes=[pltpu.SemaphoreType.DMA((len(plan),))],
         cost_estimate=pl.CostEstimate(flops=0, bytes_accessed=size, transcendentals=0),
     )(ri_order, blocks)
@@ -214,7 +215,7 @@
 
     base = jnp.stack([occupied, virtual])
     dens, small = [base], list(range(1, outer))
-    per_phase = -(-len(small) // (outer - 2))
+    per_phase = -(-len(small) // max(1, outer - 3))
     own_in, swapped = [], []
     for k in range(outer):
         if k == 0:
@@ -231,10 +232,10 @@
         if k <= outer - 3:
             near_by = [inplane(to_send[k])]
         elif k == outer - 2:
-            near = inplane(to_near)
+            near_by = [inplane(to_near)]
         else:
             spread = jnp.broadcast_to(jnp.stack(dens)[None], (PLANE, outer, 2, orb, window))
-            near_by = [inplane(spread), near]
+            near_by = [inplane(spread)]
         moved, turn, tiny, near_by, to_send, to_near, base = barrier(
             (moved, turn, tiny, near_by, to_send, to_near, base)
         )
@@ -245,7 +246,9 @@
             ready = near_by[0]
             if k == outer - 3:
                 ready = [ready[:, :quarter], ready[:, quarter:]]
-    dens_all, near = near_by
+        elif k == outer - 2:
+            near = near_by[0]
+    dens_all = near_by[0]
     swapped.append(swap(own_in[-1]))
 
     front, back = [], []
@@ -284,7 +287,7 @@
     def copies(table):
         return sum(p[3] // ROWS for p in table)
 
-    params = pltpu.CompilerParams(vmem_limit_bytes=48 * 2**20)
+    params = pltpu.CompilerParams(vmem_limit_bytes=58 * 2**20)
     table, arrays = places(front)
     done = half + quarter
     mat = jax.ShapeDtypeStruct((window, window), kind)

time: 327 us -> 155 us (0.47)
  Pallas kernels: 186 us -> 28.7 us
  waiting for transfers between devices: 88.3 us -> 76.6 us
  local copies, waits for them, and re-layouts: 12.8 us -> 7.45 us
    pallas_call x2, Pallas kernels: 163 us -> 3.74 us  [gather(): pl.pallas_call(functools.partial(gather_kernel, plan, outer, half, len(sh...]
    ppermute x10, waiting for transfers between devices: 88.3 us -> 74.8 us  [shift(): return lax.ppermute(x, 'wide', pairs)]
    unnamed x43 -> x21, local copies, waits for them, and re-layouts: 10.7 us -> 6.54 us
  transfers between devices with their start and end apart: 17 -> 17, of which waited for: 8 -> 8; matrix products, arithmetic and copies ran while one was open for 1% -> 1% of each run, Pallas kernels for 4% -> 9%
where the time goes in v3:
time: 155 us; the launch traced here: 154 us
  waiting for transfers between devices  76.6 us (49%)
  starting transfers between devices  32.2 us (21%)
  Pallas kernels  28.7 us (19%)
  blocking collectives  9.17 us (6%)
  local copies, waits for them, and re-layouts  7.45 us (5%)
    ppermute x10, waiting for transfers between devices, shift(): return lax.ppermute(x, 'wide', pairs)  74.8 us
    ppermute x10, starting transfers between devices, shift(): return lax.ppermute(x, 'wide', pairs)  15.8 us
    pallas_call x1, Pallas kernels, shards(): pl.pallas_call(functools.partial(front_kernel, table, [0] + order, outer,...  13.2 us
    pallas_call x1, Pallas kernels, shards(): pl.pallas_call(functools.partial(back_kernel, table, len(arrays)), out_sh...  11.8 us
    all_to_all x3, starting transfers between devices, inplane(): lax.all_to_all(x, 'wide', split_axis=0, concat_axis=0, tiled=True, axis_i...  11.4 us
    all_to_all x1, blocking collectives, inplane(): lax.all_to_all(x, 'wide', split_axis=0, concat_axis=0, tiled=True, axis_i...  9.17 us
    unnamed x21, local copies, waits for them, and re-layouts  6.54 us
    ppermute x4, starting transfers between devices, swap(): return lax.ppermute(x, 'groups', [(0, 1), (1, 0)])  5.01 us
  transfers between devices with their start and end apart: 17, of which 8 were waited for; matrix products, arithmetic and copies ran while one was open for 1% of the time, Pallas kernels for 9%

profile of v3, /device:TPU:0, one launch (start us, length us, event | category | flops | bytes accessed | tf_op | source)
XLA Modules:
  0.0 154.4 jit_solution(4561314299809906397)
XLA Ops:
  0.0 3.4 %copy-done = bf16[1024,16,256]{2,1,0:T(8,128)(2,1)S(1)} copy-done((bf16[1024,16,256]{2,1,0:T(8,128)(2,1)S(1)}, bf16[1024,16,256]{2,1,0:T(8,128)(2,1)}, u32[]{:S(2)}) %copy-start) | copy-done | bytes 8388632
  3.4 0.7 copy-done.1
  4.0 0.7 shard_map.55
  4.7 0.0 copy-start.7
  4.7 0.0 copy-start.8
  4.8 3.1 %shard_map.56 = (bf16[4,32,16,256]{3,2,1,0:T(8,128)(2,1)}, bf16[4,32,16,256]{3,2,1,0:T(8,128)(2,1)}, bf16[4,64,16,256]{3,2,1,0:T(8,128)(2,1)}) custom-call(s32[16]{0:T(128)S(1)} %copy-done.1, bf16[16,64,16,256]{3,2,1,0:T(8,128)(2,1)S(1)} %bitcast.14), custom_call_target="tpu_custom_call" | custom-call | bytes 8388608 | tf_op jit(solution)/shard_map/pallas_call | solution.py:40
  7.8 4.3 %all-to-all-start = ((bf16[4,32,16,256]{3,2,1,0:T(8,128)(2,1)}), bf16[4,32,16,256]{3,2,1,0:T(8,128)(2,1)}, u32[]{:S(2)}, u32[]{:S(2)}) async-start(bf16[4,32,16,256]{3,2,1,0:T(8,128)(2,1)} %get-tuple-element.52), calls=%async_computation | async-start | bytes 2097152 | tf_op jit(solution)/shard_map/all_to_all | solution.py:184
  12.1 0.0 copy-start.6
  12.1 3.1 %collective-permute-start = (bf16[32,16,256]{2,1,0:T(8,128)(2,1)S(1)}, bf16[32,16,256]{2,1,0:T(8,128)(2,1)S(1)}, u32[]{:S(2)}, u32[]{:S(2)}) collective-permute-start(bf16[32,16,256]{2,1,0:T(8,128)(2,1)S(1)} %get-tuple-element.47), channel_id=1, source_target_pairs={{0,4},{1,5},{2,6},{3,7},{4,8},{5,9},{6,10},{7,11},{8,12},{9,13},{1... | collective-permute-start | bytes 786440 | tf_op jit(solution)/shard_map/ppermute | solution.py:193
  15.2 1.3 collective-permute-start.1
  16.5 2.6 %collective-permute-start.2 = (bf16[32,16,256]{2,1,0:T(8,128)(2,1)S(1)}, bf16[32,16,256]{2,1,0:T(8,128)(2,1)S(1)}, u32[]{:S(2)}, u32[]{:S(2)}) collective-permute-start(bf16[32,16,256]{2,1,0:T(8,128)(2,1)S(1)} %get-tuple-element.49), channel_id=1, source_target_pairs={{0,6},{1,7},{2,4},{3,5},{4,10},{5,11},{6,8},{7,9},{8,14},{9,15},{1... | collective-permute-start | bytes 786440 | tf_op jit(solution)/shard_map/ppermute | solution.py:193
  19.2 0.3 collective-permute-start.3
  19.4 4.9 %collective-permute-done = bf16[32,16,256]{2,1,0:T(8,128)(2,1)S(1)} collective-permute-done((bf16[32,16,256]{2,1,0:T(8,128)(2,1)S(1)}, bf16[32,16,256]{2,1,0:T(8,128)(2,1)S(1)}, u32[]{:S(2)}, u32[]{:S(2)}) %collective-permute-start) | collective-permute-done | bytes 262176 | tf_op jit(solution)/shard_map/ppermute | solution.py:193
  24.4 5.0 %collective-permute-done.1 = bf16[32,16,256]{2,1,0:T(8,128)(2,1)S(1)} collective-permute-done((bf16[32,16,256]{2,1,0:T(8,128)(2,1)S(1)}, bf16[32,16,256]{2,1,0:T(8,128)(2,1)S(1)}, u32[]{:S(2)}, u32[]{:S(2)}) %collective-permute-start.1) | collective-permute-done | bytes 262176 | tf_op jit(solution)/shard_map/ppermute | solution.py:193
  29.4 7.5 %collective-permute-done.2 = bf16[32,16,256]{2,1,0:T(8,128)(2,1)S(1)} collective-permute-done((bf16[32,16,256]{2,1,0:T(8,128)(2,1)S(1)}, bf16[32,16,256]{2,1,0:T(8,128)(2,1)S(1)}, u32[]{:S(2)}, u32[]{:S(2)}) %collective-permute-start.2) | collective-permute-done | bytes 262176 | tf_op jit(solution)/shard_map/ppermute | solution.py:193
  36.9 4.7 %collective-permute-done.3 = bf16[32,16,256]{2,1,0:T(8,128)(2,1)S(1)} collective-permute-done((bf16[32,16,256]{2,1,0:T(8,128)(2,1)S(1)}, bf16[32,16,256]{2,1,0:T(8,128)(2,1)S(1)}, u32[]{:S(2)}, u32[]{:S(2)}) %collective-permute-start.3) | collective-permute-done | bytes 262176 | tf_op jit(solution)/shard_map/ppermute | solution.py:193
  41.5 0.0 all-to-all-done
  41.5 0.1 pad_maximum_fusion.rest_1_
  41.7 1.3 collective-permute-start.5
  43.0 1.7 %collective-permute-start.4 = (bf16[4,32,16,256]{3,2,1,0:T(8,128)(2,1)}, bf16[4,32,16,256]{3,2,1,0:T(8,128)(2,1)}, u32[]{:S(2)}, u32[]{:S(2)}) collective-permute-start(bf16[4,32,16,256]{3,2,1,0:T(8,128)(2,1)} %all-to-all-done), channel_id=1, source_target_pairs={{0,12},{1,13},{2,14},{3,15},{4,0},{5,1},{6,2},{7,3},{8,4},{9,5},{1... | collective-permute-start | bytes 3145736 | tf_op jit(solution)/shard_map/ppermute | solution.py:193
  44.7 3.5 %all-to-all-start.1 = ((bf16[4,32,16,256]{3,2,1,0:T(8,128)(2,1)}), bf16[4,32,16,256]{3,2,1,0:T(8,128)(2,1)S(1)}, u32[]{:S(2)}, u32[]{:S(2)}) async-start(bf16[4,32,16,256]{3,2,1,0:T(8,128)(2,1)} %get-tuple-element.61), calls=%async_computation.1 | async-start | bytes 2097152 | tf_op jit(solution)/shard_map/all_to_all | solution.py:184
  48.2 0.4 collective-permute-start.6
  48.6 0.7 collective-permute-start.7
  49.3 2.8 %collective-permute-start.8 = (bf16[2,16,256]{2,1,0:T(8,128)(2,1)S(1)}, bf16[2,16,256]{2,1,0:T(8,128)(2,1)S(1)}, u32[]{:S(2)}, u32[]{:S(2)}) collective-permute-start(bf16[2,16,256]{2,1,0:T(8,128)(2,1)S(1)} %get-tuple-element.60), channel_id=1, source_target_pairs={{0,12},{1,13},{2,14},{3,15},{4,0},{5,1},{6,2},{7,3},{8,4},{9,5},{1... | collective-permute-start | bytes 49160 | tf_op jit(solution)/shard_map/ppermute | solution.py:193
  52.1 17.4 %collective-permute-done.6 = bf16[2,16,256]{2,1,0:T(8,128)(2,1)S(1)} collective-permute-done((bf16[2,16,256]{2,1,0:T(8,128)(2,1)S(1)}, bf16[2,16,256]{2,1,0:T(8,128)(2,1)S(1)}, u32[]{:S(2)}, u32[]{:S(2)}) %collective-permute-start.6) | collective-permute-done | bytes 16416 | tf_op jit(solution)/shard_map/ppermute | solution.py:193
  69.5 0.0 collective-permute-done.7
  69.5 0.1 collective-permute-done.8
  69.6 0.0 all-to-all-done.1
  69.6 0.0 collective-permute-done.5.rest_2_.rest_1_
  69.6 0.0 collective-permute-done.4.rest_3_
  69.7 1.0 copy-done.3
  70.6 3.6 %all-to-all-start.2 = ((bf16[4,64,16,256]{3,2,1,0:T(8,128)(2,1)}), bf16[4,64,16,256]{3,2,1,0:T(8,128)(2,1)S(1)}, u32[]{:S(2)}, u32[]{:S(2)}) async-start(bf16[4,64,16,256]{3,2,1,0:T(8,128)(2,1)} %get-tuple-element.65), calls=%async_computation.2 | async-start | bytes 4194304 | tf_op jit(solution)/shard_map/all_to_all | solution.py:184
  74.2 0.6 collective-permute-start.11
  74.8 0.9 fusion.1
  75.7 2.5 %collective-permute-start.10 = (bf16[4,16,16,256]{3,2,1,0:T(8,128)(2,1)S(1)}, bf16[4,16,16,256]{3,2,1,0:T(8,128)(2,1)S(1)}, u32[]{:S(2)}, u32[]{:S(2)}) collective-permute-start(bf16[4,16,16,256]{3,2,1,0:T(8,128)(2,1)S(1)} %get-tuple-element.81), channel_id=1, source_target_pairs={{0,8},{1,9},{2,10},{3,11},{4,12},{5,13},{6,14},{7,15},{8,0},{9,1},... | collective-permute-start | bytes 1572872 | tf_op jit(solution)/shard_map/ppermute | solution.py:193
  78.2 0.4 collective-permute-start.9
  78.6 35.2 %collective-permute-done.10.rest_5_ = bf16[4,16,16,256]{3,2,1,0:T(8,128)(2,1)S(1)} collective-permute-done((bf16[4,16,16,256]{3,2,1,0:T(8,128)(2,1)S(1)}, bf16[4,16,16,256]{3,2,1,0:T(8,128)(2,1)S(1)}, u32[]{:S(2)}, u32[]{:S(2)}) %collective-permute-start.10) | collective-permute-done | bytes 524320 | tf_op jit(solution)/shard_map/ppermute | solution.py:193
  113.8 0.0 collective-permute-done.11.rest_4_.rest_2_
  113.8 0.0 all-to-all-done.2.rest_0_
  113.9 1.6 %collective-permute-start.12 = (bf16[4,16,16,256]{3,2,1,0:T(8,128)(2,1)S(1)}, bf16[4,16,16,256]{3,2,1,0:T(8,128)(2,1)}, u32[]{:S(2)}, u32[]{:S(2)}) collective-permute-start(bf16[4,16,16,256]{3,2,1,0:T(8,128)(2,1)S(1)} %collective-permute-done.10.rest_5_), channel_id=1, source_target_pairs={{0,16},{16,0},{1,17},{17,1},{2,18},{18,2},{3,19},{19,3},{4,20},{20... | collective-permute-start | bytes 1572872 | tf_op jit(solution)/shard_map/ppermute | solution.py:196
  115.5 9.2 %all_to_all.20 = bf16[4,4,2,16,256]{4,3,2,1,0:T(8,128)(2,1)} all-to-all(bf16[4,4,2,16,256]{4,3,2,1,0:T(8,128)(2,1)S(1)} %broadcast_in_dim.2), channel_id=1, replica_groups={{0,1,2,3},{4,5,6,7},{8,9,10,11},{12,13,14,15},{16,17,18,19},{20,21,22,2..., dimensions={0} | all-to-all | bytes 524288 | tf_op jit(solution)/shard_map/all_to_all | solution.py:184
  124.7 1.7 %collective-permute-done.12.rest_7_ = bf16[4,16,16,256]{3,2,1,0:T(8,128)(2,1)} collective-permute-done((bf16[4,16,16,256]{3,2,1,0:T(8,128)(2,1)S(1)}, bf16[4,16,16,256]{3,2,1,0:T(8,128)(2,1)}, u32[]{:S(2)}, u32[]{:S(2)}) %collective-permute-start.12) | collective-permute-done | bytes 524320 | tf_op jit(solution)/shard_map/ppermute | solution.py:196
  126.4 1.5 collective-permute-start.13
  127.9 0.7 copy.6.mask_ref
  128.6 13.2 %shard_map.57 = (bf16[256,48,256]{2,1,0:T(8,128)(2,1)}, bf16[256,48,256]{2,1,0:T(8,128)(2,1)}, bf16[256,256]{1,0:T(8,128)(2,1)}, bf16[256,256]{1,0:T(8,128)(2,1)}, bf16[256,256]{1,0:T(8,128)(2,1)}) custom-call(s32[16]{0:T(128)} %order_ref.5, s32[16,4,4]{2,1,0:T(4,128)} %copy.6.mask_ref, bf16[512,256]{1,0:T(8,128)(2,1)} %bitcast.15, ...), custom_call_target="tpu_custom_call" | custom-call | flops 3221225472 | bytes 18874368 | tf_op jit(solution)/shard_map/pallas_call | solution.py:295
  141.9 0.0 collective-permute-done.13.rest_3_
  141.9 0.8 copy-done.5
  142.7 11.8 %shard_map.58 = f32[64,64]{1,0:T(8,128)} custom-call(bf16[256,256]{1,0:T(8,128)(2,1)} %get-tuple-element.76.occ_ref, bf16[256,256]{1,0:T(8,128)(2,1)} %get-tuple-element.77.vir_ref, bf16[256,256]{1,0:T(8,128)(2,1)} %get-tuple-element.78.keep_ref, bf16[256,48,256]{2,1,0:T(8,128)(2,1)} %get-tuple-element.79.front_mask, ...), custom_call_target="tpu_custom_call" | custom-call | flops 1073741824 | bytes 16777216 | tf_op jit(solution)/shard_map/pallas_call | solution.py:310
  (17 shorter events, 0.1 us)
Async XLA Ops:
  0.0 3.4 %copy-start = (bf16[1024,16,256]{2,1,0:T(8,128)(2,1)S(1)}, bf16[1024,16,256]{2,1,0:T(8,128)(2,1)}, u32[]{:S(2)}) copy-start(bf16[1024,16,256]{2,1,0:T(8,128)(2,1)} %param.5) | copy-start | bytes 25165828
  3.4 0.7 copy-start.1
  4.7 14.7 %copy-start.7 = (bf16[16,256]{1,0:T(8,128)(2,1)S(1)}, bf16[16,256]{1,0:T(8,128)(2,1)}, u32[]{:S(2)}) copy-start(bf16[16,256]{1,0:T(8,128)(2,1)} %param.7) | copy-start | bytes 24580
  4.7 14.7 %copy-start.8 = (bf16[16,256]{1,0:T(8,128)(2,1)S(1)}, bf16[16,256]{1,0:T(8,128)(2,1)}, u32[]{:S(2)}) copy-start(bf16[16,256]{1,0:T(8,128)(2,1)} %param.6) | copy-start | bytes 24580
  7.8 33.7 %all-to-all-start = ((bf16[4,32,16,256]{3,2,1,0:T(8,128)(2,1)}), bf16[4,32,16,256]{3,2,1,0:T(8,128)(2,1)}, u32[]{:S(2)}, u32[]{:S(2)}) async-start(bf16[4,32,16,256]{3,2,1,0:T(8,128)(2,1)} %get-tuple-element.52), calls=%async_computation | async-start | bytes 2097152 | tf_op jit(solution)/shard_map/all_to_all | solution.py:184
  12.1 115.8 %copy-start.6 = (s32[16,4,4]{0,2,1:T(4,128)S(1)}, s32[16,4,4]{0,2,1:T(4,128)}, u32[]{:S(2)}) copy-start(s32[16,4,4]{0,2,1:T(4,128)} %param.8) | copy-start | bytes 3076
  12.1 12.3 %collective-permute-start = (bf16[32,16,256]{2,1,0:T(8,128)(2,1)S(1)}, bf16[32,16,256]{2,1,0:T(8,128)(2,1)S(1)}, u32[]{:S(2)}, u32[]{:S(2)}) collective-permute-start(bf16[32,16,256]{2,1,0:T(8,128)(2,1)S(1)} %get-tuple-element.47), channel_id=1, source_target_pairs={{0,4},{1,5},{2,6},{3,7},{4,8},{5,9},{6,10},{7,11},{8,12},{9,13},{1... | collective-permute-start | bytes 786440 | tf_op jit(solution)/shard_map/ppermute | solution.py:193
  15.2 14.2 %collective-permute-start.1 = (bf16[32,16,256]{2,1,0:T(8,128)(2,1)S(1)}, bf16[32,16,256]{2,1,0:T(8,128)(2,1)S(1)}, u32[]{:S(2)}, u32[]{:S(2)}) collective-permute-start(bf16[32,16,256]{2,1,0:T(8,128)(2,1)S(1)} %get-tuple-element.48), channel_id=1, source_target_pairs={{0,5},{1,4},{2,7},{3,6},{4,9},{5,8},{6,11},{7,10},{8,13},{9,12},{1... | collective-permute-start | bytes 786440 | tf_op jit(solution)/shard_map/ppermute | solution.py:193
  16.5 20.4 %collective-permute-start.2 = (bf16[32,16,256]{2,1,0:T(8,128)(2,1)S(1)}, bf16[32,16,256]{2,1,0:T(8,128)(2,1)S(1)}, u32[]{:S(2)}, u32[]{:S(2)}) collective-permute-start(bf16[32,16,256]{2,1,0:T(8,128)(2,1)S(1)} %get-tuple-element.49), channel_id=1, source_target_pairs={{0,6},{1,7},{2,4},{3,5},{4,10},{5,11},{6,8},{7,9},{8,14},{9,15},{1... | collective-permute-start | bytes 786440 | tf_op jit(solution)/shard_map/ppermute | solution.py:193
  19.2 22.4 %collective-permute-start.3 = (bf16[32,16,256]{2,1,0:T(8,128)(2,1)S(1)}, bf16[32,16,256]{2,1,0:T(8,128)(2,1)S(1)}, u32[]{:S(2)}, u32[]{:S(2)}) collective-permute-start(bf16[32,16,256]{2,1,0:T(8,128)(2,1)S(1)} %get-tuple-element.50), channel_id=1, source_target_pairs={{0,7},{1,6},{2,5},{3,4},{4,11},{5,10},{6,9},{7,8},{8,15},{9,14},{1... | collective-permute-start | bytes 786440 | tf_op jit(solution)/shard_map/ppermute | solution.py:193
  41.7 28.0 %copy-start.4 = (bf16[4,32,16,256]{3,2,1,0:T(8,128)(2,1)}, bf16[4,32,16,256]{3,2,1,0:T(8,128)(2,1)S(1)}, u32[]{:S(2)}) copy-start(bf16[4,32,16,256]{3,2,1,0:T(8,128)(2,1)S(1)} %pad_maximum_fusion.rest_1_) | copy-start | bytes 3145732
  41.7 27.9 %collective-permute-start.5 = (bf16[4,32,16,256]{3,2,1,0:T(8,128)(2,1)S(1)}, bf16[4,32,16,256]{3,2,1,0:T(8,128)(2,1)S(1)}, u32[]{:S(2)}, u32[]{:S(2)}) collective-permute-start(bf16[4,32,16,256]{3,2,1,0:T(8,128)(2,1)S(1)} %pad_maximum_fusion.rest_1_), channel_id=1, source_target_pairs={{0,16},{16,0},{1,17},{17,1},{2,18},{18,2},{3,19},{19,3},{4,20},{20... | collective-permute-start | bytes 3145736 | tf_op jit(solution)/shard_map/ppermute | solution.py:196
  43.0 26.6 %collective-permute-start.4 = (bf16[4,32,16,256]{3,2,1,0:T(8,128)(2,1)}, bf16[4,32,16,256]{3,2,1,0:T(8,128)(2,1)}, u32[]{:S(2)}, u32[]{:S(2)}) collective-permute-start(bf16[4,32,16,256]{3,2,1,0:T(8,128)(2,1)} %all-to-all-done), channel_id=1, source_target_pairs={{0,12},{1,13},{2,14},{3,15},{4,0},{5,1},{6,2},{7,3},{8,4},{9,5},{1... | collective-permute-start | bytes 3145736 | tf_op jit(solution)/shard_map/ppermute | solution.py:193
  44.7 24.9 %all-to-all-start.1 = ((bf16[4,32,16,256]{3,2,1,0:T(8,128)(2,1)}), bf16[4,32,16,256]{3,2,1,0:T(8,128)(2,1)S(1)}, u32[]{:S(2)}, u32[]{:S(2)}) async-start(bf16[4,32,16,256]{3,2,1,0:T(8,128)(2,1)} %get-tuple-element.61), calls=%async_computation.1 | async-start | bytes 2097152 | tf_op jit(solution)/shard_map/all_to_all | solution.py:184
  48.2 21.3 %collective-permute-start.6 = (bf16[2,16,256]{2,1,0:T(8,128)(2,1)S(1)}, bf16[2,16,256]{2,1,0:T(8,128)(2,1)S(1)}, u32[]{:S(2)}, u32[]{:S(2)}) collective-permute-start(bf16[2,16,256]{2,1,0:T(8,128)(2,1)S(1)} %get-tuple-element.60), channel_id=1, source_target_pairs={{0,4},{1,5},{2,6},{3,7},{4,8},{5,9},{6,10},{7,11},{8,12},{9,13},{1... | collective-permute-start | bytes 49160 | tf_op jit(solution)/shard_map/ppermute | solution.py:193
  48.6 20.9 %collective-permute-start.7 = (bf16[2,16,256]{2,1,0:T(8,128)(2,1)S(1)}, bf16[2,16,256]{2,1,0:T(8,128)(2,1)S(1)}, u32[]{:S(2)}, u32[]{:S(2)}) collective-permute-start(bf16[2,16,256]{2,1,0:T(8,128)(2,1)S(1)} %get-tuple-element.60), channel_id=1, source_target_pairs={{0,8},{1,9},{2,10},{3,11},{4,12},{5,13},{6,14},{7,15},{8,0},{9,1},... | collective-permute-start | bytes 49160 | tf_op jit(solution)/shard_map/ppermute | solution.py:193
  49.3 20.3 %collective-permute-start.8 = (bf16[2,16,256]{2,1,0:T(8,128)(2,1)S(1)}, bf16[2,16,256]{2,1,0:T(8,128)(2,1)S(1)}, u32[]{:S(2)}, u32[]{:S(2)}) collective-permute-start(bf16[2,16,256]{2,1,0:T(8,128)(2,1)S(1)} %get-tuple-element.60), channel_id=1, source_target_pairs={{0,12},{1,13},{2,14},{3,15},{4,0},{5,1},{6,2},{7,3},{8,4},{9,5},{1... | collective-permute-start | bytes 49160 | tf_op jit(solution)/shard_map/ppermute | solution.py:193
  69.6 1.0 copy-start.3
  70.6 43.2 %all-to-all-start.2 = ((bf16[4,64,16,256]{3,2,1,0:T(8,128)(2,1)}), bf16[4,64,16,256]{3,2,1,0:T(8,128)(2,1)S(1)}, u32[]{:S(2)}, u32[]{:S(2)}) async-start(bf16[4,64,16,256]{3,2,1,0:T(8,128)(2,1)} %get-tuple-element.65), calls=%async_computation.2 | async-start | bytes 4194304 | tf_op jit(solution)/shard_map/all_to_all | solution.py:184
  74.2 39.6 %collective-permute-start.11 = (bf16[4,32,16,256]{3,2,1,0:T(8,128)(2,1)}, bf16[4,32,16,256]{3,2,1,0:T(8,128)(2,1)}, u32[]{:S(2)}, u32[]{:S(2)}) collective-permute-start(bf16[4,32,16,256]{3,2,1,0:T(8,128)(2,1)} %collective-permute-done.4.rest_3_), channel_id=1, source_target_pairs={{0,16},{16,0},{1,17},{17,1},{2,18},{18,2},{3,19},{19,3},{4,20},{20... | collective-permute-start | bytes 3145736 | tf_op jit(solution)/shard_map/ppermute | solution.py:196
  75.7 38.1 %collective-permute-start.10 = (bf16[4,16,16,256]{3,2,1,0:T(8,128)(2,1)S(1)}, bf16[4,16,16,256]{3,2,1,0:T(8,128)(2,1)S(1)}, u32[]{:S(2)}, u32[]{:S(2)}) collective-permute-start(bf16[4,16,16,256]{3,2,1,0:T(8,128)(2,1)S(1)} %get-tuple-element.81), channel_id=1, source_target_pairs={{0,8},{1,9},{2,10},{3,11},{4,12},{5,13},{6,14},{7,15},{8,0},{9,1},... | collective-permute-start | bytes 1572872 | tf_op jit(solution)/shard_map/ppermute | solution.py:193
  78.2 46.4 %collective-permute-start.9 = (bf16[4,16,16,256]{3,2,1,0:T(8,128)(2,1)}, bf16[4,16,16,256]{3,2,1,0:T(8,128)(2,1)}, u32[]{:S(2)}, u32[]{:S(2)}) collective-permute-start(bf16[4,16,16,256]{3,2,1,0:T(8,128)(2,1)} %get-tuple-element.82), channel_id=1, source_target_pairs={{0,8},{1,9},{2,10},{3,11},{4,12},{5,13},{6,14},{7,15},{8,0},{9,1},... | collective-permute-start | bytes 1572872 | tf_op jit(solution)/shard_map/ppermute | solution.py:193
  113.8 14.8 %copy-start.9 = (bf16[4,16,16,256]{3,2,1,0:T(8,128)(2,1)}, bf16[4,16,16,256]{3,2,1,0:T(8,128)(2,1)S(1)}, u32[]{:S(2)}) copy-start(bf16[4,16,16,256]{3,2,1,0:T(8,128)(2,1)S(1)} %collective-permute-done.10.rest_5_) | copy-start | bytes 1572868
  113.8 14.8 %copy-start.2 = (bf16[4,64,16,256]{3,2,1,0:T(8,128)(2,1)}, bf16[4,64,16,256]{3,2,1,0:T(8,128)(2,1)S(1)}, u32[]{:S(2)}) copy-start(bf16[4,64,16,256]{3,2,1,0:T(8,128)(2,1)S(1)} %all-to-all-done.2.rest_0_) | copy-start | bytes 6291460
  113.9 12.5 %collective-permute-start.12 = (bf16[4,16,16,256]{3,2,1,0:T(8,128)(2,1)S(1)}, bf16[4,16,16,256]{3,2,1,0:T(8,128)(2,1)}, u32[]{:S(2)}, u32[]{:S(2)}) collective-permute-start(bf16[4,16,16,256]{3,2,1,0:T(8,128)(2,1)S(1)} %collective-permute-done.10.rest_5_), channel_id=1, source_target_pairs={{0,16},{16,0},{1,17},{17,1},{2,18},{18,2},{3,19},{19,3},{4,20},{20... | collective-permute-start | bytes 1572872 | tf_op jit(solution)/shard_map/ppermute | solution.py:196
  126.4 15.5 %collective-permute-start.13 = (bf16[4,16,16,256]{3,2,1,0:T(8,128)(2,1)}, bf16[4,16,16,256]{3,2,1,0:T(8,128)(2,1)S(1)}, u32[]{:S(2)}, u32[]{:S(2)}) collective-permute-start(bf16[4,16,16,256]{3,2,1,0:T(8,128)(2,1)} %collective-permute-done.9.rest_6_), channel_id=1, source_target_pairs={{0,16},{16,0},{1,17},{17,1},{2,18},{18,2},{3,19},{19,3},{4,20},{20... | collective-permute-start | bytes 1572872 | tf_op jit(solution)/shard_map/ppermute | solution.py:196
  141.9 0.8 copy-start.5

commit v4 on v3

--- a/solution.py
+++ b/solution.py
@@ -42,7 +42,7 @@
         out_shape=shapes,
         in_specs=[SMEM, HBM],
         out_specs=[VMEM] * len(shapes),
-        compiler_params=pltpu.CompilerParams(vmem_limit_bytes=24 * 2**20),
+        compiler_params=pltpu.CompilerParams(vmem_limit_bytes=58 * 2**20),
         scratch_shapes=[pltpu.SemaphoreType.DMA((len(plan),))],
         cost_estimate=pl.CostEstimate(flops=0, bytes_accessed=size, transcendentals=0),
     )(ri_order, blocks)
@@ -134,23 +134,38 @@
         half_step(held, g * ROWS, occ, vir, keep, mask_t, mix_t, g * ROWS)
 
 
-def back_kernel(places, count, occ_ref, vir_ref, keep_ref, front_mask, front_mix, *rest):
+def middle_kernel(places, count, occ_ref, vir_ref, keep_ref, *rest):
+    refs = rest[:count]
+    mask_t, mix_t, held, sems = rest[count:]
+    groups = load([(refs[p[0]],) + p[1:] for p in places], held, sems)
+    occ, vir, keep = occ_ref[...], vir_ref[...], keep_ref[...]
+    for g in sorted(groups):
+        for copy in groups[g]:
+            copy.wait()
+        half_step(held, g * ROWS, occ, vir, keep, mask_t, mix_t, g * ROWS)
+
+
+def back_kernel(places, count, occ_ref, vir_ref, keep_ref, mask_a, mask_b, mix_a, mix_b, *rest):
     refs = rest[:count]
     out_ref, mask_t, mix_t, held, sems = rest[count:]
-    done = front_mask.shape[1]
-    pieces = [(refs[p[0]],) + p[1:] for p in places]
-    groups = load(pieces, held, sems, 2)
-    first = pltpu.make_async_copy(front_mask, mask_t.at[:, pl.ds(0, done)], sems.at[0])
-    second = pltpu.make_async_copy(front_mix, mix_t.at[:, pl.ds(0, done)], sems.at[1])
-    first.start()
-    second.start()
+    early, done = mask_a.shape[1], mask_a.shape[1] + mask_b.shape[1]
+    groups = load([(refs[p[0]],) + p[1:] for p in places], held, sems, 4)
+    before = []
+    for n, (src, to) in enumerate(
+        ((mask_a, mask_t), (mix_a, mix_t), (mask_b, mask_t), (mix_b, mix_t))
+    ):
+        low = 0 if n < 2 else early
+        size = src.shape[1]
+        before.append(pltpu.make_async_copy(src, to.at[:, pl.ds(low, size)], sems.at[n]))
+    for copy in before:
+        copy.start()
     occ, vir, keep = occ_ref[...], vir_ref[...], keep_ref[...]
     for g in sorted(groups):
         for copy in groups[g]:
             copy.wait()
         half_step(held, g * ROWS, occ, vir, keep, mask_t, mix_t, done + g * ROWS)
-    first.wait()
-    second.wait()
+    for copy in before:
+        copy.wait()
     window, rows = mask_t.shape[0], mask_t.shape[1]
     deep = 16
 
@@ -202,71 +217,73 @@
 
     plan = [(q, None, first, q, True, 0, half, True) for q in range(PLANE)]
     pieces = gather(plan, [shape(half)] * PLANE, outer, half, ri_order, blocks)
-    held_back, *pieces = barrier((blocks, *pieces))
+    base = jnp.stack([occupied, virtual])
+    pieces, base = barrier((pieces, base))
+    sent = [shift(p, first, q) for q, p in enumerate(pieces)]
+    early = shift(base, first)
+    held_back, early, base = barrier((blocks, early, base))
     plan, shapes = [], []
     for d in order[1:]:
         plan += [(len(shapes), (i, 0), d, i, False, 0, half, True) for i in range(PLANE)]
         shapes.append(shape(PLANE, half))
     for own in (True, False):
-        low = 0 if own else half
-        plan += [(len(shapes), (i, low), 0, i, False, 0, half, own) for i in range(PLANE)]
-    shapes.append(shape(PLANE, rows))
-    *to_send, to_near = gather(plan, shapes, outer, half, ri_order, held_back)
-
-    base = jnp.stack([occupied, virtual])
-    dens, small = [base], list(range(1, outer))
+        plan += [(len(shapes), (i, 0), 0, i, False, 0, half, own) for i in range(PLANE)]
+        shapes.append(shape(PLANE, half))
+    to_send = gather(plan, shapes, outer, half, ri_order, held_back)
+
+    dens, small = {0: base, first: early}, [d for d in range(1, outer) if d != first]
     per_phase = -(-len(small) // max(1, outer - 3))
-    own_in, swapped = [], []
+    own_in, swapped, near = [], [], []
+    ready = []
     for k in range(outer):
         if k == 0:
-            moved = [shift(p, first, q) for q, p in enumerate(pieces)]
+            moved = sent
         elif k <= outer - 3:
-            moved = [shift(ready, order[k])]
+            moved = [shift(ready[0], order[k])]
         else:
             moved = [shift(ready[k - outer + 2], last)]
         turn = [swap(own_in[-1])] if k else []
-        tiny, near_by = [], []
-        if 1 <= k <= outer - 2:
-            tiny = [shift(base, d) for d in small[:per_phase]]
-            small = small[per_phase:]
-        if k <= outer - 3:
-            near_by = [inplane(to_send[k])]
-        elif k == outer - 2:
-            near_by = [inplane(to_near)]
+        tiny = []
+        if 1 <= k <= outer - 3:
+            now, small = small[:per_phase], small[per_phase:]
+            tiny = [shift(base, d) for d in now]
+        if k == outer - 2:
+            spread = jnp.stack([dens[d] for d in range(outer)]).reshape(1, 2 * outer, orb, window)
+            spread = jnp.broadcast_to(spread, (PLANE, 2 * outer, orb, window))
+            around = inplane(jnp.concatenate([to_send[0], spread], axis=1))
         else:
-            spread = jnp.broadcast_to(jnp.stack(dens)[None], (PLANE, outer, 2, orb, window))
-            near_by = [inplane(spread)]
-        moved, turn, tiny, near_by, to_send, to_near, base = barrier(
-            (moved, turn, tiny, near_by, to_send, to_near, base)
+            around = inplane(to_send[0])
+        moved, turn, tiny, around, to_send, base, ready = barrier(
+            (moved, turn, tiny, around, to_send[1:], base, ready)
         )
         own_in.append(moved[0] if k else jnp.stack(moved))
         swapped += turn
-        dens += tiny
-        if k <= outer - 3:
-            ready = near_by[0]
-            if k == outer - 3:
-                ready = [ready[:, :quarter], ready[:, quarter:]]
-        elif k == outer - 2:
-            near = near_by[0]
-    dens_all = near_by[0]
+        dens.update(zip(now, tiny)) if tiny else None
+        if k < outer - 3:
+            ready = [around]
+        elif k == outer - 3:
+            ready = [around[:, :quarter], around[:, quarter:]]
+        else:
+            near.append(around)
     swapped.append(swap(own_in[-1]))
-
-    front, back = [], []
+    dens_all = near[0][:, half:].reshape(2 * window, window)
+
+    table = {0: [], 1: [], 2: []}
     for i in range(PLANE):
         for n in range(outer):
             at = (n * PLANE + i) * orb
             if n == 0:
-                front += [(near, i, 0, half + quarter, 0, at)]
-                back += [(near, i, half + quarter, quarter, 0, at)]
+                low, high, low_y, high_y = near[0], near[0], near[1], near[1]
+                second, second_y = quarter, quarter
             elif n < outer - 1:
-                front += [(own_in[n - 1], i, 0, half, 0, at)]
-                front += [(swapped[n - 1], i, 0, quarter, half, at)]
-                back += [(swapped[n - 1], i, quarter, quarter, 0, at)]
+                low, high, low_y, high_y = own_in[n - 1], own_in[n - 1], swapped[n - 1], swapped[n - 1]
+                second, second_y = quarter, quarter
             else:
-                front += [(own_in[-2], i, 0, quarter, 0, at)]
-                front += [(own_in[-1], i, 0, quarter, quarter, at)]
-                front += [(swapped[-2], i, 0, quarter, half, at)]
-                back += [(swapped[-1], i, 0, quarter, 0, at)]
+                low, high, low_y, high_y = own_in[-2], own_in[-1], swapped[-2], swapped[-1]
+                second, second_y = 0, 0
+            table[0] += [(low, i, 0, quarter, 0, at)]
+            table[1] += [(high, i, second, quarter, 0, at), (low_y, i, 0, quarter, quarter, at)]
+            table[2] += [(high_y, i, second_y, quarter, 0, at)]
 
     def places(listed):
         if orb % ROWS == 0:
@@ -288,41 +305,54 @@
         return sum(p[3] // ROWS for p in table)
 
     params = pltpu.CompilerParams(vmem_limit_bytes=58 * 2**20)
-    table, arrays = places(front)
-    done = half + quarter
     mat = jax.ShapeDtypeStruct((window, window), kind)
-    tall = jax.ShapeDtypeStruct((window, done, window), kind)
-    front_mask, front_mix, occ, vir, keep = pl.pallas_call(
-        functools.partial(front_kernel, table, [0] + order, outer, orb, len(arrays)),
-        out_shape=[tall, tall, mat, mat, mat],
+    tall = lambda n: jax.ShapeDtypeStruct((window, n, window), kind)
+
+    def cost(n, moved):
+        return pl.CostEstimate(
+            flops=4 * n * window**3, bytes_accessed=moved * window**2, transcendentals=0
+        )
+
+    def scratch(n, extra):
+        return [
+            pltpu.VMEM((n, window, window), kind),
+            pltpu.SemaphoreType.DMA((extra,)),
+        ]
+
+    rows_of, arrays = places(table[0])
+    mask_a, mix_a, occ, vir, keep = pl.pallas_call(
+        functools.partial(front_kernel, rows_of, [0] + order, outer, orb, len(arrays)),
+        out_shape=[tall(quarter), tall(quarter), mat, mat, mat],
         in_specs=[SMEM, SMEM, VMEM] + [HBM] * len(arrays),
         out_specs=[VMEM] * 5,
-        scratch_shapes=[
-            pltpu.VMEM((done, window, window), kind),
-            pltpu.SemaphoreType.DMA((copies(table),)),
-        ],
+        scratch_shapes=scratch(quarter, copies(rows_of)),
         compiler_params=params,
-        cost_estimate=pl.CostEstimate(
-            flops=4 * done * window**3, bytes_accessed=6 * done * window**2, transcendentals=0
-        ),
-    )(ri_order, block_mask, dens_all.reshape(2 * window, window), *arrays)
-    table, arrays = places(back)
+        cost_estimate=cost(quarter, 6 * quarter),
+    )(ri_order, block_mask, dens_all, *arrays)
+    rows_of, arrays = places(table[1])
+    mask_b, mix_b = pl.pallas_call(
+        functools.partial(middle_kernel, rows_of, len(arrays)),
+        out_shape=[tall(half), tall(half)],
+        in_specs=[VMEM] * 3 + [HBM] * len(arrays),
+        out_specs=[VMEM] * 2,
+        scratch_shapes=scratch(half, copies(rows_of)),
+        compiler_params=params,
+        cost_estimate=cost(half, 6 * half),
+    )(occ, vir, keep, *arrays)
+    rows_of, arrays = places(table[2])
     return pl.pallas_call(
-        functools.partial(back_kernel, table, len(arrays)),
+        functools.partial(back_kernel, rows_of, len(arrays)),
         out_shape=jax.ShapeDtypeStruct((rows, rows), jnp.float32),
-        in_specs=[VMEM] * 3 + [HBM] * (2 + len(arrays)),
+        in_specs=[VMEM] * 3 + [HBM] * (4 + len(arrays)),
         out_specs=VMEM,
         scratch_shapes=[
             pltpu.VMEM((window, rows, window), kind),
             pltpu.VMEM((window, rows, window), kind),
-            pltpu.VMEM((quarter, window, window), kind),
-            pltpu.SemaphoreType.DMA((2 + copies(table),)),
-        ],
+        ]
+        + scratch(quarter, 4 + copies(rows_of)),
         compiler_params=params,
-        cost_estimate=pl.CostEstimate(
-            flops=4 * quarter * window**3, bytes_accessed=4 * rows * window**2, transcendentals=0
-        ),
-    )(occ, vir, keep, front_mask, front_mix, *arrays)
+        cost_estimate=cost(quarter, 4 * rows),
+    )(occ, vir, keep, mask_a, mask_b, mix_a, mix_b, *arrays)
 
 
 def solution(mesh):

time: 155 us -> 172 us (1.11)
  waiting for transfers between devices: 76.6 us -> 93.2 us
  blocking collectives: 9.17 us -> 0 us
  Pallas kernels: 28.7 us -> 35.8 us
  other arithmetic: 0.15 us -> 2.91 us
  local copies, waits for them, and re-layouts: 7.45 us -> 5.31 us
  starting transfers between devices: 32.2 us -> 34.2 us
    ppermute x10, waiting for transfers between devices: 74.8 us -> 93.2 us  [shift(): return lax.ppermute(x, 'wide', pairs)]
    all_to_all x1 -> x0, blocking collectives: 9.17 us -> none  [inplane(): lax.all_to_all(x, 'wide', split_axis=0, concat_axis=0, tiled=True, axis_i...]
    pallas_call x2, Pallas kernels: 3.74 us -> 7.97 us  [gather(): pl.pallas_call(functools.partial(gather_kernel, plan, outer, half, len(sh...]
    all_to_all x3 -> x4, starting transfers between devices: 11.4 us -> 15 us  [inplane(): lax.all_to_all(x, 'wide', split_axis=0, concat_axis=0, tiled=True, axis_i...]
    unnamed x21 -> x33, local copies, waits for them, and re-layouts: 6.54 us -> 3.27 us
    pallas_call x2 -> x3, Pallas kernels: 25 us -> 27.9 us  [the longest x1 11.8 us: shards(): pl.pallas_call(functools.partial(back_kernel, rows_of, len(arrays)), out_...]
    concatenate x0 -> x1, other arithmetic: none -> 2.76 us  [shards(): around = inplane(jnp.concatenate([to_send[0], spread], axis=1))]
    ppermute x4, waiting for transfers between devices: 1.73 us -> 0.01 us  [swap(): return lax.ppermute(x, 'groups', [(0, 1), (1, 0)])]
  transfers between devices with their start and end apart: 17 -> 18, of which waited for: 8 -> 9; matrix products, arithmetic and copies ran while one was open for 1% -> 3% of each run, Pallas kernels for 9% -> 9%
where the time goes in v4:
time: 172 us
  waiting for transfers between devices  93.2 us (54%)
  Pallas kernels  35.8 us (21%)
  starting transfers between devices  34.2 us (20%)
  local copies, waits for them, and re-layouts  5.31 us (3%)
  other arithmetic  2.91 us (2%)
    ppermute x10, waiting for transfers between devices, shift(): return lax.ppermute(x, 'wide', pairs)  93.2 us
    all_to_all x4, starting transfers between devices, inplane(): lax.all_to_all(x, 'wide', split_axis=0, concat_axis=0, tiled=True, axis_i...  15 us
    ppermute x10, starting transfers between devices, shift(): return lax.ppermute(x, 'wide', pairs)  14.1 us
    pallas_call x1, Pallas kernels, shards(): pl.pallas_call(functools.partial(back_kernel, rows_of, len(arrays)), out_...  11.8 us
    pallas_call x1, Pallas kernels, shards(): pl.pallas_call(functools.partial(middle_kernel, rows_of, len(arrays)), ou...  9.65 us
    pallas_call x2, Pallas kernels, gather(): pl.pallas_call(functools.partial(gather_kernel, plan, outer, half, len(sh...  7.97 us
    pallas_call x1, Pallas kernels, shards(): pl.pallas_call(functools.partial(front_kernel, rows_of, [0] + order, oute...  6.39 us
    ppermute x4, starting transfers between devices, swap(): return lax.ppermute(x, 'groups', [(0, 1), (1, 0)])  5.08 us
  transfers between devices with their start and end apart: 18, of which 9 were waited for; matrix products, arithmetic and copies ran while one was open for 3% of the time, Pallas kernels for 9%

profile of v4, /device:TPU:0, one launch (start us, length us, event | category | flops | bytes accessed | tf_op | source)
XLA Modules:
  0.0 171.7 jit_solution(17119866962677749448)
XLA Ops:
  0.0 3.0 %shard_map.55 = (bf16[32,16,256]{2,1,0:T(8,128)(2,1)}, bf16[32,16,256]{2,1,0:T(8,128)(2,1)}, bf16[32,16,256]{2,1,0:T(8,128)(2,1)}, bf16[32,16,256]{2,1,0:T(8,128)(2,1)}) custom-call(s32[16]{0:T(128)} %order_ref.5, bf16[16,64,16,256]{3,2,1,0:T(8,128)(2,1)} %bitcast.13), custom_call_target="tpu_custom_call" | custom-call | bytes 2097152 | tf_op jit(solution)/shard_map/pallas_call | solution.py:40
  3.1 3.1 %collective-permute-start.4 = (bf16[2,16,256]{2,1,0:T(8,128)(2,1)S(1)}, bf16[2,16,256]{2,1,0:T(8,128)(2,1)S(1)}, u32[]{:S(2)}, u32[]{:S(2)}) collective-permute-start(bf16[2,16,256]{2,1,0:T(8,128)(2,1)S(1)} %pad_maximum_fusion.3), channel_id=1, source_target_pairs={{0,4},{1,5},{2,6},{3,7},{4,8},{5,9},{6,10},{7,11},{8,12},{9,13},{1... | collective-permute-start | bytes 49160 | tf_op jit(solution)/shard_map/ppermute | solution.py:208
  6.2 3.7 %collective-permute-done.4 = bf16[2,16,256]{2,1,0:T(8,128)(2,1)S(1)} collective-permute-done((bf16[2,16,256]{2,1,0:T(8,128)(2,1)S(1)}, bf16[2,16,256]{2,1,0:T(8,128)(2,1)S(1)}, u32[]{:S(2)}, u32[]{:S(2)}) %collective-permute-start.4) | collective-permute-done | bytes 16416 | tf_op jit(solution)/shard_map/ppermute | solution.py:208
  9.9 4.9 %shard_map.56 = (bf16[4,32,16,256]{3,2,1,0:T(8,128)(2,1)}, bf16[4,32,16,256]{3,2,1,0:T(8,128)(2,1)}, bf16[4,32,16,256]{3,2,1,0:T(8,128)(2,1)}, bf16[4,32,16,256]{3,2,1,0:T(8,128)(2,1)}) custom-call(s32[16]{0:T(128)} %order_ref.5, bf16[16,64,16,256]{3,2,1,0:T(8,128)(2,1)} %bitcast.14), custom_call_target="tpu_custom_call" | custom-call | bytes 8388608 | tf_op jit(solution)/shard_map/pallas_call | solution.py:40
  14.9 3.7 %all-to-all-start = ((bf16[4,32,16,256]{3,2,1,0:T(8,128)(2,1)}), bf16[4,32,16,256]{3,2,1,0:T(8,128)(2,1)S(1)}, u32[]{:S(2)}, u32[]{:S(2)}) async-start(bf16[4,32,16,256]{3,2,1,0:T(8,128)(2,1)} %get-tuple-element.62), calls=%async_computation | async-start | bytes 2097152 | tf_op jit(solution)/shard_map/all_to_all | solution.py:199
  18.6 0.1 collective-permute-start
  18.6 1.3 collective-permute-start.1
  20.0 2.6 %collective-permute-start.2 = (bf16[32,16,256]{2,1,0:T(8,128)(2,1)S(1)}, bf16[32,16,256]{2,1,0:T(8,128)(2,1)S(1)}, u32[]{:S(2)}, u32[]{:S(2)}) collective-permute-start(bf16[32,16,256]{2,1,0:T(8,128)(2,1)S(1)} %copy-done.13), channel_id=1, source_target_pairs={{0,6},{1,7},{2,4},{3,5},{4,10},{5,11},{6,8},{7,9},{8,14},{9,15},{1... | collective-permute-start | bytes 786440 | tf_op jit(solution)/shard_map/ppermute | solution.py:208
  22.6 1.3 collective-permute-start.3
  23.9 5.6 %collective-permute-done = bf16[32,16,256]{2,1,0:T(8,128)(2,1)S(1)} collective-permute-done((bf16[32,16,256]{2,1,0:T(8,128)(2,1)S(1)}, bf16[32,16,256]{2,1,0:T(8,128)(2,1)S(1)}, u32[]{:S(2)}, u32[]{:S(2)}) %collective-permute-start) | collective-permute-done | bytes 262176 | tf_op jit(solution)/shard_map/ppermute | solution.py:208
  29.5 4.7 %collective-permute-done.1 = bf16[32,16,256]{2,1,0:T(8,128)(2,1)S(1)} collective-permute-done((bf16[32,16,256]{2,1,0:T(8,128)(2,1)S(1)}, bf16[32,16,256]{2,1,0:T(8,128)(2,1)S(1)}, u32[]{:S(2)}, u32[]{:S(2)}) %collective-permute-start.1) | collective-permute-done | bytes 262176 | tf_op jit(solution)/shard_map/ppermute | solution.py:208
  34.2 8.0 %collective-permute-done.2 = bf16[32,16,256]{2,1,0:T(8,128)(2,1)S(1)} collective-permute-done((bf16[32,16,256]{2,1,0:T(8,128)(2,1)S(1)}, bf16[32,16,256]{2,1,0:T(8,128)(2,1)S(1)}, u32[]{:S(2)}, u32[]{:S(2)}) %collective-permute-start.2) | collective-permute-done | bytes 262176 | tf_op jit(solution)/shard_map/ppermute | solution.py:208
  42.2 4.0 %collective-permute-done.3 = bf16[32,16,256]{2,1,0:T(8,128)(2,1)S(1)} collective-permute-done((bf16[32,16,256]{2,1,0:T(8,128)(2,1)S(1)}, bf16[32,16,256]{2,1,0:T(8,128)(2,1)S(1)}, u32[]{:S(2)}, u32[]{:S(2)}) %collective-permute-start.3) | collective-permute-done | bytes 262176 | tf_op jit(solution)/shard_map/ppermute | solution.py:208
  46.2 0.0 all-to-all-done
  46.2 0.1 pad_maximum_fusion.1.rest_1_.rest_2_
  46.3 0.9 copy-done.5
  47.2 1.7 %collective-permute-start.6 = (bf16[4,32,16,256]{3,2,1,0:T(8,128)(2,1)S(1)}, bf16[4,32,16,256]{3,2,1,0:T(8,128)(2,1)S(1)}, u32[]{:S(2)}, u32[]{:S(2)}) collective-permute-start(bf16[4,32,16,256]{3,2,1,0:T(8,128)(2,1)S(1)} %pad_maximum_fusion.1.rest_1_.rest_2_), channel_id=1, source_target_pairs={{0,16},{16,0},{1,17},{17,1},{2,18},{18,2},{3,19},{19,3},{4,20},{20... | collective-permute-start | bytes 3145736 | tf_op jit(solution)/shard_map/ppermute | solution.py:211
  49.0 0.0 collective-permute-start.5
  49.0 4.2 %all-to-all-start.1 = ((bf16[4,32,16,256]{3,2,1,0:T(8,128)(2,1)}), bf16[4,32,16,256]{3,2,1,0:T(8,128)(2,1)}, u32[]{:S(2)}, u32[]{:S(2)}) async-start(bf16[4,32,16,256]{3,2,1,0:T(8,128)(2,1)} %get-tuple-element.73), calls=%async_computation.1 | async-start | bytes 2097152 | tf_op jit(solution)/shard_map/all_to_all | solution.py:199
  53.2 0.4 collective-permute-start.7
  53.6 4.1 %collective-permute-start.8 = (bf16[2,16,256]{2,1,0:T(8,128)(2,1)S(1)}, bf16[2,16,256]{2,1,0:T(8,128)(2,1)S(1)}, u32[]{:S(2)}, u32[]{:S(2)}) collective-permute-start(bf16[2,16,256]{2,1,0:T(8,128)(2,1)S(1)} %pad_maximum_fusion.3), channel_id=1, source_target_pairs={{0,12},{1,13},{2,14},{3,15},{4,0},{5,1},{6,2},{7,3},{8,4},{9,5},{1... | collective-permute-start | bytes 49160 | tf_op jit(solution)/shard_map/ppermute | solution.py:208
  57.7 15.6 %collective-permute-done.7 = bf16[2,16,256]{2,1,0:T(8,128)(2,1)S(1)} collective-permute-done((bf16[2,16,256]{2,1,0:T(8,128)(2,1)S(1)}, bf16[2,16,256]{2,1,0:T(8,128)(2,1)S(1)}, u32[]{:S(2)}, u32[]{:S(2)}) %collective-permute-start.7) | collective-permute-done | bytes 16416 | tf_op jit(solution)/shard_map/ppermute | solution.py:208
  73.3 2.0 %collective-permute-done.8 = bf16[2,16,256]{2,1,0:T(8,128)(2,1)S(1)} collective-permute-done((bf16[2,16,256]{2,1,0:T(8,128)(2,1)S(1)}, bf16[2,16,256]{2,1,0:T(8,128)(2,1)S(1)}, u32[]{:S(2)}, u32[]{:S(2)}) %collective-permute-start.8) | collective-permute-done | bytes 16416 | tf_op jit(solution)/shard_map/ppermute | solution.py:208
  75.3 0.0 all-to-all-done.1
  75.3 0.0 collective-permute-done.6.rest_3_.rest_1_
  75.3 0.0 collective-permute-done.5.rest_2_.rest_4_
  75.3 0.4 collective-permute-start.10
  75.7 2.8 %pad_maximum_fusion = bf16[4,40,16,256]{3,2,1,0:T(8,128)(2,1)} fusion(bf16[4,8,16,256]{3,2,1,0:T(8,128)(2,1)S(1)} %broadcast_in_dim.8, bf16[4,32,16,256]{3,2,1,0:T(8,128)(2,1)} %get-tuple-element.78), kind=kLoop, calls=%fused_computation | loop fusion | flops 655360 | bytes 2621440 | tf_op jit(solution)/shard_map/concatenate | solution.py:253
  78.5 3.6 %all-to-all-start.2 = ((bf16[4,40,16,256]{3,2,1,0:T(8,128)(2,1)}), bf16[4,40,16,256]{3,2,1,0:T(8,128)(2,1)S(1)}, u32[]{:S(2)}, u32[]{:S(2)}) async-start(bf16[4,40,16,256]{3,2,1,0:T(8,128)(2,1)} %pad_maximum_fusion), calls=%async_computation.2 | async-start | bytes 2621440 | tf_op jit(solution)/shard_map/all_to_all | solution.py:199
  82.0 0.0 copy-start.9
  82.0 1.3 fusion
  83.4 1.2 collective-permute-start.9
  84.5 25.1 %collective-permute-done.9.rest_3_ = bf16[4,16,16,256]{3,2,1,0:T(8,128)(2,1)S(1)} collective-permute-done((bf16[4,16,16,256]{3,2,1,0:T(8,128)(2,1)S(1)}, bf16[4,16,16,256]{3,2,1,0:T(8,128)(2,1)S(1)}, u32[]{:S(2)}, u32[]{:S(2)}) %collective-permute-start.9) | collective-permute-done | bytes 524320 | tf_op jit(solution)/shard_map/ppermute | solution.py:208
  109.7 0.0 all-to-all-done.2.rest_0_
  109.7 0.0 collective-permute-done.10.rest_5_.rest_2_
  109.7 3.5 %all-to-all-start.3 = ((bf16[4,32,16,256]{3,2,1,0:T(8,128)(2,1)}), bf16[4,32,16,256]{3,2,1,0:T(8,128)(2,1)S(1)}, u32[]{:S(2)}, u32[]{:S(2)}) async-start(bf16[4,32,16,256]{3,2,1,0:T(8,128)(2,1)} %get-tuple-element.90), calls=%async_computation.3 | async-start | bytes 2097152 | tf_op jit(solution)/shard_map/all_to_all | solution.py:199
  113.2 0.1 collective-permute-start.11
  113.3 1.5 collective-permute-start.12
  114.8 24.4 %collective-permute-done.11.rest_6_ = bf16[4,16,16,256]{3,2,1,0:T(8,128)(2,1)S(1)} collective-permute-done((bf16[4,16,16,256]{3,2,1,0:T(8,128)(2,1)S(1)}, bf16[4,16,16,256]{3,2,1,0:T(8,128)(2,1)S(1)}, u32[]{:S(2)}, u32[]{:S(2)}) %collective-permute-start.11) | collective-permute-done | bytes 524320 | tf_op jit(solution)/shard_map/ppermute | solution.py:208
  139.2 0.8 copy-done.8
  140.0 1.5 collective-permute-start.13
  141.5 0.7 copy.6.mask_ref
  142.2 0.7 slice.11
  142.9 6.4 %shard_map.57 = (bf16[256,16,256]{2,1,0:T(8,128)(2,1)}, bf16[256,16,256]{2,1,0:T(8,128)(2,1)}, bf16[256,256]{1,0:T(8,128)(2,1)}, bf16[256,256]{1,0:T(8,128)(2,1)}, bf16[256,256]{1,0:T(8,128)(2,1)}) custom-call(s32[16]{0:T(128)} %order_ref.5, s32[16,4,4]{2,1,0:T(4,128)} %copy.6.mask_ref, bf16[512,256]{1,0:T(8,128)(2,1)} %bitcast.15, ...), custom_call_target="tpu_custom_call" | custom-call | flops 1073741824 | bytes 6291456 | tf_op jit(solution)/shard_map/pallas_call | solution.py:323
  149.3 9.6 %shard_map.58 = (bf16[256,32,256]{2,1,0:T(8,128)(2,1)}, bf16[256,32,256]{2,1,0:T(8,128)(2,1)}) custom-call(bf16[256,256]{1,0:T(8,128)(2,1)} %get-tuple-element.85.occ_ref, bf16[256,256]{1,0:T(8,128)(2,1)} %get-tuple-element.86.vir_ref, bf16[256,256]{1,0:T(8,128)(2,1)} %get-tuple-element.87.keep_ref, bf16[4,40,16,256]{3,2,1,0:T(8,128)(2,1)} %copy-done, ...), custom_call_target="tpu_custom_call" | custom-call | flops 2147483648 | bytes 12582912 | tf_op jit(solution)/shard_map/pallas_call | solution.py:333
  159.0 0.0 collective-permute-done.13.rest_3_
  159.0 0.8 copy-done.7
  159.8 11.8 %shard_map.59 = f32[64,64]{1,0:T(8,128)} custom-call(bf16[256,256]{1,0:T(8,128)(2,1)} %get-tuple-element.85.occ_ref, bf16[256,256]{1,0:T(8,128)(2,1)} %get-tuple-element.86.vir_ref, bf16[256,256]{1,0:T(8,128)(2,1)} %get-tuple-element.87.keep_ref, bf16[256,16,256]{2,1,0:T(8,128)(2,1)} %get-tuple-element.88.mask_a, ...), custom_call_target="tpu_custom_call" | custom-call | flops 1073741824 | bytes 16777216 | tf_op jit(solution)/shard_map/pallas_call | solution.py:343
  (33 shorter events, 0.1 us)
Async XLA Ops:
  0.0 3.0 %copy-start.10 = (bf16[16,256]{1,0:T(8,128)(2,1)S(1)}, bf16[16,256]{1,0:T(8,128)(2,1)}, u32[]{:S(2)}) copy-start(bf16[16,256]{1,0:T(8,128)(2,1)} %param.7) | copy-start | bytes 24580
  0.0 3.1 %copy-start.11 = (bf16[16,256]{1,0:T(8,128)(2,1)S(1)}, bf16[16,256]{1,0:T(8,128)(2,1)}, u32[]{:S(2)}) copy-start(bf16[16,256]{1,0:T(8,128)(2,1)} %param.6) | copy-start | bytes 24580
  3.1 6.8 %collective-permute-start.4 = (bf16[2,16,256]{2,1,0:T(8,128)(2,1)S(1)}, bf16[2,16,256]{2,1,0:T(8,128)(2,1)S(1)}, u32[]{:S(2)}, u32[]{:S(2)}) collective-permute-start(bf16[2,16,256]{2,1,0:T(8,128)(2,1)S(1)} %pad_maximum_fusion.3), channel_id=1, source_target_pairs={{0,4},{1,5},{2,6},{3,7},{4,8},{5,9},{6,10},{7,11},{8,12},{9,13},{1... | collective-permute-start | bytes 49160 | tf_op jit(solution)/shard_map/ppermute | solution.py:208
  14.8 3.7 %copy-start.15 = (bf16[32,16,256]{2,1,0:T(8,128)(2,1)S(1)}, bf16[32,16,256]{2,1,0:T(8,128)(2,1)}, u32[]{:S(2)}) copy-start(bf16[32,16,256]{2,1,0:T(8,128)(2,1)} %get-tuple-element.56) | copy-start | bytes 786436
  14.9 3.8 %copy-start.14 = (bf16[32,16,256]{2,1,0:T(8,128)(2,1)S(1)}, bf16[32,16,256]{2,1,0:T(8,128)(2,1)}, u32[]{:S(2)}) copy-start(bf16[32,16,256]{2,1,0:T(8,128)(2,1)} %get-tuple-element.57) | copy-start | bytes 786436
  14.9 5.1 %copy-start.13 = (bf16[32,16,256]{2,1,0:T(8,128)(2,1)S(1)}, bf16[32,16,256]{2,1,0:T(8,128)(2,1)}, u32[]{:S(2)}) copy-start(bf16[32,16,256]{2,1,0:T(8,128)(2,1)} %get-tuple-element.58) | copy-start | bytes 786436
  14.9 7.7 %copy-start.12 = (bf16[32,16,256]{2,1,0:T(8,128)(2,1)S(1)}, bf16[32,16,256]{2,1,0:T(8,128)(2,1)}, u32[]{:S(2)}) copy-start(bf16[32,16,256]{2,1,0:T(8,128)(2,1)} %get-tuple-element.59) | copy-start | bytes 786436
  14.9 31.3 %all-to-all-start = ((bf16[4,32,16,256]{3,2,1,0:T(8,128)(2,1)}), bf16[4,32,16,256]{3,2,1,0:T(8,128)(2,1)S(1)}, u32[]{:S(2)}, u32[]{:S(2)}) async-start(bf16[4,32,16,256]{3,2,1,0:T(8,128)(2,1)} %get-tuple-element.62), calls=%async_computation | async-start | bytes 2097152 | tf_op jit(solution)/shard_map/all_to_all | solution.py:199
  18.6 11.0 %collective-permute-start = (bf16[32,16,256]{2,1,0:T(8,128)(2,1)S(1)}, bf16[32,16,256]{2,1,0:T(8,128)(2,1)S(1)}, u32[]{:S(2)}, u32[]{:S(2)}) collective-permute-start(bf16[32,16,256]{2,1,0:T(8,128)(2,1)S(1)} %copy-done.15), channel_id=1, source_target_pairs={{0,4},{1,5},{2,6},{3,7},{4,8},{5,9},{6,10},{7,11},{8,12},{9,13},{1... | collective-permute-start | bytes 786440 | tf_op jit(solution)/shard_map/ppermute | solution.py:208
  18.6 15.6 %collective-permute-start.1 = (bf16[32,16,256]{2,1,0:T(8,128)(2,1)S(1)}, bf16[32,16,256]{2,1,0:T(8,128)(2,1)S(1)}, u32[]{:S(2)}, u32[]{:S(2)}) collective-permute-start(bf16[32,16,256]{2,1,0:T(8,128)(2,1)S(1)} %copy-done.14), channel_id=1, source_target_pairs={{0,5},{1,4},{2,7},{3,6},{4,9},{5,8},{6,11},{7,10},{8,13},{9,12},{1... | collective-permute-start | bytes 786440 | tf_op jit(solution)/shard_map/ppermute | solution.py:208
  20.0 22.2 %collective-permute-start.2 = (bf16[32,16,256]{2,1,0:T(8,128)(2,1)S(1)}, bf16[32,16,256]{2,1,0:T(8,128)(2,1)S(1)}, u32[]{:S(2)}, u32[]{:S(2)}) collective-permute-start(bf16[32,16,256]{2,1,0:T(8,128)(2,1)S(1)} %copy-done.13), channel_id=1, source_target_pairs={{0,6},{1,7},{2,4},{3,5},{4,10},{5,11},{6,8},{7,9},{8,14},{9,15},{1... | collective-permute-start | bytes 786440 | tf_op jit(solution)/shard_map/ppermute | solution.py:208
  22.6 23.6 %collective-permute-start.3 = (bf16[32,16,256]{2,1,0:T(8,128)(2,1)S(1)}, bf16[32,16,256]{2,1,0:T(8,128)(2,1)S(1)}, u32[]{:S(2)}, u32[]{:S(2)}) collective-permute-start(bf16[32,16,256]{2,1,0:T(8,128)(2,1)S(1)} %copy-done.12), channel_id=1, source_target_pairs={{0,7},{1,6},{2,5},{3,4},{4,11},{5,10},{6,9},{7,8},{8,15},{9,14},{1... | collective-permute-start | bytes 786440 | tf_op jit(solution)/shard_map/ppermute | solution.py:208
  46.2 1.0 copy-start.5
  47.2 31.2 %copy-start.1 = (bf16[4,32,16,256]{3,2,1,0:T(8,128)(2,1)}, bf16[4,32,16,256]{3,2,1,0:T(8,128)(2,1)S(1)}, u32[]{:S(2)}) copy-start(bf16[4,32,16,256]{3,2,1,0:T(8,128)(2,1)S(1)} %pad_maximum_fusion.1.rest_1_.rest_2_) | copy-start | bytes 3145732
  47.2 28.1 %collective-permute-start.6 = (bf16[4,32,16,256]{3,2,1,0:T(8,128)(2,1)S(1)}, bf16[4,32,16,256]{3,2,1,0:T(8,128)(2,1)S(1)}, u32[]{:S(2)}, u32[]{:S(2)}) collective-permute-start(bf16[4,32,16,256]{3,2,1,0:T(8,128)(2,1)S(1)} %pad_maximum_fusion.1.rest_1_.rest_2_), channel_id=1, source_target_pairs={{0,16},{16,0},{1,17},{17,1},{2,18},{18,2},{3,19},{19,3},{4,20},{20... | collective-permute-start | bytes 3145736 | tf_op jit(solution)/shard_map/ppermute | solution.py:211
  49.0 26.3 %collective-permute-start.5 = (bf16[4,32,16,256]{3,2,1,0:T(8,128)(2,1)}, bf16[4,32,16,256]{3,2,1,0:T(8,128)(2,1)S(1)}, u32[]{:S(2)}, u32[]{:S(2)}) collective-permute-start(bf16[4,32,16,256]{3,2,1,0:T(8,128)(2,1)} %copy-done.5), channel_id=1, source_target_pairs={{0,12},{1,13},{2,14},{3,15},{4,0},{5,1},{6,2},{7,3},{8,4},{9,5},{1... | collective-permute-start | bytes 3145736 | tf_op jit(solution)/shard_map/ppermute | solution.py:208
  49.0 26.3 %all-to-all-start.1 = ((bf16[4,32,16,256]{3,2,1,0:T(8,128)(2,1)}), bf16[4,32,16,256]{3,2,1,0:T(8,128)(2,1)}, u32[]{:S(2)}, u32[]{:S(2)}) async-start(bf16[4,32,16,256]{3,2,1,0:T(8,128)(2,1)} %get-tuple-element.73), calls=%async_computation.1 | async-start | bytes 2097152 | tf_op jit(solution)/shard_map/all_to_all | solution.py:199
  53.2 20.1 %collective-permute-start.7 = (bf16[2,16,256]{2,1,0:T(8,128)(2,1)S(1)}, bf16[2,16,256]{2,1,0:T(8,128)(2,1)S(1)}, u32[]{:S(2)}, u32[]{:S(2)}) collective-permute-start(bf16[2,16,256]{2,1,0:T(8,128)(2,1)S(1)} %pad_maximum_fusion.3), channel_id=1, source_target_pairs={{0,8},{1,9},{2,10},{3,11},{4,12},{5,13},{6,14},{7,15},{8,0},{9,1},... | collective-permute-start | bytes 49160 | tf_op jit(solution)/shard_map/ppermute | solution.py:208
  53.6 21.7 %collective-permute-start.8 = (bf16[2,16,256]{2,1,0:T(8,128)(2,1)S(1)}, bf16[2,16,256]{2,1,0:T(8,128)(2,1)S(1)}, u32[]{:S(2)}, u32[]{:S(2)}) collective-permute-start(bf16[2,16,256]{2,1,0:T(8,128)(2,1)S(1)} %pad_maximum_fusion.3), channel_id=1, source_target_pairs={{0,12},{1,13},{2,14},{3,15},{4,0},{5,1},{6,2},{7,3},{8,4},{9,5},{1... | collective-permute-start | bytes 49160 | tf_op jit(solution)/shard_map/ppermute | solution.py:208
  75.3 3.2 %copy-start.3 = (bf16[4,32,16,256]{3,2,1,0:T(8,128)(2,1)}, bf16[4,32,16,256]{3,2,1,0:T(8,128)(2,1)S(1)}, u32[]{:S(2)}) copy-start(bf16[4,32,16,256]{3,2,1,0:T(8,128)(2,1)S(1)} %collective-permute-done.6.rest_3_.rest_1_) | copy-start | bytes 3145732
  75.3 3.2 %copy-start.4 = (bf16[4,32,16,256]{3,2,1,0:T(8,128)(2,1)}, bf16[4,32,16,256]{3,2,1,0:T(8,128)(2,1)S(1)}, u32[]{:S(2)}) copy-start(bf16[4,32,16,256]{3,2,1,0:T(8,128)(2,1)S(1)} %collective-permute-done.5.rest_2_.rest_4_) | copy-start | bytes 3145732
  75.3 34.4 %collective-permute-start.10 = (bf16[4,32,16,256]{3,2,1,0:T(8,128)(2,1)S(1)}, bf16[4,32,16,256]{3,2,1,0:T(8,128)(2,1)}, u32[]{:S(2)}, u32[]{:S(2)}) collective-permute-start(bf16[4,32,16,256]{3,2,1,0:T(8,128)(2,1)S(1)} %collective-permute-done.5.rest_2_.rest_4_), channel_id=1, source_target_pairs={{0,16},{16,0},{1,17},{17,1},{2,18},{18,2},{3,19},{19,3},{4,20},{20... | collective-permute-start | bytes 3145736 | tf_op jit(solution)/shard_map/ppermute | solution.py:211
  78.5 31.2 %all-to-all-start.2 = ((bf16[4,40,16,256]{3,2,1,0:T(8,128)(2,1)}), bf16[4,40,16,256]{3,2,1,0:T(8,128)(2,1)S(1)}, u32[]{:S(2)}, u32[]{:S(2)}) async-start(bf16[4,40,16,256]{3,2,1,0:T(8,128)(2,1)} %pad_maximum_fusion), calls=%async_computation.2 | async-start | bytes 2621440 | tf_op jit(solution)/shard_map/all_to_all | solution.py:199
  82.0 59.5 %copy-start.9 = (s32[16,4,4]{0,2,1:T(4,128)S(1)}, s32[16,4,4]{0,2,1:T(4,128)}, u32[]{:S(2)}) copy-start(s32[16,4,4]{0,2,1:T(4,128)} %param.8) | copy-start | bytes 3076
  83.4 26.3 %collective-permute-start.9 = (bf16[4,16,16,256]{3,2,1,0:T(8,128)(2,1)S(1)}, bf16[4,16,16,256]{3,2,1,0:T(8,128)(2,1)S(1)}, u32[]{:S(2)}, u32[]{:S(2)}) collective-permute-start(bf16[4,16,16,256]{3,2,1,0:T(8,128)(2,1)S(1)} %get-tuple-element.100), channel_id=1, source_target_pairs={{0,8},{1,9},{2,10},{3,11},{4,12},{5,13},{6,14},{7,15},{8,0},{9,1},... | collective-permute-start | bytes 1572872 | tf_op jit(solution)/shard_map/ppermute | solution.py:208
  109.7 33.3 %copy-start.6 = (bf16[4,16,16,256]{3,2,1,0:T(8,128)(2,1)}, bf16[4,16,16,256]{3,2,1,0:T(8,128)(2,1)S(1)}, u32[]{:S(2)}) copy-start(bf16[4,16,16,256]{3,2,1,0:T(8,128)(2,1)S(1)} %collective-permute-done.9.rest_3_) | copy-start | bytes 1572868
  109.7 33.3 %copy-start = (bf16[4,40,16,256]{3,2,1,0:T(8,128)(2,1)}, bf16[4,40,16,256]{3,2,1,0:T(8,128)(2,1)S(1)}, u32[]{:S(2)}) copy-start(bf16[4,40,16,256]{3,2,1,0:T(8,128)(2,1)S(1)} %all-to-all-done.2.rest_0_) | copy-start | bytes 3932164
  109.7 30.3 %all-to-all-start.3 = ((bf16[4,32,16,256]{3,2,1,0:T(8,128)(2,1)}), bf16[4,32,16,256]{3,2,1,0:T(8,128)(2,1)S(1)}, u32[]{:S(2)}, u32[]{:S(2)}) async-start(bf16[4,32,16,256]{3,2,1,0:T(8,128)(2,1)} %get-tuple-element.90), calls=%async_computation.3 | async-start | bytes 2097152 | tf_op jit(solution)/shard_map/all_to_all | solution.py:199
  113.2 26.0 %collective-permute-start.11 = (bf16[4,16,16,256]{3,2,1,0:T(8,128)(2,1)S(1)}, bf16[4,16,16,256]{3,2,1,0:T(8,128)(2,1)S(1)}, u32[]{:S(2)}, u32[]{:S(2)}) collective-permute-start(bf16[4,16,16,256]{3,2,1,0:T(8,128)(2,1)S(1)} %get-tuple-element.89), channel_id=1, source_target_pairs={{0,8},{1,9},{2,10},{3,11},{4,12},{5,13},{6,14},{7,15},{8,0},{9,1},... | collective-permute-start | bytes 1572872 | tf_op jit(solution)/shard_map/ppermute | solution.py:208
  113.3 26.7 %collective-permute-start.12 = (bf16[4,16,16,256]{3,2,1,0:T(8,128)(2,1)S(1)}, bf16[4,16,16,256]{3,2,1,0:T(8,128)(2,1)}, u32[]{:S(2)}, u32[]{:S(2)}) collective-permute-start(bf16[4,16,16,256]{3,2,1,0:T(8,128)(2,1)S(1)} %collective-permute-done.9.rest_3_), channel_id=1, source_target_pairs={{0,16},{16,0},{1,17},{17,1},{2,18},{18,2},{3,19},{19,3},{4,20},{20... | collective-permute-start | bytes 1572872 | tf_op jit(solution)/shard_map/ppermute | solution.py:211
  139.2 0.8 copy-start.8
  140.0 9.3 %copy-start.2 = (bf16[4,32,16,256]{3,2,1,0:T(8,128)(2,1)}, bf16[4,32,16,256]{3,2,1,0:T(8,128)(2,1)S(1)}, u32[]{:S(2)}) copy-start(bf16[4,32,16,256]{3,2,1,0:T(8,128)(2,1)S(1)} %all-to-all-done.3.rest_1_.rest_0_) | copy-start | bytes 3145732
  140.0 19.0 %collective-permute-start.13 = (bf16[4,16,16,256]{3,2,1,0:T(8,128)(2,1)}, bf16[4,16,16,256]{3,2,1,0:T(8,128)(2,1)S(1)}, u32[]{:S(2)}, u32[]{:S(2)}) collective-permute-start(bf16[4,16,16,256]{3,2,1,0:T(8,128)(2,1)} %copy-done.8), channel_id=1, source_target_pairs={{0,16},{16,0},{1,17},{17,1},{2,18},{18,2},{3,19},{19,3},{4,20},{20... | collective-permute-start | bytes 1572872 | tf_op jit(solution)/shard_map/ppermute | solution.py:211
  159.0 0.8 copy-start.7

commit v5 on v4

--- a/solution.py
+++ b/solution.py
@@ -8,6 +8,7 @@
 from jax.sharding import PartitionSpec as P
 
 PLANE = 4
+WINDOW = 2
 ROWS = 16
 VMEM = pl.BlockSpec(memory_space=pltpu.VMEM)
 SMEM = pl.BlockSpec(memory_space=pltpu.SMEM)
@@ -15,37 +16,43 @@
 DOT = functools.partial(jnp.dot, preferred_element_type=jnp.float32)
 
 
-def gather_kernel(plan, outer, half, count, order_ref, blocks_ref, *rest):
+def gather_kernel(plan, tails, outer, half, count, order_ref, blocks_ref, occ_ref, vir_ref, *rest):
     outs, sems = rest[:count], rest[count]
     me = lax.axis_index("wide")
     group = lax.axis_index("groups")
     plane, lane = me // PLANE, me % PLANE
     copies = []
-    for n, (out, place, dz, target, flip, start, rows, own) in enumerate(plan):
+    for n, (out, entry, row, dz, target, flip, start, rows, own) in enumerate(plan):
         who = (lane ^ target) if flip else target
         block = order_ref[lax.rem(plane + dz, outer) * PLANE + who]
         low = (group if own else 1 - group) * half + start
-        to = outs[out] if place is None else outs[out].at[place[0], pl.ds(place[1], rows)]
+        to = outs[out] if entry is None else outs[out].at[entry]
         copies.append(
-            pltpu.make_async_copy(blocks_ref.at[block, pl.ds(low, rows)], to, sems.at[n])
+            pltpu.make_async_copy(
+                blocks_ref.at[block, pl.ds(low, rows)], to.at[pl.ds(row, rows)], sems.at[n]
+            )
         )
+    for n, (out, row) in enumerate(tails):
+        for m, part in enumerate((occ_ref, vir_ref)):
+            to = outs[out].at[row + m]
+            copies.append(pltpu.make_async_copy(part, to, sems.at[len(plan) + 2 * n + m]))
     for copy in copies:
         copy.start()
     for copy in copies:
         copy.wait()
 
 
-def gather(plan, shapes, outer, half, ri_order, blocks):
+def gather(plan, tails, shapes, outer, half, ri_order, blocks, occupied, virtual):
     size = sum(s.size for s in shapes) * 4
     return pl.pallas_call(
-        functools.partial(gather_kernel, plan, outer, half, len(shapes)),
+        functools.partial(gather_kernel, plan, tails, outer, half, len(shapes)),
         out_shape=shapes,
-        in_specs=[SMEM, HBM],
+        in_specs=[SMEM] + [HBM] * 3,
         out_specs=[VMEM] * len(shapes),
         compiler_params=pltpu.CompilerParams(vmem_limit_bytes=58 * 2**20),
-        scratch_shapes=[pltpu.SemaphoreType.DMA((len(plan),))],
+        scratch_shapes=[pltpu.SemaphoreType.DMA((len(plan) + 2 * len(tails),))],
         cost_estimate=pl.CostEstimate(flops=0, bytes_accessed=size, transcendentals=0),
-    )(ri_order, blocks)
+    )(ri_order, blocks, occupied, virtual)
 
 
 def load(pieces, held, sems, base=0):
@@ -87,7 +94,7 @@
     me = lax.axis_index("wide")
     plane, lane = me // PLANE, me % PLANE
     window = occ_ref.shape[0]
-    nblk = mask_ref.shape[2]
+    nblk = mask_ref.shape[0]
     block_rows = window // nblk
 
     def assembled(shape, dim):
@@ -96,16 +103,19 @@
         device = (at // orb) % PLANE
         source = jnp.zeros(shape, jnp.int32)
         for n, dz in enumerate(shifts):
-            who = (device ^ lane) if n == 1 else device
+            who = device if n == outer - 1 else device ^ lane
             from_plane = lax.rem(plane + (outer - dz), outer)
             source = jnp.where(place == n, from_plane * PLANE + who, source)
         return source * orb + at % orb
 
     arrived = lax.broadcasted_iota(jnp.int32, (window, 2 * window), 1)
     kind = (arrived // orb) % 2
-    dz = (arrived // (2 * orb)) % outer
-    device = arrived // (2 * orb * outer)
-    source = lax.rem(plane - dz + outer, outer) * PLANE + device
+    place = (arrived // (2 * orb)) % outer
+    device = (arrived // (2 * orb * outer)) ^ lane
+    source = jnp.zeros(arrived.shape, jnp.int32)
+    for n, dz in enumerate(shifts):
+        from_plane = lax.rem(plane + (outer - dz), outer)
+        source = jnp.where(place == n, from_plane * PLANE + device, source)
     orbital = source * orb + arrived % orb
     rows = lax.broadcasted_iota(jnp.int32, (window, 2 * window), 0)
     pick = jnp.where((rows == orbital) & (kind == 0), 1.0, 0.0).astype(jnp.bfloat16)
@@ -123,7 +133,7 @@
     keep = jnp.zeros((window, window), jnp.int32)
     for a in range(nblk):
         for b in range(nblk):
-            keep = jnp.where((lam == a) & (sig == b), mask_ref[block, a, b], keep)
+            keep = jnp.where((lam == a) & (sig == b), mask_ref[a, b, block], keep)
     keep = jnp.where(keep > 0, 1.0, 0.0).astype(jnp.bfloat16)
     occ_ref[...] = occ
     vir_ref[...] = vir
@@ -215,75 +225,68 @@
     shape = lambda *s: jax.ShapeDtypeStruct(s + (orb, window), kind)
     blocks = tensor.reshape(wide_count, rows, orb, window)
 
-    plan = [(q, None, first, q, True, 0, half, True) for q in range(PLANE)]
-    pieces = gather(plan, [shape(half)] * PLANE, outer, half, ri_order, blocks)
+    def straight(d, at):
+        plan = [(at + q, None, 0, d, q, True, 0, half, True) for q in range(PLANE)]
+        return plan, [(at, half)], [shape(half + 2)] + [shape(half)] * (PLANE - 1)
+
+    plan, tails, shapes = straight(first, 0)
+    pieces = gather(plan, tails, shapes, outer, half, ri_order, blocks, occupied, virtual)
+    pieces, held_back = barrier((pieces, blocks))
+    plan, tails, shapes = [], [], []
+    for d in order[1:-1]:
+        more = straight(d, len(shapes))
+        plan, tails, shapes = plan + more[0], tails + more[1], shapes + more[2]
+    plan += [(len(shapes), i, 0, last, i, False, 0, half, True) for i in range(PLANE)]
+    shapes.append(shape(PLANE, half))
+    for q in range(PLANE):
+        plan += [(len(shapes), None, 0, 0, q, True, 0, half, True)]
+        plan += [(len(shapes), None, half, 0, q, True, 0, half, False)]
+        shapes.append(shape(rows))
+    to_send = gather(plan, tails, shapes, outer, half, ri_order, held_back, occupied, virtual)
+
+    def after(x, other):
+        return barrier((x, other))[0]
+
+    direct = list(pieces) + list(to_send[: PLANE * (outer - 3)])
+    to_last, near_out = to_send[PLANE * (outer - 3)], to_send[PLANE * (outer - 3) + 1 :]
     base = jnp.stack([occupied, virtual])
-    pieces, base = barrier((pieces, base))
-    sent = [shift(p, first, q) for q, p in enumerate(pieces)]
-    early = shift(base, first)
-    held_back, early, base = barrier((blocks, early, base))
-    plan, shapes = [], []
-    for d in order[1:]:
-        plan += [(len(shapes), (i, 0), d, i, False, 0, half, True) for i in range(PLANE)]
-        shapes.append(shape(PLANE, half))
-    for own in (True, False):
-        plan += [(len(shapes), (i, 0), 0, i, False, 0, half, own) for i in range(PLANE)]
-        shapes.append(shape(PLANE, half))
-    to_send = gather(plan, shapes, outer, half, ri_order, held_back)
-
-    dens, small = {0: base, first: early}, [d for d in range(1, outer) if d != first]
-    per_phase = -(-len(small) // max(1, outer - 3))
-    own_in, swapped, near = [], [], []
-    ready = []
-    for k in range(outer):
-        if k == 0:
-            moved = sent
-        elif k <= outer - 3:
-            moved = [shift(ready[0], order[k])]
-        else:
-            moved = [shift(ready[k - outer + 2], last)]
-        turn = [swap(own_in[-1])] if k else []
-        tiny = []
-        if 1 <= k <= outer - 3:
-            now, small = small[:per_phase], small[per_phase:]
-            tiny = [shift(base, d) for d in now]
-        if k == outer - 2:
-            spread = jnp.stack([dens[d] for d in range(outer)]).reshape(1, 2 * outer, orb, window)
-            spread = jnp.broadcast_to(spread, (PLANE, 2 * outer, orb, window))
-            around = inplane(jnp.concatenate([to_send[0], spread], axis=1))
-        else:
-            around = inplane(to_send[0])
-        moved, turn, tiny, around, to_send, base, ready = barrier(
-            (moved, turn, tiny, around, to_send[1:], base, ready)
-        )
-        own_in.append(moved[0] if k else jnp.stack(moved))
-        swapped += turn
-        dens.update(zip(now, tiny)) if tiny else None
-        if k < outer - 3:
-            ready = [around]
-        elif k == outer - 3:
-            ready = [around[:, :quarter], around[:, quarter:]]
-        else:
-            near.append(around)
-    swapped.append(swap(own_in[-1]))
-    dens_all = near[0][:, half:].reshape(2 * window, window)
-
-    table = {0: [], 1: [], 2: []}
+    far = shift(base, last)
+    came, swapped = [], []
+    for n, piece in enumerate(direct):
+        if n >= WINDOW:
+            piece = after(piece, came[n - WINDOW])
+        came.append(shift(piece, order[n // PLANE], n % PLANE))
+    ready = inplane(after(to_last, came[1]))
+    low = shift(after(ready[:, :quarter], came[-2]), last)
+    high = shift(after(ready[:, quarter:], came[-1]), last)
+    for n in range(outer - 2):
+        group_in = came[PLANE * n : PLANE * (n + 1)]
+        swapped.append(swap(jnp.stack([group_in[0][:half]] + group_in[1:])))
+    near = [near_out[0]]
+    for q in range(1, PLANE):
+        near.append(shift(after(near_out[q], near[-1] if q > 1 else came[-PLANE]), 0, q))
+    mine = jnp.stack([base] + [came[PLANE * n][half:] for n in range(outer - 2)] + [far])
+    dens = [mine] + [shift(mine, 0, q) for q in range(1, PLANE)]
+    dens_all = jnp.stack(dens).reshape(2 * window, window)
+    swapped.append(swap(low))
+
+    early, front, back = [], [], []
     for i in range(PLANE):
         for n in range(outer):
             at = (n * PLANE + i) * orb
             if n == 0:
-                low, high, low_y, high_y = near[0], near[0], near[1], near[1]
-                second, second_y = quarter, quarter
+                early += [(near[i], None, 0, quarter, 0, at)]
+                front += [(near[i], None, quarter, half, 0, at)]
+                back += [(near[i], None, half + quarter, quarter, 0, at)]
             elif n < outer - 1:
-                low, high, low_y, high_y = own_in[n - 1], own_in[n - 1], swapped[n - 1], swapped[n - 1]
-                second, second_y = quarter, quarter
+                early += [(came[PLANE * (n - 1) + i], None, 0, quarter, 0, at)]
+                front += [(came[PLANE * (n - 1) + i], None, quarter, quarter, 0, at)]
+                front += [(swapped[n - 1], i, 0, quarter, quarter, at)]
+                back += [(swapped[n - 1], i, quarter, quarter, 0, at)]
             else:
-                low, high, low_y, high_y = own_in[-2], own_in[-1], swapped[-2], swapped[-1]
-                second, second_y = 0, 0
-            table[0] += [(low, i, 0, quarter, 0, at)]
-            table[1] += [(high, i, second, quarter, 0, at), (low_y, i, 0, quarter, quarter, at)]
-            table[2] += [(high_y, i, second_y, quarter, 0, at)]
+                early += [(low, i, 0, quarter, 0, at)]
+                front += [(high, i, 0, quarter, 0, at)]
+                front += [(swapped[-1], i, 0, quarter, quarter, at)]
 
     def places(listed):
         if orb % ROWS == 0:
@@ -297,7 +300,7 @@
         whole = []
         for r in range(0, size, ROWS):
             row = sorted((p for p in listed if p[4] <= r < p[4] + p[3]), key=lambda p: p[5])
-            cut = [lax.slice_in_dim(p[0][p[1]], p[2] + r - p[4], p[2] + r - p[4] + ROWS) for p in row]
+            cut = [lax.slice_in_dim(p[0] if p[1] is None else p[0][p[1]], p[2] + r - p[4], p[2] + r - p[4] + ROWS) for p in row]
             whole.append(jnp.concatenate(cut, axis=1))
         return [(0, None, 0, size, 0, 0)], [jnp.concatenate(whole)]
 
@@ -319,7 +322,7 @@
             pltpu.SemaphoreType.DMA((extra,)),
         ]
 
-    rows_of, arrays = places(table[0])
+    rows_of, arrays = places(early)
     mask_a, mix_a, occ, vir, keep = pl.pallas_call(
         functools.partial(front_kernel, rows_of, [0] + order, outer, orb, len(arrays)),
         out_shape=[tall(quarter), tall(quarter), mat, mat, mat],
@@ -328,8 +331,10 @@
         scratch_shapes=scratch(quarter, copies(rows_of)),
         compiler_params=params,
         cost_estimate=cost(quarter, 6 * quarter),
-    )(ri_order, block_mask, dens_all, *arrays)
-    rows_of, arrays = places(table[1])
+    )(ri_order, block_mask.transpose(1, 2, 0), dens_all, *arrays)
+    final = swap(after(high, mask_a))
+    back += [(final, i, 0, quarter, 0, ((outer - 1) * PLANE + i) * orb) for i in range(PLANE)]
+    rows_of, arrays = places(front)
     mask_b, mix_b = pl.pallas_call(
         functools.partial(middle_kernel, rows_of, len(arrays)),
         out_shape=[tall(half), tall(half)],
@@ -339,7 +344,7 @@
         compiler_params=params,
         cost_estimate=cost(half, 6 * half),
     )(occ, vir, keep, *arrays)
-    rows_of, arrays = places(table[2])
+    rows_of, arrays = places(back)
     return pl.pallas_call(
         functools.partial(back_kernel, rows_of, len(arrays)),
         out_shape=jax.ShapeDtypeStruct((rows, rows), jnp.float32),

time: 172 us -> 137 us (0.80)
  waiting for transfers between devices: 93.2 us -> 62.2 us
  starting transfers between devices: 34.2 us -> 31.9 us
  local copies, waits for them, and re-layouts: 5.31 us -> 3.46 us
    ppermute x10 -> x17, waiting for transfers between devices: 93.2 us -> 62 us  [shift(): return lax.ppermute(x, 'wide', pairs)]
    all_to_all x4 -> x1, starting transfers between devices: 15 us -> 3.53 us  [inplane(): lax.all_to_all(x, 'wide', split_axis=0, concat_axis=0, tiled=True, axis_i...]
    ppermute x10 -> x17, starting transfers between devices: 14.1 us -> 22.2 us  [shift(): return lax.ppermute(x, 'wide', pairs)]
    another operation x3 -> x5, other arithmetic: 0.15 us -> 3.07 us  [the longest x2 2.29 us: shards(): swapped.append(swap(jnp.stack([group_in[0][:half]] + group_in[1:])))]
    concatenate x1 -> x0, other arithmetic: 2.76 us -> none  [shards(): around = inplane(jnp.concatenate([to_send[0], spread], axis=1))]
  transfers between devices with their start and end apart: 18 -> 22, of which waited for: 9 -> 11; matrix products, arithmetic and copies ran while one was open for 3% -> 3% of each run, Pallas kernels for 9% -> 15%
where the time goes in v5:
time: 137 us; the launch traced here: 136 us
  waiting for transfers between devices  62.2 us (45%)
  Pallas kernels  35.6 us (26%)
  starting transfers between devices  31.9 us (23%)
  local copies, waits for them, and re-layouts  3.46 us (3%)
  other arithmetic  3.07 us (2%)
    ppermute x17, waiting for transfers between devices, shift(): return lax.ppermute(x, 'wide', pairs)  62 us
    ppermute x17, starting transfers between devices, shift(): return lax.ppermute(x, 'wide', pairs)  22.2 us
    pallas_call x1, Pallas kernels, shards(): pl.pallas_call(functools.partial(back_kernel, rows_of, len(arrays)), out_...  11.8 us
    pallas_call x1, Pallas kernels, shards(): pl.pallas_call(functools.partial(middle_kernel, rows_of, len(arrays)), ou...  9.62 us
    pallas_call x2, Pallas kernels, gather(): pl.pallas_call(functools.partial(gather_kernel, plan, tails, outer, half,...  7.99 us
    ppermute x4, starting transfers between devices, swap(): return lax.ppermute(x, 'groups', [(0, 1), (1, 0)])  6.14 us
    pallas_call x1, Pallas kernels, shards(): pl.pallas_call(functools.partial(front_kernel, rows_of, [0] + order, oute...  6.14 us
    all_to_all x1, starting transfers between devices, inplane(): lax.all_to_all(x, 'wide', split_axis=0, concat_axis=0, tiled=True, axis_i...  3.53 us
  transfers between devices with their start and end apart: 22, of which 11 were waited for; matrix products, arithmetic and copies ran while one was open for 3% of the time, Pallas kernels for 15%

profile of v5, /device:TPU:0, one launch (start us, length us, event | category | flops | bytes accessed | tf_op | source)
XLA Modules:
  0.0 136.4 jit_solution(7692480014052087832)
XLA Ops:
  0.0 3.0 %shard_map.55 = (bf16[34,16,256]{2,1,0:T(8,128)(2,1)}, bf16[32,16,256]{2,1,0:T(8,128)(2,1)}, bf16[32,16,256]{2,1,0:T(8,128)(2,1)}, bf16[32,16,256]{2,1,0:T(8,128)(2,1)}) custom-call(s32[16]{0:T(128)} %order_ref.5, bf16[16,64,16,256]{3,2,1,0:T(8,128)(2,1)} %bitcast.27, bf16[16,256]{1,0:T(8,128)(2,1)} %occ_ref.3, bf16[16,256]{1,0:T(8,128)(2,1)} %vir_ref.3), custom_call_target="tpu_custom_call" | custom-call | bytes 2129920 | tf_op jit(solution)/shard_map/pallas_call | solution.py:47
  3.0 3.1 %collective-permute-start = (bf16[34,16,256]{2,1,0:T(8,128)(2,1)}, bf16[34,16,256]{2,1,0:T(8,128)(2,1)S(1)}, u32[]{:S(2)}, u32[]{:S(2)}) collective-permute-start(bf16[34,16,256]{2,1,0:T(8,128)(2,1)} %get-tuple-element.47), channel_id=1, source_target_pairs={{0,4},{1,5},{2,6},{3,7},{4,8},{5,9},{6,10},{7,11},{8,12},{9,13},{1... | collective-permute-start | bytes 835592 | tf_op jit(solution)/shard_map/ppermute | solution.py:218
  6.1 0.7 collective-permute-start.7
  6.9 9.0 %collective-permute-done.rest_1_ = bf16[34,16,256]{2,1,0:T(8,128)(2,1)S(1)} collective-permute-done((bf16[34,16,256]{2,1,0:T(8,128)(2,1)}, bf16[34,16,256]{2,1,0:T(8,128)(2,1)S(1)}, u32[]{:S(2)}, u32[]{:S(2)}) %collective-permute-start) | collective-permute-done | bytes 278560 | tf_op jit(solution)/shard_map/ppermute | solution.py:218
  15.8 1.0 collective-permute-start.1
  16.8 3.0 %collective-permute-done.7.rest_5_.rest_8_ = bf16[32,16,256]{2,1,0:T(8,128)(2,1)S(1)} collective-permute-done((bf16[32,16,256]{2,1,0:T(8,128)(2,1)}, bf16[32,16,256]{2,1,0:T(8,128)(2,1)S(1)}, u32[]{:S(2)}, u32[]{:S(2)}) %collective-permute-start.7) | collective-permute-done | bytes 262176 | tf_op jit(solution)/shard_map/ppermute | solution.py:218
  19.8 2.3 %collective-permute-start.11 = (bf16[32,16,256]{2,1,0:T(8,128)(2,1)}, bf16[32,16,256]{2,1,0:T(8,128)(2,1)S(1)}, u32[]{:S(2)}, u32[]{:S(2)}) collective-permute-start(bf16[32,16,256]{2,1,0:T(8,128)(2,1)} %get-tuple-element.64), channel_id=1, source_target_pairs={{0,7},{1,6},{2,5},{3,4},{4,11},{5,10},{6,9},{7,8},{8,15},{9,14},{1... | collective-permute-start | bytes 786440 | tf_op jit(solution)/shard_map/ppermute | solution.py:218
  22.2 2.7 %collective-permute-start.3 = (bf16[2,16,256]{2,1,0:T(8,128)(2,1)S(1)}, bf16[2,16,256]{2,1,0:T(8,128)(2,1)S(1)}, u32[]{:S(2)}, u32[]{:S(2)}) collective-permute-start(bf16[2,16,256]{2,1,0:T(8,128)(2,1)S(1)} %get-tuple-element.86), channel_id=1, source_target_pairs={{0,8},{1,9},{2,10},{3,11},{4,12},{5,13},{6,14},{7,15},{8,0},{9,1},... | collective-permute-start | bytes 49160 | tf_op jit(solution)/shard_map/ppermute | solution.py:218
  24.8 5.0 %shard_map.56 = (bf16[34,16,256]{2,1,0:T(8,128)(2,1)}, bf16[32,16,256]{2,1,0:T(8,128)(2,1)}, bf16[32,16,256]{2,1,0:T(8,128)(2,1)}, bf16[32,16,256]{2,1,0:T(8,128...) custom-call(s32[16]{0:T(128)} %order_ref.5, ...), custom_call_target="tpu_custom_call" | custom-call | bytes 8421376 | tf_op jit(solution)/shard_map/pallas_call | solution.py:47
  29.8 3.5 %all-to-all-start = ((bf16[4,32,16,256]{3,2,1,0:T(8,128)(2,1)}), bf16[4,32,16,256]{3,2,1,0:T(8,128)(2,1)S(1)}, u32[]{:S(2)}, u32[]{:S(2)}) async-start(bf16[4,32,16,256]{3,2,1,0:T(8,128)(2,1)} %get-tuple-element.56), calls=%async_computation | async-start | bytes 2097152 | tf_op jit(solution)/shard_map/all_to_all | solution.py:209
  33.3 0.0 collective-permute-done.1.rest_8_.rest_11_
  33.3 1.4 %collective-permute-start.2 = (bf16[34,16,256]{2,1,0:T(8,128)(2,1)}, bf16[34,16,256]{2,1,0:T(8,128)(2,1)S(1)}, u32[]{:S(2)}, u32[]{:S(2)}) collective-permute-start(bf16[34,16,256]{2,1,0:T(8,128)(2,1)} %get-tuple-element.52), channel_id=1, source_target_pairs={{0,12},{1,13},{2,14},{3,15},{4,0},{5,1},{6,2},{7,3},{8,4},{9,5},{1... | collective-permute-start | bytes 835592 | tf_op jit(solution)/shard_map/ppermute | solution.py:218
  34.8 0.3 collective-permute-start.12
  35.0 8.0 %collective-permute-done.2.rest_2_.rest_3_ = bf16[34,16,256]{2,1,0:T(8,128)(2,1)S(1)} collective-permute-done((bf16[34,16,256]{2,1,0:T(8,128)(2,1)}, bf16[34,16,256]{2,1,0:T(8,128)(2,1)S(1)}, u32[]{:S(2)}, u32[]{:S(2)}) %collective-permute-start.2) | collective-permute-done | bytes 278560 | tf_op jit(solution)/shard_map/ppermute | solution.py:218
  43.1 1.1 pad_maximum_fusion
  44.2 1.5 %collective-permute-start.16 = (bf16[4,32,16,256]{3,2,1,0:T(8,128)(2,1)}, bf16[4,32,16,256]{3,2,1,0:T(8,128)(2,1)}, u32[]{:S(2)}, u32[]{:S(2)}) collective-permute-start(bf16[4,32,16,256]{3,2,1,0:T(8,128)(2,1)} %pad_maximum_fusion), channel_id=1, source_target_pairs={{0,16},{16,0},{1,17},{17,1},{2,18},{18,2},{3,19},{19,3},{4,20},{20... | collective-permute-start | bytes 3145736 | tf_op jit(solution)/shard_map/ppermute | solution.py:221
  45.7 2.0 %collective-permute-done.12.rest_6_.rest_9_ = bf16[32,16,256]{2,1,0:T(8,128)(2,1)S(1)} collective-permute-done((bf16[32,16,256]{2,1,0:T(8,128)(2,1)}, bf16[32,16,256]{2,1,0:T(8,128)(2,1)S(1)}, u32[]{:S(2)}, u32[]{:S(2)}) %collective-permute-start.12) | collective-permute-done | bytes 262176 | tf_op jit(solution)/shard_map/ppermute | solution.py:218
  47.7 4.1 %collective-permute-start.15 = (bf16[32,16,256]{2,1,0:T(8,128)(2,1)}, bf16[32,16,256]{2,1,0:T(8,128)(2,1)}, u32[]{:S(2)}, u32[]{:S(2)}) collective-permute-start(bf16[32,16,256]{2,1,0:T(8,128)(2,1)} %get-tuple-element.71), channel_id=1, source_target_pairs={{0,15},{1,14},{2,13},{3,12},{4,3},{5,2},{6,1},{7,0},{8,7},{9,6},{1... | collective-permute-start | bytes 786440 | tf_op jit(solution)/shard_map/ppermute | solution.py:218
  51.9 0.0 collective-permute-start.8
  51.9 0.6 collective-permute-start.13
  52.5 0.0 all-to-all-done
  52.5 0.9 fusion.2
  53.4 10.3 %collective-permute-done.8.rest_9_.rest_12_ = bf16[32,16,256]{2,1,0:T(8,128)(2,1)} collective-permute-done((bf16[32,16,256]{2,1,0:T(8,128)(2,1)}, bf16[32,16,256]{2,1,0:T(8,128)(2,1)}, u32[]{:S(2)}, u32[]{:S(2)}) %collective-permute-start.8) | collective-permute-done | bytes 262176 | tf_op jit(solution)/shard_map/ppermute | solution.py:218
  63.7 1.6 %collective-permute-start.9 = (bf16[4,16,16,256]{3,2,1,0:T(8,128)(2,1)S(1)}, bf16[4,16,16,256]{3,2,1,0:T(8,128)(2,1)S(1)}, u32[]{:S(2)}, u32[]{:S(2)}) collective-permute-start(bf16[4,16,16,256]{3,2,1,0:T(8,128)(2,1)S(1)} %get-tuple-element.59), channel_id=1, source_target_pairs={{0,8},{1,9},{2,10},{3,11},{4,12},{5,13},{6,14},{7,15},{8,0},{9,1},... | collective-permute-start | bytes 1572872 | tf_op jit(solution)/shard_map/ppermute | solution.py:218
  65.3 1.2 pad_maximum_fusion.1
  66.5 1.6 %collective-permute-start.17 = (bf16[4,32,16,256]{3,2,1,0:T(8,128)(2,1)S(1)}, bf16[4,32,16,256]{3,2,1,0:T(8,128)(2,1)S(1)}, u32[]{:S(2)}, u32[]{:S(2)}) collective-permute-start(bf16[4,32,16,256]{3,2,1,0:T(8,128)(2,1)S(1)} %pad_maximum_fusion.1), channel_id=1, source_target_pairs={{0,16},{16,0},{1,17},{17,1},{2,18},{18,2},{3,19},{19,3},{4,20},{20... | collective-permute-start | bytes 3145736 | tf_op jit(solution)/shard_map/ppermute | solution.py:221
  68.1 0.1 collective-permute-start.6
  68.2 6.2 %collective-permute-done.13.rest_7_.rest_10_.rest_4_ = bf16[64,16,256]{2,1,0:T(8,128)(2,1)S(1)} collective-permute-done((bf16[64,16,256]{2,1,0:T(8,128)(2,1)}, bf16[64,16,256]{2,1,0:T(8,128)(2,1)S(1)}, u32[]{:S(2)}, u32[]{:S(2)}) %collective-permute-start.13) | collective-permute-done | bytes 524320 | tf_op jit(solution)/shard_map/ppermute | solution.py:218
  74.4 1.2 collective-permute-start.5
  75.7 0.0 collective-permute-done.6
  75.7 1.1 collective-permute-start.14
  76.7 2.0 %collective-permute-done.5 = bf16[4,2,16,256]{3,2,1,0:T(8,128)(2,1)S(1)} collective-permute-done((bf16[4,2,16,256]{3,2,1,0:T(8,128)(2,1)S(1)}, bf16[4,2,16,256]{3,2,1,0:T(8,128)(2,1)S(1)}, u32[]{:S(2)}, u32[]{:S(2)}) %collective-permute-start.5) | collective-permute-done | bytes 65568 | tf_op jit(solution)/shard_map/ppermute | solution.py:218
  78.8 1.3 collective-permute-done.4
  80.0 2.1 %collective-permute-start.18 = (bf16[4,16,16,256]{3,2,1,0:T(8,128)(2,1)}, bf16[4,16,16,256]{3,2,1,0:T(8,128)(2,1)S(1)}, u32[]{:S(2)}, u32[]{:S(2)}) collective-permute-start(bf16[4,16,16,256]{3,2,1,0:T(8,128)(2,1)} %get-tuple-element.76), channel_id=1, source_target_pairs={{0,8},{1,9},{2,10},{3,11},{4,12},{5,13},{6,14},{7,15},{8,0},{9,1},... | collective-permute-start | bytes 1572872 | tf_op jit(solution)/shard_map/ppermute | solution.py:218
  82.1 19.8 %collective-permute-done.9.rest_3_ = bf16[4,16,16,256]{3,2,1,0:T(8,128)(2,1)S(1)} collective-permute-done((bf16[4,16,16,256]{3,2,1,0:T(8,128)(2,1)S(1)}, bf16[4,16,16,256]{3,2,1,0:T(8,128)(2,1)S(1)}, u32[]{:S(2)}, u32[]{:S(2)}) %collective-permute-start.9) | collective-permute-done | bytes 524320 | tf_op jit(solution)/shard_map/ppermute | solution.py:218
  101.9 1.5 %collective-permute-start.19 = (bf16[4,16,16,256]{3,2,1,0:T(8,128)(2,1)S(1)}, bf16[4,16,16,256]{3,2,1,0:T(8,128)(2,1)}, u32[]{:S(2)}, u32[]{:S(2)}) collective-permute-start(bf16[4,16,16,256]{3,2,1,0:T(8,128)(2,1)S(1)} %collective-permute-done.9.rest_3_), channel_id=1, source_target_pairs={{0,16},{16,0},{1,17},{17,1},{2,18},{18,2},{3,19},{19,3},{4,20},{20... | collective-permute-start | bytes 1572872 | tf_op jit(solution)/shard_map/ppermute | solution.py:221
  103.4 0.8 pad_maximum_fusion.2
  104.2 0.0 collective-permute-done.14.rest_10_.rest_13_.rest_5_
  104.3 0.7 copy-done.2
  105.0 6.1 %shard_map.57 = (bf16[256,16,256]{2,1,0:T(8,128)(2,1)}, bf16[256,16,256]{2,1,0:T(8,128)(2,1)}, bf16[256,256]{1,0:T(8,128)(2,1)}, bf16[256,256]{1,0:T(8,128)(2,1)}, bf16[256,256]{1,0:T(8,128)(2,1)}) custom-call(s32[16]{0:T(128)} %order_ref.5, s32[4,4,16]{2,1,0:T(4,128)} %bitcast.40, bf16[512,256]{1,0:T(8,128)(2,1)} %bitcast.29, ...), custom_call_target="tpu_custom_call" | custom-call | flops 1073741824 | bytes 6291456 | tf_op jit(solution)/shard_map/pallas_call | solution.py:326
  111.2 0.3 collective-permute-done.18.rest_5_
  111.5 1.5 %collective-permute-start.20 = (bf16[4,16,16,256]{3,2,1,0:T(8,128)(2,1)S(1)}, bf16[4,16,16,256]{3,2,1,0:T(8,128)(2,1)S(1)}, u32[]{:S(2)}, u32[]{:S(2)}) collective-permute-start(bf16[4,16,16,256]{3,2,1,0:T(8,128)(2,1)S(1)} %collective-permute-done.18.rest_5_), channel_id=1, source_target_pairs={{0,16},{16,0},{1,17},{17,1},{2,18},{18,2},{3,19},{19,3},{4,20},{20... | collective-permute-start | bytes 1572872 | tf_op jit(solution)/shard_map/ppermute | solution.py:221
  113.0 0.0 collective-permute-done.19.rest_6_
  113.0 0.9 copy-done.5
  114.0 9.6 %shard_map.58 = (bf16[256,32,256]{2,1,0:T(8,128)(2,1)}, bf16[256,32,256]{2,1,0:T(8,128)(2,1)}) custom-call(bf16[256,256]{1,0:T(8,128)(2,1)} %get-tuple-element.72.occ_ref, bf16[256,256]{1,0:T(8,128)(2,1)} %get-tuple-element.73.vir_ref, bf16[256,256]{1,0:T(8,128)(2,1)} %get-tuple-element.74.keep_ref, bf16[64,16,256]{2,1,0:T(8,128)(2,1)} %get-tuple-element.53.rest_0_, ...), custom_call_target="tpu_custom_call" | custom-call | flops 2147483648 | bytes 12582912 | tf_op jit(solution)/shard_map/pallas_call | solution.py:338
  123.6 0.1 collective-permute-done.20.rest_6_
  123.7 0.8 copy-done.10
  124.5 11.8 %shard_map.59 = f32[64,64]{1,0:T(8,128)} custom-call(bf16[256,256]{1,0:T(8,128)(2,1)} %get-tuple-element.72.occ_ref, bf16[256,256]{1,0:T(8,128)(2,1)} %get-tuple-element.73.vir_ref, bf16[256,256]{1,0:T(8,128)(2,1)} %get-tuple-element.74.keep_ref, bf16[256,16,256]{2,1,0:T(8,128)(2,1)} %get-tuple-element.75.mask_a, ...), custom_call_target="tpu_custom_call" | custom-call | flops 1073741824 | bytes 16777216 | tf_op jit(solution)/shard_map/pallas_call | solution.py:348
  (43 shorter events, 0.1 us)
Async XLA Ops:
  0.0 22.1 %copy-start.12 = (bf16[16,256]{1,0:T(8,128)(2,1)S(1)}, bf16[16,256]{1,0:T(8,128)(2,1)}, u32[]{:S(2)}) copy-start(bf16[16,256]{1,0:T(8,128)(2,1)} %vir_ref.3) | copy-start | bytes 24580
  0.0 22.1 %copy-start.13 = (bf16[16,256]{1,0:T(8,128)(2,1)S(1)}, bf16[16,256]{1,0:T(8,128)(2,1)}, u32[]{:S(2)}) copy-start(bf16[16,256]{1,0:T(8,128)(2,1)} %occ_ref.3) | copy-start | bytes 24580
  3.0 12.8 %collective-permute-start = (bf16[34,16,256]{2,1,0:T(8,128)(2,1)}, bf16[34,16,256]{2,1,0:T(8,128)(2,1)S(1)}, u32[]{:S(2)}, u32[]{:S(2)}) collective-permute-start(bf16[34,16,256]{2,1,0:T(8,128)(2,1)} %get-tuple-element.47), channel_id=1, source_target_pairs={{0,4},{1,5},{2,6},{3,7},{4,8},{5,9},{6,10},{7,11},{8,12},{9,13},{1... | collective-permute-start | bytes 835592 | tf_op jit(solution)/shard_map/ppermute | solution.py:218
  6.1 13.7 %collective-permute-start.7 = (bf16[32,16,256]{2,1,0:T(8,128)(2,1)}, bf16[32,16,256]{2,1,0:T(8,128)(2,1)S(1)}, u32[]{:S(2)}, u32[]{:S(2)}) collective-permute-start(bf16[32,16,256]{2,1,0:T(8,128)(2,1)} %get-tuple-element.55), channel_id=1, source_target_pairs={{0,5},{1,4},{2,7},{3,6},{4,9},{5,8},{6,11},{7,10},{8,13},{9,12},{1... | collective-permute-start | bytes 786440 | tf_op jit(solution)/shard_map/ppermute | solution.py:218
  15.8 19.2 %copy-start.3 = (bf16[34,16,256]{2,1,0:T(8,128)(2,1)}, bf16[34,16,256]{2,1,0:T(8,128)(2,1)S(1)}, u32[]{:S(2)}) copy-start(bf16[34,16,256]{2,1,0:T(8,128)(2,1)S(1)} %collective-permute-done.rest_1_) | copy-start | bytes 835588
  15.8 17.5 %collective-permute-start.1 = (bf16[32,16,256]{2,1,0:T(8,128)(2,1)}, bf16[32,16,256]{2,1,0:T(8,128)(2,1)S(1)}, u32[]{:S(2)}, u32[]{:S(2)}) collective-permute-start(bf16[32,16,256]{2,1,0:T(8,128)(2,1)} %get-tuple-element.51), channel_id=1, source_target_pairs={{0,6},{1,7},{2,4},{3,5},{4,10},{5,11},{6,8},{7,9},{8,14},{9,15},{1... | collective-permute-start | bytes 786440 | tf_op jit(solution)/shard_map/ppermute | solution.py:218
  19.8 23.3 %copy-start.6 = (bf16[32,16,256]{2,1,0:T(8,128)(2,1)}, bf16[32,16,256]{2,1,0:T(8,128)(2,1)S(1)}, u32[]{:S(2)}) copy-start(bf16[32,16,256]{2,1,0:T(8,128)(2,1)S(1)} %collective-permute-done.7.rest_5_.rest_8_) | copy-start | bytes 786436
  19.8 15.0 %collective-permute-start.11 = (bf16[32,16,256]{2,1,0:T(8,128)(2,1)}, bf16[32,16,256]{2,1,0:T(8,128)(2,1)S(1)}, u32[]{:S(2)}, u32[]{:S(2)}) collective-permute-start(bf16[32,16,256]{2,1,0:T(8,128)(2,1)} %get-tuple-element.64), channel_id=1, source_target_pairs={{0,7},{1,6},{2,5},{3,4},{4,11},{5,10},{6,9},{7,8},{8,15},{9,14},{1... | collective-permute-start | bytes 786440 | tf_op jit(solution)/shard_map/ppermute | solution.py:218
  22.2 45.9 %collective-permute-start.3 = (bf16[2,16,256]{2,1,0:T(8,128)(2,1)S(1)}, bf16[2,16,256]{2,1,0:T(8,128)(2,1)S(1)}, u32[]{:S(2)}, u32[]{:S(2)}) collective-permute-start(bf16[2,16,256]{2,1,0:T(8,128)(2,1)S(1)} %get-tuple-element.86), channel_id=1, source_target_pairs={{0,8},{1,9},{2,10},{3,11},{4,12},{5,13},{6,14},{7,15},{8,0},{9,1},... | collective-permute-start | bytes 49160 | tf_op jit(solution)/shard_map/ppermute | solution.py:218
  29.8 22.7 %all-to-all-start = ((bf16[4,32,16,256]{3,2,1,0:T(8,128)(2,1)}), bf16[4,32,16,256]{3,2,1,0:T(8,128)(2,1)S(1)}, u32[]{:S(2)}, u32[]{:S(2)}) async-start(bf16[4,32,16,256]{3,2,1,0:T(8,128)(2,1)} %get-tuple-element.56), calls=%async_computation | async-start | bytes 2097152 | tf_op jit(solution)/shard_map/all_to_all | solution.py:209
  33.3 70.9 %copy-start.7 = (bf16[32,16,256]{2,1,0:T(8,128)(2,1)}, bf16[32,16,256]{2,1,0:T(8,128)(2,1)S(1)}, u32[]{:S(2)}) copy-start(bf16[32,16,256]{2,1,0:T(8,128)(2,1)S(1)} %collective-permute-done.1.rest_8_.rest_11_) | copy-start | bytes 786436
  33.3 9.7 %collective-permute-start.2 = (bf16[34,16,256]{2,1,0:T(8,128)(2,1)}, bf16[34,16,256]{2,1,0:T(8,128)(2,1)S(1)}, u32[]{:S(2)}, u32[]{:S(2)}) collective-permute-start(bf16[34,16,256]{2,1,0:T(8,128)(2,1)} %get-tuple-element.52), channel_id=1, source_target_pairs={{0,12},{1,13},{2,14},{3,15},{4,0},{5,1},{6,2},{7,3},{8,4},{9,5},{1... | collective-permute-start | bytes 835592 | tf_op jit(solution)/shard_map/ppermute | solution.py:218
  34.8 69.4 %copy-start.8 = (bf16[32,16,256]{2,1,0:T(8,128)(2,1)}, bf16[32,16,256]{2,1,0:T(8,128)(2,1)S(1)}, u32[]{:S(2)}) copy-start(bf16[32,16,256]{2,1,0:T(8,128)(2,1)S(1)} %collective-permute-done.11.rest_11_.rest_14_) | copy-start | bytes 786436
  34.8 13.0 %collective-permute-start.12 = (bf16[32,16,256]{2,1,0:T(8,128)(2,1)}, bf16[32,16,256]{2,1,0:T(8,128)(2,1)S(1)}, u32[]{:S(2)}, u32[]{:S(2)}) collective-permute-start(bf16[32,16,256]{2,1,0:T(8,128)(2,1)} %get-tuple-element.65), channel_id=1, source_target_pairs={{0,13},{1,12},{2,15},{3,14},{4,1},{5,0},{6,3},{7,2},{8,5},{9,4},{1... | collective-permute-start | bytes 786440 | tf_op jit(solution)/shard_map/ppermute | solution.py:218
  43.1 61.2 %copy-start.4 = (bf16[34,16,256]{2,1,0:T(8,128)(2,1)}, bf16[34,16,256]{2,1,0:T(8,128)(2,1)S(1)}, u32[]{:S(2)}) copy-start(bf16[34,16,256]{2,1,0:T(8,128)(2,1)S(1)} %collective-permute-done.2.rest_2_.rest_3_) | copy-start | bytes 835588
  43.1 8.8 %collective-permute-start.10 = (bf16[64,16,256]{2,1,0:T(8,128)(2,1)}, bf16[64,16,256]{2,1,0:T(8,128)(2,1)S(1)}, u32[]{:S(2)}, u32[]{:S(2)}) collective-permute-start(bf16[64,16,256]{2,1,0:T(8,128)(2,1)} %get-tuple-element.61), channel_id=1, source_target_pairs={{0,1},{1,0},{2,3},{3,2},{4,5},{5,4},{6,7},{7,6},{8,9},{9,8},{10,11... | collective-permute-start | bytes 1572872 | tf_op jit(solution)/shard_map/ppermute | solution.py:218
  44.2 68.8 %collective-permute-start.16 = (bf16[4,32,16,256]{3,2,1,0:T(8,128)(2,1)}, bf16[4,32,16,256]{3,2,1,0:T(8,128)(2,1)}, u32[]{:S(2)}, u32[]{:S(2)}) collective-permute-start(bf16[4,32,16,256]{3,2,1,0:T(8,128)(2,1)} %pad_maximum_fusion), channel_id=1, source_target_pairs={{0,16},{16,0},{1,17},{17,1},{2,18},{18,2},{3,19},{19,3},{4,20},{20... | collective-permute-start | bytes 3145736 | tf_op jit(solution)/shard_map/ppermute | solution.py:221
  47.7 56.5 %copy-start.9 = (bf16[32,16,256]{2,1,0:T(8,128)(2,1)}, bf16[32,16,256]{2,1,0:T(8,128)(2,1)S(1)}, u32[]{:S(2)}) copy-start(bf16[32,16,256]{2,1,0:T(8,128)(2,1)S(1)} %collective-permute-done.12.rest_6_.rest_9_) | copy-start | bytes 786436
  47.7 17.6 %collective-permute-start.15 = (bf16[32,16,256]{2,1,0:T(8,128)(2,1)}, bf16[32,16,256]{2,1,0:T(8,128)(2,1)}, u32[]{:S(2)}, u32[]{:S(2)}) collective-permute-start(bf16[32,16,256]{2,1,0:T(8,128)(2,1)} %get-tuple-element.71), channel_id=1, source_target_pairs={{0,15},{1,14},{2,13},{3,12},{4,3},{5,2},{6,1},{7,0},{8,7},{9,6},{1... | collective-permute-start | bytes 786440 | tf_op jit(solution)/shard_map/ppermute | solution.py:218
  51.9 11.8 %collective-permute-start.8 = (bf16[32,16,256]{2,1,0:T(8,128)(2,1)}, bf16[32,16,256]{2,1,0:T(8,128)(2,1)}, u32[]{:S(2)}, u32[]{:S(2)}) collective-permute-start(bf16[32,16,256]{2,1,0:T(8,128)(2,1)} %get-tuple-element.58), channel_id=1, source_target_pairs={{0,14},{1,15},{2,12},{3,13},{4,2},{5,3},{6,0},{7,1},{8,6},{9,7},{1... | collective-permute-start | bytes 786440 | tf_op jit(solution)/shard_map/ppermute | solution.py:218
  51.9 52.3 %copy-start = (bf16[64,16,256]{2,1,0:T(8,128)(2,1)}, bf16[64,16,256]{2,1,0:T(8,128)(2,1)S(1)}, u32[]{:S(2)}) copy-start(bf16[64,16,256]{2,1,0:T(8,128)(2,1)S(1)} %collective-permute-done.10.rest_4_.rest_7_.rest_3_) | copy-start | bytes 1572868
  51.9 22.5 %collective-permute-start.13 = (bf16[64,16,256]{2,1,0:T(8,128)(2,1)}, bf16[64,16,256]{2,1,0:T(8,128)(2,1)S(1)}, u32[]{:S(2)}, u32[]{:S(2)}) collective-permute-start(bf16[64,16,256]{2,1,0:T(8,128)(2,1)} %get-tuple-element.67), channel_id=1, source_target_pairs={{0,2},{1,3},{2,0},{3,1},{4,6},{5,7},{6,4},{7,5},{8,10},{9,11},{10,... | collective-permute-start | bytes 1572872 | tf_op jit(solution)/shard_map/ppermute | solution.py:218
  52.5 23.2 %copy-start.14 = (bf16[64,16,256]{2,1,0:T(8,128)(2,1)S(1)}, bf16[64,16,256]{2,1,0:T(8,128)(2,1)}, u32[]{:S(2)}) copy-start(bf16[64,16,256]{2,1,0:T(8,128)(2,1)} %get-tuple-element.69) | copy-start | bytes 1572868
  63.7 38.2 %collective-permute-start.9 = (bf16[4,16,16,256]{3,2,1,0:T(8,128)(2,1)S(1)}, bf16[4,16,16,256]{3,2,1,0:T(8,128)(2,1)S(1)}, u32[]{:S(2)}, u32[]{:S(2)}) collective-permute-start(bf16[4,16,16,256]{3,2,1,0:T(8,128)(2,1)S(1)} %get-tuple-element.59), channel_id=1, source_target_pairs={{0,8},{1,9},{2,10},{3,11},{4,12},{5,13},{6,14},{7,15},{8,0},{9,1},... | collective-permute-start | bytes 1572872 | tf_op jit(solution)/shard_map/ppermute | solution.py:218
  66.5 46.5 %collective-permute-start.17 = (bf16[4,32,16,256]{3,2,1,0:T(8,128)(2,1)S(1)}, bf16[4,32,16,256]{3,2,1,0:T(8,128)(2,1)S(1)}, u32[]{:S(2)}, u32[]{:S(2)}) collective-permute-start(bf16[4,32,16,256]{3,2,1,0:T(8,128)(2,1)S(1)} %pad_maximum_fusion.1), channel_id=1, source_target_pairs={{0,16},{16,0},{1,17},{17,1},{2,18},{18,2},{3,19},{19,3},{4,20},{20... | collective-permute-start | bytes 3145736 | tf_op jit(solution)/shard_map/ppermute | solution.py:221
  68.1 7.6 %collective-permute-start.6 = (bf16[4,2,16,256]{3,2,1,0:T(8,128)(2,1)S(1)}, bf16[4,2,16,256]{3,2,1,0:T(8,128)(2,1)S(1)}, u32[]{:S(2)}, u32[]{:S(2)}) collective-permute-start(bf16[4,2,16,256]{3,2,1,0:T(8,128)(2,1)S(1)} %get-tuple-element.84), channel_id=1, source_target_pairs={{0,3},{1,2},{2,1},{3,0},{4,7},{5,6},{6,5},{7,4},{8,11},{9,10},{10,... | collective-permute-start | bytes 196616 | tf_op jit(solution)/shard_map/ppermute | solution.py:218
  74.4 29.8 %copy-start.1 = (bf16[64,16,256]{2,1,0:T(8,128)(2,1)}, bf16[64,16,256]{2,1,0:T(8,128)(2,1)S(1)}, u32[]{:S(2)}) copy-start(bf16[64,16,256]{2,1,0:T(8,128)(2,1)S(1)} %collective-permute-done.13.rest_7_.rest_10_.rest_4_) | copy-start | bytes 1572868
  74.4 4.3 %collective-permute-start.5 = (bf16[4,2,16,256]{3,2,1,0:T(8,128)(2,1)S(1)}, bf16[4,2,16,256]{3,2,1,0:T(8,128)(2,1)S(1)}, u32[]{:S(2)}, u32[]{:S(2)}) collective-permute-start(bf16[4,2,16,256]{3,2,1,0:T(8,128)(2,1)S(1)} %get-tuple-element.84), channel_id=1, source_target_pairs={{0,2},{1,3},{2,0},{3,1},{4,6},{5,7},{6,4},{7,5},{8,10},{9,11},{10,... | collective-permute-start | bytes 196616 | tf_op jit(solution)/shard_map/ppermute | solution.py:218
  75.7 28.5 %collective-permute-start.14 = (bf16[64,16,256]{2,1,0:T(8,128)(2,1)S(1)}, bf16[64,16,256]{2,1,0:T(8,128)(2,1)S(1)}, u32[]{:S(2)}, u32[]{:S(2)}) collective-permute-start(bf16[64,16,256]{2,1,0:T(8,128)(2,1)S(1)} %copy-done.14), channel_id=1, source_target_pairs={{0,3},{1,2},{2,1},{3,0},{4,7},{5,6},{6,5},{7,4},{8,11},{9,10},{10,... | collective-permute-start | bytes 1572872 | tf_op jit(solution)/shard_map/ppermute | solution.py:218
  78.8 1.3 collective-permute-start.4
  80.0 31.5 %collective-permute-start.18 = (bf16[4,16,16,256]{3,2,1,0:T(8,128)(2,1)}, bf16[4,16,16,256]{3,2,1,0:T(8,128)(2,1)S(1)}, u32[]{:S(2)}, u32[]{:S(2)}) collective-permute-start(bf16[4,16,16,256]{3,2,1,0:T(8,128)(2,1)} %get-tuple-element.76), channel_id=1, source_target_pairs={{0,8},{1,9},{2,10},{3,11},{4,12},{5,13},{6,14},{7,15},{8,0},{9,1},... | collective-permute-start | bytes 1572872 | tf_op jit(solution)/shard_map/ppermute | solution.py:218
  101.9 2.3 %copy-start.11 = (bf16[4,16,16,256]{3,2,1,0:T(8,128)(2,1)}, bf16[4,16,16,256]{3,2,1,0:T(8,128)(2,1)S(1)}, u32[]{:S(2)}) copy-start(bf16[4,16,16,256]{3,2,1,0:T(8,128)(2,1)S(1)} %collective-permute-done.9.rest_3_) | copy-start | bytes 1572868
  101.9 11.1 %collective-permute-start.19 = (bf16[4,16,16,256]{3,2,1,0:T(8,128)(2,1)S(1)}, bf16[4,16,16,256]{3,2,1,0:T(8,128)(2,1)}, u32[]{:S(2)}, u32[]{:S(2)}) collective-permute-start(bf16[4,16,16,256]{3,2,1,0:T(8,128)(2,1)S(1)} %collective-permute-done.9.rest_3_), channel_id=1, source_target_pairs={{0,16},{16,0},{1,17},{17,1},{2,18},{18,2},{3,19},{19,3},{4,20},{20... | collective-permute-start | bytes 1572872 | tf_op jit(solution)/shard_map/ppermute | solution.py:221
  104.2 0.8 copy-start.2
  111.5 1.5 %copy-start.15 = (bf16[4,16,16,256]{3,2,1,0:T(8,128)(2,1)}, bf16[4,16,16,256]{3,2,1,0:T(8,128)(2,1)S(1)}, u32[]{:S(2)}) copy-start(bf16[4,16,16,256]{3,2,1,0:T(8,128)(2,1)S(1)} %collective-permute-done.18.rest_5_) | copy-start | bytes 1572868
  111.5 12.3 %collective-permute-start.20 = (bf16[4,16,16,256]{3,2,1,0:T(8,128)(2,1)S(1)}, bf16[4,16,16,256]{3,2,1,0:T(8,128)(2,1)S(1)}, u32[]{:S(2)}, u32[]{:S(2)}) collective-permute-start(bf16[4,16,16,256]{3,2,1,0:T(8,128)(2,1)S(1)} %collective-permute-done.18.rest_5_), channel_id=1, source_target_pairs={{0,16},{16,0},{1,17},{17,1},{2,18},{18,2},{3,19},{19,3},{4,20},{20... | collective-permute-start | bytes 1572872 | tf_op jit(solution)/shard_map/ppermute | solution.py:221
  113.0 1.0 copy-start.5
  123.7 0.8 copy-start.10

commit v6 on v5

--- a/solution.py
+++ b/solution.py
@@ -9,6 +9,8 @@
 
 PLANE = 4
 WINDOW = 2
+LIM = (16, 24, 28)
+CHUNKS = 4
 ROWS = 16
 VMEM = pl.BlockSpec(memory_space=pltpu.VMEM)
 SMEM = pl.BlockSpec(memory_space=pltpu.SMEM)
@@ -157,37 +159,27 @@
 
 def back_kernel(places, count, occ_ref, vir_ref, keep_ref, mask_a, mask_b, mix_a, mix_b, *rest):
     refs = rest[:count]
-    out_ref, mask_t, mix_t, held, sems = rest[count:]
-    early, done = mask_a.shape[1], mask_a.shape[1] + mask_b.shape[1]
-    groups = load([(refs[p[0]],) + p[1:] for p in places], held, sems, 4)
-    before = []
-    for n, (src, to) in enumerate(
-        ((mask_a, mask_t), (mix_a, mix_t), (mask_b, mask_t), (mix_b, mix_t))
-    ):
-        low = 0 if n < 2 else early
-        size = src.shape[1]
-        before.append(pltpu.make_async_copy(src, to.at[:, pl.ds(low, size)], sems.at[n]))
-    for copy in before:
-        copy.start()
+    out_ref, mask_c, mix_c, held, sems = rest[count:]
+    groups = load([(refs[p[0]],) + p[1:] for p in places], held, sems)
     occ, vir, keep = occ_ref[...], vir_ref[...], keep_ref[...]
     for g in sorted(groups):
         for copy in groups[g]:
             copy.wait()
-        half_step(held, g * ROWS, occ, vir, keep, mask_t, mix_t, done + g * ROWS)
-    for copy in before:
-        copy.wait()
-    window, rows = mask_t.shape[0], mask_t.shape[1]
-    deep = 16
+        half_step(held, g * ROWS, occ, vir, keep, mask_c, mix_c, g * ROWS)
+    window, rows = mask_c.shape[0], out_ref.shape[0]
+    deep = window // CHUNKS
 
     def body(step, total):
         for k in range(deep):
             m = step * deep + k
+            left = jnp.concatenate([mask_a[m], mask_b[m], mask_c[m]])
+            right = jnp.concatenate([mix_a[m], mix_b[m], mix_c[m]])
             total += lax.dot_general(
-                mask_t[m], mix_t[m], (((1,), (1,)), ((), ())), preferred_element_type=jnp.float32
+                left, right, (((1,), (1,)), ((), ())), preferred_element_type=jnp.float32
             )
         return total
 
-    total = lax.fori_loop(0, window // deep, body, jnp.zeros((rows, rows), jnp.float32))
+    total = lax.fori_loop(0, CHUNKS, body, jnp.zeros((rows, rows), jnp.float32))
     half = rows // 2
     turned = jnp.concatenate([total[half:], total[:half]], axis=0)
     turned = jnp.concatenate([turned[:, half:], turned[:, :half]], axis=1)
@@ -307,7 +299,7 @@
     def copies(table):
         return sum(p[3] // ROWS for p in table)
 
-    params = pltpu.CompilerParams(vmem_limit_bytes=58 * 2**20)
+    params = lambda m: pltpu.CompilerParams(vmem_limit_bytes=m * 2**20)
     mat = jax.ShapeDtypeStruct((window, window), kind)
     tall = lambda n: jax.ShapeDtypeStruct((window, n, window), kind)
 
@@ -329,7 +321,7 @@
         in_specs=[SMEM, SMEM, VMEM] + [HBM] * len(arrays),
         out_specs=[VMEM] * 5,
         scratch_shapes=scratch(quarter, copies(rows_of)),
-        compiler_params=params,
+        compiler_params=params(LIM[0]),
         cost_estimate=cost(quarter, 6 * quarter),
     )(ri_order, block_mask.transpose(1, 2, 0), dens_all, *arrays)
     final = swap(after(high, mask_a))
@@ -341,21 +333,18 @@
         in_specs=[VMEM] * 3 + [HBM] * len(arrays),
         out_specs=[VMEM] * 2,
         scratch_shapes=scratch(half, copies(rows_of)),
-        compiler_params=params,
+        compiler_params=params(LIM[1]),
         cost_estimate=cost(half, 6 * half),
     )(occ, vir, keep, *arrays)
     rows_of, arrays = places(back)
     return pl.pallas_call(
         functools.partial(back_kernel, rows_of, len(arrays)),
         out_shape=jax.ShapeDtypeStruct((rows, rows), jnp.float32),
-        in_specs=[VMEM] * 3 + [HBM] * (4 + len(arrays)),
+        in_specs=[VMEM] * 7 + [HBM] * len(arrays),
         out_specs=VMEM,
-        scratch_shapes=[
-            pltpu.VMEM((window, rows, window), kind),
-            pltpu.VMEM((window, rows, window), kind),
-        ]
-        + scratch(quarter, 4 + copies(rows_of)),
-        compiler_params=params,
+        scratch_shapes=[pltpu.VMEM((window, quarter, window), kind)] * 2
+        + scratch(quarter, copies(rows_of)),
+        compiler_params=params(LIM[2]),
         cost_estimate=cost(quarter, 4 * rows),
     )(occ, vir, keep, mask_a, mask_b, mix_a, mix_b, *arrays)
 

time: 137 us -> 131 us (0.956)
  Pallas kernels: 35.6 us -> 23.3 us
  waiting for transfers between devices: 62.2 us -> 69.6 us
    pallas_call x1, Pallas kernels: 11.8 us -> 5.83 us  [shards(): pl.pallas_call(functools.partial(back_kernel, rows_of, len(arrays)), out_...]
    ppermute x4, waiting for transfers between devices: 0.14 us -> 5.18 us  [swap(): return lax.ppermute(x, 'groups', [(0, 1), (1, 0)])]
    pallas_call x1, Pallas kernels: 9.62 us -> 5.54 us  [shards(): pl.pallas_call(functools.partial(middle_kernel, rows_of, len(arrays)), ou...]
    unnamed x32 -> x24, local copies, waits for them, and re-layouts: 2.52 us -> 0.05 us
    ppermute x17, waiting for transfers between devices: 62 us -> 64.4 us  [shift(): return lax.ppermute(x, 'wide', pairs)]
    pallas_call x1, Pallas kernels: 6.14 us -> 3.92 us  [shards(): pl.pallas_call(functools.partial(front_kernel, rows_of, [0] + order, oute...]
  transfers between devices with their start and end apart: 22 -> 22, of which waited for: 11 -> 11; matrix products, arithmetic and copies ran while one was open for 3% -> 4% of each run, Pallas kernels for 15% -> 11%
where the time goes in v6:
time: 131 us; the launch traced here: 130 us
  waiting for transfers between devices  69.6 us (53%)
  starting transfers between devices  32.6 us (25%)
  Pallas kernels  23.3 us (18%)
  other arithmetic  2.47 us (2%)
  local copies, waits for them, and re-layouts  2.16 us (2%)
    ppermute x17, waiting for transfers between devices, shift(): return lax.ppermute(x, 'wide', pairs)  64.4 us
    ppermute x17, starting transfers between devices, shift(): return lax.ppermute(x, 'wide', pairs)  22.2 us
    pallas_call x2, Pallas kernels, gather(): pl.pallas_call(functools.partial(gather_kernel, plan, tails, outer, half,...  8 us
    ppermute x4, starting transfers between devices, swap(): return lax.ppermute(x, 'groups', [(0, 1), (1, 0)])  6.14 us
    pallas_call x1, Pallas kernels, shards(): pl.pallas_call(functools.partial(back_kernel, rows_of, len(arrays)), out_...  5.83 us
    pallas_call x1, Pallas kernels, shards(): pl.pallas_call(functools.partial(middle_kernel, rows_of, len(arrays)), ou...  5.54 us
    ppermute x4, waiting for transfers between devices, swap(): return lax.ppermute(x, 'groups', [(0, 1), (1, 0)])  5.18 us
    all_to_all x1, starting transfers between devices, inplane(): lax.all_to_all(x, 'wide', split_axis=0, concat_axis=0, tiled=True, axis_i...  4.26 us
  transfers between devices with their start and end apart: 22, of which 11 were waited for; matrix products, arithmetic and copies ran while one was open for 4% of the time, Pallas kernels for 11%

profile of v6, /device:TPU:0, one launch (start us, length us, event | category | flops | bytes accessed | tf_op | source)
XLA Modules:
  0.0 130.4 jit_solution(13347889939273144164)
XLA Ops:
  0.0 3.1 %shard_map.55 = (bf16[34,16,256]{2,1,0:T(8,128)(2,1)}, bf16[32,16,256]{2,1,0:T(8,128)(2,1)}, bf16[32,16,256]{2,1,0:T(8,128)(2,1)}, bf16[32,16,256]{2,1,0:T(8,128)(2,1)}) custom-call(s32[16]{0:T(128)} %order_ref.5, bf16[16,64,16,256]{3,2,1,0:T(8,128)(2,1)} %bitcast.33, bf16[16,256]{1,0:T(8,128)(2,1)} %occ_ref.3, bf16[16,256]{1,0:T(8,128)(2,1)} %vir_ref.3), custom_call_target="tpu_custom_call" | custom-call | bytes 2129920 | tf_op jit(solution)/shard_map/pallas_call | solution.py:49
  3.1 3.1 %collective-permute-start = (bf16[34,16,256]{2,1,0:T(8,128)(2,1)}, bf16[34,16,256]{2,1,0:T(8,128)(2,1)S(1)}, u32[]{:S(2)}, u32[]{:S(2)}) collective-permute-start(bf16[34,16,256]{2,1,0:T(8,128)(2,1)} %get-tuple-element.47), channel_id=1, source_target_pairs={{0,4},{1,5},{2,6},{3,7},{4,8},{5,9},{6,10},{7,11},{8,12},{9,13},{1... | collective-permute-start | bytes 835592 | tf_op jit(solution)/shard_map/ppermute | solution.py:210
  6.2 0.7 collective-permute-start.7
  6.9 9.0 %collective-permute-done.rest_1_ = bf16[34,16,256]{2,1,0:T(8,128)(2,1)S(1)} collective-permute-done((bf16[34,16,256]{2,1,0:T(8,128)(2,1)}, bf16[34,16,256]{2,1,0:T(8,128)(2,1)S(1)}, u32[]{:S(2)}, u32[]{:S(2)}) %collective-permute-start) | collective-permute-done | bytes 278560 | tf_op jit(solution)/shard_map/ppermute | solution.py:210
  15.9 1.0 collective-permute-start.1
  16.8 3.0 %collective-permute-done.7.rest_5_.rest_8_ = bf16[32,16,256]{2,1,0:T(8,128)(2,1)S(1)} collective-permute-done((bf16[32,16,256]{2,1,0:T(8,128)(2,1)}, bf16[32,16,256]{2,1,0:T(8,128)(2,1)S(1)}, u32[]{:S(2)}, u32[]{:S(2)}) %collective-permute-start.7) | collective-permute-done | bytes 262176 | tf_op jit(solution)/shard_map/ppermute | solution.py:210
  19.8 2.3 %collective-permute-start.11 = (bf16[32,16,256]{2,1,0:T(8,128)(2,1)}, bf16[32,16,256]{2,1,0:T(8,128)(2,1)S(1)}, u32[]{:S(2)}, u32[]{:S(2)}) collective-permute-start(bf16[32,16,256]{2,1,0:T(8,128)(2,1)} %get-tuple-element.64), channel_id=1, source_target_pairs={{0,7},{1,6},{2,5},{3,4},{4,11},{5,10},{6,9},{7,8},{8,15},{9,14},{1... | collective-permute-start | bytes 786440 | tf_op jit(solution)/shard_map/ppermute | solution.py:210
  22.2 2.7 %collective-permute-start.3 = (bf16[2,16,256]{2,1,0:T(8,128)(2,1)S(1)}, bf16[2,16,256]{2,1,0:T(8,128)(2,1)S(1)}, u32[]{:S(2)}, u32[]{:S(2)}) collective-permute-start(bf16[2,16,256]{2,1,0:T(8,128)(2,1)S(1)} %get-tuple-element.86), channel_id=1, source_target_pairs={{0,8},{1,9},{2,10},{3,11},{4,12},{5,13},{6,14},{7,15},{8,0},{9,1},... | collective-permute-start | bytes 49160 | tf_op jit(solution)/shard_map/ppermute | solution.py:210
  24.8 4.9 %shard_map.56 = (bf16[34,16,256]{2,1,0:T(8,128)(2,1)}, bf16[32,16,256]{2,1,0:T(8,128)(2,1)}, bf16[32,16,256]{2,1,0:T(8,128)(2,1)}, bf16[32,16,256]{2,1,0:T(8,128...) custom-call(s32[16]{0:T(128)} %order_ref.5, ...), custom_call_target="tpu_custom_call" | custom-call | bytes 8421376 | tf_op jit(solution)/shard_map/pallas_call | solution.py:49
  29.8 4.3 %all-to-all-start = ((bf16[4,32,16,256]{3,2,1,0:T(8,128)(2,1)}), bf16[4,32,16,256]{3,2,1,0:T(8,128)(2,1)}, u32[]{:S(2)}, u32[]{:S(2)}) async-start(bf16[4,32,16,256]{3,2,1,0:T(8,128)(2,1)} %get-tuple-element.56), calls=%async_computation | async-start | bytes 2097152 | tf_op jit(solution)/shard_map/all_to_all | solution.py:201
  34.1 0.0 copy-start.7
  34.1 0.0 copy-start.8
  34.1 0.0 collective-permute-done.1.rest_8_.rest_11_
  34.1 1.4 %collective-permute-start.2 = (bf16[34,16,256]{2,1,0:T(8,128)(2,1)}, bf16[34,16,256]{2,1,0:T(8,128)(2,1)S(1)}, u32[]{:S(2)}, u32[]{:S(2)}) collective-permute-start(bf16[34,16,256]{2,1,0:T(8,128)(2,1)} %get-tuple-element.52), channel_id=1, source_target_pairs={{0,12},{1,13},{2,14},{3,15},{4,0},{5,1},{6,2},{7,3},{8,4},{9,5},{1... | collective-permute-start | bytes 835592 | tf_op jit(solution)/shard_map/ppermute | solution.py:210
  35.5 0.0 collective-permute-done.11.rest_11_.rest_14_
  35.6 0.3 collective-permute-start.12
  35.8 8.0 %collective-permute-done.2.rest_2_.rest_3_ = bf16[34,16,256]{2,1,0:T(8,128)(2,1)S(1)} collective-permute-done((bf16[34,16,256]{2,1,0:T(8,128)(2,1)}, bf16[34,16,256]{2,1,0:T(8,128)(2,1)S(1)}, u32[]{:S(2)}, u32[]{:S(2)}) %collective-permute-start.2) | collective-permute-done | bytes 278560 | tf_op jit(solution)/shard_map/ppermute | solution.py:210
  43.8 1.1 pad_maximum_fusion
  44.9 1.5 %collective-permute-start.16 = (bf16[4,32,16,256]{3,2,1,0:T(8,128)(2,1)}, bf16[4,32,16,256]{3,2,1,0:T(8,128)(2,1)S(1)}, u32[]{:S(2)}, u32[]{:S(2)}) collective-permute-start(bf16[4,32,16,256]{3,2,1,0:T(8,128)(2,1)} %pad_maximum_fusion), channel_id=1, source_target_pairs={{0,16},{16,0},{1,17},{17,1},{2,18},{18,2},{3,19},{19,3},{4,20},{20... | collective-permute-start | bytes 3145736 | tf_op jit(solution)/shard_map/ppermute | solution.py:213
  46.5 2.1 %collective-permute-done.12.rest_6_.rest_9_ = bf16[32,16,256]{2,1,0:T(8,128)(2,1)S(1)} collective-permute-done((bf16[32,16,256]{2,1,0:T(8,128)(2,1)}, bf16[32,16,256]{2,1,0:T(8,128)(2,1)S(1)}, u32[]{:S(2)}, u32[]{:S(2)}) %collective-permute-start.12) | collective-permute-done | bytes 262176 | tf_op jit(solution)/shard_map/ppermute | solution.py:210
  48.5 4.1 %collective-permute-start.15 = (bf16[32,16,256]{2,1,0:T(8,128)(2,1)}, bf16[32,16,256]{2,1,0:T(8,128)(2,1)}, u32[]{:S(2)}, u32[]{:S(2)}) collective-permute-start(bf16[32,16,256]{2,1,0:T(8,128)(2,1)} %get-tuple-element.71), channel_id=1, source_target_pairs={{0,15},{1,14},{2,13},{3,12},{4,3},{5,2},{6,1},{7,0},{8,7},{9,6},{1... | collective-permute-start | bytes 786440 | tf_op jit(solution)/shard_map/ppermute | solution.py:210
  52.7 0.0 collective-permute-start.8
  52.7 0.7 slice_bitcast_fusion
  53.4 0.0 collective-permute-done.10.rest_4_.rest_7_.rest_3_
  53.4 0.6 collective-permute-start.13
  54.0 0.0 all-to-all-done
  54.0 1.4 %fusion.2 = (bf16[4,16,16,256]{3,2,1,0:T(8,128)(2,1)S(1)}, bf16[4,16,16,256]{3,2,1,0:T(8,128)(2,1)S(1)}) fusion(bf16[4,32,16,256]{3,2,1,0:T(8,128)(2,1)} %all-to-all-done), kind=kLoop, calls=%fused_computation.11 | loop fusion | bytes 2097152 | tf_op jit(solution)/shard_map/slice | solution.py:253
  55.4 9.1 %collective-permute-done.8.rest_9_.rest_12_ = bf16[32,16,256]{2,1,0:T(8,128)(2,1)} collective-permute-done((bf16[32,16,256]{2,1,0:T(8,128)(2,1)}, bf16[32,16,256]{2,1,0:T(8,128)(2,1)}, u32[]{:S(2)}, u32[]{:S(2)}) %collective-permute-start.8) | collective-permute-done | bytes 262176 | tf_op jit(solution)/shard_map/ppermute | solution.py:210
  64.5 1.6 %collective-permute-start.9 = (bf16[4,16,16,256]{3,2,1,0:T(8,128)(2,1)S(1)}, bf16[4,16,16,256]{3,2,1,0:T(8,128)(2,1)S(1)}, u32[]{:S(2)}, u32[]{:S(2)}) collective-permute-start(bf16[4,16,16,256]{3,2,1,0:T(8,128)(2,1)S(1)} %get-tuple-element.59), channel_id=1, source_target_pairs={{0,8},{1,9},{2,10},{3,11},{4,12},{5,13},{6,14},{7,15},{8,0},{9,1},... | collective-permute-start | bytes 1572872 | tf_op jit(solution)/shard_map/ppermute | solution.py:210
  66.1 1.3 %pad_maximum_fusion.1 = bf16[4,32,16,256]{3,2,1,0:T(8,128)(2,1)S(1)} fusion(bf16[1,32,16,256]{3,2,1,0:T(8,128)(2,1)} %bitcast.20, bf16[1,32,16,256]{3,2,1,0:T(8,128)(2,1)} %bitcast.19, bf16[1,32,16,256]{3,2,1,0:T(8,128)(2,1)} %bitcast.31, bf16[1,32,16,256]{3,2,1,0:T(8,128)(2,1)} %slice_bitcast_fusion), kind=kLoop, calls=%fused_computation.1 | loop fusion | flops 1572864 | bytes 2097152 | tf_op jit(solution)/shard_map/stack | solution.py:256
  67.4 1.6 %collective-permute-start.17 = (bf16[4,32,16,256]{3,2,1,0:T(8,128)(2,1)S(1)}, bf16[4,32,16,256]{3,2,1,0:T(8,128)(2,1)S(1)}, u32[]{:S(2)}, u32[]{:S(2)}) collective-permute-start(bf16[4,32,16,256]{3,2,1,0:T(8,128)(2,1)S(1)} %pad_maximum_fusion.1), channel_id=1, source_target_pairs={{0,16},{16,0},{1,17},{17,1},{2,18},{18,2},{3,19},{19,3},{4,20},{20... | collective-permute-start | bytes 3145736 | tf_op jit(solution)/shard_map/ppermute | solution.py:213
  69.0 0.0 collective-permute-done.3
  69.1 0.1 collective-permute-start.6
  69.1 6.1 %collective-permute-done.13.rest_7_.rest_10_.rest_4_ = bf16[64,16,256]{2,1,0:T(8,128)(2,1)S(1)} collective-permute-done((bf16[64,16,256]{2,1,0:T(8,128)(2,1)}, bf16[64,16,256]{2,1,0:T(8,128)(2,1)S(1)}, u32[]{:S(2)}, u32[]{:S(2)}) %collective-permute-start.13) | collective-permute-done | bytes 524320 | tf_op jit(solution)/shard_map/ppermute | solution.py:210
  75.2 1.2 collective-permute-start.5
  76.5 0.0 collective-permute-done.6
  76.5 1.1 collective-permute-start.14
  77.5 2.0 %collective-permute-done.5 = bf16[4,2,16,256]{3,2,1,0:T(8,128)(2,1)S(1)} collective-permute-done((bf16[4,2,16,256]{3,2,1,0:T(8,128)(2,1)S(1)}, bf16[4,2,16,256]{3,2,1,0:T(8,128)(2,1)S(1)}, u32[]{:S(2)}, u32[]{:S(2)}) %collective-permute-start.5) | collective-permute-done | bytes 65568 | tf_op jit(solution)/shard_map/ppermute | solution.py:210
  79.6 1.3 collective-permute-done.4
  80.8 2.1 %collective-permute-start.18 = (bf16[4,16,16,256]{3,2,1,0:T(8,128)(2,1)S(1)}, bf16[4,16,16,256]{3,2,1,0:T(8,128)(2,1)S(1)}, u32[]{:S(2)}, u32[]{:S(2)}) collective-permute-start(bf16[4,16,16,256]{3,2,1,0:T(8,128)(2,1)S(1)} %get-tuple-element.76), channel_id=1, source_target_pairs={{0,8},{1,9},{2,10},{3,11},{4,12},{5,13},{6,14},{7,15},{8,0},{9,1},... | collective-permute-start | bytes 1572872 | tf_op jit(solution)/shard_map/ppermute | solution.py:210
  82.9 19.8 %collective-permute-done.9.rest_3_ = bf16[4,16,16,256]{3,2,1,0:T(8,128)(2,1)S(1)} collective-permute-done((bf16[4,16,16,256]{3,2,1,0:T(8,128)(2,1)S(1)}, bf16[4,16,16,256]{3,2,1,0:T(8,128)(2,1)S(1)}, u32[]{:S(2)}, u32[]{:S(2)}) %collective-permute-start.9) | collective-permute-done | bytes 524320 | tf_op jit(solution)/shard_map/ppermute | solution.py:210
  102.7 1.5 %collective-permute-start.19 = (bf16[4,16,16,256]{3,2,1,0:T(8,128)(2,1)S(1)}, bf16[4,16,16,256]{3,2,1,0:T(8,128)(2,1)S(1)}, u32[]{:S(2)}, u32[]{:S(2)}) collective-permute-start(bf16[4,16,16,256]{3,2,1,0:T(8,128)(2,1)S(1)} %collective-permute-done.9.rest_3_), channel_id=1, source_target_pairs={{0,16},{16,0},{1,17},{17,1},{2,18},{18,2},{3,19},{19,3},{4,20},{20... | collective-permute-start | bytes 1572872 | tf_op jit(solution)/shard_map/ppermute | solution.py:213
  104.4 3.9 %shard_map.57 = (bf16[256,16,256]{2,1,0:T(8,128)(2,1)S(1)}, bf16[256,16,256]{2,1,0:T(8,128)(2,1)S(1)}, bf16[256,256]{1,0:T(8,128)(2,1)S(1)}, bf16[256,256]{1,0:T(8,128)(2,1)S(1)}, bf16[256,256]{1,0:T(8,128)(2,1)S(1)}) custom-call(s32[16]{0:T(128)S(1)} %copy-done.8, s32[4,4,16]{2,1,0:T(4,128)S(1)} %bitcast.32, bf16[512,256]{1,0:T(8,128)(2,1)S(1)} %bitcast.27, ...), custom_call_target="tpu_custom_call" | custom-call | flops 1073741824 | bytes 6291456 | tf_op jit(solution)/shard_map/pallas_call | solution.py:318
  108.3 4.0 %collective-permute-done.18.rest_5_ = bf16[4,16,16,256]{3,2,1,0:T(8,128)(2,1)S(1)} collective-permute-done((bf16[4,16,16,256]{3,2,1,0:T(8,128)(2,1)S(1)}, bf16[4,16,16,256]{3,2,1,0:T(8,128)(2,1)S(1)}, u32[]{:S(2)}, u32[]{:S(2)}) %collective-permute-start.18) | collective-permute-done | bytes 524320 | tf_op jit(solution)/shard_map/ppermute | solution.py:210
  112.3 1.5 %collective-permute-start.20 = (bf16[4,16,16,256]{3,2,1,0:T(8,128)(2,1)S(1)}, bf16[4,16,16,256]{3,2,1,0:T(8,128)(2,1)S(1)}, u32[]{:S(2)}, u32[]{:S(2)}) collective-permute-start(bf16[4,16,16,256]{3,2,1,0:T(8,128)(2,1)S(1)} %collective-permute-done.18.rest_5_), channel_id=1, source_target_pairs={{0,16},{16,0},{1,17},{17,1},{2,18},{18,2},{3,19},{19,3},{4,20},{20... | collective-permute-start | bytes 1572872 | tf_op jit(solution)/shard_map/ppermute | solution.py:213
  113.8 5.5 %shard_map.58 = (bf16[256,32,256]{2,1,0:T(8,128)(2,1)S(1)}, bf16[256,32,256]{2,1,0:T(8,128)(2,1)S(1)}) custom-call(bf16[256,256]{1,0:T(8,128)(2,1)S(1)} %get-tuple-element.72.occ_ref, bf16[256,256]{1,0:T(8,128)(2,1)S(1)} %get-tuple-element.73.vir_ref, bf16[256,256]{1,0:T(8,128)(2,1)S(1)} %get-tuple-element.74.keep_ref, bf16[64,16,256]{2,1,0:T(8,128)(2,1)S(1)} %copy-done, ...), custom_call_target="tpu_custom_call" | custom-call | flops 2147483648 | bytes 12582912 | tf_op jit(solution)/shard_map/pallas_call | solution.py:330
  119.4 5.2 %collective-permute-done.20.rest_6_ = bf16[4,16,16,256]{3,2,1,0:T(8,128)(2,1)S(1)} collective-permute-done((bf16[4,16,16,256]{3,2,1,0:T(8,128)(2,1)S(1)}, bf16[4,16,16,256]{3,2,1,0:T(8,128)(2,1)S(1)}, u32[]{:S(2)}, u32[]{:S(2)}) %collective-permute-start.20) | collective-permute-done | bytes 524320 | tf_op jit(solution)/shard_map/ppermute | solution.py:213
  124.5 5.8 %shard_map.59 = f32[64,64]{1,0:T(8,128)} custom-call(bf16[256,256]{1,0:T(8,128)(2,1)S(1)} %get-tuple-element.72.occ_ref, bf16[256,256]{1,0:T(8,128)(2,1)S(1)} %get-tuple-element.73.vir_ref, bf16[256,256]{1,0:T(8,128)(2,1)S(1)} %get-tuple-element.74.keep_ref, bf16[256,16,256]{2,1,0:T(8,128)(2,1)S(1)} %get-tuple-element.75.mask_a, ...), custom_call_target="tpu_custom_call" | custom-call | flops 1073741824 | bytes 16777216 | tf_op jit(solution)/shard_map/pallas_call | solution.py:340
  (35 shorter events, 0.1 us)
Async XLA Ops:
  0.0 22.2 %copy-start.9 = (bf16[16,256]{1,0:T(8,128)(2,1)S(1)}, bf16[16,256]{1,0:T(8,128)(2,1)}, u32[]{:S(2)}) copy-start(bf16[16,256]{1,0:T(8,128)(2,1)} %vir_ref.3) | copy-start | bytes 24580
  0.0 22.2 %copy-start.10 = (bf16[16,256]{1,0:T(8,128)(2,1)S(1)}, bf16[16,256]{1,0:T(8,128)(2,1)}, u32[]{:S(2)}) copy-start(bf16[16,256]{1,0:T(8,128)(2,1)} %occ_ref.3) | copy-start | bytes 24580
  3.1 12.8 %collective-permute-start = (bf16[34,16,256]{2,1,0:T(8,128)(2,1)}, bf16[34,16,256]{2,1,0:T(8,128)(2,1)S(1)}, u32[]{:S(2)}, u32[]{:S(2)}) collective-permute-start(bf16[34,16,256]{2,1,0:T(8,128)(2,1)} %get-tuple-element.47), channel_id=1, source_target_pairs={{0,4},{1,5},{2,6},{3,7},{4,8},{5,9},{6,10},{7,11},{8,12},{9,13},{1... | collective-permute-start | bytes 835592 | tf_op jit(solution)/shard_map/ppermute | solution.py:210
  6.2 13.7 %collective-permute-start.7 = (bf16[32,16,256]{2,1,0:T(8,128)(2,1)}, bf16[32,16,256]{2,1,0:T(8,128)(2,1)S(1)}, u32[]{:S(2)}, u32[]{:S(2)}) collective-permute-start(bf16[32,16,256]{2,1,0:T(8,128)(2,1)} %get-tuple-element.55), channel_id=1, source_target_pairs={{0,5},{1,4},{2,7},{3,6},{4,9},{5,8},{6,11},{7,10},{8,13},{9,12},{1... | collective-permute-start | bytes 786440 | tf_op jit(solution)/shard_map/ppermute | solution.py:210
  15.9 18.2 %collective-permute-start.1 = (bf16[32,16,256]{2,1,0:T(8,128)(2,1)}, bf16[32,16,256]{2,1,0:T(8,128)(2,1)S(1)}, u32[]{:S(2)}, u32[]{:S(2)}) collective-permute-start(bf16[32,16,256]{2,1,0:T(8,128)(2,1)} %get-tuple-element.51), channel_id=1, source_target_pairs={{0,6},{1,7},{2,4},{3,5},{4,10},{5,11},{6,8},{7,9},{8,14},{9,15},{1... | collective-permute-start | bytes 786440 | tf_op jit(solution)/shard_map/ppermute | solution.py:210
  19.8 15.7 %collective-permute-start.11 = (bf16[32,16,256]{2,1,0:T(8,128)(2,1)}, bf16[32,16,256]{2,1,0:T(8,128)(2,1)S(1)}, u32[]{:S(2)}, u32[]{:S(2)}) collective-permute-start(bf16[32,16,256]{2,1,0:T(8,128)(2,1)} %get-tuple-element.64), channel_id=1, source_target_pairs={{0,7},{1,6},{2,5},{3,4},{4,11},{5,10},{6,9},{7,8},{8,15},{9,14},{1... | collective-permute-start | bytes 786440 | tf_op jit(solution)/shard_map/ppermute | solution.py:210
  22.2 46.9 %collective-permute-start.3 = (bf16[2,16,256]{2,1,0:T(8,128)(2,1)S(1)}, bf16[2,16,256]{2,1,0:T(8,128)(2,1)S(1)}, u32[]{:S(2)}, u32[]{:S(2)}) collective-permute-start(bf16[2,16,256]{2,1,0:T(8,128)(2,1)S(1)} %get-tuple-element.86), channel_id=1, source_target_pairs={{0,8},{1,9},{2,10},{3,11},{4,12},{5,13},{6,14},{7,15},{8,0},{9,1},... | collective-permute-start | bytes 49160 | tf_op jit(solution)/shard_map/ppermute | solution.py:210
  29.8 24.2 %all-to-all-start = ((bf16[4,32,16,256]{3,2,1,0:T(8,128)(2,1)}), bf16[4,32,16,256]{3,2,1,0:T(8,128)(2,1)}, u32[]{:S(2)}, u32[]{:S(2)}) async-start(bf16[4,32,16,256]{3,2,1,0:T(8,128)(2,1)} %get-tuple-element.56), calls=%async_computation | async-start | bytes 2097152 | tf_op jit(solution)/shard_map/all_to_all | solution.py:201
  34.1 70.2 %copy-start = (bf16[64,16,256]{2,1,0:T(8,128)(2,1)S(1)}, bf16[64,16,256]{2,1,0:T(8,128)(2,1)}, u32[]{:S(2)}) copy-start(bf16[64,16,256]{2,1,0:T(8,128)(2,1)} %get-tuple-element.53.rest_0_) | copy-start | bytes 1572868
  34.1 70.2 %copy-start.7 = (s32[16,4,4]{0,2,1:T(4,128)S(1)}, s32[16,4,4]{0,2,1:T(4,128)}, u32[]{:S(2)}) copy-start(s32[16,4,4]{0,2,1:T(4,128)} %param.8) | copy-start | bytes 3076
  34.1 70.2 %copy-start.8 = (s32[16]{0:T(128)S(1)}, s32[16]{0:T(128)}, u32[]{:S(2)}) copy-start(s32[16]{0:T(128)} %order_ref.5) | copy-start | bytes 196
  34.1 19.3 %copy-start.1 = (bf16[32,16,256]{2,1,0:T(8,128)(2,1)}, bf16[32,16,256]{2,1,0:T(8,128)(2,1)S(1)}, u32[]{:S(2)}) copy-start(bf16[32,16,256]{2,1,0:T(8,128)(2,1)S(1)} %collective-permute-done.1.rest_8_.rest_11_) | copy-start | bytes 786436
  34.1 9.7 %collective-permute-start.2 = (bf16[34,16,256]{2,1,0:T(8,128)(2,1)}, bf16[34,16,256]{2,1,0:T(8,128)(2,1)S(1)}, u32[]{:S(2)}, u32[]{:S(2)}) collective-permute-start(bf16[34,16,256]{2,1,0:T(8,128)(2,1)} %get-tuple-element.52), channel_id=1, source_target_pairs={{0,12},{1,13},{2,14},{3,15},{4,0},{5,1},{6,2},{7,3},{8,4},{9,5},{1... | collective-permute-start | bytes 835592 | tf_op jit(solution)/shard_map/ppermute | solution.py:210
  35.5 17.8 %copy-start.3 = (bf16[32,16,256]{2,1,0:T(8,128)(2,1)}, bf16[32,16,256]{2,1,0:T(8,128)(2,1)S(1)}, u32[]{:S(2)}) copy-start(bf16[32,16,256]{2,1,0:T(8,128)(2,1)S(1)} %collective-permute-done.11.rest_11_.rest_14_) | copy-start | bytes 786436
  35.6 13.0 %collective-permute-start.12 = (bf16[32,16,256]{2,1,0:T(8,128)(2,1)}, bf16[32,16,256]{2,1,0:T(8,128)(2,1)S(1)}, u32[]{:S(2)}, u32[]{:S(2)}) collective-permute-start(bf16[32,16,256]{2,1,0:T(8,128)(2,1)} %get-tuple-element.65), channel_id=1, source_target_pairs={{0,13},{1,12},{2,15},{3,14},{4,1},{5,0},{6,3},{7,2},{8,5},{9,4},{1... | collective-permute-start | bytes 786440 | tf_op jit(solution)/shard_map/ppermute | solution.py:210
  43.8 9.5 %collective-permute-start.10 = (bf16[64,16,256]{2,1,0:T(8,128)(2,1)}, bf16[64,16,256]{2,1,0:T(8,128)(2,1)S(1)}, u32[]{:S(2)}, u32[]{:S(2)}) collective-permute-start(bf16[64,16,256]{2,1,0:T(8,128)(2,1)} %get-tuple-element.61), channel_id=1, source_target_pairs={{0,1},{1,0},{2,3},{3,2},{4,5},{5,4},{6,7},{7,6},{8,9},{9,8},{10,11... | collective-permute-start | bytes 1572872 | tf_op jit(solution)/shard_map/ppermute | solution.py:210
  44.9 68.9 %collective-permute-start.16 = (bf16[4,32,16,256]{3,2,1,0:T(8,128)(2,1)}, bf16[4,32,16,256]{3,2,1,0:T(8,128)(2,1)S(1)}, u32[]{:S(2)}, u32[]{:S(2)}) collective-permute-start(bf16[4,32,16,256]{3,2,1,0:T(8,128)(2,1)} %pad_maximum_fusion), channel_id=1, source_target_pairs={{0,16},{16,0},{1,17},{17,1},{2,18},{18,2},{3,19},{19,3},{4,20},{20... | collective-permute-start | bytes 3145736 | tf_op jit(solution)/shard_map/ppermute | solution.py:213
  48.5 4.9 %copy-start.5 = (bf16[32,16,256]{2,1,0:T(8,128)(2,1)}, bf16[32,16,256]{2,1,0:T(8,128)(2,1)S(1)}, u32[]{:S(2)}) copy-start(bf16[32,16,256]{2,1,0:T(8,128)(2,1)S(1)} %collective-permute-done.12.rest_6_.rest_9_) | copy-start | bytes 786436
  48.5 17.6 %collective-permute-start.15 = (bf16[32,16,256]{2,1,0:T(8,128)(2,1)}, bf16[32,16,256]{2,1,0:T(8,128)(2,1)}, u32[]{:S(2)}, u32[]{:S(2)}) collective-permute-start(bf16[32,16,256]{2,1,0:T(8,128)(2,1)} %get-tuple-element.71), channel_id=1, source_target_pairs={{0,15},{1,14},{2,13},{3,12},{4,3},{5,2},{6,1},{7,0},{8,7},{9,6},{1... | collective-permute-start | bytes 786440 | tf_op jit(solution)/shard_map/ppermute | solution.py:210
  52.7 11.8 %collective-permute-start.8 = (bf16[32,16,256]{2,1,0:T(8,128)(2,1)}, bf16[32,16,256]{2,1,0:T(8,128)(2,1)}, u32[]{:S(2)}, u32[]{:S(2)}) collective-permute-start(bf16[32,16,256]{2,1,0:T(8,128)(2,1)} %get-tuple-element.58), channel_id=1, source_target_pairs={{0,14},{1,15},{2,12},{3,13},{4,2},{5,3},{6,0},{7,1},{8,6},{9,7},{1... | collective-permute-start | bytes 786440 | tf_op jit(solution)/shard_map/ppermute | solution.py:210
  53.4 21.8 %collective-permute-start.13 = (bf16[64,16,256]{2,1,0:T(8,128)(2,1)}, bf16[64,16,256]{2,1,0:T(8,128)(2,1)S(1)}, u32[]{:S(2)}, u32[]{:S(2)}) collective-permute-start(bf16[64,16,256]{2,1,0:T(8,128)(2,1)} %get-tuple-element.67), channel_id=1, source_target_pairs={{0,2},{1,3},{2,0},{3,1},{4,6},{5,7},{6,4},{7,5},{8,10},{9,11},{10,... | collective-permute-start | bytes 1572872 | tf_op jit(solution)/shard_map/ppermute | solution.py:210
  54.0 22.5 %copy-start.11 = (bf16[64,16,256]{2,1,0:T(8,128)(2,1)S(1)}, bf16[64,16,256]{2,1,0:T(8,128)(2,1)}, u32[]{:S(2)}) copy-start(bf16[64,16,256]{2,1,0:T(8,128)(2,1)} %get-tuple-element.69) | copy-start | bytes 1572868
  54.0 50.3 %copy-start.2 = (bf16[32,16,256]{2,1,0:T(8,128)(2,1)S(1)}, bf16[32,16,256]{2,1,0:T(8,128)(2,1)}, u32[]{:S(2)}) copy-start(bf16[32,16,256]{2,1,0:T(8,128)(2,1)} %copy-done.1) | copy-start | bytes 786436
  54.0 50.4 %copy-start.4 = (bf16[32,16,256]{2,1,0:T(8,128)(2,1)S(1)}, bf16[32,16,256]{2,1,0:T(8,128)(2,1)}, u32[]{:S(2)}) copy-start(bf16[32,16,256]{2,1,0:T(8,128)(2,1)} %copy-done.3) | copy-start | bytes 786436
  54.0 50.4 %copy-start.6 = (bf16[32,16,256]{2,1,0:T(8,128)(2,1)S(1)}, bf16[32,16,256]{2,1,0:T(8,128)(2,1)}, u32[]{:S(2)}) copy-start(bf16[32,16,256]{2,1,0:T(8,128)(2,1)} %copy-done.5) | copy-start | bytes 786436
  64.5 38.2 %collective-permute-start.9 = (bf16[4,16,16,256]{3,2,1,0:T(8,128)(2,1)S(1)}, bf16[4,16,16,256]{3,2,1,0:T(8,128)(2,1)S(1)}, u32[]{:S(2)}, u32[]{:S(2)}) collective-permute-start(bf16[4,16,16,256]{3,2,1,0:T(8,128)(2,1)S(1)} %get-tuple-element.59), channel_id=1, source_target_pairs={{0,8},{1,9},{2,10},{3,11},{4,12},{5,13},{6,14},{7,15},{8,0},{9,1},... | collective-permute-start | bytes 1572872 | tf_op jit(solution)/shard_map/ppermute | solution.py:210
  67.4 46.4 %collective-permute-start.17 = (bf16[4,32,16,256]{3,2,1,0:T(8,128)(2,1)S(1)}, bf16[4,32,16,256]{3,2,1,0:T(8,128)(2,1)S(1)}, u32[]{:S(2)}, u32[]{:S(2)}) collective-permute-start(bf16[4,32,16,256]{3,2,1,0:T(8,128)(2,1)S(1)} %pad_maximum_fusion.1), channel_id=1, source_target_pairs={{0,16},{16,0},{1,17},{17,1},{2,18},{18,2},{3,19},{19,3},{4,20},{20... | collective-permute-start | bytes 3145736 | tf_op jit(solution)/shard_map/ppermute | solution.py:213
  69.1 7.4 %collective-permute-start.6 = (bf16[4,2,16,256]{3,2,1,0:T(8,128)(2,1)S(1)}, bf16[4,2,16,256]{3,2,1,0:T(8,128)(2,1)S(1)}, u32[]{:S(2)}, u32[]{:S(2)}) collective-permute-start(bf16[4,2,16,256]{3,2,1,0:T(8,128)(2,1)S(1)} %get-tuple-element.84), channel_id=1, source_target_pairs={{0,3},{1,2},{2,1},{3,0},{4,7},{5,6},{6,5},{7,4},{8,11},{9,10},{10,... | collective-permute-start | bytes 196616 | tf_op jit(solution)/shard_map/ppermute | solution.py:210
  75.2 4.3 %collective-permute-start.5 = (bf16[4,2,16,256]{3,2,1,0:T(8,128)(2,1)S(1)}, bf16[4,2,16,256]{3,2,1,0:T(8,128)(2,1)S(1)}, u32[]{:S(2)}, u32[]{:S(2)}) collective-permute-start(bf16[4,2,16,256]{3,2,1,0:T(8,128)(2,1)S(1)} %get-tuple-element.84), channel_id=1, source_target_pairs={{0,2},{1,3},{2,0},{3,1},{4,6},{5,7},{6,4},{7,5},{8,10},{9,11},{10,... | collective-permute-start | bytes 196616 | tf_op jit(solution)/shard_map/ppermute | solution.py:210
  76.5 27.8 %collective-permute-start.14 = (bf16[64,16,256]{2,1,0:T(8,128)(2,1)S(1)}, bf16[64,16,256]{2,1,0:T(8,128)(2,1)S(1)}, u32[]{:S(2)}, u32[]{:S(2)}) collective-permute-start(bf16[64,16,256]{2,1,0:T(8,128)(2,1)S(1)} %copy-done.11), channel_id=1, source_target_pairs={{0,3},{1,2},{2,1},{3,0},{4,7},{5,6},{6,5},{7,4},{8,11},{9,10},{10,... | collective-permute-start | bytes 1572872 | tf_op jit(solution)/shard_map/ppermute | solution.py:210
  79.6 1.3 collective-permute-start.4
  80.8 31.5 %collective-permute-start.18 = (bf16[4,16,16,256]{3,2,1,0:T(8,128)(2,1)S(1)}, bf16[4,16,16,256]{3,2,1,0:T(8,128)(2,1)S(1)}, u32[]{:S(2)}, u32[]{:S(2)}) collective-permute-start(bf16[4,16,16,256]{3,2,1,0:T(8,128)(2,1)S(1)} %get-tuple-element.76), channel_id=1, source_target_pairs={{0,8},{1,9},{2,10},{3,11},{4,12},{5,13},{6,14},{7,15},{8,0},{9,1},... | collective-permute-start | bytes 1572872 | tf_op jit(solution)/shard_map/ppermute | solution.py:210
  102.7 11.1 %collective-permute-start.19 = (bf16[4,16,16,256]{3,2,1,0:T(8,128)(2,1)S(1)}, bf16[4,16,16,256]{3,2,1,0:T(8,128)(2,1)S(1)}, u32[]{:S(2)}, u32[]{:S(2)}) collective-permute-start(bf16[4,16,16,256]{3,2,1,0:T(8,128)(2,1)S(1)} %collective-permute-done.9.rest_3_), channel_id=1, source_target_pairs={{0,16},{16,0},{1,17},{17,1},{2,18},{18,2},{3,19},{19,3},{4,20},{20... | collective-permute-start | bytes 1572872 | tf_op jit(solution)/shard_map/ppermute | solution.py:213
  112.3 12.3 %collective-permute-start.20 = (bf16[4,16,16,256]{3,2,1,0:T(8,128)(2,1)S(1)}, bf16[4,16,16,256]{3,2,1,0:T(8,128)(2,1)S(1)}, u32[]{:S(2)}, u32[]{:S(2)}) collective-permute-start(bf16[4,16,16,256]{3,2,1,0:T(8,128)(2,1)S(1)} %collective-permute-done.18.rest_5_), channel_id=1, source_target_pairs={{0,16},{16,0},{1,17},{17,1},{2,18},{18,2},{3,19},{19,3},{4,20},{20... | collective-permute-start | bytes 1572872 | tf_op jit(solution)/shard_map/ppermute | solution.py:213

commit v7 on v6

--- a/solution.py
+++ b/solution.py
@@ -246,7 +246,7 @@
     came, swapped = [], []
     for n, piece in enumerate(direct):
         if n >= WINDOW:
-            piece = after(piece, came[n - WINDOW])
+            piece = after(piece, (came[n - WINDOW], to_last) if n == WINDOW else came[n - WINDOW])
         came.append(shift(piece, order[n // PLANE], n % PLANE))
     ready = inplane(after(to_last, came[1]))
     low = shift(after(ready[:, :quarter], came[-2]), last)

time: 131 us -> 126 us (0.962)
  waiting for transfers between devices: 69.6 us -> 63.5 us
    ppermute x17, waiting for transfers between devices: 64.4 us -> 58.3 us  [shift(): return lax.ppermute(x, 'wide', pairs)]
  transfers between devices with their start and end apart: 22 -> 22, of which waited for: 11 -> 13; matrix products, arithmetic and copies ran while one was open for 4% -> 4% of each run, Pallas kernels for 11% -> 11%
where the time goes in v7:
time: 126 us; the launch traced here: 125 us
  waiting for transfers between devices  63.5 us (50%)
  starting transfers between devices  33.8 us (27%)
  Pallas kernels  23.1 us (18%)
  other arithmetic  2.48 us (2%)
  local copies, waits for them, and re-layouts  2.18 us (2%)
    ppermute x17, waiting for transfers between devices, shift(): return lax.ppermute(x, 'wide', pairs)  58.3 us
    ppermute x17, starting transfers between devices, shift(): return lax.ppermute(x, 'wide', pairs)  23.4 us
    pallas_call x2, Pallas kernels, gather(): pl.pallas_call(functools.partial(gather_kernel, plan, tails, outer, half,...  7.84 us
    ppermute x4, starting transfers between devices, swap(): return lax.ppermute(x, 'groups', [(0, 1), (1, 0)])  6.14 us
    pallas_call x1, Pallas kernels, shards(): pl.pallas_call(functools.partial(back_kernel, rows_of, len(arrays)), out_...  5.83 us
    pallas_call x1, Pallas kernels, shards(): pl.pallas_call(functools.partial(middle_kernel, rows_of, len(arrays)), ou...  5.54 us
    ppermute x4, waiting for transfers between devices, swap(): return lax.ppermute(x, 'groups', [(0, 1), (1, 0)])  5.18 us
    all_to_all x1, starting transfers between devices, inplane(): lax.all_to_all(x, 'wide', split_axis=0, concat_axis=0, tiled=True, axis_i...  4.25 us
  transfers between devices with their start and end apart: 22, of which 13 were waited for; matrix products, arithmetic and copies ran while one was open for 4% of the time, Pallas kernels for 11%

profile of v7, /device:TPU:0, one launch (start us, length us, event | category | flops | bytes accessed | tf_op | source)
XLA Modules:
  0.0 125.3 jit_solution(6306522186314400628)
XLA Ops:
  0.0 2.9 %shard_map.55 = (bf16[34,16,256]{2,1,0:T(8,128)(2,1)}, bf16[32,16,256]{2,1,0:T(8,128)(2,1)}, bf16[32,16,256]{2,1,0:T(8,128)(2,1)}, bf16[32,16,256]{2,1,0:T(8,128)(2,1)}) custom-call(s32[16]{0:T(128)} %order_ref.5, bf16[16,64,16,256]{3,2,1,0:T(8,128)(2,1)} %bitcast.33, bf16[16,256]{1,0:T(8,128)(2,1)} %occ_ref.3, bf16[16,256]{1,0:T(8,128)(2,1)} %vir_ref.3), custom_call_target="tpu_custom_call" | custom-call | bytes 2129920 | tf_op jit(solution)/shard_map/pallas_call | solution.py:49
  2.9 0.0 copy-start.9
  2.9 0.0 copy-start.10
  3.0 3.1 %collective-permute-start = (bf16[34,16,256]{2,1,0:T(8,128)(2,1)}, bf16[34,16,256]{2,1,0:T(8,128)(2,1)S(1)}, u32[]{:S(2)}, u32[]{:S(2)}) collective-permute-start(bf16[34,16,256]{2,1,0:T(8,128)(2,1)} %get-tuple-element.47), channel_id=1, source_target_pairs={{0,4},{1,5},{2,6},{3,7},{4,8},{5,9},{6,10},{7,11},{8,12},{9,13},{1... | collective-permute-start | bytes 835592 | tf_op jit(solution)/shard_map/ppermute | solution.py:210
  6.0 0.7 collective-permute-start.7
  6.8 4.9 %shard_map.56 = (bf16[34,16,256]{2,1,0:T(8,128)(2,1)}, bf16[32,16,256]{2,1,0:T(8,128)(2,1)}, bf16[32,16,256]{2,1,0:T(8,128)(2,1)}, bf16[32,16,256]{2,1,0:T(8,128...) custom-call(s32[16]{0:T(128)} %order_ref.5, ...), custom_call_target="tpu_custom_call" | custom-call | bytes 8421376 | tf_op jit(solution)/shard_map/pallas_call | solution.py:49
  11.7 4.0 %collective-permute-done.rest_1_ = bf16[34,16,256]{2,1,0:T(8,128)(2,1)S(1)} collective-permute-done((bf16[34,16,256]{2,1,0:T(8,128)(2,1)}, bf16[34,16,256]{2,1,0:T(8,128)(2,1)S(1)}, u32[]{:S(2)}, u32[]{:S(2)}) %collective-permute-start) | collective-permute-done | bytes 278560 | tf_op jit(solution)/shard_map/ppermute | solution.py:210
  15.8 1.0 collective-permute-start.1
  16.7 3.0 %collective-permute-done.7.rest_5_.rest_8_ = bf16[32,16,256]{2,1,0:T(8,128)(2,1)S(1)} collective-permute-done((bf16[32,16,256]{2,1,0:T(8,128)(2,1)}, bf16[32,16,256]{2,1,0:T(8,128)(2,1)S(1)}, u32[]{:S(2)}, u32[]{:S(2)}) %collective-permute-start.7) | collective-permute-done | bytes 262176 | tf_op jit(solution)/shard_map/ppermute | solution.py:210
  19.7 2.3 %collective-permute-start.11 = (bf16[32,16,256]{2,1,0:T(8,128)(2,1)S(1)}, bf16[32,16,256]{2,1,0:T(8,128)(2,1)S(1)}, u32[]{:S(2)}, u32[]{:S(2)}) collective-permute-start(bf16[32,16,256]{2,1,0:T(8,128)(2,1)S(1)} %copy-done.12), channel_id=1, source_target_pairs={{0,7},{1,6},{2,5},{3,4},{4,11},{5,10},{6,9},{7,8},{8,15},{9,14},{1... | collective-permute-start | bytes 786440 | tf_op jit(solution)/shard_map/ppermute | solution.py:210
  22.1 2.7 %collective-permute-start.3 = (bf16[2,16,256]{2,1,0:T(8,128)(2,1)S(1)}, bf16[2,16,256]{2,1,0:T(8,128)(2,1)S(1)}, u32[]{:S(2)}, u32[]{:S(2)}) collective-permute-start(bf16[2,16,256]{2,1,0:T(8,128)(2,1)S(1)} %get-tuple-element.86), channel_id=1, source_target_pairs={{0,8},{1,9},{2,10},{3,11},{4,12},{5,13},{6,14},{7,15},{8,0},{9,1},... | collective-permute-start | bytes 49160 | tf_op jit(solution)/shard_map/ppermute | solution.py:210
  24.7 4.2 %all-to-all-start = ((bf16[4,32,16,256]{3,2,1,0:T(8,128)(2,1)}), bf16[4,32,16,256]{3,2,1,0:T(8,128)(2,1)}, u32[]{:S(2)}, u32[]{:S(2)}) async-start(bf16[4,32,16,256]{3,2,1,0:T(8,128)(2,1)} %get-tuple-element.56), calls=%async_computation | async-start | bytes 2097152 | tf_op jit(solution)/shard_map/all_to_all | solution.py:201
  29.0 0.0 copy-start.7
  29.0 0.0 copy-start.8
  29.0 0.0 collective-permute-done.1.rest_8_.rest_11_
  29.0 1.4 %collective-permute-start.2 = (bf16[34,16,256]{2,1,0:T(8,128)(2,1)}, bf16[34,16,256]{2,1,0:T(8,128)(2,1)S(1)}, u32[]{:S(2)}, u32[]{:S(2)}) collective-permute-start(bf16[34,16,256]{2,1,0:T(8,128)(2,1)} %get-tuple-element.53), channel_id=1, source_target_pairs={{0,12},{1,13},{2,14},{3,15},{4,0},{5,1},{6,2},{7,3},{8,4},{9,5},{1... | collective-permute-start | bytes 835592 | tf_op jit(solution)/shard_map/ppermute | solution.py:210
  30.5 1.3 %collective-permute-done.11.rest_11_.rest_14_ = bf16[32,16,256]{2,1,0:T(8,128)(2,1)S(1)} collective-permute-done((bf16[32,16,256]{2,1,0:T(8,128)(2,1)S(1)}, bf16[32,16,256]{2,1,0:T(8,128)(2,1)S(1)}, u32[]{:S(2)}, u32[]{:S(2)}) %collective-permute-start.11) | collective-permute-done | bytes 262176 | tf_op jit(solution)/shard_map/ppermute | solution.py:210
  31.7 2.4 %collective-permute-start.12 = (bf16[32,16,256]{2,1,0:T(8,128)(2,1)}, bf16[32,16,256]{2,1,0:T(8,128)(2,1)S(1)}, u32[]{:S(2)}, u32[]{:S(2)}) collective-permute-start(bf16[32,16,256]{2,1,0:T(8,128)(2,1)} %get-tuple-element.65), channel_id=1, source_target_pairs={{0,13},{1,12},{2,15},{3,14},{4,1},{5,0},{6,3},{7,2},{8,5},{9,4},{1... | collective-permute-start | bytes 786440 | tf_op jit(solution)/shard_map/ppermute | solution.py:210
  34.2 4.6 %collective-permute-done.2.rest_2_.rest_3_ = bf16[34,16,256]{2,1,0:T(8,128)(2,1)S(1)} collective-permute-done((bf16[34,16,256]{2,1,0:T(8,128)(2,1)}, bf16[34,16,256]{2,1,0:T(8,128)(2,1)S(1)}, u32[]{:S(2)}, u32[]{:S(2)}) %collective-permute-start.2) | collective-permute-done | bytes 278560 | tf_op jit(solution)/shard_map/ppermute | solution.py:210
  38.8 0.0 collective-permute-start.10
  38.8 1.1 pad_maximum_fusion
  39.9 1.5 %collective-permute-start.16 = (bf16[4,32,16,256]{3,2,1,0:T(8,128)(2,1)}, bf16[4,32,16,256]{3,2,1,0:T(8,128)(2,1)S(1)}, u32[]{:S(2)}, u32[]{:S(2)}) collective-permute-start(bf16[4,32,16,256]{3,2,1,0:T(8,128)(2,1)} %pad_maximum_fusion), channel_id=1, source_target_pairs={{0,16},{16,0},{1,17},{17,1},{2,18},{18,2},{3,19},{19,3},{4,20},{20... | collective-permute-start | bytes 3145736 | tf_op jit(solution)/shard_map/ppermute | solution.py:213
  41.4 2.4 %collective-permute-done.12.rest_6_.rest_9_ = bf16[32,16,256]{2,1,0:T(8,128)(2,1)S(1)} collective-permute-done((bf16[32,16,256]{2,1,0:T(8,128)(2,1)}, bf16[32,16,256]{2,1,0:T(8,128)(2,1)S(1)}, u32[]{:S(2)}, u32[]{:S(2)}) %collective-permute-start.12) | collective-permute-done | bytes 262176 | tf_op jit(solution)/shard_map/ppermute | solution.py:210
  43.8 3.8 %collective-permute-start.15 = (bf16[32,16,256]{2,1,0:T(8,128)(2,1)}, bf16[32,16,256]{2,1,0:T(8,128)(2,1)}, u32[]{:S(2)}, u32[]{:S(2)}) collective-permute-start(bf16[32,16,256]{2,1,0:T(8,128)(2,1)} %get-tuple-element.71), channel_id=1, source_target_pairs={{0,15},{1,14},{2,13},{3,12},{4,3},{5,2},{6,1},{7,0},{8,7},{9,6},{1... | collective-permute-start | bytes 786440 | tf_op jit(solution)/shard_map/ppermute | solution.py:210
  47.6 0.7 slice_bitcast_fusion
  48.3 0.6 collective-permute-start.13
  48.9 1.4 %fusion.2 = (bf16[4,16,16,256]{3,2,1,0:T(8,128)(2,1)S(1)}, bf16[4,16,16,256]{3,2,1,0:T(8,128)(2,1)S(1)}) fusion(bf16[4,32,16,256]{3,2,1,0:T(8,128)(2,1)} %all-to-all-done), kind=kLoop, calls=%fused_computation.11 | loop fusion | bytes 2097152 | tf_op jit(solution)/shard_map/slice | solution.py:253
  50.3 9.1 %collective-permute-done.8.rest_9_.rest_12_ = bf16[32,16,256]{2,1,0:T(8,128)(2,1)} collective-permute-done((bf16[32,16,256]{2,1,0:T(8,128)(2,1)}, bf16[32,16,256]{2,1,0:T(8,128)(2,1)}, u32[]{:S(2)}, u32[]{:S(2)}) %collective-permute-start.8) | collective-permute-done | bytes 262176 | tf_op jit(solution)/shard_map/ppermute | solution.py:210
  59.4 1.6 %collective-permute-start.9 = (bf16[4,16,16,256]{3,2,1,0:T(8,128)(2,1)S(1)}, bf16[4,16,16,256]{3,2,1,0:T(8,128)(2,1)S(1)}, u32[]{:S(2)}, u32[]{:S(2)}) collective-permute-start(bf16[4,16,16,256]{3,2,1,0:T(8,128)(2,1)S(1)} %get-tuple-element.59), channel_id=1, source_target_pairs={{0,8},{1,9},{2,10},{3,11},{4,12},{5,13},{6,14},{7,15},{8,0},{9,1},... | collective-permute-start | bytes 1572872 | tf_op jit(solution)/shard_map/ppermute | solution.py:210
  61.0 0.0 collective-permute-done.15.rest_12_.rest_15_
  61.1 1.3 %pad_maximum_fusion.1 = bf16[4,32,16,256]{3,2,1,0:T(8,128)(2,1)S(1)} fusion(bf16[1,32,16,256]{3,2,1,0:T(8,128)(2,1)} %bitcast.20, bf16[1,32,16,256]{3,2,1,0:T(8,128)(2,1)} %bitcast.19, bf16[1,32,16,256]{3,2,1,0:T(8,128)(2,1)} %bitcast.31, bf16[1,32,16,256]{3,2,1,0:T(8,128)(2,1)} %slice_bitcast_fusion), kind=kLoop, calls=%fused_computation.1 | loop fusion | flops 1572864 | bytes 2097152 | tf_op jit(solution)/shard_map/stack | solution.py:256
  62.4 1.6 %collective-permute-start.17 = (bf16[4,32,16,256]{3,2,1,0:T(8,128)(2,1)S(1)}, bf16[4,32,16,256]{3,2,1,0:T(8,128)(2,1)S(1)}, u32[]{:S(2)}, u32[]{:S(2)}) collective-permute-start(bf16[4,32,16,256]{3,2,1,0:T(8,128)(2,1)S(1)} %pad_maximum_fusion.1), channel_id=1, source_target_pairs={{0,16},{16,0},{1,17},{17,1},{2,18},{18,2},{3,19},{19,3},{4,20},{20... | collective-permute-start | bytes 3145736 | tf_op jit(solution)/shard_map/ppermute | solution.py:213
  64.0 0.1 collective-permute-start.6
  64.1 6.3 %collective-permute-done.13.rest_7_.rest_10_.rest_4_ = bf16[64,16,256]{2,1,0:T(8,128)(2,1)S(1)} collective-permute-done((bf16[64,16,256]{2,1,0:T(8,128)(2,1)}, bf16[64,16,256]{2,1,0:T(8,128)(2,1)S(1)}, u32[]{:S(2)}, u32[]{:S(2)}) %collective-permute-start.13) | collective-permute-done | bytes 524320 | tf_op jit(solution)/shard_map/ppermute | solution.py:210
  70.4 1.0 collective-permute-start.5
  71.4 0.3 collective-permute-done.6
  71.7 0.8 collective-permute-start.14
  72.5 2.2 %collective-permute-done.5 = bf16[4,2,16,256]{3,2,1,0:T(8,128)(2,1)S(1)} collective-permute-done((bf16[4,2,16,256]{3,2,1,0:T(8,128)(2,1)S(1)}, bf16[4,2,16,256]{3,2,1,0:T(8,128)(2,1)S(1)}, u32[]{:S(2)}, u32[]{:S(2)}) %collective-permute-start.5) | collective-permute-done | bytes 65568 | tf_op jit(solution)/shard_map/ppermute | solution.py:210
  74.7 1.3 collective-permute-done.4
  76.0 1.8 %collective-permute-start.18 = (bf16[4,16,16,256]{3,2,1,0:T(8,128)(2,1)S(1)}, bf16[4,16,16,256]{3,2,1,0:T(8,128)(2,1)S(1)}, u32[]{:S(2)}, u32[]{:S(2)}) collective-permute-start(bf16[4,16,16,256]{3,2,1,0:T(8,128)(2,1)S(1)} %get-tuple-element.76), channel_id=1, source_target_pairs={{0,8},{1,9},{2,10},{3,11},{4,12},{5,13},{6,14},{7,15},{8,0},{9,1},... | collective-permute-start | bytes 1572872 | tf_op jit(solution)/shard_map/ppermute | solution.py:210
  77.8 19.8 %collective-permute-done.9.rest_3_ = bf16[4,16,16,256]{3,2,1,0:T(8,128)(2,1)S(1)} collective-permute-done((bf16[4,16,16,256]{3,2,1,0:T(8,128)(2,1)S(1)}, bf16[4,16,16,256]{3,2,1,0:T(8,128)(2,1)S(1)}, u32[]{:S(2)}, u32[]{:S(2)}) %collective-permute-start.9) | collective-permute-done | bytes 524320 | tf_op jit(solution)/shard_map/ppermute | solution.py:210
  97.7 1.5 %collective-permute-start.19 = (bf16[4,16,16,256]{3,2,1,0:T(8,128)(2,1)S(1)}, bf16[4,16,16,256]{3,2,1,0:T(8,128)(2,1)S(1)}, u32[]{:S(2)}, u32[]{:S(2)}) collective-permute-start(bf16[4,16,16,256]{3,2,1,0:T(8,128)(2,1)S(1)} %collective-permute-done.9.rest_3_), channel_id=1, source_target_pairs={{0,16},{16,0},{1,17},{17,1},{2,18},{18,2},{3,19},{19,3},{4,20},{20... | collective-permute-start | bytes 1572872 | tf_op jit(solution)/shard_map/ppermute | solution.py:213
  99.3 3.9 %shard_map.57 = (bf16[256,16,256]{2,1,0:T(8,128)(2,1)S(1)}, bf16[256,16,256]{2,1,0:T(8,128)(2,1)S(1)}, bf16[256,256]{1,0:T(8,128)(2,1)S(1)}, bf16[256,256]{1,0:T(8,128)(2,1)S(1)}, bf16[256,256]{1,0:T(8,128)(2,1)S(1)}) custom-call(s32[16]{0:T(128)S(1)} %copy-done.8, s32[4,4,16]{2,1,0:T(4,128)S(1)} %bitcast.32, bf16[512,256]{1,0:T(8,128)(2,1)S(1)} %bitcast.27, ...), custom_call_target="tpu_custom_call" | custom-call | flops 1073741824 | bytes 6291456 | tf_op jit(solution)/shard_map/pallas_call | solution.py:318
  103.2 4.0 %collective-permute-done.18.rest_5_ = bf16[4,16,16,256]{3,2,1,0:T(8,128)(2,1)S(1)} collective-permute-done((bf16[4,16,16,256]{3,2,1,0:T(8,128)(2,1)S(1)}, bf16[4,16,16,256]{3,2,1,0:T(8,128)(2,1)S(1)}, u32[]{:S(2)}, u32[]{:S(2)}) %collective-permute-start.18) | collective-permute-done | bytes 524320 | tf_op jit(solution)/shard_map/ppermute | solution.py:210
  107.2 1.5 %collective-permute-start.20 = (bf16[4,16,16,256]{3,2,1,0:T(8,128)(2,1)S(1)}, bf16[4,16,16,256]{3,2,1,0:T(8,128)(2,1)S(1)}, u32[]{:S(2)}, u32[]{:S(2)}) collective-permute-start(bf16[4,16,16,256]{3,2,1,0:T(8,128)(2,1)S(1)} %collective-permute-done.18.rest_5_), channel_id=1, source_target_pairs={{0,16},{16,0},{1,17},{17,1},{2,18},{18,2},{3,19},{19,3},{4,20},{20... | collective-permute-start | bytes 1572872 | tf_op jit(solution)/shard_map/ppermute | solution.py:213
  108.7 5.5 %shard_map.58 = (bf16[256,32,256]{2,1,0:T(8,128)(2,1)S(1)}, bf16[256,32,256]{2,1,0:T(8,128)(2,1)S(1)}) custom-call(bf16[256,256]{1,0:T(8,128)(2,1)S(1)} %get-tuple-element.72.occ_ref, bf16[256,256]{1,0:T(8,128)(2,1)S(1)} %get-tuple-element.73.vir_ref, bf16[256,256]{1,0:T(8,128)(2,1)S(1)} %get-tuple-element.74.keep_ref, bf16[64,16,256]{2,1,0:T(8,128)(2,1)S(1)} %copy-done, ...), custom_call_target="tpu_custom_call" | custom-call | flops 2147483648 | bytes 12582912 | tf_op jit(solution)/shard_map/pallas_call | solution.py:330
  114.3 5.2 %collective-permute-done.20.rest_6_ = bf16[4,16,16,256]{3,2,1,0:T(8,128)(2,1)S(1)} collective-permute-done((bf16[4,16,16,256]{3,2,1,0:T(8,128)(2,1)S(1)}, bf16[4,16,16,256]{3,2,1,0:T(8,128)(2,1)S(1)}, u32[]{:S(2)}, u32[]{:S(2)}) %collective-permute-start.20) | collective-permute-done | bytes 524320 | tf_op jit(solution)/shard_map/ppermute | solution.py:213
  119.5 5.8 %shard_map.59 = f32[64,64]{1,0:T(8,128)} custom-call(bf16[256,256]{1,0:T(8,128)(2,1)S(1)} %get-tuple-element.72.occ_ref, bf16[256,256]{1,0:T(8,128)(2,1)S(1)} %get-tuple-element.73.vir_ref, bf16[256,256]{1,0:T(8,128)(2,1)S(1)} %get-tuple-element.74.keep_ref, bf16[256,16,256]{2,1,0:T(8,128)(2,1)S(1)} %get-tuple-element.75.mask_a, ...), custom_call_target="tpu_custom_call" | custom-call | flops 1073741824 | bytes 16777216 | tf_op jit(solution)/shard_map/pallas_call | solution.py:340
  (39 shorter events, 0.1 us)
Async XLA Ops:
  2.9 12.8 %copy-start.13 = (bf16[32,16,256]{2,1,0:T(8,128)(2,1)S(1)}, bf16[32,16,256]{2,1,0:T(8,128)(2,1)}, u32[]{:S(2)}) copy-start(bf16[32,16,256]{2,1,0:T(8,128)(2,1)} %get-tuple-element.52) | copy-start | bytes 786436
  2.9 16.8 %copy-start.12 = (bf16[32,16,256]{2,1,0:T(8,128)(2,1)S(1)}, bf16[32,16,256]{2,1,0:T(8,128)(2,1)}, u32[]{:S(2)}) copy-start(bf16[32,16,256]{2,1,0:T(8,128)(2,1)} %get-tuple-element.64) | copy-start | bytes 786436
  2.9 19.1 %copy-start.9 = (bf16[16,256]{1,0:T(8,128)(2,1)S(1)}, bf16[16,256]{1,0:T(8,128)(2,1)}, u32[]{:S(2)}) copy-start(bf16[16,256]{1,0:T(8,128)(2,1)} %vir_ref.3) | copy-start | bytes 24580
  2.9 19.1 %copy-start.10 = (bf16[16,256]{1,0:T(8,128)(2,1)S(1)}, bf16[16,256]{1,0:T(8,128)(2,1)}, u32[]{:S(2)}) copy-start(bf16[16,256]{1,0:T(8,128)(2,1)} %occ_ref.3) | copy-start | bytes 24580
  3.0 12.8 %collective-permute-start = (bf16[34,16,256]{2,1,0:T(8,128)(2,1)}, bf16[34,16,256]{2,1,0:T(8,128)(2,1)S(1)}, u32[]{:S(2)}, u32[]{:S(2)}) collective-permute-start(bf16[34,16,256]{2,1,0:T(8,128)(2,1)} %get-tuple-element.47), channel_id=1, source_target_pairs={{0,4},{1,5},{2,6},{3,7},{4,8},{5,9},{6,10},{7,11},{8,12},{9,13},{1... | collective-permute-start | bytes 835592 | tf_op jit(solution)/shard_map/ppermute | solution.py:210
  6.0 13.7 %collective-permute-start.7 = (bf16[32,16,256]{2,1,0:T(8,128)(2,1)}, bf16[32,16,256]{2,1,0:T(8,128)(2,1)S(1)}, u32[]{:S(2)}, u32[]{:S(2)}) collective-permute-start(bf16[32,16,256]{2,1,0:T(8,128)(2,1)} %get-tuple-element.55), channel_id=1, source_target_pairs={{0,5},{1,4},{2,7},{3,6},{4,9},{5,8},{6,11},{7,10},{8,13},{9,12},{1... | collective-permute-start | bytes 786440 | tf_op jit(solution)/shard_map/ppermute | solution.py:210
  15.8 13.3 %collective-permute-start.1 = (bf16[32,16,256]{2,1,0:T(8,128)(2,1)S(1)}, bf16[32,16,256]{2,1,0:T(8,128)(2,1)S(1)}, u32[]{:S(2)}, u32[]{:S(2)}) collective-permute-start(bf16[32,16,256]{2,1,0:T(8,128)(2,1)S(1)} %copy-done.13), channel_id=1, source_target_pairs={{0,6},{1,7},{2,4},{3,5},{4,10},{5,11},{6,8},{7,9},{8,14},{9,15},{1... | collective-permute-start | bytes 786440 | tf_op jit(solution)/shard_map/ppermute | solution.py:210
  19.7 12.0 %collective-permute-start.11 = (bf16[32,16,256]{2,1,0:T(8,128)(2,1)S(1)}, bf16[32,16,256]{2,1,0:T(8,128)(2,1)S(1)}, u32[]{:S(2)}, u32[]{:S(2)}) collective-permute-start(bf16[32,16,256]{2,1,0:T(8,128)(2,1)S(1)} %copy-done.12), channel_id=1, source_target_pairs={{0,7},{1,6},{2,5},{3,4},{4,11},{5,10},{6,9},{7,8},{8,15},{9,14},{1... | collective-permute-start | bytes 786440 | tf_op jit(solution)/shard_map/ppermute | solution.py:210
  22.1 41.9 %collective-permute-start.3 = (bf16[2,16,256]{2,1,0:T(8,128)(2,1)S(1)}, bf16[2,16,256]{2,1,0:T(8,128)(2,1)S(1)}, u32[]{:S(2)}, u32[]{:S(2)}) collective-permute-start(bf16[2,16,256]{2,1,0:T(8,128)(2,1)S(1)} %get-tuple-element.86), channel_id=1, source_target_pairs={{0,8},{1,9},{2,10},{3,11},{4,12},{5,13},{6,14},{7,15},{8,0},{9,1},... | collective-permute-start | bytes 49160 | tf_op jit(solution)/shard_map/ppermute | solution.py:210
  24.7 24.2 %all-to-all-start = ((bf16[4,32,16,256]{3,2,1,0:T(8,128)(2,1)}), bf16[4,32,16,256]{3,2,1,0:T(8,128)(2,1)}, u32[]{:S(2)}, u32[]{:S(2)}) async-start(bf16[4,32,16,256]{3,2,1,0:T(8,128)(2,1)} %get-tuple-element.56), calls=%async_computation | async-start | bytes 2097152 | tf_op jit(solution)/shard_map/all_to_all | solution.py:201
  29.0 70.2 %copy-start = (bf16[64,16,256]{2,1,0:T(8,128)(2,1)S(1)}, bf16[64,16,256]{2,1,0:T(8,128)(2,1)}, u32[]{:S(2)}) copy-start(bf16[64,16,256]{2,1,0:T(8,128)(2,1)} %get-tuple-element.54.rest_0_) | copy-start | bytes 1572868
  29.0 70.2 %copy-start.7 = (s32[16,4,4]{0,2,1:T(4,128)S(1)}, s32[16,4,4]{0,2,1:T(4,128)}, u32[]{:S(2)}) copy-start(s32[16,4,4]{0,2,1:T(4,128)} %param.8) | copy-start | bytes 3076
  29.0 70.2 %copy-start.8 = (s32[16]{0:T(128)S(1)}, s32[16]{0:T(128)}, u32[]{:S(2)}) copy-start(s32[16]{0:T(128)} %order_ref.5) | copy-start | bytes 196
  29.0 19.3 %copy-start.1 = (bf16[32,16,256]{2,1,0:T(8,128)(2,1)}, bf16[32,16,256]{2,1,0:T(8,128)(2,1)S(1)}, u32[]{:S(2)}) copy-start(bf16[32,16,256]{2,1,0:T(8,128)(2,1)S(1)} %collective-permute-done.1.rest_8_.rest_11_) | copy-start | bytes 786436
  29.0 9.7 %collective-permute-start.2 = (bf16[34,16,256]{2,1,0:T(8,128)(2,1)}, bf16[34,16,256]{2,1,0:T(8,128)(2,1)S(1)}, u32[]{:S(2)}, u32[]{:S(2)}) collective-permute-start(bf16[34,16,256]{2,1,0:T(8,128)(2,1)} %get-tuple-element.53), channel_id=1, source_target_pairs={{0,12},{1,13},{2,14},{3,15},{4,0},{5,1},{6,2},{7,3},{8,4},{9,5},{1... | collective-permute-start | bytes 835592 | tf_op jit(solution)/shard_map/ppermute | solution.py:210
  31.7 16.6 %copy-start.3 = (bf16[32,16,256]{2,1,0:T(8,128)(2,1)}, bf16[32,16,256]{2,1,0:T(8,128)(2,1)S(1)}, u32[]{:S(2)}) copy-start(bf16[32,16,256]{2,1,0:T(8,128)(2,1)S(1)} %collective-permute-done.11.rest_11_.rest_14_) | copy-start | bytes 786436
  31.7 12.0 %collective-permute-start.12 = (bf16[32,16,256]{2,1,0:T(8,128)(2,1)}, bf16[32,16,256]{2,1,0:T(8,128)(2,1)S(1)}, u32[]{:S(2)}, u32[]{:S(2)}) collective-permute-start(bf16[32,16,256]{2,1,0:T(8,128)(2,1)} %get-tuple-element.65), channel_id=1, source_target_pairs={{0,13},{1,12},{2,15},{3,14},{4,1},{5,0},{6,3},{7,2},{8,5},{9,4},{1... | collective-permute-start | bytes 786440 | tf_op jit(solution)/shard_map/ppermute | solution.py:210
  38.8 9.6 %collective-permute-start.10 = (bf16[64,16,256]{2,1,0:T(8,128)(2,1)}, bf16[64,16,256]{2,1,0:T(8,128)(2,1)S(1)}, u32[]{:S(2)}, u32[]{:S(2)}) collective-permute-start(bf16[64,16,256]{2,1,0:T(8,128)(2,1)} %get-tuple-element.61), channel_id=1, source_target_pairs={{0,1},{1,0},{2,3},{3,2},{4,5},{5,4},{6,7},{7,6},{8,9},{9,8},{10,11... | collective-permute-start | bytes 1572872 | tf_op jit(solution)/shard_map/ppermute | solution.py:210
  39.9 68.9 %collective-permute-start.16 = (bf16[4,32,16,256]{3,2,1,0:T(8,128)(2,1)}, bf16[4,32,16,256]{3,2,1,0:T(8,128)(2,1)S(1)}, u32[]{:S(2)}, u32[]{:S(2)}) collective-permute-start(bf16[4,32,16,256]{3,2,1,0:T(8,128)(2,1)} %pad_maximum_fusion), channel_id=1, source_target_pairs={{0,16},{16,0},{1,17},{17,1},{2,18},{18,2},{3,19},{19,3},{4,20},{20... | collective-permute-start | bytes 3145736 | tf_op jit(solution)/shard_map/ppermute | solution.py:213
  43.8 4.6 %copy-start.5 = (bf16[32,16,256]{2,1,0:T(8,128)(2,1)}, bf16[32,16,256]{2,1,0:T(8,128)(2,1)S(1)}, u32[]{:S(2)}) copy-start(bf16[32,16,256]{2,1,0:T(8,128)(2,1)S(1)} %collective-permute-done.12.rest_6_.rest_9_) | copy-start | bytes 786436
  43.8 17.3 %collective-permute-start.15 = (bf16[32,16,256]{2,1,0:T(8,128)(2,1)}, bf16[32,16,256]{2,1,0:T(8,128)(2,1)}, u32[]{:S(2)}, u32[]{:S(2)}) collective-permute-start(bf16[32,16,256]{2,1,0:T(8,128)(2,1)} %get-tuple-element.71), channel_id=1, source_target_pairs={{0,15},{1,14},{2,13},{3,12},{4,3},{5,2},{6,1},{7,0},{8,7},{9,6},{1... | collective-permute-start | bytes 786440 | tf_op jit(solution)/shard_map/ppermute | solution.py:210
  47.6 11.8 %collective-permute-start.8 = (bf16[32,16,256]{2,1,0:T(8,128)(2,1)}, bf16[32,16,256]{2,1,0:T(8,128)(2,1)}, u32[]{:S(2)}, u32[]{:S(2)}) collective-permute-start(bf16[32,16,256]{2,1,0:T(8,128)(2,1)} %get-tuple-element.58), channel_id=1, source_target_pairs={{0,14},{1,15},{2,12},{3,13},{4,2},{5,3},{6,0},{7,1},{8,6},{9,7},{1... | collective-permute-start | bytes 786440 | tf_op jit(solution)/shard_map/ppermute | solution.py:210
  48.3 22.1 %collective-permute-start.13 = (bf16[64,16,256]{2,1,0:T(8,128)(2,1)}, bf16[64,16,256]{2,1,0:T(8,128)(2,1)S(1)}, u32[]{:S(2)}, u32[]{:S(2)}) collective-permute-start(bf16[64,16,256]{2,1,0:T(8,128)(2,1)} %get-tuple-element.67), channel_id=1, source_target_pairs={{0,2},{1,3},{2,0},{3,1},{4,6},{5,7},{6,4},{7,5},{8,10},{9,11},{10,... | collective-permute-start | bytes 1572872 | tf_op jit(solution)/shard_map/ppermute | solution.py:210
  48.9 22.7 %copy-start.11 = (bf16[64,16,256]{2,1,0:T(8,128)(2,1)S(1)}, bf16[64,16,256]{2,1,0:T(8,128)(2,1)}, u32[]{:S(2)}) copy-start(bf16[64,16,256]{2,1,0:T(8,128)(2,1)} %get-tuple-element.69) | copy-start | bytes 1572868
  48.9 50.3 %copy-start.2 = (bf16[32,16,256]{2,1,0:T(8,128)(2,1)S(1)}, bf16[32,16,256]{2,1,0:T(8,128)(2,1)}, u32[]{:S(2)}) copy-start(bf16[32,16,256]{2,1,0:T(8,128)(2,1)} %copy-done.1) | copy-start | bytes 786436
  48.9 50.3 %copy-start.4 = (bf16[32,16,256]{2,1,0:T(8,128)(2,1)S(1)}, bf16[32,16,256]{2,1,0:T(8,128)(2,1)}, u32[]{:S(2)}) copy-start(bf16[32,16,256]{2,1,0:T(8,128)(2,1)} %copy-done.3) | copy-start | bytes 786436
  48.9 50.4 %copy-start.6 = (bf16[32,16,256]{2,1,0:T(8,128)(2,1)S(1)}, bf16[32,16,256]{2,1,0:T(8,128)(2,1)}, u32[]{:S(2)}) copy-start(bf16[32,16,256]{2,1,0:T(8,128)(2,1)} %copy-done.5) | copy-start | bytes 786436
  59.4 38.2 %collective-permute-start.9 = (bf16[4,16,16,256]{3,2,1,0:T(8,128)(2,1)S(1)}, bf16[4,16,16,256]{3,2,1,0:T(8,128)(2,1)S(1)}, u32[]{:S(2)}, u32[]{:S(2)}) collective-permute-start(bf16[4,16,16,256]{3,2,1,0:T(8,128)(2,1)S(1)} %get-tuple-element.59), channel_id=1, source_target_pairs={{0,8},{1,9},{2,10},{3,11},{4,12},{5,13},{6,14},{7,15},{8,0},{9,1},... | collective-permute-start | bytes 1572872 | tf_op jit(solution)/shard_map/ppermute | solution.py:210
  62.4 46.4 %collective-permute-start.17 = (bf16[4,32,16,256]{3,2,1,0:T(8,128)(2,1)S(1)}, bf16[4,32,16,256]{3,2,1,0:T(8,128)(2,1)S(1)}, u32[]{:S(2)}, u32[]{:S(2)}) collective-permute-start(bf16[4,32,16,256]{3,2,1,0:T(8,128)(2,1)S(1)} %pad_maximum_fusion.1), channel_id=1, source_target_pairs={{0,16},{16,0},{1,17},{17,1},{2,18},{18,2},{3,19},{19,3},{4,20},{20... | collective-permute-start | bytes 3145736 | tf_op jit(solution)/shard_map/ppermute | solution.py:213
  64.0 7.7 %collective-permute-start.6 = (bf16[4,2,16,256]{3,2,1,0:T(8,128)(2,1)S(1)}, bf16[4,2,16,256]{3,2,1,0:T(8,128)(2,1)S(1)}, u32[]{:S(2)}, u32[]{:S(2)}) collective-permute-start(bf16[4,2,16,256]{3,2,1,0:T(8,128)(2,1)S(1)} %get-tuple-element.84), channel_id=1, source_target_pairs={{0,3},{1,2},{2,1},{3,0},{4,7},{5,6},{6,5},{7,4},{8,11},{9,10},{10,... | collective-permute-start | bytes 196616 | tf_op jit(solution)/shard_map/ppermute | solution.py:210
  70.4 4.3 %collective-permute-start.5 = (bf16[4,2,16,256]{3,2,1,0:T(8,128)(2,1)S(1)}, bf16[4,2,16,256]{3,2,1,0:T(8,128)(2,1)S(1)}, u32[]{:S(2)}, u32[]{:S(2)}) collective-permute-start(bf16[4,2,16,256]{3,2,1,0:T(8,128)(2,1)S(1)} %get-tuple-element.84), channel_id=1, source_target_pairs={{0,2},{1,3},{2,0},{3,1},{4,6},{5,7},{6,4},{7,5},{8,10},{9,11},{10,... | collective-permute-start | bytes 196616 | tf_op jit(solution)/shard_map/ppermute | solution.py:210
  71.7 27.6 %collective-permute-start.14 = (bf16[64,16,256]{2,1,0:T(8,128)(2,1)S(1)}, bf16[64,16,256]{2,1,0:T(8,128)(2,1)S(1)}, u32[]{:S(2)}, u32[]{:S(2)}) collective-permute-start(bf16[64,16,256]{2,1,0:T(8,128)(2,1)S(1)} %copy-done.11), channel_id=1, source_target_pairs={{0,3},{1,2},{2,1},{3,0},{4,7},{5,6},{6,5},{7,4},{8,11},{9,10},{10,... | collective-permute-start | bytes 1572872 | tf_op jit(solution)/shard_map/ppermute | solution.py:210
  74.7 1.3 %collective-permute-start.4 = (bf16[4,2,16,256]{3,2,1,0:T(8,128)(2,1)S(1)}, bf16[4,2,16,256]{3,2,1,0:T(8,128)(2,1)S(1)}, u32[]{:S(2)}, u32[]{:S(2)}) collective-permute-start(bf16[4,2,16,256]{3,2,1,0:T(8,128)(2,1)S(1)} %get-tuple-element.84), channel_id=1, source_target_pairs={{0,1},{1,0},{2,3},{3,2},{4,5},{5,4},{6,7},{7,6},{8,9},{9,8},{10,11... | collective-permute-start | bytes 196616 | tf_op jit(solution)/shard_map/ppermute | solution.py:210
  76.0 31.2 %collective-permute-start.18 = (bf16[4,16,16,256]{3,2,1,0:T(8,128)(2,1)S(1)}, bf16[4,16,16,256]{3,2,1,0:T(8,128)(2,1)S(1)}, u32[]{:S(2)}, u32[]{:S(2)}) collective-permute-start(bf16[4,16,16,256]{3,2,1,0:T(8,128)(2,1)S(1)} %get-tuple-element.76), channel_id=1, source_target_pairs={{0,8},{1,9},{2,10},{3,11},{4,12},{5,13},{6,14},{7,15},{8,0},{9,1},... | collective-permute-start | bytes 1572872 | tf_op jit(solution)/shard_map/ppermute | solution.py:210
  97.7 11.1 %collective-permute-start.19 = (bf16[4,16,16,256]{3,2,1,0:T(8,128)(2,1)S(1)}, bf16[4,16,16,256]{3,2,1,0:T(8,128)(2,1)S(1)}, u32[]{:S(2)}, u32[]{:S(2)}) collective-permute-start(bf16[4,16,16,256]{3,2,1,0:T(8,128)(2,1)S(1)} %collective-permute-done.9.rest_3_), channel_id=1, source_target_pairs={{0,16},{16,0},{1,17},{17,1},{2,18},{18,2},{3,19},{19,3},{4,20},{20... | collective-permute-start | bytes 1572872 | tf_op jit(solution)/shard_map/ppermute | solution.py:213
  107.2 12.3 %collective-permute-start.20 = (bf16[4,16,16,256]{3,2,1,0:T(8,128)(2,1)S(1)}, bf16[4,16,16,256]{3,2,1,0:T(8,128)(2,1)S(1)}, u32[]{:S(2)}, u32[]{:S(2)}) collective-permute-start(bf16[4,16,16,256]{3,2,1,0:T(8,128)(2,1)S(1)} %collective-permute-done.18.rest_5_), channel_id=1, source_target_pairs={{0,16},{16,0},{1,17},{17,1},{2,18},{18,2},{3,19},{19,3},{4,20},{20... | collective-permute-start | bytes 1572872 | tf_op jit(solution)/shard_map/ppermute | solution.py:213

commit v8 on v7

--- a/solution.py
+++ b/solution.py
@@ -222,9 +222,11 @@
         return plan, [(at, half)], [shape(half + 2)] + [shape(half)] * (PLANE - 1)
 
     plan, tails, shapes = straight(first, 0)
-    pieces = gather(plan, tails, shapes, outer, half, ri_order, blocks, occupied, virtual)
+    plan_later, shapes_later = plan[WINDOW:], shapes[WINDOW:]
+    pieces = gather(plan[:WINDOW], tails, shapes[:WINDOW], outer, half, ri_order, blocks, occupied, virtual)
     pieces, held_back = barrier((pieces, blocks))
-    plan, tails, shapes = [], [], []
+    plan = [(p[0] - WINDOW,) + p[1:] for p in plan_later]
+    tails, shapes = [], list(shapes_later)
     for d in order[1:-1]:
         more = straight(d, len(shapes))
         plan, tails, shapes = plan + more[0], tails + more[1], shapes + more[2]
@@ -239,17 +241,17 @@
     def after(x, other):
         return barrier((x, other))[0]
 
-    direct = list(pieces) + list(to_send[: PLANE * (outer - 3)])
-    to_last, near_out = to_send[PLANE * (outer - 3)], to_send[PLANE * (outer - 3) + 1 :]
+    direct = list(pieces) + list(to_send[: PLANE * (outer - 2) - WINDOW])
+    to_last, near_out = to_send[-PLANE - 1], to_send[-PLANE:]
     base = jnp.stack([occupied, virtual])
-    far = shift(base, last)
     came, swapped = [], []
     for n, piece in enumerate(direct):
         if n >= WINDOW:
-            piece = after(piece, (came[n - WINDOW], to_last) if n == WINDOW else came[n - WINDOW])
+            before = came[n - WINDOW]
+            piece = after(piece, (before, to_last) if n == WINDOW else before)
         came.append(shift(piece, order[n // PLANE], n % PLANE))
     ready = inplane(after(to_last, came[1]))
-    low = shift(after(ready[:, :quarter], came[-2]), last)
+    low = shift(after(ready[:, :quarter], came[-3]), last)
     high = shift(after(ready[:, quarter:], came[-1]), last)
     for n in range(outer - 2):
         group_in = came[PLANE * n : PLANE * (n + 1)]
@@ -257,6 +259,7 @@
     near = [near_out[0]]
     for q in range(1, PLANE):
         near.append(shift(after(near_out[q], near[-1] if q > 1 else came[-PLANE]), 0, q))
+    far = shift(base, last)
     mine = jnp.stack([base] + [came[PLANE * n][half:] for n in range(outer - 2)] + [far])
     dens = [mine] + [shift(mine, 0, q) for q in range(1, PLANE)]
     dens_all = jnp.stack(dens).reshape(2 * window, window)

time: 126 us -> 124 us (0.984)
  waiting for transfers between devices: 63.5 us -> 59.7 us
  starting transfers between devices: 33.8 us -> 36.1 us
    ppermute x17, waiting for transfers between devices: 58.3 us -> 53.2 us  [shift(): return lax.ppermute(x, 'wide', pairs)]
    ppermute x17, starting transfers between devices: 23.4 us -> 25.4 us  [shift(): return lax.ppermute(x, 'wide', pairs)]
  transfers between devices with their start and end apart: 22 -> 22, of which waited for: 13 -> 15; matrix products, arithmetic and copies ran while one was open for 4% -> 4% of each run, Pallas kernels for 11% -> 12%
where the time goes in v8:
time: 124 us
  waiting for transfers between devices  59.7 us (48%)
  starting transfers between devices  36.1 us (29%)
  Pallas kernels  23.1 us (19%)
  other arithmetic  2.47 us (2%)
  local copies, waits for them, and re-layouts  2.16 us (2%)
    ppermute x17, waiting for transfers between devices, shift(): return lax.ppermute(x, 'wide', pairs)  53.2 us
    ppermute x17, starting transfers between devices, shift(): return lax.ppermute(x, 'wide', pairs)  25.4 us
    pallas_call x2, Pallas kernels, gather(): pl.pallas_call(functools.partial(gather_kernel, plan, tails, outer, half,...  7.84 us
    ppermute x4, starting transfers between devices, swap(): return lax.ppermute(x, 'groups', [(0, 1), (1, 0)])  6.46 us
    ppermute x4, waiting for transfers between devices, swap(): return lax.ppermute(x, 'groups', [(0, 1), (1, 0)])  6.42 us
    pallas_call x1, Pallas kernels, shards(): pl.pallas_call(functools.partial(back_kernel, rows_of, len(arrays)), out_...  5.83 us
    pallas_call x1, Pallas kernels, shards(): pl.pallas_call(functools.partial(middle_kernel, rows_of, len(arrays)), ou...  5.55 us
    all_to_all x1, starting transfers between devices, inplane(): lax.all_to_all(x, 'wide', split_axis=0, concat_axis=0, tiled=True, axis_i...  4.25 us
  transfers between devices with their start and end apart: 22, of which 15 were waited for; matrix products, arithmetic and copies ran while one was open for 4% of the time, Pallas kernels for 12%

profile of v8, /device:TPU:0, one launch (start us, length us, event | category | flops | bytes accessed | tf_op | source)
XLA Modules:
  0.0 123.7 jit_solution(12734585890563209912)
XLA Ops:
  0.0 2.5 %shard_map.55 = (bf16[34,16,256]{2,1,0:T(8,128)(2,1)}, bf16[32,16,256]{2,1,0:T(8,128)(2,1)}) custom-call(s32[16]{0:T(128)} %order_ref.5, bf16[16,64,16,256]{3,2,1,0:T(8,128)(2,1)} %bitcast.33, bf16[16,256]{1,0:T(8,128)(2,1)} %occ_ref.3, bf16[16,256]{1,0:T(8,128)(2,1)} %vir_ref.3), custom_call_target="tpu_custom_call" | custom-call | bytes 1081344 | tf_op jit(solution)/shard_map/pallas_call | solution.py:49
  2.6 0.0 copy-start.9
  2.6 0.0 copy-start.10
  2.6 3.1 %collective-permute-start = (bf16[34,16,256]{2,1,0:T(8,128)(2,1)}, bf16[34,16,256]{2,1,0:T(8,128)(2,1)S(1)}, u32[]{:S(2)}, u32[]{:S(2)}) collective-permute-start(bf16[34,16,256]{2,1,0:T(8,128)(2,1)} %get-tuple-element.43), channel_id=1, source_target_pairs={{0,4},{1,5},{2,6},{3,7},{4,8},{5,9},{6,10},{7,11},{8,12},{9,13},{1... | collective-permute-start | bytes 835592 | tf_op jit(solution)/shard_map/ppermute | solution.py:210
  5.7 0.7 collective-permute-start.7
  6.4 5.3 %shard_map.56 = (bf16[32,16,256]{2,1,0:T(8,128)(2,1)}, bf16[32,16,256]{2,1,0:T(8,128)(2,1)}, bf16[34,16,256]{2,1,0:T(8,128)(2,1)}, bf16[32,16,256]{2,1,0:T(8,128...) custom-call(s32[16]{0:T(128)} %order_ref.5, ...), custom_call_target="tpu_custom_call" | custom-call | bytes 9469952 | tf_op jit(solution)/shard_map/pallas_call | solution.py:49
  11.7 3.7 %collective-permute-done.rest_1_ = bf16[34,16,256]{2,1,0:T(8,128)(2,1)S(1)} collective-permute-done((bf16[34,16,256]{2,1,0:T(8,128)(2,1)}, bf16[34,16,256]{2,1,0:T(8,128)(2,1)S(1)}, u32[]{:S(2)}, u32[]{:S(2)}) %collective-permute-start) | collective-permute-done | bytes 278560 | tf_op jit(solution)/shard_map/ppermute | solution.py:210
  15.4 1.0 collective-permute-start.1
  16.3 3.0 %collective-permute-done.7.rest_5_.rest_8_ = bf16[32,16,256]{2,1,0:T(8,128)(2,1)S(1)} collective-permute-done((bf16[32,16,256]{2,1,0:T(8,128)(2,1)}, bf16[32,16,256]{2,1,0:T(8,128)(2,1)S(1)}, u32[]{:S(2)}, u32[]{:S(2)}) %collective-permute-start.7) | collective-permute-done | bytes 262176 | tf_op jit(solution)/shard_map/ppermute | solution.py:210
  19.3 2.3 %collective-permute-start.8 = (bf16[32,16,256]{2,1,0:T(8,128)(2,1)}, bf16[32,16,256]{2,1,0:T(8,128)(2,1)S(1)}, u32[]{:S(2)}, u32[]{:S(2)}) collective-permute-start(bf16[32,16,256]{2,1,0:T(8,128)(2,1)} %get-tuple-element.55), channel_id=1, source_target_pairs={{0,7},{1,6},{2,5},{3,4},{4,11},{5,10},{6,9},{7,8},{8,15},{9,14},{1... | collective-permute-start | bytes 786440 | tf_op jit(solution)/shard_map/ppermute | solution.py:210
  21.7 2.7 %collective-permute-start.3 = (bf16[2,16,256]{2,1,0:T(8,128)(2,1)S(1)}, bf16[2,16,256]{2,1,0:T(8,128)(2,1)S(1)}, u32[]{:S(2)}, u32[]{:S(2)}) collective-permute-start(bf16[2,16,256]{2,1,0:T(8,128)(2,1)S(1)} %get-tuple-element.82), channel_id=1, source_target_pairs={{0,8},{1,9},{2,10},{3,11},{4,12},{5,13},{6,14},{7,15},{8,0},{9,1},... | collective-permute-start | bytes 49160 | tf_op jit(solution)/shard_map/ppermute | solution.py:210
  24.3 4.2 %all-to-all-start = ((bf16[4,32,16,256]{3,2,1,0:T(8,128)(2,1)}), bf16[4,32,16,256]{3,2,1,0:T(8,128)(2,1)}, u32[]{:S(2)}, u32[]{:S(2)}) async-start(bf16[4,32,16,256]{3,2,1,0:T(8,128)(2,1)} %get-tuple-element.52), calls=%async_computation | async-start | bytes 2097152 | tf_op jit(solution)/shard_map/all_to_all | solution.py:201
  28.6 0.0 copy-start.7
  28.6 0.0 copy-start.8
  28.6 0.0 collective-permute-done.1.rest_8_.rest_11_
  28.7 1.4 %collective-permute-start.2 = (bf16[34,16,256]{2,1,0:T(8,128)(2,1)}, bf16[34,16,256]{2,1,0:T(8,128)(2,1)S(1)}, u32[]{:S(2)}, u32[]{:S(2)}) collective-permute-start(bf16[34,16,256]{2,1,0:T(8,128)(2,1)} %get-tuple-element.49), channel_id=1, source_target_pairs={{0,12},{1,13},{2,14},{3,15},{4,0},{5,1},{6,2},{7,3},{8,4},{9,5},{1... | collective-permute-start | bytes 835592 | tf_op jit(solution)/shard_map/ppermute | solution.py:210
  30.1 1.3 %collective-permute-done.8.rest_11_.rest_14_ = bf16[32,16,256]{2,1,0:T(8,128)(2,1)S(1)} collective-permute-done((bf16[32,16,256]{2,1,0:T(8,128)(2,1)}, bf16[32,16,256]{2,1,0:T(8,128)(2,1)S(1)}, u32[]{:S(2)}, u32[]{:S(2)}) %collective-permute-start.8) | collective-permute-done | bytes 262176 | tf_op jit(solution)/shard_map/ppermute | solution.py:210
  31.3 2.4 %collective-permute-start.9 = (bf16[32,16,256]{2,1,0:T(8,128)(2,1)}, bf16[32,16,256]{2,1,0:T(8,128)(2,1)S(1)}, u32[]{:S(2)}, u32[]{:S(2)}) collective-permute-start(bf16[32,16,256]{2,1,0:T(8,128)(2,1)} %get-tuple-element.56), channel_id=1, source_target_pairs={{0,13},{1,12},{2,15},{3,14},{4,1},{5,0},{6,3},{7,2},{8,5},{9,4},{1... | collective-permute-start | bytes 786440 | tf_op jit(solution)/shard_map/ppermute | solution.py:210
  33.8 4.6 %collective-permute-done.2.rest_2_.rest_3_ = bf16[34,16,256]{2,1,0:T(8,128)(2,1)S(1)} collective-permute-done((bf16[34,16,256]{2,1,0:T(8,128)(2,1)}, bf16[34,16,256]{2,1,0:T(8,128)(2,1)S(1)}, u32[]{:S(2)}, u32[]{:S(2)}) %collective-permute-start.2) | collective-permute-done | bytes 278560 | tf_op jit(solution)/shard_map/ppermute | solution.py:210
  38.4 1.1 pad_maximum_fusion
  39.5 1.5 %collective-permute-start.16 = (bf16[4,32,16,256]{3,2,1,0:T(8,128)(2,1)}, bf16[4,32,16,256]{3,2,1,0:T(8,128)(2,1)S(1)}, u32[]{:S(2)}, u32[]{:S(2)}) collective-permute-start(bf16[4,32,16,256]{3,2,1,0:T(8,128)(2,1)} %pad_maximum_fusion), channel_id=1, source_target_pairs={{0,16},{16,0},{1,17},{17,1},{2,18},{18,2},{3,19},{19,3},{4,20},{20... | collective-permute-start | bytes 3145736 | tf_op jit(solution)/shard_map/ppermute | solution.py:213
  41.0 2.4 %collective-permute-done.9.rest_6_.rest_9_ = bf16[32,16,256]{2,1,0:T(8,128)(2,1)S(1)} collective-permute-done((bf16[32,16,256]{2,1,0:T(8,128)(2,1)}, bf16[32,16,256]{2,1,0:T(8,128)(2,1)S(1)}, u32[]{:S(2)}, u32[]{:S(2)}) %collective-permute-start.9) | collective-permute-done | bytes 262176 | tf_op jit(solution)/shard_map/ppermute | solution.py:210
  43.4 3.8 %collective-permute-start.15 = (bf16[32,16,256]{2,1,0:T(8,128)(2,1)}, bf16[32,16,256]{2,1,0:T(8,128)(2,1)}, u32[]{:S(2)}, u32[]{:S(2)}) collective-permute-start(bf16[32,16,256]{2,1,0:T(8,128)(2,1)} %get-tuple-element.67), channel_id=1, source_target_pairs={{0,15},{1,14},{2,13},{3,12},{4,3},{5,2},{6,1},{7,0},{8,7},{9,6},{1... | collective-permute-start | bytes 786440 | tf_op jit(solution)/shard_map/ppermute | solution.py:210
  47.2 0.7 slice_bitcast_fusion
  47.9 0.6 collective-permute-start.12
  48.5 1.4 %fusion.2 = (bf16[4,16,16,256]{3,2,1,0:T(8,128)(2,1)S(1)}, bf16[4,16,16,256]{3,2,1,0:T(8,128)(2,1)S(1)}) fusion(bf16[4,32,16,256]{3,2,1,0:T(8,128)(2,1)} %all-to-all-done), kind=kLoop, calls=%fused_computation.11 | loop fusion | bytes 2097152 | tf_op jit(solution)/shard_map/slice | solution.py:255
  49.9 4.3 %collective-permute-done.15.rest_12_.rest_15_ = bf16[32,16,256]{2,1,0:T(8,128)(2,1)} collective-permute-done((bf16[32,16,256]{2,1,0:T(8,128)(2,1)}, bf16[32,16,256]{2,1,0:T(8,128)(2,1)}, u32[]{:S(2)}, u32[]{:S(2)}) %collective-permute-start.15) | collective-permute-done | bytes 262176 | tf_op jit(solution)/shard_map/ppermute | solution.py:210
  54.2 0.8 collective-permute-start.10
  55.0 4.9 %collective-permute-done.13.rest_9_.rest_12_ = bf16[32,16,256]{2,1,0:T(8,128)(2,1)} collective-permute-done((bf16[32,16,256]{2,1,0:T(8,128)(2,1)}, bf16[32,16,256]{2,1,0:T(8,128)(2,1)}, u32[]{:S(2)}, u32[]{:S(2)}) %collective-permute-start.13) | collective-permute-done | bytes 262176 | tf_op jit(solution)/shard_map/ppermute | solution.py:210
  59.8 1.3 %pad_maximum_fusion.1 = bf16[4,32,16,256]{3,2,1,0:T(8,128)(2,1)S(1)} fusion(bf16[1,32,16,256]{3,2,1,0:T(8,128)(2,1)} %bitcast.20, bf16[1,32,16,256]{3,2,1,0:T(8,128)(2,1)} %bitcast.19, bf16[1,32,16,256]{3,2,1,0:T(8,128)(2,1)} %bitcast.31, bf16[1,32,16,256]{3,2,1,0:T(8,128)(2,1)} %slice_bitcast_fusion), kind=kLoop, calls=%fused_computation.1 | loop fusion | flops 1572864 | bytes 2097152 | tf_op jit(solution)/shard_map/stack | solution.py:258
  61.2 1.6 %collective-permute-start.17 = (bf16[4,32,16,256]{3,2,1,0:T(8,128)(2,1)S(1)}, bf16[4,32,16,256]{3,2,1,0:T(8,128)(2,1)S(1)}, u32[]{:S(2)}, u32[]{:S(2)}) collective-permute-start(bf16[4,32,16,256]{3,2,1,0:T(8,128)(2,1)S(1)} %pad_maximum_fusion.1), channel_id=1, source_target_pairs={{0,16},{16,0},{1,17},{17,1},{2,18},{18,2},{3,19},{19,3},{4,20},{20... | collective-permute-start | bytes 3145736 | tf_op jit(solution)/shard_map/ppermute | solution.py:213
  62.8 0.1 collective-permute-start.6
  62.8 7.2 %collective-permute-done.12.rest_7_.rest_10_.rest_4_ = bf16[64,16,256]{2,1,0:T(8,128)(2,1)S(1)} collective-permute-done((bf16[64,16,256]{2,1,0:T(8,128)(2,1)}, bf16[64,16,256]{2,1,0:T(8,128)(2,1)S(1)}, u32[]{:S(2)}, u32[]{:S(2)}) %collective-permute-start.12) | collective-permute-done | bytes 524320 | tf_op jit(solution)/shard_map/ppermute | solution.py:210
  70.0 1.0 collective-permute-start.5
  71.0 0.3 collective-permute-done.6
  71.3 0.8 collective-permute-start.14
  72.1 2.3 %collective-permute-done.5 = bf16[4,2,16,256]{3,2,1,0:T(8,128)(2,1)S(1)} collective-permute-done((bf16[4,2,16,256]{3,2,1,0:T(8,128)(2,1)S(1)}, bf16[4,2,16,256]{3,2,1,0:T(8,128)(2,1)S(1)}, u32[]{:S(2)}, u32[]{:S(2)}) %collective-permute-start.5) | collective-permute-done | bytes 65568 | tf_op jit(solution)/shard_map/ppermute | solution.py:210
  74.4 1.3 %collective-permute-done.4 = bf16[4,2,16,256]{3,2,1,0:T(8,128)(2,1)S(1)} collective-permute-done((bf16[4,2,16,256]{3,2,1,0:T(8,128)(2,1)S(1)}, bf16[4,2,16,256]{3,2,1,0:T(8,128)(2,1)S(1)}, u32[]{:S(2)}, u32[]{:S(2)}) %collective-permute-start.4) | collective-permute-done | bytes 65568 | tf_op jit(solution)/shard_map/ppermute | solution.py:210
  75.6 4.7 %collective-permute-start.18 = (bf16[4,16,16,256]{3,2,1,0:T(8,128)(2,1)S(1)}, bf16[4,16,16,256]{3,2,1,0:T(8,128)(2,1)S(1)}, u32[]{:S(2)}, u32[]{:S(2)}) collective-permute-start(bf16[4,16,16,256]{3,2,1,0:T(8,128)(2,1)S(1)} %get-tuple-element.72), channel_id=1, source_target_pairs={{0,8},{1,9},{2,10},{3,11},{4,12},{5,13},{6,14},{7,15},{8,0},{9,1},... | collective-permute-start | bytes 1572872 | tf_op jit(solution)/shard_map/ppermute | solution.py:210
  80.4 2.0 %collective-permute-done.10.rest_3_ = bf16[4,16,16,256]{3,2,1,0:T(8,128)(2,1)S(1)} collective-permute-done((bf16[4,16,16,256]{3,2,1,0:T(8,128)(2,1)S(1)}, bf16[4,16,16,256]{3,2,1,0:T(8,128)(2,1)S(1)}, u32[]{:S(2)}, u32[]{:S(2)}) %collective-permute-start.10) | collective-permute-done | bytes 524320 | tf_op jit(solution)/shard_map/ppermute | solution.py:210
  82.4 1.8 %collective-permute-start.19 = (bf16[4,16,16,256]{3,2,1,0:T(8,128)(2,1)S(1)}, bf16[4,16,16,256]{3,2,1,0:T(8,128)(2,1)S(1)}, u32[]{:S(2)}, u32[]{:S(2)}) collective-permute-start(bf16[4,16,16,256]{3,2,1,0:T(8,128)(2,1)S(1)} %collective-permute-done.10.rest_3_), channel_id=1, source_target_pairs={{0,16},{16,0},{1,17},{17,1},{2,18},{18,2},{3,19},{19,3},{4,20},{20... | collective-permute-start | bytes 1572872 | tf_op jit(solution)/shard_map/ppermute | solution.py:213
  84.3 1.0 collective-permute-done.14.rest_10_.rest_13_.rest_5_
  85.3 3.9 %shard_map.57 = (bf16[256,16,256]{2,1,0:T(8,128)(2,1)S(1)}, bf16[256,16,256]{2,1,0:T(8,128)(2,1)S(1)}, bf16[256,256]{1,0:T(8,128)(2,1)S(1)}, bf16[256,256]{1,0:T(8,128)(2,1)S(1)}, bf16[256,256]{1,0:T(8,128)(2,1)S(1)}) custom-call(s32[16]{0:T(128)S(1)} %copy-done.8, s32[4,4,16]{2,1,0:T(4,128)S(1)} %bitcast.32, bf16[512,256]{1,0:T(8,128)(2,1)S(1)} %bitcast.27, ...), custom_call_target="tpu_custom_call" | custom-call | flops 1073741824 | bytes 6291456 | tf_op jit(solution)/shard_map/pallas_call | solution.py:321
  89.2 15.2 %collective-permute-done.18.rest_5_ = bf16[4,16,16,256]{3,2,1,0:T(8,128)(2,1)S(1)} collective-permute-done((bf16[4,16,16,256]{3,2,1,0:T(8,128)(2,1)S(1)}, bf16[4,16,16,256]{3,2,1,0:T(8,128)(2,1)S(1)}, u32[]{:S(2)}, u32[]{:S(2)}) %collective-permute-start.18) | collective-permute-done | bytes 524320 | tf_op jit(solution)/shard_map/ppermute | solution.py:210
  104.4 1.5 %collective-permute-start.20 = (bf16[4,16,16,256]{3,2,1,0:T(8,128)(2,1)S(1)}, bf16[4,16,16,256]{3,2,1,0:T(8,128)(2,1)S(1)}, u32[]{:S(2)}, u32[]{:S(2)}) collective-permute-start(bf16[4,16,16,256]{3,2,1,0:T(8,128)(2,1)S(1)} %collective-permute-done.18.rest_5_), channel_id=1, source_target_pairs={{0,16},{16,0},{1,17},{17,1},{2,18},{18,2},{3,19},{19,3},{4,20},{20... | collective-permute-start | bytes 1572872 | tf_op jit(solution)/shard_map/ppermute | solution.py:213
  105.9 5.5 %shard_map.58 = (bf16[256,32,256]{2,1,0:T(8,128)(2,1)S(1)}, bf16[256,32,256]{2,1,0:T(8,128)(2,1)S(1)}) custom-call(bf16[256,256]{1,0:T(8,128)(2,1)S(1)} %get-tuple-element.68.occ_ref, bf16[256,256]{1,0:T(8,128)(2,1)S(1)} %get-tuple-element.69.vir_ref, bf16[256,256]{1,0:T(8,128)(2,1)S(1)} %get-tuple-element.70.keep_ref, bf16[64,16,256]{2,1,0:T(8,128)(2,1)S(1)} %copy-done, ...), custom_call_target="tpu_custom_call" | custom-call | flops 2147483648 | bytes 12582912 | tf_op jit(solution)/shard_map/pallas_call | solution.py:333
  111.5 6.4 %collective-permute-done.20.rest_6_ = bf16[4,16,16,256]{3,2,1,0:T(8,128)(2,1)S(1)} collective-permute-done((bf16[4,16,16,256]{3,2,1,0:T(8,128)(2,1)S(1)}, bf16[4,16,16,256]{3,2,1,0:T(8,128)(2,1)S(1)}, u32[]{:S(2)}, u32[]{:S(2)}) %collective-permute-start.20) | collective-permute-done | bytes 524320 | tf_op jit(solution)/shard_map/ppermute | solution.py:213
  117.9 5.8 %shard_map.59 = f32[64,64]{1,0:T(8,128)} custom-call(bf16[256,256]{1,0:T(8,128)(2,1)S(1)} %get-tuple-element.68.occ_ref, bf16[256,256]{1,0:T(8,128)(2,1)S(1)} %get-tuple-element.69.vir_ref, bf16[256,256]{1,0:T(8,128)(2,1)S(1)} %get-tuple-element.70.keep_ref, bf16[256,16,256]{2,1,0:T(8,128)(2,1)S(1)} %get-tuple-element.71.mask_a, ...), custom_call_target="tpu_custom_call" | custom-call | flops 1073741824 | bytes 16777216 | tf_op jit(solution)/shard_map/pallas_call | solution.py:343
  (35 shorter events, 0.1 us)
Async XLA Ops:
  2.6 19.1 %copy-start.9 = (bf16[16,256]{1,0:T(8,128)(2,1)S(1)}, bf16[16,256]{1,0:T(8,128)(2,1)}, u32[]{:S(2)}) copy-start(bf16[16,256]{1,0:T(8,128)(2,1)} %vir_ref.3) | copy-start | bytes 24580
  2.6 19.1 %copy-start.10 = (bf16[16,256]{1,0:T(8,128)(2,1)S(1)}, bf16[16,256]{1,0:T(8,128)(2,1)}, u32[]{:S(2)}) copy-start(bf16[16,256]{1,0:T(8,128)(2,1)} %occ_ref.3) | copy-start | bytes 24580
  2.6 12.8 %collective-permute-start = (bf16[34,16,256]{2,1,0:T(8,128)(2,1)}, bf16[34,16,256]{2,1,0:T(8,128)(2,1)S(1)}, u32[]{:S(2)}, u32[]{:S(2)}) collective-permute-start(bf16[34,16,256]{2,1,0:T(8,128)(2,1)} %get-tuple-element.43), channel_id=1, source_target_pairs={{0,4},{1,5},{2,6},{3,7},{4,8},{5,9},{6,10},{7,11},{8,12},{9,13},{1... | collective-permute-start | bytes 835592 | tf_op jit(solution)/shard_map/ppermute | solution.py:210
  5.7 13.7 %collective-permute-start.7 = (bf16[32,16,256]{2,1,0:T(8,128)(2,1)}, bf16[32,16,256]{2,1,0:T(8,128)(2,1)S(1)}, u32[]{:S(2)}, u32[]{:S(2)}) collective-permute-start(bf16[32,16,256]{2,1,0:T(8,128)(2,1)} %get-tuple-element.51), channel_id=1, source_target_pairs={{0,5},{1,4},{2,7},{3,6},{4,9},{5,8},{6,11},{7,10},{8,13},{9,12},{1... | collective-permute-start | bytes 786440 | tf_op jit(solution)/shard_map/ppermute | solution.py:210
  15.4 13.3 %collective-permute-start.1 = (bf16[32,16,256]{2,1,0:T(8,128)(2,1)}, bf16[32,16,256]{2,1,0:T(8,128)(2,1)S(1)}, u32[]{:S(2)}, u32[]{:S(2)}) collective-permute-start(bf16[32,16,256]{2,1,0:T(8,128)(2,1)} %get-tuple-element.48), channel_id=1, source_target_pairs={{0,6},{1,7},{2,4},{3,5},{4,10},{5,11},{6,8},{7,9},{8,14},{9,15},{1... | collective-permute-start | bytes 786440 | tf_op jit(solution)/shard_map/ppermute | solution.py:210
  19.3 12.0 %collective-permute-start.8 = (bf16[32,16,256]{2,1,0:T(8,128)(2,1)}, bf16[32,16,256]{2,1,0:T(8,128)(2,1)S(1)}, u32[]{:S(2)}, u32[]{:S(2)}) collective-permute-start(bf16[32,16,256]{2,1,0:T(8,128)(2,1)} %get-tuple-element.55), channel_id=1, source_target_pairs={{0,7},{1,6},{2,5},{3,4},{4,11},{5,10},{6,9},{7,8},{8,15},{9,14},{1... | collective-permute-start | bytes 786440 | tf_op jit(solution)/shard_map/ppermute | solution.py:210
  21.7 41.1 %collective-permute-start.3 = (bf16[2,16,256]{2,1,0:T(8,128)(2,1)S(1)}, bf16[2,16,256]{2,1,0:T(8,128)(2,1)S(1)}, u32[]{:S(2)}, u32[]{:S(2)}) collective-permute-start(bf16[2,16,256]{2,1,0:T(8,128)(2,1)S(1)} %get-tuple-element.82), channel_id=1, source_target_pairs={{0,8},{1,9},{2,10},{3,11},{4,12},{5,13},{6,14},{7,15},{8,0},{9,1},... | collective-permute-start | bytes 49160 | tf_op jit(solution)/shard_map/ppermute | solution.py:210
  24.3 24.2 %all-to-all-start = ((bf16[4,32,16,256]{3,2,1,0:T(8,128)(2,1)}), bf16[4,32,16,256]{3,2,1,0:T(8,128)(2,1)}, u32[]{:S(2)}, u32[]{:S(2)}) async-start(bf16[4,32,16,256]{3,2,1,0:T(8,128)(2,1)} %get-tuple-element.52), calls=%async_computation | async-start | bytes 2097152 | tf_op jit(solution)/shard_map/all_to_all | solution.py:201
  28.6 56.7 %copy-start = (bf16[64,16,256]{2,1,0:T(8,128)(2,1)S(1)}, bf16[64,16,256]{2,1,0:T(8,128)(2,1)}, u32[]{:S(2)}) copy-start(bf16[64,16,256]{2,1,0:T(8,128)(2,1)} %get-tuple-element.50.rest_0_) | copy-start | bytes 1572868
  28.6 56.7 %copy-start.7 = (s32[16,4,4]{0,2,1:T(4,128)S(1)}, s32[16,4,4]{0,2,1:T(4,128)}, u32[]{:S(2)}) copy-start(s32[16,4,4]{0,2,1:T(4,128)} %param.8) | copy-start | bytes 3076
  28.6 56.7 %copy-start.8 = (s32[16]{0:T(128)S(1)}, s32[16]{0:T(128)}, u32[]{:S(2)}) copy-start(s32[16]{0:T(128)} %order_ref.5) | copy-start | bytes 196
  28.6 19.3 %copy-start.1 = (bf16[32,16,256]{2,1,0:T(8,128)(2,1)}, bf16[32,16,256]{2,1,0:T(8,128)(2,1)S(1)}, u32[]{:S(2)}) copy-start(bf16[32,16,256]{2,1,0:T(8,128)(2,1)S(1)} %collective-permute-done.1.rest_8_.rest_11_) | copy-start | bytes 786436
  28.7 9.7 %collective-permute-start.2 = (bf16[34,16,256]{2,1,0:T(8,128)(2,1)}, bf16[34,16,256]{2,1,0:T(8,128)(2,1)S(1)}, u32[]{:S(2)}, u32[]{:S(2)}) collective-permute-start(bf16[34,16,256]{2,1,0:T(8,128)(2,1)} %get-tuple-element.49), channel_id=1, source_target_pairs={{0,12},{1,13},{2,14},{3,15},{4,0},{5,1},{6,2},{7,3},{8,4},{9,5},{1... | collective-permute-start | bytes 835592 | tf_op jit(solution)/shard_map/ppermute | solution.py:210
  31.3 16.6 %copy-start.3 = (bf16[32,16,256]{2,1,0:T(8,128)(2,1)}, bf16[32,16,256]{2,1,0:T(8,128)(2,1)S(1)}, u32[]{:S(2)}) copy-start(bf16[32,16,256]{2,1,0:T(8,128)(2,1)S(1)} %collective-permute-done.8.rest_11_.rest_14_) | copy-start | bytes 786436
  31.3 12.0 %collective-permute-start.9 = (bf16[32,16,256]{2,1,0:T(8,128)(2,1)}, bf16[32,16,256]{2,1,0:T(8,128)(2,1)S(1)}, u32[]{:S(2)}, u32[]{:S(2)}) collective-permute-start(bf16[32,16,256]{2,1,0:T(8,128)(2,1)} %get-tuple-element.56), channel_id=1, source_target_pairs={{0,13},{1,12},{2,15},{3,14},{4,1},{5,0},{6,3},{7,2},{8,5},{9,4},{1... | collective-permute-start | bytes 786440 | tf_op jit(solution)/shard_map/ppermute | solution.py:210
  38.4 9.5 %collective-permute-start.11 = (bf16[64,16,256]{2,1,0:T(8,128)(2,1)}, bf16[64,16,256]{2,1,0:T(8,128)(2,1)S(1)}, u32[]{:S(2)}, u32[]{:S(2)}) collective-permute-start(bf16[64,16,256]{2,1,0:T(8,128)(2,1)} %get-tuple-element.59), channel_id=1, source_target_pairs={{0,1},{1,0},{2,3},{3,2},{4,5},{5,4},{6,7},{7,6},{8,9},{9,8},{10,11... | collective-permute-start | bytes 1572872 | tf_op jit(solution)/shard_map/ppermute | solution.py:210
  39.5 66.4 %collective-permute-start.16 = (bf16[4,32,16,256]{3,2,1,0:T(8,128)(2,1)}, bf16[4,32,16,256]{3,2,1,0:T(8,128)(2,1)S(1)}, u32[]{:S(2)}, u32[]{:S(2)}) collective-permute-start(bf16[4,32,16,256]{3,2,1,0:T(8,128)(2,1)} %pad_maximum_fusion), channel_id=1, source_target_pairs={{0,16},{16,0},{1,17},{17,1},{2,18},{18,2},{3,19},{19,3},{4,20},{20... | collective-permute-start | bytes 3145736 | tf_op jit(solution)/shard_map/ppermute | solution.py:213
  43.4 4.6 %copy-start.5 = (bf16[32,16,256]{2,1,0:T(8,128)(2,1)}, bf16[32,16,256]{2,1,0:T(8,128)(2,1)S(1)}, u32[]{:S(2)}) copy-start(bf16[32,16,256]{2,1,0:T(8,128)(2,1)S(1)} %collective-permute-done.9.rest_6_.rest_9_) | copy-start | bytes 786436
  43.4 10.8 %collective-permute-start.15 = (bf16[32,16,256]{2,1,0:T(8,128)(2,1)}, bf16[32,16,256]{2,1,0:T(8,128)(2,1)}, u32[]{:S(2)}, u32[]{:S(2)}) collective-permute-start(bf16[32,16,256]{2,1,0:T(8,128)(2,1)} %get-tuple-element.67), channel_id=1, source_target_pairs={{0,15},{1,14},{2,13},{3,12},{4,3},{5,2},{6,1},{7,0},{8,7},{9,6},{1... | collective-permute-start | bytes 786440 | tf_op jit(solution)/shard_map/ppermute | solution.py:210
  47.2 12.6 %collective-permute-start.13 = (bf16[32,16,256]{2,1,0:T(8,128)(2,1)}, bf16[32,16,256]{2,1,0:T(8,128)(2,1)}, u32[]{:S(2)}, u32[]{:S(2)}) collective-permute-start(bf16[32,16,256]{2,1,0:T(8,128)(2,1)} %get-tuple-element.63), channel_id=1, source_target_pairs={{0,14},{1,15},{2,12},{3,13},{4,2},{5,3},{6,0},{7,1},{8,6},{9,7},{1... | collective-permute-start | bytes 786440 | tf_op jit(solution)/shard_map/ppermute | solution.py:210
  47.9 22.1 %collective-permute-start.12 = (bf16[64,16,256]{2,1,0:T(8,128)(2,1)}, bf16[64,16,256]{2,1,0:T(8,128)(2,1)S(1)}, u32[]{:S(2)}, u32[]{:S(2)}) collective-permute-start(bf16[64,16,256]{2,1,0:T(8,128)(2,1)} %get-tuple-element.61), channel_id=1, source_target_pairs={{0,2},{1,3},{2,0},{3,1},{4,6},{5,7},{6,4},{7,5},{8,10},{9,11},{10,... | collective-permute-start | bytes 1572872 | tf_op jit(solution)/shard_map/ppermute | solution.py:210
  48.5 22.8 %copy-start.11 = (bf16[64,16,256]{2,1,0:T(8,128)(2,1)S(1)}, bf16[64,16,256]{2,1,0:T(8,128)(2,1)}, u32[]{:S(2)}) copy-start(bf16[64,16,256]{2,1,0:T(8,128)(2,1)} %get-tuple-element.65) | copy-start | bytes 1572868
  48.5 36.8 %copy-start.2 = (bf16[32,16,256]{2,1,0:T(8,128)(2,1)S(1)}, bf16[32,16,256]{2,1,0:T(8,128)(2,1)}, u32[]{:S(2)}) copy-start(bf16[32,16,256]{2,1,0:T(8,128)(2,1)} %copy-done.1) | copy-start | bytes 786436
  48.5 36.8 %copy-start.4 = (bf16[32,16,256]{2,1,0:T(8,128)(2,1)S(1)}, bf16[32,16,256]{2,1,0:T(8,128)(2,1)}, u32[]{:S(2)}) copy-start(bf16[32,16,256]{2,1,0:T(8,128)(2,1)} %copy-done.3) | copy-start | bytes 786436
  48.5 36.8 %copy-start.6 = (bf16[32,16,256]{2,1,0:T(8,128)(2,1)S(1)}, bf16[32,16,256]{2,1,0:T(8,128)(2,1)}, u32[]{:S(2)}) copy-start(bf16[32,16,256]{2,1,0:T(8,128)(2,1)} %copy-done.5) | copy-start | bytes 786436
  54.2 28.2 %collective-permute-start.10 = (bf16[4,16,16,256]{3,2,1,0:T(8,128)(2,1)S(1)}, bf16[4,16,16,256]{3,2,1,0:T(8,128)(2,1)S(1)}, u32[]{:S(2)}, u32[]{:S(2)}) collective-permute-start(bf16[4,16,16,256]{3,2,1,0:T(8,128)(2,1)S(1)} %get-tuple-element.57), channel_id=1, source_target_pairs={{0,8},{1,9},{2,10},{3,11},{4,12},{5,13},{6,14},{7,15},{8,0},{9,1},... | collective-permute-start | bytes 1572872 | tf_op jit(solution)/shard_map/ppermute | solution.py:210
  61.2 44.8 %collective-permute-start.17 = (bf16[4,32,16,256]{3,2,1,0:T(8,128)(2,1)S(1)}, bf16[4,32,16,256]{3,2,1,0:T(8,128)(2,1)S(1)}, u32[]{:S(2)}, u32[]{:S(2)}) collective-permute-start(bf16[4,32,16,256]{3,2,1,0:T(8,128)(2,1)S(1)} %pad_maximum_fusion.1), channel_id=1, source_target_pairs={{0,16},{16,0},{1,17},{17,1},{2,18},{18,2},{3,19},{19,3},{4,20},{20... | collective-permute-start | bytes 3145736 | tf_op jit(solution)/shard_map/ppermute | solution.py:213
  62.8 8.5 %collective-permute-start.6 = (bf16[4,2,16,256]{3,2,1,0:T(8,128)(2,1)S(1)}, bf16[4,2,16,256]{3,2,1,0:T(8,128)(2,1)S(1)}, u32[]{:S(2)}, u32[]{:S(2)}) collective-permute-start(bf16[4,2,16,256]{3,2,1,0:T(8,128)(2,1)S(1)} %get-tuple-element.80), channel_id=1, source_target_pairs={{0,3},{1,2},{2,1},{3,0},{4,7},{5,6},{6,5},{7,4},{8,11},{9,10},{10,... | collective-permute-start | bytes 196616 | tf_op jit(solution)/shard_map/ppermute | solution.py:210
  70.0 4.3 %collective-permute-start.5 = (bf16[4,2,16,256]{3,2,1,0:T(8,128)(2,1)S(1)}, bf16[4,2,16,256]{3,2,1,0:T(8,128)(2,1)S(1)}, u32[]{:S(2)}, u32[]{:S(2)}) collective-permute-start(bf16[4,2,16,256]{3,2,1,0:T(8,128)(2,1)S(1)} %get-tuple-element.80), channel_id=1, source_target_pairs={{0,2},{1,3},{2,0},{3,1},{4,6},{5,7},{6,4},{7,5},{8,10},{9,11},{10,... | collective-permute-start | bytes 196616 | tf_op jit(solution)/shard_map/ppermute | solution.py:210
  71.3 14.0 %collective-permute-start.14 = (bf16[64,16,256]{2,1,0:T(8,128)(2,1)S(1)}, bf16[64,16,256]{2,1,0:T(8,128)(2,1)S(1)}, u32[]{:S(2)}, u32[]{:S(2)}) collective-permute-start(bf16[64,16,256]{2,1,0:T(8,128)(2,1)S(1)} %copy-done.11), channel_id=1, source_target_pairs={{0,3},{1,2},{2,1},{3,0},{4,7},{5,6},{6,5},{7,4},{8,11},{9,10},{10,... | collective-permute-start | bytes 1572872 | tf_op jit(solution)/shard_map/ppermute | solution.py:210
  74.4 1.3 %collective-permute-start.4 = (bf16[4,2,16,256]{3,2,1,0:T(8,128)(2,1)S(1)}, bf16[4,2,16,256]{3,2,1,0:T(8,128)(2,1)S(1)}, u32[]{:S(2)}, u32[]{:S(2)}) collective-permute-start(bf16[4,2,16,256]{3,2,1,0:T(8,128)(2,1)S(1)} %get-tuple-element.80), channel_id=1, source_target_pairs={{0,1},{1,0},{2,3},{3,2},{4,5},{5,4},{6,7},{7,6},{8,9},{9,8},{10,11... | collective-permute-start | bytes 196616 | tf_op jit(solution)/shard_map/ppermute | solution.py:210
  75.6 28.8 %collective-permute-start.18 = (bf16[4,16,16,256]{3,2,1,0:T(8,128)(2,1)S(1)}, bf16[4,16,16,256]{3,2,1,0:T(8,128)(2,1)S(1)}, u32[]{:S(2)}, u32[]{:S(2)}) collective-permute-start(bf16[4,16,16,256]{3,2,1,0:T(8,128)(2,1)S(1)} %get-tuple-element.72), channel_id=1, source_target_pairs={{0,8},{1,9},{2,10},{3,11},{4,12},{5,13},{6,14},{7,15},{8,0},{9,1},... | collective-permute-start | bytes 1572872 | tf_op jit(solution)/shard_map/ppermute | solution.py:210
  82.4 23.6 %collective-permute-start.19 = (bf16[4,16,16,256]{3,2,1,0:T(8,128)(2,1)S(1)}, bf16[4,16,16,256]{3,2,1,0:T(8,128)(2,1)S(1)}, u32[]{:S(2)}, u32[]{:S(2)}) collective-permute-start(bf16[4,16,16,256]{3,2,1,0:T(8,128)(2,1)S(1)} %collective-permute-done.10.rest_3_), channel_id=1, source_target_pairs={{0,16},{16,0},{1,17},{17,1},{2,18},{18,2},{3,19},{19,3},{4,20},{20... | collective-permute-start | bytes 1572872 | tf_op jit(solution)/shard_map/ppermute | solution.py:213
  104.4 13.5 %collective-permute-start.20 = (bf16[4,16,16,256]{3,2,1,0:T(8,128)(2,1)S(1)}, bf16[4,16,16,256]{3,2,1,0:T(8,128)(2,1)S(1)}, u32[]{:S(2)}, u32[]{:S(2)}) collective-permute-start(bf16[4,16,16,256]{3,2,1,0:T(8,128)(2,1)S(1)} %collective-permute-done.18.rest_5_), channel_id=1, source_target_pairs={{0,16},{16,0},{1,17},{17,1},{2,18},{18,2},{3,19},{19,3},{4,20},{20... | collective-permute-start | bytes 1572872 | tf_op jit(solution)/shard_map/ppermute | solution.py:213

commit v9 on v8

--- a/solution.py
+++ b/solution.py
@@ -245,20 +245,23 @@
     to_last, near_out = to_send[-PLANE - 1], to_send[-PLANE:]
     base = jnp.stack([occupied, virtual])
     came, swapped = [], []
-    for n, piece in enumerate(direct):
+    came = [None] * len(direct)
+    row = [PLANE * (n // PLANE) + (1, 0, 3, 2, 1, 0, 3, 2)[n % 8] for n in range(len(direct))]
+    for n, at in enumerate(row):
+        piece = direct[at]
         if n >= WINDOW:
-            before = came[n - WINDOW]
+            before = came[row[n - WINDOW]]
             piece = after(piece, (before, to_last) if n == WINDOW else before)
-        came.append(shift(piece, order[n // PLANE], n % PLANE))
-    ready = inplane(after(to_last, came[1]))
-    low = shift(after(ready[:, :quarter], came[-3]), last)
-    high = shift(after(ready[:, quarter:], came[-1]), last)
+        came[at] = shift(piece, order[at // PLANE], at % PLANE)
+    ready = inplane(after(to_last, came[row[1]]))
+    low = shift(after(ready[:, :quarter], came[row[-3]]), last)
+    high = shift(after(ready[:, quarter:], came[row[-2]]), last)
     for n in range(outer - 2):
         group_in = came[PLANE * n : PLANE * (n + 1)]
         swapped.append(swap(jnp.stack([group_in[0][:half]] + group_in[1:])))
     near = [near_out[0]]
     for q in range(1, PLANE):
-        near.append(shift(after(near_out[q], near[-1] if q > 1 else came[-PLANE]), 0, q))
+        near.append(shift(after(near_out[q], near[-1] if q > 1 else came[row[-PLANE]]), 0, q))
     far = shift(base, last)
     mine = jnp.stack([base] + [came[PLANE * n][half:] for n in range(outer - 2)] + [far])
     dens = [mine] + [shift(mine, 0, q) for q in range(1, PLANE)]

time: 124 us -> 124 us (level)
  waiting for transfers between devices: 59.7 us -> 58.1 us
    ppermute x17, starting transfers between devices: 25.4 us -> 29 us  [shift(): return lax.ppermute(x, 'wide', pairs)]
    ppermute x4, starting transfers between devices: 6.46 us -> 3.21 us  [swap(): return lax.ppermute(x, 'groups', [(0, 1), (1, 0)])]
    ppermute x17, waiting for transfers between devices: 53.2 us -> 50.2 us  [shift(): return lax.ppermute(x, 'wide', pairs)]
    ppermute x4, waiting for transfers between devices: 6.42 us -> 7.82 us  [swap(): return lax.ppermute(x, 'groups', [(0, 1), (1, 0)])]
  transfers between devices with their start and end apart: 22 -> 22, of which waited for: 15 -> 13; matrix products, arithmetic and copies ran while one was open for 4% -> 4% of each run, Pallas kernels for 12% -> 12%
where the time goes in v9:
time: 124 us; the launch traced here: 123 us
  waiting for transfers between devices  58.1 us (47%)
  starting transfers between devices  36.5 us (29%)
  Pallas kernels  23.2 us (19%)
  local copies, waits for them, and re-layouts  2.88 us (2%)
  other arithmetic  2.47 us (2%)
    ppermute x17, waiting for transfers between devices, shift(): return lax.ppermute(x, 'wide', pairs)  50.2 us
    ppermute x17, starting transfers between devices, shift(): return lax.ppermute(x, 'wide', pairs)  29 us
    pallas_call x2, Pallas kernels, gather(): pl.pallas_call(functools.partial(gather_kernel, plan, tails, outer, half,...  7.88 us
    ppermute x4, waiting for transfers between devices, swap(): return lax.ppermute(x, 'groups', [(0, 1), (1, 0)])  7.82 us
    pallas_call x1, Pallas kernels, shards(): pl.pallas_call(functools.partial(back_kernel, rows_of, len(arrays)), out_...  5.83 us
    pallas_call x1, Pallas kernels, shards(): pl.pallas_call(functools.partial(middle_kernel, rows_of, len(arrays)), ou...  5.54 us
    all_to_all x1, starting transfers between devices, inplane(): lax.all_to_all(x, 'wide', split_axis=0, concat_axis=0, tiled=True, axis_i...  4.25 us
    pallas_call x1, Pallas kernels, shards(): pl.pallas_call(functools.partial(front_kernel, rows_of, [0] + order, oute...  3.92 us
  transfers between devices with their start and end apart: 22, of which 13 were waited for; matrix products, arithmetic and copies ran while one was open for 4% of the time, Pallas kernels for 12%

profile of v9, /device:TPU:0, one launch (start us, length us, event | category | flops | bytes accessed | tf_op | source)
XLA Modules:
  0.0 123.2 jit_solution(15717112310951352581)
XLA Ops:
  0.0 2.6 %shard_map.55 = (bf16[34,16,256]{2,1,0:T(8,128)(2,1)}, bf16[32,16,256]{2,1,0:T(8,128)(2,1)}) custom-call(s32[16]{0:T(128)} %order_ref.5, bf16[16,64,16,256]{3,2,1,0:T(8,128)(2,1)} %bitcast.33, bf16[16,256]{1,0:T(8,128)(2,1)} %occ_ref.3, bf16[16,256]{1,0:T(8,128)(2,1)} %vir_ref.3), custom_call_target="tpu_custom_call" | custom-call | bytes 1081344 | tf_op jit(solution)/shard_map/pallas_call | solution.py:49
  2.6 0.0 copy-start.9
  2.6 0.0 copy-start.10
  2.6 2.5 %collective-permute-start.8 = (bf16[32,16,256]{2,1,0:T(8,128)(2,1)}, bf16[32,16,256]{2,1,0:T(8,128)(2,1)S(1)}, u32[]{:S(2)}, u32[]{:S(2)}) collective-permute-start(bf16[32,16,256]{2,1,0:T(8,128)(2,1)} %get-tuple-element.56), channel_id=1, source_target_pairs={{0,5},{1,4},{2,7},{3,6},{4,9},{5,8},{6,11},{7,10},{8,13},{9,12},{1... | collective-permute-start | bytes 786440 | tf_op jit(solution)/shard_map/ppermute | solution.py:210
  5.1 1.6 %collective-permute-start = (bf16[34,16,256]{2,1,0:T(8,128)(2,1)}, bf16[34,16,256]{2,1,0:T(8,128)(2,1)S(1)}, u32[]{:S(2)}, u32[]{:S(2)}) collective-permute-start(bf16[34,16,256]{2,1,0:T(8,128)(2,1)} %get-tuple-element.43), channel_id=1, source_target_pairs={{0,4},{1,5},{2,6},{3,7},{4,8},{5,9},{6,10},{7,11},{8,12},{9,13},{1... | collective-permute-start | bytes 835592 | tf_op jit(solution)/shard_map/ppermute | solution.py:210
  6.7 5.3 %shard_map.56 = (bf16[32,16,256]{2,1,0:T(8,128)(2,1)}, bf16[32,16,256]{2,1,0:T(8,128)(2,1)}, bf16[34,16,256]{2,1,0:T(8,128)(2,1)}, bf16[32,16,256]{2,1,0:T(8,128...) custom-call(s32[16]{0:T(128)} %order_ref.5, ...), custom_call_target="tpu_custom_call" | custom-call | bytes 9469952 | tf_op jit(solution)/shard_map/pallas_call | solution.py:49
  12.0 1.4 %collective-permute-done.8.rest_5_.rest_8_ = bf16[32,16,256]{2,1,0:T(8,128)(2,1)S(1)} collective-permute-done((bf16[32,16,256]{2,1,0:T(8,128)(2,1)}, bf16[32,16,256]{2,1,0:T(8,128)(2,1)S(1)}, u32[]{:S(2)}, u32[]{:S(2)}) %collective-permute-start.8) | collective-permute-done | bytes 262176 | tf_op jit(solution)/shard_map/ppermute | solution.py:210
  13.4 1.7 %collective-permute-start.9 = (bf16[32,16,256]{2,1,0:T(8,128)(2,1)}, bf16[32,16,256]{2,1,0:T(8,128)(2,1)S(1)}, u32[]{:S(2)}, u32[]{:S(2)}) collective-permute-start(bf16[32,16,256]{2,1,0:T(8,128)(2,1)} %get-tuple-element.57), channel_id=1, source_target_pairs={{0,7},{1,6},{2,5},{3,4},{4,11},{5,10},{6,9},{7,8},{8,15},{9,14},{1... | collective-permute-start | bytes 786440 | tf_op jit(solution)/shard_map/ppermute | solution.py:210
  15.1 5.1 %collective-permute-done.rest_1_ = bf16[34,16,256]{2,1,0:T(8,128)(2,1)S(1)} collective-permute-done((bf16[34,16,256]{2,1,0:T(8,128)(2,1)}, bf16[34,16,256]{2,1,0:T(8,128)(2,1)S(1)}, u32[]{:S(2)}, u32[]{:S(2)}) %collective-permute-start) | collective-permute-done | bytes 278560 | tf_op jit(solution)/shard_map/ppermute | solution.py:210
  20.2 1.2 collective-permute-start.1
  21.4 2.7 %collective-permute-start.3 = (bf16[2,16,256]{2,1,0:T(8,128)(2,1)S(1)}, bf16[2,16,256]{2,1,0:T(8,128)(2,1)S(1)}, u32[]{:S(2)}, u32[]{:S(2)}) collective-permute-start(bf16[2,16,256]{2,1,0:T(8,128)(2,1)S(1)} %get-tuple-element.82), channel_id=1, source_target_pairs={{0,8},{1,9},{2,10},{3,11},{4,12},{5,13},{6,14},{7,15},{8,0},{9,1},... | collective-permute-start | bytes 49160 | tf_op jit(solution)/shard_map/ppermute | solution.py:210
  24.1 4.2 %all-to-all-start = ((bf16[4,32,16,256]{3,2,1,0:T(8,128)(2,1)}), bf16[4,32,16,256]{3,2,1,0:T(8,128)(2,1)}, u32[]{:S(2)}, u32[]{:S(2)}) async-start(bf16[4,32,16,256]{3,2,1,0:T(8,128)(2,1)} %get-tuple-element.51), calls=%async_computation | async-start | bytes 2097152 | tf_op jit(solution)/shard_map/all_to_all | solution.py:201
  28.4 0.0 copy-start.7
  28.4 0.0 copy-start.8
  28.4 1.8 %collective-permute-start.10 = (bf16[32,16,256]{2,1,0:T(8,128)(2,1)}, bf16[32,16,256]{2,1,0:T(8,128)(2,1)S(1)}, u32[]{:S(2)}, u32[]{:S(2)}) collective-permute-start(bf16[32,16,256]{2,1,0:T(8,128)(2,1)} %get-tuple-element.58), channel_id=1, source_target_pairs={{0,13},{1,12},{2,15},{3,14},{4,1},{5,0},{6,3},{7,2},{8,5},{9,4},{1... | collective-permute-start | bytes 786440 | tf_op jit(solution)/shard_map/ppermute | solution.py:210
  30.3 2.9 %collective-permute-done.1.rest_8_.rest_11_ = bf16[32,16,256]{2,1,0:T(8,128)(2,1)S(1)} collective-permute-done((bf16[32,16,256]{2,1,0:T(8,128)(2,1)}, bf16[32,16,256]{2,1,0:T(8,128)(2,1)S(1)}, u32[]{:S(2)}, u32[]{:S(2)}) %collective-permute-start.1) | collective-permute-done | bytes 262176 | tf_op jit(solution)/shard_map/ppermute | solution.py:210
  33.2 1.6 %collective-permute-start.2 = (bf16[34,16,256]{2,1,0:T(8,128)(2,1)}, bf16[34,16,256]{2,1,0:T(8,128)(2,1)S(1)}, u32[]{:S(2)}, u32[]{:S(2)}) collective-permute-start(bf16[34,16,256]{2,1,0:T(8,128)(2,1)} %get-tuple-element.48), channel_id=1, source_target_pairs={{0,12},{1,13},{2,14},{3,15},{4,0},{5,1},{6,2},{7,3},{8,4},{9,5},{1... | collective-permute-start | bytes 835592 | tf_op jit(solution)/shard_map/ppermute | solution.py:210
  34.8 2.9 %collective-permute-done.10.rest_6_.rest_9_ = bf16[32,16,256]{2,1,0:T(8,128)(2,1)S(1)} collective-permute-done((bf16[32,16,256]{2,1,0:T(8,128)(2,1)}, bf16[32,16,256]{2,1,0:T(8,128)(2,1)S(1)}, u32[]{:S(2)}, u32[]{:S(2)}) %collective-permute-start.10) | collective-permute-done | bytes 262176 | tf_op jit(solution)/shard_map/ppermute | solution.py:210
  37.7 0.7 copy-done.5
  38.4 0.7 collective-permute-start.11
  39.0 1.1 pad_maximum_fusion
  40.1 1.6 %collective-permute-start.16 = (bf16[4,32,16,256]{3,2,1,0:T(8,128)(2,1)}, bf16[4,32,16,256]{3,2,1,0:T(8,128)(2,1)S(1)}, u32[]{:S(2)}, u32[]{:S(2)}) collective-permute-start(bf16[4,32,16,256]{3,2,1,0:T(8,128)(2,1)} %pad_maximum_fusion), channel_id=1, source_target_pairs={{0,16},{16,0},{1,17},{17,1},{2,18},{18,2},{3,19},{19,3},{4,20},{20... | collective-permute-start | bytes 3145736 | tf_op jit(solution)/shard_map/ppermute | solution.py:213
  41.7 3.3 %collective-permute-start.15 = (bf16[32,16,256]{2,1,0:T(8,128)(2,1)}, bf16[32,16,256]{2,1,0:T(8,128)(2,1)}, u32[]{:S(2)}, u32[]{:S(2)}) collective-permute-start(bf16[32,16,256]{2,1,0:T(8,128)(2,1)} %get-tuple-element.67), channel_id=1, source_target_pairs={{0,15},{1,14},{2,13},{3,12},{4,3},{5,2},{6,1},{7,0},{8,7},{9,6},{1... | collective-permute-start | bytes 786440 | tf_op jit(solution)/shard_map/ppermute | solution.py:210
  45.0 3.1 %collective-permute-start.13 = (bf16[32,16,256]{2,1,0:T(8,128)(2,1)}, bf16[32,16,256]{2,1,0:T(8,128)(2,1)}, u32[]{:S(2)}, u32[]{:S(2)}) collective-permute-start(bf16[32,16,256]{2,1,0:T(8,128)(2,1)} %get-tuple-element.63), channel_id=1, source_target_pairs={{0,14},{1,15},{2,12},{3,13},{4,2},{5,3},{6,0},{7,1},{8,6},{9,7},{1... | collective-permute-start | bytes 786440 | tf_op jit(solution)/shard_map/ppermute | solution.py:210
  48.2 0.7 slice_bitcast_fusion
  48.9 0.1 collective-permute-start.12
  49.1 1.4 %fusion.2 = (bf16[4,16,16,256]{3,2,1,0:T(8,128)(2,1)S(1)}, bf16[4,16,16,256]{3,2,1,0:T(8,128)(2,1)S(1)}) fusion(bf16[4,32,16,256]{3,2,1,0:T(8,128)(2,1)} %all-to-all-done), kind=kLoop, calls=%fused_computation.11 | loop fusion | bytes 2097152 | tf_op jit(solution)/shard_map/slice | solution.py:258
  50.4 1.5 %collective-permute-done.15.rest_12_.rest_15_ = bf16[32,16,256]{2,1,0:T(8,128)(2,1)} collective-permute-done((bf16[32,16,256]{2,1,0:T(8,128)(2,1)}, bf16[32,16,256]{2,1,0:T(8,128)(2,1)}, u32[]{:S(2)}, u32[]{:S(2)}) %collective-permute-start.15) | collective-permute-done | bytes 262176 | tf_op jit(solution)/shard_map/ppermute | solution.py:210
  52.0 0.6 collective-permute-start.7
  52.5 5.1 %collective-permute-done.13.rest_9_.rest_12_ = bf16[32,16,256]{2,1,0:T(8,128)(2,1)} collective-permute-done((bf16[32,16,256]{2,1,0:T(8,128)(2,1)}, bf16[32,16,256]{2,1,0:T(8,128)(2,1)}, u32[]{:S(2)}, u32[]{:S(2)}) %collective-permute-start.13) | collective-permute-done | bytes 262176 | tf_op jit(solution)/shard_map/ppermute | solution.py:210
  57.6 1.3 %pad_maximum_fusion.1 = bf16[4,32,16,256]{3,2,1,0:T(8,128)(2,1)S(1)} fusion(bf16[1,32,16,256]{3,2,1,0:T(8,128)(2,1)} %bitcast.20, bf16[1,32,16,256]{3,2,1,0:T(8,128)(2,1)} %bitcast.19, bf16[1,32,16,256]{3,2,1,0:T(8,128)(2,1)} %bitcast.31, bf16[1,32,16,256]{3,2,1,0:T(8,128)(2,1)} %slice_bitcast_fusion), kind=kLoop, calls=%fused_computation.1 | loop fusion | flops 1572864 | bytes 2097152 | tf_op jit(solution)/shard_map/stack | solution.py:261
  58.9 0.6 collective-permute-start.17
  59.5 0.7 collective-permute-start.6
  60.2 8.1 %collective-permute-done.12.rest_7_.rest_10_.rest_4_ = bf16[64,16,256]{2,1,0:T(8,128)(2,1)S(1)} collective-permute-done((bf16[64,16,256]{2,1,0:T(8,128)(2,1)}, bf16[64,16,256]{2,1,0:T(8,128)(2,1)S(1)}, u32[]{:S(2)}, u32[]{:S(2)}) %collective-permute-start.12) | collective-permute-done | bytes 524320 | tf_op jit(solution)/shard_map/ppermute | solution.py:210
  68.3 1.7 %collective-permute-start.5 = (bf16[4,2,16,256]{3,2,1,0:T(8,128)(2,1)S(1)}, bf16[4,2,16,256]{3,2,1,0:T(8,128)(2,1)S(1)}, u32[]{:S(2)}, u32[]{:S(2)}) collective-permute-start(bf16[4,2,16,256]{3,2,1,0:T(8,128)(2,1)S(1)} %get-tuple-element.80), channel_id=1, source_target_pairs={{0,2},{1,3},{2,0},{3,1},{4,6},{5,7},{6,4},{7,5},{8,10},{9,11},{10,... | collective-permute-start | bytes 196616 | tf_op jit(solution)/shard_map/ppermute | solution.py:210
  70.1 1.0 collective-permute-start.14
  71.1 1.5 %collective-permute-done.5 = bf16[4,2,16,256]{3,2,1,0:T(8,128)(2,1)S(1)} collective-permute-done((bf16[4,2,16,256]{3,2,1,0:T(8,128)(2,1)S(1)}, bf16[4,2,16,256]{3,2,1,0:T(8,128)(2,1)S(1)}, u32[]{:S(2)}, u32[]{:S(2)}) %collective-permute-start.5) | collective-permute-done | bytes 65568 | tf_op jit(solution)/shard_map/ppermute | solution.py:210
  72.6 1.3 %collective-permute-done.4 = bf16[4,2,16,256]{3,2,1,0:T(8,128)(2,1)S(1)} collective-permute-done((bf16[4,2,16,256]{3,2,1,0:T(8,128)(2,1)S(1)}, bf16[4,2,16,256]{3,2,1,0:T(8,128)(2,1)S(1)}, u32[]{:S(2)}, u32[]{:S(2)}) %collective-permute-start.4) | collective-permute-done | bytes 65568 | tf_op jit(solution)/shard_map/ppermute | solution.py:210
  73.9 4.6 %collective-permute-start.18 = (bf16[4,16,16,256]{3,2,1,0:T(8,128)(2,1)S(1)}, bf16[4,16,16,256]{3,2,1,0:T(8,128)(2,1)S(1)}, u32[]{:S(2)}, u32[]{:S(2)}) collective-permute-start(bf16[4,16,16,256]{3,2,1,0:T(8,128)(2,1)S(1)} %get-tuple-element.72), channel_id=1, source_target_pairs={{0,8},{1,9},{2,10},{3,11},{4,12},{5,13},{6,14},{7,15},{8,0},{9,1},... | collective-permute-start | bytes 1572872 | tf_op jit(solution)/shard_map/ppermute | solution.py:210
  78.4 2.6 %collective-permute-done.7.rest_3_ = bf16[4,16,16,256]{3,2,1,0:T(8,128)(2,1)S(1)} collective-permute-done((bf16[4,16,16,256]{3,2,1,0:T(8,128)(2,1)S(1)}, bf16[4,16,16,256]{3,2,1,0:T(8,128)(2,1)S(1)}, u32[]{:S(2)}, u32[]{:S(2)}) %collective-permute-start.7) | collective-permute-done | bytes 524320 | tf_op jit(solution)/shard_map/ppermute | solution.py:210
  81.0 0.5 collective-permute-start.19
  81.5 2.7 %collective-permute-done.14.rest_10_.rest_13_.rest_5_ = bf16[64,16,256]{2,1,0:T(8,128)(2,1)S(1)} collective-permute-done((bf16[64,16,256]{2,1,0:T(8,128)(2,1)S(1)}, bf16[64,16,256]{2,1,0:T(8,128)(2,1)S(1)}, u32[]{:S(2)}, u32[]{:S(2)}) %collective-permute-start.14) | collective-permute-done | bytes 524320 | tf_op jit(solution)/shard_map/ppermute | solution.py:210
  84.2 3.9 %shard_map.57 = (bf16[256,16,256]{2,1,0:T(8,128)(2,1)S(1)}, bf16[256,16,256]{2,1,0:T(8,128)(2,1)S(1)}, bf16[256,256]{1,0:T(8,128)(2,1)S(1)}, bf16[256,256]{1,0:T(8,128)(2,1)S(1)}, bf16[256,256]{1,0:T(8,128)(2,1)S(1)}) custom-call(s32[16]{0:T(128)S(1)} %copy-done.8, s32[4,4,16]{2,1,0:T(4,128)S(1)} %bitcast.32, bf16[512,256]{1,0:T(8,128)(2,1)S(1)} %bitcast.27, ...), custom_call_target="tpu_custom_call" | custom-call | flops 1073741824 | bytes 6291456 | tf_op jit(solution)/shard_map/pallas_call | solution.py:324
  88.1 15.3 %collective-permute-done.18.rest_5_ = bf16[4,16,16,256]{3,2,1,0:T(8,128)(2,1)S(1)} collective-permute-done((bf16[4,16,16,256]{3,2,1,0:T(8,128)(2,1)S(1)}, bf16[4,16,16,256]{3,2,1,0:T(8,128)(2,1)S(1)}, u32[]{:S(2)}, u32[]{:S(2)}) %collective-permute-start.18) | collective-permute-done | bytes 524320 | tf_op jit(solution)/shard_map/ppermute | solution.py:210
  103.5 0.6 collective-permute-start.20
  104.0 5.5 %shard_map.58 = (bf16[256,32,256]{2,1,0:T(8,128)(2,1)S(1)}, bf16[256,32,256]{2,1,0:T(8,128)(2,1)S(1)}) custom-call(bf16[256,256]{1,0:T(8,128)(2,1)S(1)} %get-tuple-element.68.occ_ref, bf16[256,256]{1,0:T(8,128)(2,1)S(1)} %get-tuple-element.69.vir_ref, bf16[256,256]{1,0:T(8,128)(2,1)S(1)} %get-tuple-element.70.keep_ref, bf16[64,16,256]{2,1,0:T(8,128)(2,1)S(1)} %copy-done, ...), custom_call_target="tpu_custom_call" | custom-call | flops 2147483648 | bytes 12582912 | tf_op jit(solution)/shard_map/pallas_call | solution.py:336
  109.6 7.8 %collective-permute-done.20.rest_6_ = bf16[4,16,16,256]{3,2,1,0:T(8,128)(2,1)S(1)} collective-permute-done((bf16[4,16,16,256]{3,2,1,0:T(8,128)(2,1)S(1)}, bf16[4,16,16,256]{3,2,1,0:T(8,128)(2,1)S(1)}, u32[]{:S(2)}, u32[]{:S(2)}) %collective-permute-start.20) | collective-permute-done | bytes 524320 | tf_op jit(solution)/shard_map/ppermute | solution.py:213
  117.4 5.8 %shard_map.59 = f32[64,64]{1,0:T(8,128)} custom-call(bf16[256,256]{1,0:T(8,128)(2,1)S(1)} %get-tuple-element.68.occ_ref, bf16[256,256]{1,0:T(8,128)(2,1)S(1)} %get-tuple-element.69.vir_ref, bf16[256,256]{1,0:T(8,128)(2,1)S(1)} %get-tuple-element.70.keep_ref, bf16[256,16,256]{2,1,0:T(8,128)(2,1)S(1)} %get-tuple-element.71.mask_a, ...), custom_call_target="tpu_custom_call" | custom-call | flops 1073741824 | bytes 16777216 | tf_op jit(solution)/shard_map/pallas_call | solution.py:346
  (35 shorter events, 0.1 us)
Async XLA Ops:
  2.6 18.8 %copy-start.9 = (bf16[16,256]{1,0:T(8,128)(2,1)S(1)}, bf16[16,256]{1,0:T(8,128)(2,1)}, u32[]{:S(2)}) copy-start(bf16[16,256]{1,0:T(8,128)(2,1)} %vir_ref.3) | copy-start | bytes 24580
  2.6 18.8 %copy-start.10 = (bf16[16,256]{1,0:T(8,128)(2,1)S(1)}, bf16[16,256]{1,0:T(8,128)(2,1)}, u32[]{:S(2)}) copy-start(bf16[16,256]{1,0:T(8,128)(2,1)} %occ_ref.3) | copy-start | bytes 24580
  2.6 10.8 %collective-permute-start.8 = (bf16[32,16,256]{2,1,0:T(8,128)(2,1)}, bf16[32,16,256]{2,1,0:T(8,128)(2,1)S(1)}, u32[]{:S(2)}, u32[]{:S(2)}) collective-permute-start(bf16[32,16,256]{2,1,0:T(8,128)(2,1)} %get-tuple-element.56), channel_id=1, source_target_pairs={{0,5},{1,4},{2,7},{3,6},{4,9},{5,8},{6,11},{7,10},{8,13},{9,12},{1... | collective-permute-start | bytes 786440 | tf_op jit(solution)/shard_map/ppermute | solution.py:210
  5.1 15.1 %collective-permute-start = (bf16[34,16,256]{2,1,0:T(8,128)(2,1)}, bf16[34,16,256]{2,1,0:T(8,128)(2,1)S(1)}, u32[]{:S(2)}, u32[]{:S(2)}) collective-permute-start(bf16[34,16,256]{2,1,0:T(8,128)(2,1)} %get-tuple-element.43), channel_id=1, source_target_pairs={{0,4},{1,5},{2,6},{3,7},{4,8},{5,9},{6,10},{7,11},{8,12},{9,13},{1... | collective-permute-start | bytes 835592 | tf_op jit(solution)/shard_map/ppermute | solution.py:210
  13.4 15.0 %collective-permute-start.9 = (bf16[32,16,256]{2,1,0:T(8,128)(2,1)}, bf16[32,16,256]{2,1,0:T(8,128)(2,1)S(1)}, u32[]{:S(2)}, u32[]{:S(2)}) collective-permute-start(bf16[32,16,256]{2,1,0:T(8,128)(2,1)} %get-tuple-element.57), channel_id=1, source_target_pairs={{0,7},{1,6},{2,5},{3,4},{4,11},{5,10},{6,9},{7,8},{8,15},{9,14},{1... | collective-permute-start | bytes 786440 | tf_op jit(solution)/shard_map/ppermute | solution.py:210
  20.2 13.0 %collective-permute-start.1 = (bf16[32,16,256]{2,1,0:T(8,128)(2,1)}, bf16[32,16,256]{2,1,0:T(8,128)(2,1)S(1)}, u32[]{:S(2)}, u32[]{:S(2)}) collective-permute-start(bf16[32,16,256]{2,1,0:T(8,128)(2,1)} %get-tuple-element.47), channel_id=1, source_target_pairs={{0,6},{1,7},{2,4},{3,5},{4,10},{5,11},{6,8},{7,9},{8,14},{9,15},{1... | collective-permute-start | bytes 786440 | tf_op jit(solution)/shard_map/ppermute | solution.py:210
  21.4 38.1 %collective-permute-start.3 = (bf16[2,16,256]{2,1,0:T(8,128)(2,1)S(1)}, bf16[2,16,256]{2,1,0:T(8,128)(2,1)S(1)}, u32[]{:S(2)}, u32[]{:S(2)}) collective-permute-start(bf16[2,16,256]{2,1,0:T(8,128)(2,1)S(1)} %get-tuple-element.82), channel_id=1, source_target_pairs={{0,8},{1,9},{2,10},{3,11},{4,12},{5,13},{6,14},{7,15},{8,0},{9,1},... | collective-permute-start | bytes 49160 | tf_op jit(solution)/shard_map/ppermute | solution.py:210
  24.1 25.0 %all-to-all-start = ((bf16[4,32,16,256]{3,2,1,0:T(8,128)(2,1)}), bf16[4,32,16,256]{3,2,1,0:T(8,128)(2,1)}, u32[]{:S(2)}, u32[]{:S(2)}) async-start(bf16[4,32,16,256]{3,2,1,0:T(8,128)(2,1)} %get-tuple-element.51), calls=%async_computation | async-start | bytes 2097152 | tf_op jit(solution)/shard_map/all_to_all | solution.py:201
  28.3 55.8 %copy-start = (bf16[64,16,256]{2,1,0:T(8,128)(2,1)S(1)}, bf16[64,16,256]{2,1,0:T(8,128)(2,1)}, u32[]{:S(2)}) copy-start(bf16[64,16,256]{2,1,0:T(8,128)(2,1)} %get-tuple-element.49.rest_0_) | copy-start | bytes 1572868
  28.4 55.8 %copy-start.7 = (s32[16,4,4]{0,2,1:T(4,128)S(1)}, s32[16,4,4]{0,2,1:T(4,128)}, u32[]{:S(2)}) copy-start(s32[16,4,4]{0,2,1:T(4,128)} %param.8) | copy-start | bytes 3076
  28.4 55.8 %copy-start.8 = (s32[16]{0:T(128)S(1)}, s32[16]{0:T(128)}, u32[]{:S(2)}) copy-start(s32[16]{0:T(128)} %order_ref.5) | copy-start | bytes 196
  28.4 20.5 %copy-start.1 = (bf16[32,16,256]{2,1,0:T(8,128)(2,1)}, bf16[32,16,256]{2,1,0:T(8,128)(2,1)S(1)}, u32[]{:S(2)}) copy-start(bf16[32,16,256]{2,1,0:T(8,128)(2,1)S(1)} %collective-permute-done.9.rest_11_.rest_14_) | copy-start | bytes 786436
  28.4 9.3 %collective-permute-start.10 = (bf16[32,16,256]{2,1,0:T(8,128)(2,1)}, bf16[32,16,256]{2,1,0:T(8,128)(2,1)S(1)}, u32[]{:S(2)}, u32[]{:S(2)}) collective-permute-start(bf16[32,16,256]{2,1,0:T(8,128)(2,1)} %get-tuple-element.58), channel_id=1, source_target_pairs={{0,13},{1,12},{2,15},{3,14},{4,1},{5,0},{6,3},{7,2},{8,5},{9,4},{1... | collective-permute-start | bytes 786440 | tf_op jit(solution)/shard_map/ppermute | solution.py:210
  33.2 15.7 %copy-start.3 = (bf16[32,16,256]{2,1,0:T(8,128)(2,1)}, bf16[32,16,256]{2,1,0:T(8,128)(2,1)S(1)}, u32[]{:S(2)}) copy-start(bf16[32,16,256]{2,1,0:T(8,128)(2,1)S(1)} %collective-permute-done.1.rest_8_.rest_11_) | copy-start | bytes 786436
  33.2 11.8 %collective-permute-start.2 = (bf16[34,16,256]{2,1,0:T(8,128)(2,1)}, bf16[34,16,256]{2,1,0:T(8,128)(2,1)S(1)}, u32[]{:S(2)}, u32[]{:S(2)}) collective-permute-start(bf16[34,16,256]{2,1,0:T(8,128)(2,1)} %get-tuple-element.48), channel_id=1, source_target_pairs={{0,12},{1,13},{2,14},{3,15},{4,0},{5,1},{6,2},{7,3},{8,4},{9,5},{1... | collective-permute-start | bytes 835592 | tf_op jit(solution)/shard_map/ppermute | solution.py:210
  37.7 0.7 copy-start.5
  38.4 10.5 %collective-permute-start.11 = (bf16[64,16,256]{2,1,0:T(8,128)(2,1)}, bf16[64,16,256]{2,1,0:T(8,128)(2,1)S(1)}, u32[]{:S(2)}, u32[]{:S(2)}) collective-permute-start(bf16[64,16,256]{2,1,0:T(8,128)(2,1)} %get-tuple-element.59), channel_id=1, source_target_pairs={{0,1},{1,0},{2,3},{3,2},{4,5},{5,4},{6,7},{7,6},{8,9},{9,8},{10,11... | collective-permute-start | bytes 1572872 | tf_op jit(solution)/shard_map/ppermute | solution.py:210
  40.1 63.9 %collective-permute-start.16 = (bf16[4,32,16,256]{3,2,1,0:T(8,128)(2,1)}, bf16[4,32,16,256]{3,2,1,0:T(8,128)(2,1)S(1)}, u32[]{:S(2)}, u32[]{:S(2)}) collective-permute-start(bf16[4,32,16,256]{3,2,1,0:T(8,128)(2,1)} %pad_maximum_fusion), channel_id=1, source_target_pairs={{0,16},{16,0},{1,17},{17,1},{2,18},{18,2},{3,19},{19,3},{4,20},{20... | collective-permute-start | bytes 3145736 | tf_op jit(solution)/shard_map/ppermute | solution.py:213
  41.7 10.3 %collective-permute-start.15 = (bf16[32,16,256]{2,1,0:T(8,128)(2,1)}, bf16[32,16,256]{2,1,0:T(8,128)(2,1)}, u32[]{:S(2)}, u32[]{:S(2)}) collective-permute-start(bf16[32,16,256]{2,1,0:T(8,128)(2,1)} %get-tuple-element.67), channel_id=1, source_target_pairs={{0,15},{1,14},{2,13},{3,12},{4,3},{5,2},{6,1},{7,0},{8,7},{9,6},{1... | collective-permute-start | bytes 786440 | tf_op jit(solution)/shard_map/ppermute | solution.py:210
  45.0 12.6 %collective-permute-start.13 = (bf16[32,16,256]{2,1,0:T(8,128)(2,1)}, bf16[32,16,256]{2,1,0:T(8,128)(2,1)}, u32[]{:S(2)}, u32[]{:S(2)}) collective-permute-start(bf16[32,16,256]{2,1,0:T(8,128)(2,1)} %get-tuple-element.63), channel_id=1, source_target_pairs={{0,14},{1,15},{2,12},{3,13},{4,2},{5,3},{6,0},{7,1},{8,6},{9,7},{1... | collective-permute-start | bytes 786440 | tf_op jit(solution)/shard_map/ppermute | solution.py:210
  48.9 19.5 %collective-permute-start.12 = (bf16[64,16,256]{2,1,0:T(8,128)(2,1)}, bf16[64,16,256]{2,1,0:T(8,128)(2,1)S(1)}, u32[]{:S(2)}, u32[]{:S(2)}) collective-permute-start(bf16[64,16,256]{2,1,0:T(8,128)(2,1)} %get-tuple-element.61), channel_id=1, source_target_pairs={{0,2},{1,3},{2,0},{3,1},{4,6},{5,7},{6,4},{7,5},{8,10},{9,11},{10,... | collective-permute-start | bytes 1572872 | tf_op jit(solution)/shard_map/ppermute | solution.py:210
  49.0 21.0 %copy-start.11 = (bf16[64,16,256]{2,1,0:T(8,128)(2,1)S(1)}, bf16[64,16,256]{2,1,0:T(8,128)(2,1)}, u32[]{:S(2)}) copy-start(bf16[64,16,256]{2,1,0:T(8,128)(2,1)} %get-tuple-element.65) | copy-start | bytes 1572868
  49.0 35.2 %copy-start.2 = (bf16[32,16,256]{2,1,0:T(8,128)(2,1)S(1)}, bf16[32,16,256]{2,1,0:T(8,128)(2,1)}, u32[]{:S(2)}) copy-start(bf16[32,16,256]{2,1,0:T(8,128)(2,1)} %copy-done.1) | copy-start | bytes 786436
  49.0 35.2 %copy-start.4 = (bf16[32,16,256]{2,1,0:T(8,128)(2,1)S(1)}, bf16[32,16,256]{2,1,0:T(8,128)(2,1)}, u32[]{:S(2)}) copy-start(bf16[32,16,256]{2,1,0:T(8,128)(2,1)} %copy-done.3) | copy-start | bytes 786436
  49.1 35.2 %copy-start.6 = (bf16[32,16,256]{2,1,0:T(8,128)(2,1)S(1)}, bf16[32,16,256]{2,1,0:T(8,128)(2,1)}, u32[]{:S(2)}) copy-start(bf16[32,16,256]{2,1,0:T(8,128)(2,1)} %copy-done.5) | copy-start | bytes 786436
  52.0 29.0 %collective-permute-start.7 = (bf16[4,16,16,256]{3,2,1,0:T(8,128)(2,1)S(1)}, bf16[4,16,16,256]{3,2,1,0:T(8,128)(2,1)S(1)}, u32[]{:S(2)}, u32[]{:S(2)}) collective-permute-start(bf16[4,16,16,256]{3,2,1,0:T(8,128)(2,1)S(1)} %get-tuple-element.52), channel_id=1, source_target_pairs={{0,8},{1,9},{2,10},{3,11},{4,12},{5,13},{6,14},{7,15},{8,0},{9,1},... | collective-permute-start | bytes 1572872 | tf_op jit(solution)/shard_map/ppermute | solution.py:210
  58.9 45.1 %collective-permute-start.17 = (bf16[4,32,16,256]{3,2,1,0:T(8,128)(2,1)S(1)}, bf16[4,32,16,256]{3,2,1,0:T(8,128)(2,1)S(1)}, u32[]{:S(2)}, u32[]{:S(2)}) collective-permute-start(bf16[4,32,16,256]{3,2,1,0:T(8,128)(2,1)S(1)} %pad_maximum_fusion.1), channel_id=1, source_target_pairs={{0,16},{16,0},{1,17},{17,1},{2,18},{18,2},{3,19},{19,3},{4,20},{20... | collective-permute-start | bytes 3145736 | tf_op jit(solution)/shard_map/ppermute | solution.py:213
  59.5 10.5 %collective-permute-start.6 = (bf16[4,2,16,256]{3,2,1,0:T(8,128)(2,1)S(1)}, bf16[4,2,16,256]{3,2,1,0:T(8,128)(2,1)S(1)}, u32[]{:S(2)}, u32[]{:S(2)}) collective-permute-start(bf16[4,2,16,256]{3,2,1,0:T(8,128)(2,1)S(1)} %get-tuple-element.80), channel_id=1, source_target_pairs={{0,3},{1,2},{2,1},{3,0},{4,7},{5,6},{6,5},{7,4},{8,11},{9,10},{10,... | collective-permute-start | bytes 196616 | tf_op jit(solution)/shard_map/ppermute | solution.py:210
  68.3 4.3 %collective-permute-start.5 = (bf16[4,2,16,256]{3,2,1,0:T(8,128)(2,1)S(1)}, bf16[4,2,16,256]{3,2,1,0:T(8,128)(2,1)S(1)}, u32[]{:S(2)}, u32[]{:S(2)}) collective-permute-start(bf16[4,2,16,256]{3,2,1,0:T(8,128)(2,1)S(1)} %get-tuple-element.80), channel_id=1, source_target_pairs={{0,2},{1,3},{2,0},{3,1},{4,6},{5,7},{6,4},{7,5},{8,10},{9,11},{10,... | collective-permute-start | bytes 196616 | tf_op jit(solution)/shard_map/ppermute | solution.py:210
  70.1 14.1 %collective-permute-start.14 = (bf16[64,16,256]{2,1,0:T(8,128)(2,1)S(1)}, bf16[64,16,256]{2,1,0:T(8,128)(2,1)S(1)}, u32[]{:S(2)}, u32[]{:S(2)}) collective-permute-start(bf16[64,16,256]{2,1,0:T(8,128)(2,1)S(1)} %copy-done.11), channel_id=1, source_target_pairs={{0,3},{1,2},{2,1},{3,0},{4,7},{5,6},{6,5},{7,4},{8,11},{9,10},{10,... | collective-permute-start | bytes 1572872 | tf_op jit(solution)/shard_map/ppermute | solution.py:210
  72.6 1.3 %collective-permute-start.4 = (bf16[4,2,16,256]{3,2,1,0:T(8,128)(2,1)S(1)}, bf16[4,2,16,256]{3,2,1,0:T(8,128)(2,1)S(1)}, u32[]{:S(2)}, u32[]{:S(2)}) collective-permute-start(bf16[4,2,16,256]{3,2,1,0:T(8,128)(2,1)S(1)} %get-tuple-element.80), channel_id=1, source_target_pairs={{0,1},{1,0},{2,3},{3,2},{4,5},{5,4},{6,7},{7,6},{8,9},{9,8},{10,11... | collective-permute-start | bytes 196616 | tf_op jit(solution)/shard_map/ppermute | solution.py:210
  73.9 29.6 %collective-permute-start.18 = (bf16[4,16,16,256]{3,2,1,0:T(8,128)(2,1)S(1)}, bf16[4,16,16,256]{3,2,1,0:T(8,128)(2,1)S(1)}, u32[]{:S(2)}, u32[]{:S(2)}) collective-permute-start(bf16[4,16,16,256]{3,2,1,0:T(8,128)(2,1)S(1)} %get-tuple-element.72), channel_id=1, source_target_pairs={{0,8},{1,9},{2,10},{3,11},{4,12},{5,13},{6,14},{7,15},{8,0},{9,1},... | collective-permute-start | bytes 1572872 | tf_op jit(solution)/shard_map/ppermute | solution.py:210
  81.0 23.0 %collective-permute-start.19 = (bf16[4,16,16,256]{3,2,1,0:T(8,128)(2,1)S(1)}, bf16[4,16,16,256]{3,2,1,0:T(8,128)(2,1)S(1)}, u32[]{:S(2)}, u32[]{:S(2)}) collective-permute-start(bf16[4,16,16,256]{3,2,1,0:T(8,128)(2,1)S(1)} %collective-permute-done.7.rest_3_), channel_id=1, source_target_pairs={{0,16},{16,0},{1,17},{17,1},{2,18},{18,2},{3,19},{19,3},{4,20},{20... | collective-permute-start | bytes 1572872 | tf_op jit(solution)/shard_map/ppermute | solution.py:213
  103.5 13.9 %collective-permute-start.20 = (bf16[4,16,16,256]{3,2,1,0:T(8,128)(2,1)S(1)}, bf16[4,16,16,256]{3,2,1,0:T(8,128)(2,1)S(1)}, u32[]{:S(2)}, u32[]{:S(2)}) collective-permute-start(bf16[4,16,16,256]{3,2,1,0:T(8,128)(2,1)S(1)} %collective-permute-done.18.rest_5_), channel_id=1, source_target_pairs={{0,16},{16,0},{1,17},{17,1},{2,18},{18,2},{3,19},{19,3},{4,20},{20... | collective-permute-start | bytes 1572872 | tf_op jit(solution)/shard_map/ppermute | solution.py:213

commit v10 on v9

--- a/solution.py
+++ b/solution.py
@@ -246,7 +246,7 @@
     base = jnp.stack([occupied, virtual])
     came, swapped = [], []
     came = [None] * len(direct)
-    row = [PLANE * (n // PLANE) + (1, 0, 3, 2, 1, 0, 3, 2)[n % 8] for n in range(len(direct))]
+    row = [PLANE * (n // PLANE) + (0, 1, 3, 2, 0, 3, 2, 1)[n % 8] for n in range(len(direct))]
     for n, at in enumerate(row):
         piece = direct[at]
         if n >= WINDOW:

time: 124 us -> 123 us (level)
  waiting for transfers between devices: 58.1 us -> 66.2 us
  starting transfers between devices: 36.5 us -> 29 us
    ppermute x17, starting transfers between devices: 29 us -> 18.6 us  [shift(): return lax.ppermute(x, 'wide', pairs)]
    ppermute x17, waiting for transfers between devices: 50.2 us -> 59.1 us  [shift(): return lax.ppermute(x, 'wide', pairs)]
    ppermute x4, starting transfers between devices: 3.21 us -> 6.12 us  [swap(): return lax.ppermute(x, 'groups', [(0, 1), (1, 0)])]
    ppermute x4, waiting for transfers between devices: 7.82 us -> 6.53 us  [swap(): return lax.ppermute(x, 'groups', [(0, 1), (1, 0)])]
  transfers between devices with their start and end apart: 22 -> 22, of which waited for: 13 -> 16; matrix products, arithmetic and copies ran while one was open for 4% -> 4% of each run, Pallas kernels for 12% -> 12%
where the time goes in v10:
time: 123 us
  waiting for transfers between devices  66.2 us (54%)
  starting transfers between devices  29 us (24%)
  Pallas kernels  23 us (19%)
  other arithmetic  2.47 us (2%)
  local copies, waits for them, and re-layouts  2.17 us (2%)
    ppermute x17, waiting for transfers between devices, shift(): return lax.ppermute(x, 'wide', pairs)  59.1 us
    ppermute x17, starting transfers between devices, shift(): return lax.ppermute(x, 'wide', pairs)  18.6 us
    pallas_call x2, Pallas kernels, gather(): pl.pallas_call(functools.partial(gather_kernel, plan, tails, outer, half,...  7.84 us
    ppermute x4, waiting for transfers between devices, swap(): return lax.ppermute(x, 'groups', [(0, 1), (1, 0)])  6.53 us
    ppermute x4, starting transfers between devices, swap(): return lax.ppermute(x, 'groups', [(0, 1), (1, 0)])  6.12 us
    pallas_call x1, Pallas kernels, shards(): pl.pallas_call(functools.partial(back_kernel, rows_of, len(arrays)), out_...  5.83 us
    pallas_call x1, Pallas kernels, shards(): pl.pallas_call(functools.partial(middle_kernel, rows_of, len(arrays)), ou...  5.48 us
    all_to_all x1, starting transfers between devices, inplane(): lax.all_to_all(x, 'wide', split_axis=0, concat_axis=0, tiled=True, axis_i...  4.25 us
  transfers between devices with their start and end apart: 22, of which 16 were waited for; matrix products, arithmetic and copies ran while one was open for 4% of the time, Pallas kernels for 12%

profile of v10, /device:TPU:0, one launch (start us, length us, event | category | flops | bytes accessed | tf_op | source)
XLA Modules:
  0.0 123.0 jit_solution(16735828539283995960)
XLA Ops:
  0.0 2.5 %shard_map.55 = (bf16[34,16,256]{2,1,0:T(8,128)(2,1)}, bf16[32,16,256]{2,1,0:T(8,128)(2,1)}) custom-call(s32[16]{0:T(128)} %order_ref.5, bf16[16,64,16,256]{3,2,1,0:T(8,128)(2,1)} %bitcast.33, bf16[16,256]{1,0:T(8,128)(2,1)} %occ_ref.3, bf16[16,256]{1,0:T(8,128)(2,1)} %vir_ref.3), custom_call_target="tpu_custom_call" | custom-call | bytes 1081344 | tf_op jit(solution)/shard_map/pallas_call | solution.py:49
  2.6 0.0 copy-start.9
  2.6 0.0 copy-start.10
  2.6 3.1 %collective-permute-start = (bf16[34,16,256]{2,1,0:T(8,128)(2,1)}, bf16[34,16,256]{2,1,0:T(8,128)(2,1)S(1)}, u32[]{:S(2)}, u32[]{:S(2)}) collective-permute-start(bf16[34,16,256]{2,1,0:T(8,128)(2,1)} %get-tuple-element.43), channel_id=1, source_target_pairs={{0,4},{1,5},{2,6},{3,7},{4,8},{5,9},{6,10},{7,11},{8,12},{9,13},{1... | collective-permute-start | bytes 835592 | tf_op jit(solution)/shard_map/ppermute | solution.py:210
  5.7 0.7 collective-permute-start.7
  6.4 5.3 %shard_map.56 = (bf16[32,16,256]{2,1,0:T(8,128)(2,1)}, bf16[32,16,256]{2,1,0:T(8,128)(2,1)}, bf16[34,16,256]{2,1,0:T(8,128)(2,1)}, bf16[32,16,256]{2,1,0:T(8,128...) custom-call(s32[16]{0:T(128)} %order_ref.5, ...), custom_call_target="tpu_custom_call" | custom-call | bytes 9469952 | tf_op jit(solution)/shard_map/pallas_call | solution.py:49
  11.7 3.7 %collective-permute-done.rest_1_ = bf16[34,16,256]{2,1,0:T(8,128)(2,1)S(1)} collective-permute-done((bf16[34,16,256]{2,1,0:T(8,128)(2,1)}, bf16[34,16,256]{2,1,0:T(8,128)(2,1)S(1)}, u32[]{:S(2)}, u32[]{:S(2)}) %collective-permute-start) | collective-permute-done | bytes 278560 | tf_op jit(solution)/shard_map/ppermute | solution.py:210
  15.4 4.0 %collective-permute-done.7.rest_5_.rest_8_ = bf16[32,16,256]{2,1,0:T(8,128)(2,1)S(1)} collective-permute-done((bf16[32,16,256]{2,1,0:T(8,128)(2,1)}, bf16[32,16,256]{2,1,0:T(8,128)(2,1)S(1)}, u32[]{:S(2)}, u32[]{:S(2)}) %collective-permute-start.7) | collective-permute-done | bytes 262176 | tf_op jit(solution)/shard_map/ppermute | solution.py:210
  19.3 1.8 %collective-permute-start.8 = (bf16[32,16,256]{2,1,0:T(8,128)(2,1)}, bf16[32,16,256]{2,1,0:T(8,128)(2,1)S(1)}, u32[]{:S(2)}, u32[]{:S(2)}) collective-permute-start(bf16[32,16,256]{2,1,0:T(8,128)(2,1)} %get-tuple-element.55), channel_id=1, source_target_pairs={{0,6},{1,7},{2,4},{3,5},{4,10},{5,11},{6,8},{7,9},{8,14},{9,15},{1... | collective-permute-start | bytes 786440 | tf_op jit(solution)/shard_map/ppermute | solution.py:210
  21.2 1.2 collective-permute-start.3
  22.3 4.2 %all-to-all-start = ((bf16[4,32,16,256]{3,2,1,0:T(8,128)(2,1)}), bf16[4,32,16,256]{3,2,1,0:T(8,128)(2,1)}, u32[]{:S(2)}, u32[]{:S(2)}) async-start(bf16[4,32,16,256]{3,2,1,0:T(8,128)(2,1)} %get-tuple-element.52), calls=%async_computation | async-start | bytes 2097152 | tf_op jit(solution)/shard_map/all_to_all | solution.py:201
  26.6 0.0 copy-start.7
  26.6 0.0 copy-start.8
  26.6 0.4 collective-permute-done.1.rest_11_.rest_14_
  27.1 2.5 %collective-permute-start.2 = (bf16[34,16,256]{2,1,0:T(8,128)(2,1)}, bf16[34,16,256]{2,1,0:T(8,128)(2,1)S(1)}, u32[]{:S(2)}, u32[]{:S(2)}) collective-permute-start(bf16[34,16,256]{2,1,0:T(8,128)(2,1)} %get-tuple-element.49), channel_id=1, source_target_pairs={{0,12},{1,13},{2,14},{3,15},{4,0},{5,1},{6,2},{7,3},{8,4},{9,5},{1... | collective-permute-start | bytes 835592 | tf_op jit(solution)/shard_map/ppermute | solution.py:210
  29.6 2.8 %collective-permute-done.8.rest_8_.rest_11_ = bf16[32,16,256]{2,1,0:T(8,128)(2,1)S(1)} collective-permute-done((bf16[32,16,256]{2,1,0:T(8,128)(2,1)}, bf16[32,16,256]{2,1,0:T(8,128)(2,1)S(1)}, u32[]{:S(2)}, u32[]{:S(2)}) %collective-permute-start.8) | collective-permute-done | bytes 262176 | tf_op jit(solution)/shard_map/ppermute | solution.py:210
  32.4 1.1 collective-permute-start.9
  33.5 4.2 %collective-permute-done.2.rest_2_.rest_3_ = bf16[34,16,256]{2,1,0:T(8,128)(2,1)S(1)} collective-permute-done((bf16[34,16,256]{2,1,0:T(8,128)(2,1)}, bf16[34,16,256]{2,1,0:T(8,128)(2,1)S(1)}, u32[]{:S(2)}, u32[]{:S(2)}) %collective-permute-start.2) | collective-permute-done | bytes 278560 | tf_op jit(solution)/shard_map/ppermute | solution.py:210
  37.7 0.3 collective-permute-start.11
  38.0 1.1 pad_maximum_fusion
  39.1 1.5 %collective-permute-start.16 = (bf16[4,32,16,256]{3,2,1,0:T(8,128)(2,1)}, bf16[4,32,16,256]{3,2,1,0:T(8,128)(2,1)S(1)}, u32[]{:S(2)}, u32[]{:S(2)}) collective-permute-start(bf16[4,32,16,256]{3,2,1,0:T(8,128)(2,1)} %pad_maximum_fusion), channel_id=1, source_target_pairs={{0,16},{16,0},{1,17},{17,1},{2,18},{18,2},{3,19},{19,3},{4,20},{20... | collective-permute-start | bytes 3145736 | tf_op jit(solution)/shard_map/ppermute | solution.py:213
  40.6 3.7 %collective-permute-done.9.rest_12_.rest_15_ = bf16[32,16,256]{2,1,0:T(8,128)(2,1)S(1)} collective-permute-done((bf16[32,16,256]{2,1,0:T(8,128)(2,1)}, bf16[32,16,256]{2,1,0:T(8,128)(2,1)S(1)}, u32[]{:S(2)}, u32[]{:S(2)}) %collective-permute-start.9) | collective-permute-done | bytes 262176 | tf_op jit(solution)/shard_map/ppermute | solution.py:210
  44.3 2.5 %collective-permute-start.12 = (bf16[32,16,256]{2,1,0:T(8,128)(2,1)}, bf16[32,16,256]{2,1,0:T(8,128)(2,1)}, u32[]{:S(2)}, u32[]{:S(2)}) collective-permute-start(bf16[32,16,256]{2,1,0:T(8,128)(2,1)} %get-tuple-element.61), channel_id=1, source_target_pairs={{0,13},{1,12},{2,15},{3,14},{4,1},{5,0},{6,3},{7,2},{8,5},{9,4},{1... | collective-permute-start | bytes 786440 | tf_op jit(solution)/shard_map/ppermute | solution.py:210
  46.8 0.7 slice_bitcast_fusion
  47.5 1.3 %collective-permute-start.13 = (bf16[64,16,256]{2,1,0:T(8,128)(2,1)}, bf16[64,16,256]{2,1,0:T(8,128)(2,1)S(1)}, u32[]{:S(2)}, u32[]{:S(2)}) collective-permute-start(bf16[64,16,256]{2,1,0:T(8,128)(2,1)} %get-tuple-element.63), channel_id=1, source_target_pairs={{0,2},{1,3},{2,0},{3,1},{4,6},{5,7},{6,4},{7,5},{8,10},{9,11},{10,... | collective-permute-start | bytes 1572872 | tf_op jit(solution)/shard_map/ppermute | solution.py:210
  48.8 0.6 all-to-all-done
  49.4 1.4 %fusion.2 = (bf16[4,16,16,256]{3,2,1,0:T(8,128)(2,1)S(1)}, bf16[4,16,16,256]{3,2,1,0:T(8,128)(2,1)S(1)}) fusion(bf16[4,32,16,256]{3,2,1,0:T(8,128)(2,1)} %all-to-all-done), kind=kLoop, calls=%fused_computation.11 | loop fusion | bytes 2097152 | tf_op jit(solution)/shard_map/slice | solution.py:258
  50.8 3.0 %collective-permute-done.12.rest_6_.rest_9_ = bf16[32,16,256]{2,1,0:T(8,128)(2,1)} collective-permute-done((bf16[32,16,256]{2,1,0:T(8,128)(2,1)}, bf16[32,16,256]{2,1,0:T(8,128)(2,1)}, u32[]{:S(2)}, u32[]{:S(2)}) %collective-permute-start.12) | collective-permute-done | bytes 262176 | tf_op jit(solution)/shard_map/ppermute | solution.py:210
  53.8 0.7 collective-permute-start.10
  54.5 5.0 %collective-permute-done.14.rest_9_.rest_12_ = bf16[32,16,256]{2,1,0:T(8,128)(2,1)} collective-permute-done((bf16[32,16,256]{2,1,0:T(8,128)(2,1)}, bf16[32,16,256]{2,1,0:T(8,128)(2,1)}, u32[]{:S(2)}, u32[]{:S(2)}) %collective-permute-start.14) | collective-permute-done | bytes 262176 | tf_op jit(solution)/shard_map/ppermute | solution.py:210
  59.4 1.3 %pad_maximum_fusion.1 = bf16[4,32,16,256]{3,2,1,0:T(8,128)(2,1)S(1)} fusion(bf16[1,32,16,256]{3,2,1,0:T(8,128)(2,1)} %bitcast.31, bf16[1,32,16,256]{3,2,1,0:T(8,128)(2,1)} %bitcast.19, bf16[1,32,16,256]{3,2,1,0:T(8,128)(2,1)} %bitcast.18, bf16[1,32,16,256]{3,2,1,0:T(8,128)(2,1)} %slice_bitcast_fusion), kind=kLoop, calls=%fused_computation.1 | loop fusion | flops 1572864 | bytes 2097152 | tf_op jit(solution)/shard_map/stack | solution.py:261
  60.8 1.6 %collective-permute-start.17 = (bf16[4,32,16,256]{3,2,1,0:T(8,128)(2,1)S(1)}, bf16[4,32,16,256]{3,2,1,0:T(8,128)(2,1)S(1)}, u32[]{:S(2)}, u32[]{:S(2)}) collective-permute-start(bf16[4,32,16,256]{3,2,1,0:T(8,128)(2,1)S(1)} %pad_maximum_fusion.1), channel_id=1, source_target_pairs={{0,16},{16,0},{1,17},{17,1},{2,18},{18,2},{3,19},{19,3},{4,20},{20... | collective-permute-start | bytes 3145736 | tf_op jit(solution)/shard_map/ppermute | solution.py:213
  62.4 0.3 collective-permute-start.6
  62.7 5.2 %collective-permute-done.13.rest_7_.rest_10_.rest_4_ = bf16[64,16,256]{2,1,0:T(8,128)(2,1)S(1)} collective-permute-done((bf16[64,16,256]{2,1,0:T(8,128)(2,1)}, bf16[64,16,256]{2,1,0:T(8,128)(2,1)S(1)}, u32[]{:S(2)}, u32[]{:S(2)}) %collective-permute-start.13) | collective-permute-done | bytes 524320 | tf_op jit(solution)/shard_map/ppermute | solution.py:210
  67.9 1.5 %collective-permute-start.5 = (bf16[4,2,16,256]{3,2,1,0:T(8,128)(2,1)S(1)}, bf16[4,2,16,256]{3,2,1,0:T(8,128)(2,1)S(1)}, u32[]{:S(2)}, u32[]{:S(2)}) collective-permute-start(bf16[4,2,16,256]{3,2,1,0:T(8,128)(2,1)S(1)} %get-tuple-element.80), channel_id=1, source_target_pairs={{0,2},{1,3},{2,0},{3,1},{4,6},{5,7},{6,4},{7,5},{8,10},{9,11},{10,... | collective-permute-start | bytes 196616 | tf_op jit(solution)/shard_map/ppermute | solution.py:210
  69.4 0.6 collective-permute-start.15
  70.0 2.2 %collective-permute-done.5 = bf16[4,2,16,256]{3,2,1,0:T(8,128)(2,1)S(1)} collective-permute-done((bf16[4,2,16,256]{3,2,1,0:T(8,128)(2,1)S(1)}, bf16[4,2,16,256]{3,2,1,0:T(8,128)(2,1)S(1)}, u32[]{:S(2)}, u32[]{:S(2)}) %collective-permute-start.5) | collective-permute-done | bytes 65568 | tf_op jit(solution)/shard_map/ppermute | solution.py:210
  72.1 1.3 %collective-permute-done.4 = bf16[4,2,16,256]{3,2,1,0:T(8,128)(2,1)S(1)} collective-permute-done((bf16[4,2,16,256]{3,2,1,0:T(8,128)(2,1)S(1)}, bf16[4,2,16,256]{3,2,1,0:T(8,128)(2,1)S(1)}, u32[]{:S(2)}, u32[]{:S(2)}) %collective-permute-start.4) | collective-permute-done | bytes 65568 | tf_op jit(solution)/shard_map/ppermute | solution.py:210
  73.4 1.0 collective-permute-start.18
  74.4 18.4 %collective-permute-done.10.rest_3_ = bf16[4,16,16,256]{3,2,1,0:T(8,128)(2,1)S(1)} collective-permute-done((bf16[4,16,16,256]{3,2,1,0:T(8,128)(2,1)S(1)}, bf16[4,16,16,256]{3,2,1,0:T(8,128)(2,1)S(1)}, u32[]{:S(2)}, u32[]{:S(2)}) %collective-permute-start.10) | collective-permute-done | bytes 524320 | tf_op jit(solution)/shard_map/ppermute | solution.py:210
  92.8 1.5 %collective-permute-start.19 = (bf16[4,16,16,256]{3,2,1,0:T(8,128)(2,1)S(1)}, bf16[4,16,16,256]{3,2,1,0:T(8,128)(2,1)S(1)}, u32[]{:S(2)}, u32[]{:S(2)}) collective-permute-start(bf16[4,16,16,256]{3,2,1,0:T(8,128)(2,1)S(1)} %collective-permute-done.10.rest_3_), channel_id=1, source_target_pairs={{0,16},{16,0},{1,17},{17,1},{2,18},{18,2},{3,19},{19,3},{4,20},{20... | collective-permute-start | bytes 1572872 | tf_op jit(solution)/shard_map/ppermute | solution.py:213
  94.5 3.9 %shard_map.57 = (bf16[256,16,256]{2,1,0:T(8,128)(2,1)S(1)}, bf16[256,16,256]{2,1,0:T(8,128)(2,1)S(1)}, bf16[256,256]{1,0:T(8,128)(2,1)S(1)}, bf16[256,256]{1,0:T(8,128)(2,1)S(1)}, bf16[256,256]{1,0:T(8,128)(2,1)S(1)}) custom-call(s32[16]{0:T(128)S(1)} %copy-done.8, s32[4,4,16]{2,1,0:T(4,128)S(1)} %bitcast.32, bf16[512,256]{1,0:T(8,128)(2,1)S(1)} %bitcast.27, ...), custom_call_target="tpu_custom_call" | custom-call | flops 1073741824 | bytes 6291456 | tf_op jit(solution)/shard_map/pallas_call | solution.py:324
  98.3 5.3 %collective-permute-done.18.rest_5_ = bf16[4,16,16,256]{3,2,1,0:T(8,128)(2,1)S(1)} collective-permute-done((bf16[4,16,16,256]{3,2,1,0:T(8,128)(2,1)S(1)}, bf16[4,16,16,256]{3,2,1,0:T(8,128)(2,1)S(1)}, u32[]{:S(2)}, u32[]{:S(2)}) %collective-permute-start.18) | collective-permute-done | bytes 524320 | tf_op jit(solution)/shard_map/ppermute | solution.py:210
  103.7 1.5 %collective-permute-start.20 = (bf16[4,16,16,256]{3,2,1,0:T(8,128)(2,1)S(1)}, bf16[4,16,16,256]{3,2,1,0:T(8,128)(2,1)S(1)}, u32[]{:S(2)}, u32[]{:S(2)}) collective-permute-start(bf16[4,16,16,256]{3,2,1,0:T(8,128)(2,1)S(1)} %collective-permute-done.18.rest_5_), channel_id=1, source_target_pairs={{0,16},{16,0},{1,17},{17,1},{2,18},{18,2},{3,19},{19,3},{4,20},{20... | collective-permute-start | bytes 1572872 | tf_op jit(solution)/shard_map/ppermute | solution.py:213
  105.2 0.8 collective-permute-done.19.rest_6_
  106.0 5.5 %shard_map.58 = (bf16[256,32,256]{2,1,0:T(8,128)(2,1)S(1)}, bf16[256,32,256]{2,1,0:T(8,128)(2,1)S(1)}) custom-call(bf16[256,256]{1,0:T(8,128)(2,1)S(1)} %get-tuple-element.68.occ_ref, bf16[256,256]{1,0:T(8,128)(2,1)S(1)} %get-tuple-element.69.vir_ref, bf16[256,256]{1,0:T(8,128)(2,1)S(1)} %get-tuple-element.70.keep_ref, bf16[64,16,256]{2,1,0:T(8,128)(2,1)S(1)} %copy-done, ...), custom_call_target="tpu_custom_call" | custom-call | flops 2147483648 | bytes 12582912 | tf_op jit(solution)/shard_map/pallas_call | solution.py:336
  111.5 5.7 %collective-permute-done.20.rest_6_ = bf16[4,16,16,256]{3,2,1,0:T(8,128)(2,1)S(1)} collective-permute-done((bf16[4,16,16,256]{3,2,1,0:T(8,128)(2,1)S(1)}, bf16[4,16,16,256]{3,2,1,0:T(8,128)(2,1)S(1)}, u32[]{:S(2)}, u32[]{:S(2)}) %collective-permute-start.20) | collective-permute-done | bytes 524320 | tf_op jit(solution)/shard_map/ppermute | solution.py:213
  117.2 5.8 %shard_map.59 = f32[64,64]{1,0:T(8,128)} custom-call(bf16[256,256]{1,0:T(8,128)(2,1)S(1)} %get-tuple-element.68.occ_ref, bf16[256,256]{1,0:T(8,128)(2,1)S(1)} %get-tuple-element.69.vir_ref, bf16[256,256]{1,0:T(8,128)(2,1)S(1)} %get-tuple-element.70.keep_ref, bf16[256,16,256]{2,1,0:T(8,128)(2,1)S(1)} %get-tuple-element.71.mask_a, ...), custom_call_target="tpu_custom_call" | custom-call | flops 1073741824 | bytes 16777216 | tf_op jit(solution)/shard_map/pallas_call | solution.py:346
  (35 shorter events, 0.1 us)
Async XLA Ops:
  2.6 18.6 %copy-start.9 = (bf16[16,256]{1,0:T(8,128)(2,1)S(1)}, bf16[16,256]{1,0:T(8,128)(2,1)}, u32[]{:S(2)}) copy-start(bf16[16,256]{1,0:T(8,128)(2,1)} %vir_ref.3) | copy-start | bytes 24580
  2.6 18.6 %copy-start.10 = (bf16[16,256]{1,0:T(8,128)(2,1)S(1)}, bf16[16,256]{1,0:T(8,128)(2,1)}, u32[]{:S(2)}) copy-start(bf16[16,256]{1,0:T(8,128)(2,1)} %occ_ref.3) | copy-start | bytes 24580
  2.6 12.8 %collective-permute-start = (bf16[34,16,256]{2,1,0:T(8,128)(2,1)}, bf16[34,16,256]{2,1,0:T(8,128)(2,1)S(1)}, u32[]{:S(2)}, u32[]{:S(2)}) collective-permute-start(bf16[34,16,256]{2,1,0:T(8,128)(2,1)} %get-tuple-element.43), channel_id=1, source_target_pairs={{0,4},{1,5},{2,6},{3,7},{4,8},{5,9},{6,10},{7,11},{8,12},{9,13},{1... | collective-permute-start | bytes 835592 | tf_op jit(solution)/shard_map/ppermute | solution.py:210
  5.7 13.7 %collective-permute-start.7 = (bf16[32,16,256]{2,1,0:T(8,128)(2,1)}, bf16[32,16,256]{2,1,0:T(8,128)(2,1)S(1)}, u32[]{:S(2)}, u32[]{:S(2)}) collective-permute-start(bf16[32,16,256]{2,1,0:T(8,128)(2,1)} %get-tuple-element.51), channel_id=1, source_target_pairs={{0,5},{1,4},{2,7},{3,6},{4,9},{5,8},{6,11},{7,10},{8,13},{9,12},{1... | collective-permute-start | bytes 786440 | tf_op jit(solution)/shard_map/ppermute | solution.py:210
  15.4 11.7 %collective-permute-start.1 = (bf16[32,16,256]{2,1,0:T(8,128)(2,1)}, bf16[32,16,256]{2,1,0:T(8,128)(2,1)S(1)}, u32[]{:S(2)}, u32[]{:S(2)}) collective-permute-start(bf16[32,16,256]{2,1,0:T(8,128)(2,1)} %get-tuple-element.48), channel_id=1, source_target_pairs={{0,7},{1,6},{2,5},{3,4},{4,11},{5,10},{6,9},{7,8},{8,15},{9,14},{1... | collective-permute-start | bytes 786440 | tf_op jit(solution)/shard_map/ppermute | solution.py:210
  19.3 13.0 %collective-permute-start.8 = (bf16[32,16,256]{2,1,0:T(8,128)(2,1)}, bf16[32,16,256]{2,1,0:T(8,128)(2,1)S(1)}, u32[]{:S(2)}, u32[]{:S(2)}) collective-permute-start(bf16[32,16,256]{2,1,0:T(8,128)(2,1)} %get-tuple-element.55), channel_id=1, source_target_pairs={{0,6},{1,7},{2,4},{3,5},{4,10},{5,11},{6,8},{7,9},{8,14},{9,15},{1... | collective-permute-start | bytes 786440 | tf_op jit(solution)/shard_map/ppermute | solution.py:210
  21.2 41.2 %collective-permute-start.3 = (bf16[2,16,256]{2,1,0:T(8,128)(2,1)S(1)}, bf16[2,16,256]{2,1,0:T(8,128)(2,1)S(1)}, u32[]{:S(2)}, u32[]{:S(2)}) collective-permute-start(bf16[2,16,256]{2,1,0:T(8,128)(2,1)S(1)} %get-tuple-element.82), channel_id=1, source_target_pairs={{0,8},{1,9},{2,10},{3,11},{4,12},{5,13},{6,14},{7,15},{8,0},{9,1},... | collective-permute-start | bytes 49160 | tf_op jit(solution)/shard_map/ppermute | solution.py:210
  22.3 27.1 %all-to-all-start = ((bf16[4,32,16,256]{3,2,1,0:T(8,128)(2,1)}), bf16[4,32,16,256]{3,2,1,0:T(8,128)(2,1)}, u32[]{:S(2)}, u32[]{:S(2)}) async-start(bf16[4,32,16,256]{3,2,1,0:T(8,128)(2,1)} %get-tuple-element.52), calls=%async_computation | async-start | bytes 2097152 | tf_op jit(solution)/shard_map/all_to_all | solution.py:201
  26.6 67.8 %copy-start = (bf16[64,16,256]{2,1,0:T(8,128)(2,1)S(1)}, bf16[64,16,256]{2,1,0:T(8,128)(2,1)}, u32[]{:S(2)}) copy-start(bf16[64,16,256]{2,1,0:T(8,128)(2,1)} %get-tuple-element.50.rest_0_) | copy-start | bytes 1572868
  26.6 67.8 %copy-start.7 = (s32[16,4,4]{0,2,1:T(4,128)S(1)}, s32[16,4,4]{0,2,1:T(4,128)}, u32[]{:S(2)}) copy-start(s32[16,4,4]{0,2,1:T(4,128)} %param.8) | copy-start | bytes 3076
  26.6 67.8 %copy-start.8 = (s32[16]{0:T(128)S(1)}, s32[16]{0:T(128)}, u32[]{:S(2)}) copy-start(s32[16]{0:T(128)} %order_ref.5) | copy-start | bytes 196
  27.0 20.5 %copy-start.1 = (bf16[32,16,256]{2,1,0:T(8,128)(2,1)}, bf16[32,16,256]{2,1,0:T(8,128)(2,1)S(1)}, u32[]{:S(2)}) copy-start(bf16[32,16,256]{2,1,0:T(8,128)(2,1)S(1)} %collective-permute-done.1.rest_11_.rest_14_) | copy-start | bytes 786436
  27.1 10.7 %collective-permute-start.2 = (bf16[34,16,256]{2,1,0:T(8,128)(2,1)}, bf16[34,16,256]{2,1,0:T(8,128)(2,1)S(1)}, u32[]{:S(2)}, u32[]{:S(2)}) collective-permute-start(bf16[34,16,256]{2,1,0:T(8,128)(2,1)} %get-tuple-element.49), channel_id=1, source_target_pairs={{0,12},{1,13},{2,14},{3,15},{4,0},{5,1},{6,2},{7,3},{8,4},{9,5},{1... | collective-permute-start | bytes 835592 | tf_op jit(solution)/shard_map/ppermute | solution.py:210
  32.3 15.2 %copy-start.3 = (bf16[32,16,256]{2,1,0:T(8,128)(2,1)}, bf16[32,16,256]{2,1,0:T(8,128)(2,1)S(1)}, u32[]{:S(2)}) copy-start(bf16[32,16,256]{2,1,0:T(8,128)(2,1)S(1)} %collective-permute-done.8.rest_8_.rest_11_) | copy-start | bytes 786436
  32.4 11.9 %collective-permute-start.9 = (bf16[32,16,256]{2,1,0:T(8,128)(2,1)}, bf16[32,16,256]{2,1,0:T(8,128)(2,1)S(1)}, u32[]{:S(2)}, u32[]{:S(2)}) collective-permute-start(bf16[32,16,256]{2,1,0:T(8,128)(2,1)} %get-tuple-element.56), channel_id=1, source_target_pairs={{0,15},{1,14},{2,13},{3,12},{4,3},{5,2},{6,1},{7,0},{8,7},{9,6},{1... | collective-permute-start | bytes 786440 | tf_op jit(solution)/shard_map/ppermute | solution.py:210
  37.7 9.8 %collective-permute-start.11 = (bf16[64,16,256]{2,1,0:T(8,128)(2,1)}, bf16[64,16,256]{2,1,0:T(8,128)(2,1)S(1)}, u32[]{:S(2)}, u32[]{:S(2)}) collective-permute-start(bf16[64,16,256]{2,1,0:T(8,128)(2,1)} %get-tuple-element.59), channel_id=1, source_target_pairs={{0,1},{1,0},{2,3},{3,2},{4,5},{5,4},{6,7},{7,6},{8,9},{9,8},{10,11... | collective-permute-start | bytes 1572872 | tf_op jit(solution)/shard_map/ppermute | solution.py:210
  39.1 66.1 %collective-permute-start.16 = (bf16[4,32,16,256]{3,2,1,0:T(8,128)(2,1)}, bf16[4,32,16,256]{3,2,1,0:T(8,128)(2,1)S(1)}, u32[]{:S(2)}, u32[]{:S(2)}) collective-permute-start(bf16[4,32,16,256]{3,2,1,0:T(8,128)(2,1)} %pad_maximum_fusion), channel_id=1, source_target_pairs={{0,16},{16,0},{1,17},{17,1},{2,18},{18,2},{3,19},{19,3},{4,20},{20... | collective-permute-start | bytes 3145736 | tf_op jit(solution)/shard_map/ppermute | solution.py:213
  44.3 3.2 %copy-start.5 = (bf16[32,16,256]{2,1,0:T(8,128)(2,1)}, bf16[32,16,256]{2,1,0:T(8,128)(2,1)S(1)}, u32[]{:S(2)}) copy-start(bf16[32,16,256]{2,1,0:T(8,128)(2,1)S(1)} %collective-permute-done.9.rest_12_.rest_15_) | copy-start | bytes 786436
  44.3 9.5 %collective-permute-start.12 = (bf16[32,16,256]{2,1,0:T(8,128)(2,1)}, bf16[32,16,256]{2,1,0:T(8,128)(2,1)}, u32[]{:S(2)}, u32[]{:S(2)}) collective-permute-start(bf16[32,16,256]{2,1,0:T(8,128)(2,1)} %get-tuple-element.61), channel_id=1, source_target_pairs={{0,13},{1,12},{2,15},{3,14},{4,1},{5,0},{6,3},{7,2},{8,5},{9,4},{1... | collective-permute-start | bytes 786440 | tf_op jit(solution)/shard_map/ppermute | solution.py:210
  46.8 12.6 %collective-permute-start.14 = (bf16[32,16,256]{2,1,0:T(8,128)(2,1)}, bf16[32,16,256]{2,1,0:T(8,128)(2,1)}, u32[]{:S(2)}, u32[]{:S(2)}) collective-permute-start(bf16[32,16,256]{2,1,0:T(8,128)(2,1)} %get-tuple-element.65), channel_id=1, source_target_pairs={{0,14},{1,15},{2,12},{3,13},{4,2},{5,3},{6,0},{7,1},{8,6},{9,7},{1... | collective-permute-start | bytes 786440 | tf_op jit(solution)/shard_map/ppermute | solution.py:210
  47.5 20.3 %collective-permute-start.13 = (bf16[64,16,256]{2,1,0:T(8,128)(2,1)}, bf16[64,16,256]{2,1,0:T(8,128)(2,1)S(1)}, u32[]{:S(2)}, u32[]{:S(2)}) collective-permute-start(bf16[64,16,256]{2,1,0:T(8,128)(2,1)} %get-tuple-element.63), channel_id=1, source_target_pairs={{0,2},{1,3},{2,0},{3,1},{4,6},{5,7},{6,4},{7,5},{8,10},{9,11},{10,... | collective-permute-start | bytes 1572872 | tf_op jit(solution)/shard_map/ppermute | solution.py:210
  49.4 20.0 %copy-start.11 = (bf16[64,16,256]{2,1,0:T(8,128)(2,1)S(1)}, bf16[64,16,256]{2,1,0:T(8,128)(2,1)}, u32[]{:S(2)}) copy-start(bf16[64,16,256]{2,1,0:T(8,128)(2,1)} %get-tuple-element.67) | copy-start | bytes 1572868
  49.4 45.0 %copy-start.2 = (bf16[32,16,256]{2,1,0:T(8,128)(2,1)S(1)}, bf16[32,16,256]{2,1,0:T(8,128)(2,1)}, u32[]{:S(2)}) copy-start(bf16[32,16,256]{2,1,0:T(8,128)(2,1)} %copy-done.1) | copy-start | bytes 786436
  49.4 45.1 %copy-start.4 = (bf16[32,16,256]{2,1,0:T(8,128)(2,1)S(1)}, bf16[32,16,256]{2,1,0:T(8,128)(2,1)}, u32[]{:S(2)}) copy-start(bf16[32,16,256]{2,1,0:T(8,128)(2,1)} %copy-done.3) | copy-start | bytes 786436
  49.4 45.1 %copy-start.6 = (bf16[32,16,256]{2,1,0:T(8,128)(2,1)S(1)}, bf16[32,16,256]{2,1,0:T(8,128)(2,1)}, u32[]{:S(2)}) copy-start(bf16[32,16,256]{2,1,0:T(8,128)(2,1)} %copy-done.5) | copy-start | bytes 786436
  53.8 39.1 %collective-permute-start.10 = (bf16[4,16,16,256]{3,2,1,0:T(8,128)(2,1)S(1)}, bf16[4,16,16,256]{3,2,1,0:T(8,128)(2,1)S(1)}, u32[]{:S(2)}, u32[]{:S(2)}) collective-permute-start(bf16[4,16,16,256]{3,2,1,0:T(8,128)(2,1)S(1)} %get-tuple-element.57), channel_id=1, source_target_pairs={{0,8},{1,9},{2,10},{3,11},{4,12},{5,13},{6,14},{7,15},{8,0},{9,1},... | collective-permute-start | bytes 1572872 | tf_op jit(solution)/shard_map/ppermute | solution.py:210
  60.8 45.2 %collective-permute-start.17 = (bf16[4,32,16,256]{3,2,1,0:T(8,128)(2,1)S(1)}, bf16[4,32,16,256]{3,2,1,0:T(8,128)(2,1)S(1)}, u32[]{:S(2)}, u32[]{:S(2)}) collective-permute-start(bf16[4,32,16,256]{3,2,1,0:T(8,128)(2,1)S(1)} %pad_maximum_fusion.1), channel_id=1, source_target_pairs={{0,16},{16,0},{1,17},{17,1},{2,18},{18,2},{3,19},{19,3},{4,20},{20... | collective-permute-start | bytes 3145736 | tf_op jit(solution)/shard_map/ppermute | solution.py:213
  62.4 7.0 %collective-permute-start.6 = (bf16[4,2,16,256]{3,2,1,0:T(8,128)(2,1)S(1)}, bf16[4,2,16,256]{3,2,1,0:T(8,128)(2,1)S(1)}, u32[]{:S(2)}, u32[]{:S(2)}) collective-permute-start(bf16[4,2,16,256]{3,2,1,0:T(8,128)(2,1)S(1)} %get-tuple-element.80), channel_id=1, source_target_pairs={{0,3},{1,2},{2,1},{3,0},{4,7},{5,6},{6,5},{7,4},{8,11},{9,10},{10,... | collective-permute-start | bytes 196616 | tf_op jit(solution)/shard_map/ppermute | solution.py:210
  67.9 4.3 %collective-permute-start.5 = (bf16[4,2,16,256]{3,2,1,0:T(8,128)(2,1)S(1)}, bf16[4,2,16,256]{3,2,1,0:T(8,128)(2,1)S(1)}, u32[]{:S(2)}, u32[]{:S(2)}) collective-permute-start(bf16[4,2,16,256]{3,2,1,0:T(8,128)(2,1)S(1)} %get-tuple-element.80), channel_id=1, source_target_pairs={{0,2},{1,3},{2,0},{3,1},{4,6},{5,7},{6,4},{7,5},{8,10},{9,11},{10,... | collective-permute-start | bytes 196616 | tf_op jit(solution)/shard_map/ppermute | solution.py:210
  69.4 25.0 %collective-permute-start.15 = (bf16[64,16,256]{2,1,0:T(8,128)(2,1)S(1)}, bf16[64,16,256]{2,1,0:T(8,128)(2,1)S(1)}, u32[]{:S(2)}, u32[]{:S(2)}) collective-permute-start(bf16[64,16,256]{2,1,0:T(8,128)(2,1)S(1)} %copy-done.11), channel_id=1, source_target_pairs={{0,3},{1,2},{2,1},{3,0},{4,7},{5,6},{6,5},{7,4},{8,11},{9,10},{10,... | collective-permute-start | bytes 1572872 | tf_op jit(solution)/shard_map/ppermute | solution.py:210
  72.1 1.3 %collective-permute-start.4 = (bf16[4,2,16,256]{3,2,1,0:T(8,128)(2,1)S(1)}, bf16[4,2,16,256]{3,2,1,0:T(8,128)(2,1)S(1)}, u32[]{:S(2)}, u32[]{:S(2)}) collective-permute-start(bf16[4,2,16,256]{3,2,1,0:T(8,128)(2,1)S(1)} %get-tuple-element.80), channel_id=1, source_target_pairs={{0,1},{1,0},{2,3},{3,2},{4,5},{5,4},{6,7},{7,6},{8,9},{9,8},{10,11... | collective-permute-start | bytes 196616 | tf_op jit(solution)/shard_map/ppermute | solution.py:210
  73.4 30.3 %collective-permute-start.18 = (bf16[4,16,16,256]{3,2,1,0:T(8,128)(2,1)S(1)}, bf16[4,16,16,256]{3,2,1,0:T(8,128)(2,1)S(1)}, u32[]{:S(2)}, u32[]{:S(2)}) collective-permute-start(bf16[4,16,16,256]{3,2,1,0:T(8,128)(2,1)S(1)} %get-tuple-element.72), channel_id=1, source_target_pairs={{0,8},{1,9},{2,10},{3,11},{4,12},{5,13},{6,14},{7,15},{8,0},{9,1},... | collective-permute-start | bytes 1572872 | tf_op jit(solution)/shard_map/ppermute | solution.py:210
  92.8 13.1 %collective-permute-start.19 = (bf16[4,16,16,256]{3,2,1,0:T(8,128)(2,1)S(1)}, bf16[4,16,16,256]{3,2,1,0:T(8,128)(2,1)S(1)}, u32[]{:S(2)}, u32[]{:S(2)}) collective-permute-start(bf16[4,16,16,256]{3,2,1,0:T(8,128)(2,1)S(1)} %collective-permute-done.10.rest_3_), channel_id=1, source_target_pairs={{0,16},{16,0},{1,17},{17,1},{2,18},{18,2},{3,19},{19,3},{4,20},{20... | collective-permute-start | bytes 1572872 | tf_op jit(solution)/shard_map/ppermute | solution.py:213
  103.7 13.5 %collective-permute-start.20 = (bf16[4,16,16,256]{3,2,1,0:T(8,128)(2,1)S(1)}, bf16[4,16,16,256]{3,2,1,0:T(8,128)(2,1)S(1)}, u32[]{:S(2)}, u32[]{:S(2)}) collective-permute-start(bf16[4,16,16,256]{3,2,1,0:T(8,128)(2,1)S(1)} %collective-permute-done.18.rest_5_), channel_id=1, source_target_pairs={{0,16},{16,0},{1,17},{17,1},{2,18},{18,2},{3,19},{19,3},{4,20},{20... | collective-permute-start | bytes 1572872 | tf_op jit(solution)/shard_map/ppermute | solution.py:213
